TPU v7x, 256 devices: a whole 4x4x8 slice. The times are simulated.
256 devices in a mesh: rep: 8 (over y_lo, x), row: 32 (over z, y_hi, core).
Axes of the slice: x: 4, y: 4 (y_hi: 2, y_lo: 2; y = y_hi * 2 + y_lo), z: 8, core: 2. Of those that a mesh axis runs over, the one named last changes fastest.
Arguments:
- features: bfloat16 [8, 1024, 16384], P('rep', 'row'), may hold values from -6 to 6
- tile_tgt: int32 [8, 32, 8, 4], P('rep', 'row'), may hold values from 0 to 7
- tile_src: int32 [8, 32, 8, 4], P('rep', 'row'), may hold values from 0 to 127
- tile_count: int32 [8, 32, 8], P('rep', 'row'), may hold values from 1 to 4, as said below
- tile_vals: bfloat16 [8, 32, 8, 4, 128, 128], P('rep', 'row'), may hold values from -0.4375 to 0.4375
- weight: bfloat16 [1024, 1024], P('row'), may hold values from -0.1875 to 0.1875
- cotangent: bfloat16 [262144, 1024], P(('rep', 'row')), may hold values from -6 to 6
Outputs:
- activations: bfloat16 [262144, 1024], P(('rep', 'row'))
- weight_grad: float32 [1024, 1024], P('row')
Inputs may be any that keep to these rules, and one draw needn't show every extreme that they name: `tile_count`: slots at or past a device's count in a section are ignored. In every section some device has exactly 4 live slots.
All inputs are finite; a program needn't handle non-finite values.
Results may differ from a plain program's by a relative error of at most 0.015.
Values may be sent and summed in bfloat16 or wider, within the bound.
No kernel may reach another device: no remote copies, remote signals or barrier semaphores. Data moves between devices by JAX's collectives and lax.ppermute only.
A program may use at most 128 MiB of HBM per device.

v0:
```python
import math

import jax
import jax.numpy as jnp
from jax import lax
from jax.sharding import PartitionSpec as P


def silu_grad(preact):
    sigmoid_val = jax.nn.sigmoid(preact)
    return sigmoid_val * (1.0 + preact * (1.0 - sigmoid_val))


def per_device(features, tile_tgt, tile_src, tile_count, tile_vals, weight, cotangent):
    section_total = lax.axis_size("rep")
    group_size = lax.axis_size("row")
    block_size = tile_vals.shape[-1]
    col_width = features.shape[1]
    panel_rows = features.shape[2]
    feat_width = col_width * group_size
    tgt_rows = cotangent.shape[0]
    num_blocks = tgt_rows // block_size
    slot_count = tile_tgt.shape[-1]
    targets = tile_tgt[0, 0]
    sources = tile_src[0, 0]
    counts = tile_count[0, 0]
    values = tile_vals[0, 0]
    asked = lax.all_gather(sources[None], "row", axis=0, tiled=True)
    asked = jnp.transpose(asked, (1, 0, 2))
    wanted = lax.all_to_all(asked, "rep", split_axis=0, concat_axis=0, tiled=True)
    shard_blocks = features[0].reshape(col_width, panel_rows // block_size, block_size)
    picked = jnp.take(shard_blocks, wanted.reshape(-1), axis=1)
    picked = picked.reshape(col_width, section_total, group_size, slot_count, block_size)
    arrived = lax.all_to_all(
        lax.all_to_all(picked, "rep", split_axis=1, concat_axis=1, tiled=True),
        "row",
        split_axis=2,
        concat_axis=0,
        tiled=True,
    )
    columns_in = arrived.reshape(feat_width, section_total, slot_count, block_size)
    contrib = jnp.einsum("smij,dsmj->smid", values, columns_in, preferred_element_type=jnp.float32)
    block_ids = jnp.arange(num_blocks, dtype=jnp.int32)[:, None, None]
    slot_ids = jnp.arange(slot_count, dtype=jnp.int32)[None, None, :]
    select = ((targets[None] == block_ids) & (slot_ids < counts[None, :, None])).astype(jnp.float32)
    aggregate = jnp.einsum("bsm,smid->bid", select, contrib)
    mixed = aggregate.reshape(tgt_rows, feat_width).astype(jnp.bfloat16)
    columns = mixed
    preact = jnp.dot(
        columns,
        lax.all_gather(weight, "row", axis=0, tiled=True),
        preferred_element_type=jnp.float32,
    )
    activations = jax.nn.silu(preact).astype(jnp.bfloat16)
    dpre = (cotangent.astype(jnp.float32) * silu_grad(preact)).astype(jnp.bfloat16)
    columns = mixed
    partial_rows = lax.psum_scatter(
        lax.dot_general(
            columns, dpre, (((0,), (0,)), ((), ())), preferred_element_type=jnp.float32
        ),
        "row",
        scatter_dimension=0,
        tiled=True,
    )
    summed = lax.psum(partial_rows, "rep")
    total_rows = tgt_rows * section_total * group_size
    weight_grad = summed / math.sqrt(total_rows)
    return (activations, weight_grad)


def solution(mesh):
    in_specs = (
        P("rep", "row", None),
        P("rep", "row", None, None),
        P("rep", "row", None, None),
        P("rep", "row", None),
        P("rep", "row", None, None, None, None),
        P("row", None),
        P(("rep", "row"), None),
    )
    out_specs = (P(("rep", "row"), None), P("row", None))
    return jax.shard_map(
        per_device, mesh=mesh, in_specs=in_specs, out_specs=out_specs, check_vma=False
    )
```

profile of v0, /device:TPU:2, one launch (start us, length us, event | category | flops | bytes accessed | tf_op | source)
XLA Modules:
  0.0 654.7 jit_solution(11917496833676300576)
XLA Ops:
  7.2 0.0 copy-start
  7.2 45.4 %all-gather = s32[32,1,8,4]{2,3,1,0:T(4,128)S(1)} all-gather(s32[1,1,8,4]{2,3,1,0:T(4,128)} %param.9), channel_id=2, replica_groups=mesh['rep'=8,'row'=32] {'row'}, dimensions={0}, use_global_device_ids=true | all-gather | bytes 4224 | tf_op jit(solution)/shard_map/all_gather | solution.py:28
  52.6 0.1 copy.19
  52.7 0.7 reshape.89
  53.4 4.9 all-to-all-start
  58.3 1.5 copy.29
  59.8 0.7 copy.22
  60.5 2.5 all-to-all-done
  62.9 0.5 broadcast.51
  63.4 0.7 reduce
  64.1 0.1 reshape.90
  64.2 0.1 copy.21
  64.3 0.1 reshape.76
  64.5 0.2 copy.20
  64.6 9.9 %gather_fusion = bf16[1024,32,128]{2,1,0:T(8,128)(2,1)} fusion(bf16[32,128,128]{2,0,1:T(8,128)(2,1)S(1)} %copy.22, s32[1024]{0:T(1024)S(1)} %broadcast_clamp_fusion), kind=kCustom, calls=%fused_computation | custom fusion | bytes 16781312 | tf_op jit(solution)/shard_map/jit(_take)/gather | solution.py:32
  74.5 9.0 %copy_select_fusion = bf16[32,8,32,4,128]{4,3,0,2,1:T(4,128)(2,1)S(1)} fusion(bf16[32,8,32,4,128]{4,0,3,2,1:T(8,128)(2,1)} %bitcast.36, pred[8,32,4]{2,1,0:T(8,128)(4,1)S(1)} %copy.20), kind=kLoop, calls=%fused_computation.3 | loop fusion | flops 4194304 | bytes 16778240 | tf_op jit(solution)/shard_map/jit(_take)/select_n | solution.py:32
  83.5 97.4 %all_to_all.25 = bf16[32,8,32,4,128]{4,3,0,2,1:T(4,128)(2,1)} all-to-all(bf16[32,8,32,4,128]{4,3,0,2,1:T(4,128)(2,1)S(1)} %copy_select_fusion), channel_id=1, replica_groups=mesh['rep'=8,'row'=32] {'rep'}, dimensions={1} | all-to-all | bytes 16777216 | tf_op jit(solution)/shard_map/all_to_all | solution.py:35
  180.9 22.2 %copy.24 = bf16[32,8,32,4,128]{4,1,3,0,2:T(8,128)(2,1)} copy(bf16[32,8,32,4,128]{4,3,0,2,1:T(4,128)(2,1)} %all_to_all.25) | data formatting | bytes 16777216 | tf_op jit(solution)/shard_map/all_to_all | solution.py:35
  203.1 0.0 copy-start.4
  203.1 5.1 all-to-all-start.2
  208.2 0.0 all-gather.3.cloned.1.call-start
  208.3 0.7 all-gather.3.cloned.1.call-update
  209.0 0.0 reduce-scatter.2.cloned.1.call-start
  209.0 0.0 copy-done.4
  209.0 193.1 %all-to-all-done.2 = bf16[32,8,32,4,128]{4,1,3,0,2:T(8,128)(2,1)} async-done(((bf16[32,8,32,4,128]{4,1,3,0,2:T(8,128)(2,1)}), bf16[32,8,32,4,128]{4,1,3,0,2:T(8,128)(2,1)}, u32[]{:S(2)}, u32[]{:S(2)}) %all-to-all-start.2) | async-done | bytes 8388640 | tf_op jit(solution)/shard_map/all_to_all | solution.py:34
  402.2 0.0 copy-done
  402.2 11.7 %convolution_bitcast_fusion = bf16[8,4,128,1024]{2,3,1,0:T(8,128)(2,1)} fusion(bf16[1024,8,4,128]{3,1,2,0:T(8,128)(2,1)} %bitcast.10, bf16[1,1,8,4,128,128]{5,4,3,2,1,0:T(8,128)(2,1)S(1)} %copy-done), kind=kOutput, calls=%fused_computation.1 | convolution fusion | flops 1073741824 | bytes 17825792 | tf_op jit(solution)/shard_map/smij,dsmj->smid/dot_general | solution.py:42
  413.8 0.0 copy-start.2
  413.8 12.4 %copy.26 = bf16[8,4,128,1024]{3,0,1,2:T(8,128)(2,1)} copy(bf16[8,4,128,1024]{2,3,1,0:T(8,128)(2,1)} %convolution_bitcast_fusion) | data formatting | bytes 16777216 | tf_op jit(solution)/shard_map/smij,dsmj->smid/dot_general | solution.py:42
  426.3 0.0 copy-done.2
  426.3 8.3 %bitcast_convert_fusion = bf16[8,128,1024]{2,0,1:T(8,128)(2,1)S(1)} fusion(bf16[8,4,128,1024]{3,0,1,2:T(8,128)(2,1)} %copy.26, s32[8,4]{0,1:T(4,128)S(1)} %bitcast.45, pred[8,4]{0,1:T(4,128)(4,1)S(1)} %iota_compare_fusion.1), kind=kOutput, calls=%fused_computation.4 | convolution fusion | flops 67109376 | bytes 10485920 | tf_op jit(solution)/shard_map/bsm,smid->bid/dot_general | solution.py:46
  434.5 1.2 copy.27
  435.7 0.0 all-gather.3.cloned.1.call-done
  435.7 0.0 copy-start.3
  435.7 5.8 multiply_convert_fusion.1
  441.5 0.0 copy-done.3
  441.5 0.0 copy-start.1
  441.5 4.6 fusion.1
  446.2 0.0 reduce-scatter.2.cloned.1.call-update
  446.2 0.0 all-reduce.2.cloned.1.call-start
  446.2 123.2 %reduce-scatter.2.cloned.1.call-done = f32[32,1024]{1,0:T(8,128)} async-done(((f32[1024,1024]{1,0:T(8,128)}), f32[32,1024]{1,0:T(8,128)}) %reduce-scatter.2.cloned.1.call-update) | async-done | bytes 131088 | tf_op jit(solution)/shard_map/reduce_scatter | solution.py:57
  569.4 0.0 all-reduce.2.cloned.1.call-update
  569.5 77.1 %all-reduce.2.cloned.1.call-done = f32[32,1024]{1,0:T(8,128)} async-done(((f32[32,1024]{1,0:T(8,128)}), f32[32,1024]{1,0:T(8,128)}) %all-reduce.2.cloned.1.call-update) | async-done | bytes 131088 | tf_op jit(solution)/shard_map/psum | solution.py:65
  646.6 1.6 broadcast_multiply_fusion
  648.1 0.0 copy-done.1
  (4 shorter events, 0.0 us)
Async XLA Ops:
  7.2 395.0 %copy-start = (bf16[1,1,8,4,128,128]{5,4,3,2,1,0:T(8,128)(2,1)S(1)}, bf16[1,1,8,4,128,128]{5,4,3,2,1,0:T(8,128)(2,1)}, u32[]{:S(2)}) copy-start(bf16[1,1,8,4,128,128]{5,4,3,2,1,0:T(8,128)(2,1)} %param.11) | copy-start | bytes 3145732
  53.4 9.6 %all-to-all-start = ((s32[8,1,128]{2,1,0:T(1,128)}), s32[8,1,128]{2,1,0:T(1,128)S(1)}, u32[]{:S(2)}, u32[]{:S(2)}) async-start(s32[8,1,128]{2,1,0:T(1,128)} %reshape.89), calls=%async_computation | async-start | bytes 8192 | tf_op jit(solution)/shard_map/all_to_all | solution.py:30
  203.1 5.9 copy-start.4
  203.1 199.0 %all-to-all-start.2 = ((bf16[32,8,32,4,128]{4,1,3,0,2:T(8,128)(2,1)}), bf16[32,8,32,4,128]{4,1,3,0,2:T(8,128)(2,1)}, u32[]{:S(2)}, u32[]{:S(2)}) async-start(bf16[32,8,32,4,128]{4,1,3,0,2:T(8,128)(2,1)} %copy.24), calls=%async_computation.2 | async-start | bytes 16777216 | tf_op jit(solution)/shard_map/all_to_all | solution.py:34
  208.2 227.5 %all-gather.3.cloned.1.call-start = ((), (), s32[]{:S(2)}) async-start(), calls=%async_computation.4 | async-start | bytes 2162688 | tf_op jit(solution)/shard_map/all_gather | solution.py:51
  209.0 360.5 %reduce-scatter.2.cloned.1.call-start = ((), (), s32[]{:S(2)}) async-start(), calls=%async_computation.5 | async-start | bytes 4325376 | tf_op jit(solution)/shard_map/reduce_scatter | solution.py:57
  413.8 12.4 %copy-start.2 = (s32[1,1,8,4]{2,3,1,0:T(4,128)S(1)}, s32[1,1,8,4]{2,3,1,0:T(4,128)}, u32[]{:S(2)}) copy-start(s32[1,1,8,4]{2,3,1,0:T(4,128)} %param.8) | copy-start | bytes 388
  435.7 5.8 copy-start.3
  441.5 206.6 %copy-start.1 = (bf16[1,1,8,4,128,128]{5,4,3,2,1,0:T(8,128)(2,1)S(1)}, bf16[1,1,8,4,128,128]{5,4,3,2,1,0:T(8,128)(2,1)}, u32[]{:S(2)}) copy-start(bf16[1,1,8,4,128,128]{5,4,3,2,1,0:T(8,128)(2,1)} %param.11) | copy-start | bytes 3145732
  446.2 200.4 %all-reduce.2.cloned.1.call-start = ((), (), s32[]{:S(2)}) async-start(), calls=%async_computation.6 | async-start | bytes 262144 | tf_op jit(solution)/shard_map/psum | solution.py:65
Sparse Core Ops, SparseCore 0:
  211.9 101.0 all-gather.2
  446.3 123.0 reduce-scatter.1
  572.2 74.2 all-reduce.1
where the time goes:
time: 657 us; the launch traced here: 655 us
  waiting for transfers between devices  397 us (60%)
  blocking collectives  143 us (22%)
  local copies, waits for them, and re-layouts  49.6 us (8%)
  matrix products  30.4 us (5%)
  between operations  13.8 us (2%)
  other arithmetic  11.2 us (2%)
  starting transfers between devices  10.2 us (2%)
    all_to_all x1, waiting for transfers between devices, per_device(): lax.all_to_all(lax.all_to_all(picked, 'rep', split_axis=1, concat_axis=1,...  193 us
    reduce_scatter x1, waiting for transfers between devices, per_device(): lax.psum_scatter(lax.dot_general(columns, dpre, (((0,), (0,)), ((), ())),...  123 us
    all_to_all x1, blocking collectives, per_device(): lax.all_to_all(picked, 'rep', split_axis=1, concat_axis=1, tiled=True)  97.4 us
    psum x1, waiting for transfers between devices, per_device(): summed = lax.psum(partial_rows, 'rep')  77.1 us
    all_gather x1, blocking collectives, per_device(): asked = lax.all_gather(sources[None], 'row', axis=0, tiled=True)  45.4 us
    all_to_all x1, local copies, waits for them, and re-layouts, per_device(): lax.all_to_all(picked, 'rep', split_axis=1, concat_axis=1, tiled=True)  22.2 us
  transfers between devices with their start and end apart: 5, of which 4 were waited for; matrix products, arithmetic and copies ran while one was open for 5% of the time, Pallas kernels for 0%

commit v1 on v0

v1 whole, which is shorter than its diff:
```python
import functools
import math

import jax
import jax.numpy as jnp
from jax import lax
from jax.experimental import pallas as pl
from jax.experimental.pallas import tpu as pltpu
from jax.sharding import Mesh, PartitionSpec as P

REP = ("ylo", "x")
PLANE = ("ylo", "x", "yhi", "core")
CHIPS_XY = ("ylo", "x", "yhi")
ZN = 8
PARTS = ((0, 1, -1), (2, -2), (3, -3, 4))
VMEM = pl.BlockSpec(memory_space=pltpu.VMEM)
SMEM = pl.BlockSpec(memory_space=pltpu.SMEM)


def silu_grad(preact):
    sigmoid_val = jax.nn.sigmoid(preact)
    return sigmoid_val * (1.0 + preact * (1.0 - sigmoid_val))


def shift_z(value, step):
    return lax.ppermute(value, "z", [(i, (i + step) % ZN) for i in range(ZN)])


def exchange(value, axes):
    return lax.all_to_all(value, axes, split_axis=0, concat_axis=0, tiled=True)


def pick_kernel(pieces, block, wanted_ref, *refs):
    slices, out_ref = refs[:-1], refs[-1]
    slots = out_ref.shape[1]

    def one(step, carry):
        dest, slot = step // slots, step % slots
        start = pl.multiple_of(wanted_ref[dest, slot] * block, block)
        for ref, (place, low, high) in zip(slices, pieces):
            out_ref[dest, slot, place, low:high, :] = ref[:, pl.ds(start, block)]
        return carry

    lax.fori_loop(0, out_ref.shape[0] * slots, one, 0, unroll=4)


def pick(wanted, slices, pieces, places, rows, block):
    askers, slots = wanted.shape
    return pl.pallas_call(
        functools.partial(pick_kernel, pieces, block),
        out_shape=jax.ShapeDtypeStruct((askers, slots, places, rows, block), jnp.bfloat16),
        in_specs=[SMEM] + [VMEM] * len(slices),
        out_specs=VMEM,
        compiler_params=pltpu.CompilerParams(vmem_limit_bytes=40 * 2**20),
        cost_estimate=pl.CostEstimate(flops=0, bytes_accessed=len(slices) * 2**21, transcendentals=0),
    )(wanted, *slices)


def aggregate_kernel(zs_of, z_ref, tgt_ref, count_ref, vals_ref, *refs):
    parts, out_ref, acc = refs[: len(zs_of)], refs[-2], refs[-1]
    sections, slots, block, _ = vals_ref.shape
    rows = parts[0].shape[3]
    lanes = parts[0].shape[0] // sections
    acc[...] = jnp.zeros_like(acc)

    def one(step, carry):
        section, slot = step // slots, step % slots

        @pl.when(slot < count_ref[section])
        def _():
            column = pl.multiple_of(tgt_ref[section, slot] * block, block)
            tile = vals_ref[section, slot]
            for part, places in zip(parts, zs_of):
                for lane in range(lanes):
                    columns_in = part[section * lanes + lane, slot].reshape(len(places) * rows, block)
                    contrib = lax.dot_general(
                        columns_in, tile, (((1,), (1,)), ((), ())), preferred_element_type=jnp.float32
                    )
                    for index, place in enumerate(places):
                        low = pl.multiple_of((z_ref[place] * lanes + lane) * rows, rows)
                        acc[pl.ds(low, rows), pl.ds(column, block)] += contrib[index * rows : (index + 1) * rows]

        return carry

    lax.fori_loop(0, sections * slots, one, 0)
    out_ref[...] = acc[...].astype(out_ref.dtype)


def aggregate(zs, targets, counts, values, parts, zs_of, num_rows, num_feats):
    return pl.pallas_call(
        functools.partial(aggregate_kernel, zs_of),
        out_shape=jax.ShapeDtypeStruct((num_feats, num_rows), jnp.bfloat16),
        in_specs=[SMEM] * 3 + [VMEM] * (1 + len(parts)),
        out_specs=VMEM,
        scratch_shapes=[pltpu.VMEM((num_feats, num_rows), jnp.float32)],
        compiler_params=pltpu.CompilerParams(vmem_limit_bytes=48 * 2**20),
        cost_estimate=pl.CostEstimate(flops=10**9, bytes_accessed=12 * 2**20, transcendentals=0),
    )(zs, targets, counts, values, *parts)


def sum_over_devices(partial):
    rows, cols = partial.shape
    core, other = lax.axis_index("core"), 1 - lax.axis_index("core")
    halves = partial.reshape(16, 2, rows // 32, cols)
    gone = lax.dynamic_index_in_dim(halves, other, 1, keepdims=False).astype(jnp.bfloat16)
    kept = lax.dynamic_index_in_dim(halves, core, 1, keepdims=False)
    came = lax.ppermute(gone, "core", [(0, 1), (1, 0)])
    chip = (kept + came.astype(jnp.float32)).astype(jnp.bfloat16)
    chip = chip.reshape(8, 2, rows // 32, 8, cols // 8).transpose(3, 1, 0, 2, 4)
    chip = chip.reshape(16, 8, rows // 32, cols // 8)
    plane = exchange(chip, CHIPS_XY).astype(jnp.float32).sum(0)
    column = exchange(plane, "z").sum(0)
    whole = exchange(jnp.broadcast_to(column[None], (8, *column.shape)), REP)
    return whole.transpose(1, 0, 2).reshape(rows // 32, cols)


def per_device(features, tile_tgt, tile_src, tile_count, tile_vals, weight, cotangent):
    group_size = 32
    block_size = tile_vals.shape[-1]
    rows = features.shape[1]
    feat_width = rows * group_size
    tgt_rows = cotangent.shape[0]
    targets, sources, counts, values = tile_tgt[0, 0], tile_src[0, 0], tile_count[0, 0], tile_vals[0, 0]

    whole_weight = lax.all_gather(weight, ("z", "yhi", "core"), axis=0, tiled=True)
    wanted = exchange(jnp.repeat(sources, 4, axis=0)[:, None, :], PLANE)[:, 0]

    held = {0: features[0]}
    for step in range(1, 4):
        held[step] = shift_z(held[step - 1], 1)
        held[-step] = shift_z(held[1 - step], -1)
    up, down = shift_z(held[3][: rows // 2], 1), shift_z(held[-3][rows // 2 :], -1)

    arrived = []
    for distances in PARTS:
        slices, pieces = [], []
        for place, distance in enumerate(distances):
            if distance == 4:
                slices += [up, down]
                pieces += [(place, 0, rows // 2), (place, rows // 2, rows)]
            else:
                slices.append(held[distance])
                pieces.append((place, 0, rows))
        picked = pick(wanted, slices, tuple(pieces), len(distances), rows, block_size)
        arrived.append(exchange(picked, PLANE))
    order = [d for distances in PARTS for d in distances]
    zs = lax.rem(lax.axis_index("z") + ZN - jnp.array(order, jnp.int32), ZN)
    places = iter(range(len(order)))
    zs_of = tuple(tuple(next(places) for _ in distances) for distances in PARTS)
    mixed_t = aggregate(zs, targets, counts, values, arrived, zs_of, tgt_rows, feat_width)

    preact = lax.dot_general(
        mixed_t, whole_weight, (((0,), (0,)), ((), ())), preferred_element_type=jnp.float32
    )
    activations = jax.nn.silu(preact).astype(jnp.bfloat16)
    dpre = (cotangent.astype(jnp.float32) * silu_grad(preact)).astype(jnp.bfloat16)
    partial = jnp.dot(mixed_t, dpre, preferred_element_type=jnp.float32)
    total_rows = tgt_rows * 8 * group_size
    weight_grad = sum_over_devices(partial) / math.sqrt(total_rows)
    return (activations, weight_grad)


def solution(mesh):
    row = ("z", "yhi", "core")
    fine = Mesh(mesh.devices.reshape(2, 4, 8, 2, 2), ("ylo", "x", "z", "yhi", "core"))
    in_specs = (
        P(REP, row, None),
        P(REP, row, None, None),
        P(REP, row, None, None),
        P(REP, row, None),
        P(REP, row, None, None, None, None),
        P(row, None),
        P(REP + row, None),
    )
    out_specs = (P(REP + row, None), P(row, None))
    return jax.shard_map(per_device, mesh=fine, in_specs=in_specs, out_specs=out_specs, check_vma=False)
```

time: 657 us -> 293 us (0.45)
  waiting for transfers between devices: 397 us -> 142 us
  blocking collectives: 143 us -> 57.9 us
  local copies, waits for them, and re-layouts: 49.6 us -> 9.3 us
  starting transfers between devices: 10.2 us -> 35.6 us
  Pallas kernels: 0 us -> 21.4 us
  matrix products: 30.4 us -> 9.26 us
  other arithmetic: 11.2 us -> 2.77 us
    all_to_all x2 -> x3, waiting for transfers between devices: 196 us -> 56.8 us  [exchange(): return lax.all_to_all(value, axes, split_axis=0, concat_axis=0, tiled=True)]
    reduce_scatter x1 -> x0, waiting for transfers between devices: 123 us -> none  [per_device(): lax.psum_scatter(lax.dot_general(columns, dpre, (((0,), (0,)), ((), ())),...]
    psum x1 -> x0, waiting for transfers between devices: 77.1 us -> none  [per_device(): summed = lax.psum(partial_rows, 'rep')]
    ppermute x0 -> x9, waiting for transfers between devices: none -> 70.5 us  [the longest x8 68.1 us: shift_z(): return lax.ppermute(value, 'z', [(i, (i + step) % ZN) for i in range(ZN)])]
    all_gather x1 -> x0, blocking collectives: 45.4 us -> none  [per_device(): asked = lax.all_gather(sources[None], 'row', axis=0, tiled=True)]
    all_to_all x1 -> x4, blocking collectives: 97.4 us -> 57.9 us  [exchange(): return lax.all_to_all(value, axes, split_axis=0, concat_axis=0, tiled=True)]
    all_to_all x3 -> x1, local copies, waits for them, and re-layouts: 22.8 us -> 0.08 us  [exchange(): return lax.all_to_all(value, axes, split_axis=0, concat_axis=0, tiled=True)]
    pallas_call x0 -> x4, Pallas kernels: none -> 21.4 us  [the longest x3 13.1 us: pick(): pl.pallas_call(functools.partial(pick_kernel, pieces, block), out_shape=j...]
  transfers between devices with their start and end apart: 5 -> 13, of which waited for: 4 -> 9; matrix products, arithmetic and copies ran while one was open for 5% -> 1% of each run, Pallas kernels for 0% -> 6%
where the time goes in v1:
time: 293 us
  waiting for transfers between devices  142 us (48%)
  blocking collectives  57.9 us (20%)
  starting transfers between devices  35.6 us (12%)
  Pallas kernels  21.4 us (7%)
  between operations  14.2 us (5%)
  local copies, waits for them, and re-layouts  9.3 us (3%)
  matrix products  9.26 us (3%)
    ppermute x8, waiting for transfers between devices, shift_z(): return lax.ppermute(value, 'z', [(i, (i + step) % ZN) for i in range(ZN)])  68.1 us
    all_to_all x4, blocking collectives, exchange(): return lax.all_to_all(value, axes, split_axis=0, concat_axis=0, tiled=True)  57.9 us
    all_to_all x3, waiting for transfers between devices, exchange(): return lax.all_to_all(value, axes, split_axis=0, concat_axis=0, tiled=True)  56.8 us
    all_to_all x3, starting transfers between devices, exchange(): return lax.all_to_all(value, axes, split_axis=0, concat_axis=0, tiled=True)  19.2 us
    ppermute x8, starting transfers between devices, shift_z(): return lax.ppermute(value, 'z', [(i, (i + step) % ZN) for i in range(ZN)])  16 us
    all_gather x1, waiting for transfers between devices, per_device(): lax.all_gather(weight, ('z', 'yhi', 'core'), axis=0, tiled=True)  14.8 us
    pallas_call x3, Pallas kernels, pick(): pl.pallas_call(functools.partial(pick_kernel, pieces, block), out_shape=j...  13.1 us
    pallas_call x1, Pallas kernels, aggregate(): pl.pallas_call(functools.partial(aggregate_kernel, zs_of), out_shape=jax....  8.29 us
  transfers between devices with their start and end apart: 13, of which 9 were waited for; matrix products, arithmetic and copies ran while one was open for 1% of the time, Pallas kernels for 6%

profile of v1, /device:TPU:2, one launch (start us, length us, event | category | flops | bytes accessed | tf_op | source)
XLA Modules:
  0.0 292.6 jit_solution(4584628485631531614)
XLA Ops:
  7.2 2.0 collective-permute-start
  9.2 4.0 %collective-permute-start.1 = (bf16[32,16384]{1,0:T(8,128)(2,1)}, bf16[32,16384]{1,0:T(8,128)(2,1)S(1)}, u32[]{:S(2)}, u32[]{:S(2)}) collective-permute-start(bf16[32,16384]{1,0:T(8,128)(2,1)} %bitcast.35), channel_id=1, source_target_pairs={{0,28},{4,0},{8,4},{12,8},{16,12},{20,16},{24,20},{28,24},{1,29},{... | collective-permute-start | bytes 3145736 | tf_op jit(solution)/shard_map/ppermute | solution.py:26
  13.2 0.8 copy.52
  14.0 13.5 %all_to_all.35 = s32[32,1,4]{2,1,0:T(1,128)S(1)} all-to-all(s32[32,1,4]{2,1,0:T(1,128)S(1)} %bitcast.44), channel_id=1, replica_groups=mesh['ylo'=2,'x'=4,'z'=8,'yhi'=2,'core'=2] {'ylo','x','yhi','core'}, dimensions={0} | all-to-all | bytes 1024 | tf_op jit(solution)/shard_map/all_to_all | solution.py:30
  27.5 0.1 copy.42
  27.6 0.1 copy.43.wanted_ref
  27.6 8.8 %collective-permute-done.refs_1_ = bf16[32,16384]{1,0:T(8,128)(2,1)S(1)} collective-permute-done((bf16[32,16384]{1,0:T(8,128)(2,1)}, bf16[32,16384]{1,0:T(8,128)(2,1)S(1)}, u32[]{:S(2)}, u32[]{:S(2)}) %collective-permute-start) | collective-permute-done | bytes 1048608 | tf_op jit(solution)/shard_map/ppermute | solution.py:26
  36.5 1.2 copy-done.2
  37.7 4.4 %shard_map.95 = bf16[32,4,3,32,128]{4,3,2,1,0:T(8,128)(2,1)} custom-call(s32[32,4]{1,0:T(8,128)S(1)} %copy.43.wanted_ref, bf16[32,16384]{1,0:T(8,128)(2,1)S(1)} %bitcast.36, bf16[32,16384]{1,0:T(8,128)(2,1)S(1)} %collective-permute-done.refs_1_, bf16[32,16384]{1,0:T(8,128)(2,1)S(1)} %collective-permute-done.1.refs_2_), custom_call_target="tpu_custom_call" | custom-call | bytes 6291456 | tf_op jit(solution)/shard_map/pallas_call | solution.py:49
  42.1 7.7 %all-to-all-start.1 = ((bf16[32,4,3,32,128]{4,3,2,1,0:T(8,128)(2,1)}), bf16[32,4,3,32,128]{4,3,2,1,0:T(8,128)(2,1)}, u32[]{:S(2)}, u32[]{:S(2)}) async-start(bf16[32,4,3,32,128]{4,3,2,1,0:T(8,128)(2,1)} %shard_map.95), calls=%async_computation.1 | async-start | bytes 6291456 | tf_op jit(solution)/shard_map/all_to_all | solution.py:30
  49.8 0.1 collective-permute-start.2
  49.9 3.2 %collective-permute-start.3 = (bf16[32,16384]{1,0:T(8,128)(2,1)S(1)}, bf16[32,16384]{1,0:T(8,128)(2,1)S(1)}, u32[]{:S(2)}, u32[]{:S(2)}) collective-permute-start(bf16[32,16384]{1,0:T(8,128)(2,1)S(1)} %collective-permute-done.1.refs_2_), channel_id=1, source_target_pairs={{0,28},{4,0},{8,4},{12,8},{16,12},{20,16},{24,20},{28,24},{1,29},{... | collective-permute-start | bytes 3145736 | tf_op jit(solution)/shard_map/ppermute | solution.py:26
  53.1 23.3 %collective-permute-done.2.refs_0_ = bf16[32,16384]{1,0:T(8,128)(2,1)S(1)} collective-permute-done((bf16[32,16384]{1,0:T(8,128)(2,1)S(1)}, bf16[32,16384]{1,0:T(8,128)(2,1)S(1)}, u32[]{:S(2)}, u32[]{:S(2)}) %collective-permute-start.2) | collective-permute-done | bytes 1048608 | tf_op jit(solution)/shard_map/ppermute | solution.py:26
  76.4 3.8 %shard_map.96 = bf16[32,4,2,32,128]{4,3,2,1,0:T(8,128)(2,1)} custom-call(s32[32,4]{1,0:T(8,128)S(1)} %copy.43.wanted_ref, bf16[32,16384]{1,0:T(8,128)(2,1)S(1)} %collective-permute-done.2.refs_0_, bf16[32,16384]{1,0:T(8,128)(2,1)S(1)} %collective-permute-done.3.refs_1_), custom_call_target="tpu_custom_call" | custom-call | bytes 4194304 | tf_op jit(solution)/shard_map/pallas_call | solution.py:49
  80.2 1.0 copy-done.3
  81.2 1.1 copy-done.4
  82.2 11.3 %all-to-all-done.1.refs_0_ = bf16[32,4,3,32,128]{4,3,2,1,0:T(8,128)(2,1)} async-done(((bf16[32,4,3,32,128]{4,3,2,1,0:T(8,128)(2,1)}), bf16[32,4,3,32,128]{4,3,2,1,0:T(8,128)(2,1)}, u32[]{:S(2)}, u32[]{:S(2)}) %all-to-all-start.1) | async-done | bytes 3145760 | tf_op jit(solution)/shard_map/all_to_all | solution.py:30
  93.5 4.2 %all-to-all-start.2 = ((bf16[32,4,2,32,128]{4,3,2,1,0:T(8,128)(2,1)}), bf16[32,4,2,32,128]{4,3,2,1,0:T(8,128)(2,1)S(1)}, u32[]{:S(2)}, u32[]{:S(2)}) async-start(bf16[32,4,2,32,128]{4,3,2,1,0:T(8,128)(2,1)} %shard_map.96), calls=%async_computation.2 | async-start | bytes 4194304 | tf_op jit(solution)/shard_map/all_to_all | solution.py:30
  97.7 0.0 all-gather.2.cloned.1.call-start
  97.8 0.1 collective-permute-start.4
  97.9 3.2 %collective-permute-start.5 = (bf16[32,16384]{1,0:T(8,128)(2,1)}, bf16[32,16384]{1,0:T(8,128)(2,1)}, u32[]{:S(2)}, u32[]{:S(2)}) collective-permute-start(bf16[32,16384]{1,0:T(8,128)(2,1)} %copy-done.3), channel_id=1, source_target_pairs={{0,28},{4,0},{8,4},{12,8},{16,12},{20,16},{24,20},{28,24},{1,29},{... | collective-permute-start | bytes 3145736 | tf_op jit(solution)/shard_map/ppermute | solution.py:26
  101.1 24.0 %collective-permute-done.4.refs_0_ = bf16[32,16384]{1,0:T(8,128)(2,1)S(1)} collective-permute-done((bf16[32,16384]{1,0:T(8,128)(2,1)}, bf16[32,16384]{1,0:T(8,128)(2,1)S(1)}, u32[]{:S(2)}, u32[]{:S(2)}) %collective-permute-start.4) | collective-permute-done | bytes 1048608 | tf_op jit(solution)/shard_map/ppermute | solution.py:26
  125.1 0.1 collective-permute-start.6
  125.2 1.1 slice.9
  126.3 3.3 %collective-permute-start.7 = (bf16[16,16384]{1,0:T(8,128)(2,1)S(1)}, bf16[16,16384]{1,0:T(8,128)(2,1)S(1)}, u32[]{:S(2)}, u32[]{:S(2)}) collective-permute-start(bf16[16,16384]{1,0:T(8,128)(2,1)S(1)} %slice.9), channel_id=1, source_target_pairs={{0,28},{4,0},{8,4},{12,8},{16,12},{20,16},{24,20},{28,24},{1,29},{... | collective-permute-start | bytes 1572872 | tf_op jit(solution)/shard_map/ppermute | solution.py:26
  129.6 11.3 %collective-permute-done.6.refs_2_ = bf16[16,16384]{1,0:T(8,128)(2,1)S(1)} collective-permute-done((bf16[16,16384]{1,0:T(8,128)(2,1)S(1)}, bf16[16,16384]{1,0:T(8,128)(2,1)S(1)}, u32[]{:S(2)}, u32[]{:S(2)}) %collective-permute-start.6) | collective-permute-done | bytes 524320 | tf_op jit(solution)/shard_map/ppermute | solution.py:26
  140.9 0.7 collective-permute-done.7.refs_3_
  141.6 4.9 %shard_map.97 = bf16[32,4,3,32,128]{4,3,2,1,0:T(8,128)(2,1)} custom-call(s32[32,4]{1,0:T(8,128)S(1)} %copy.43.wanted_ref, bf16[32,16384]{1,0:T(8,128)(2,1)S(1)} %collective-permute-done.4.refs_0_, bf16[32,16384]{1,0:T(8,128)(2,1)} %collective-permute-done.5.refs_1_, bf16[16,16384]{1,0:T(8,128)(2,1)S(1)} %collective-permute-done.6.refs_2_, ...), custom_call_target="tpu_custom_call" | custom-call | bytes 8388608 | tf_op jit(solution)/shard_map/pallas_call | solution.py:49
  146.5 7.4 %all-to-all-start.3 = ((bf16[32,4,3,32,128]{4,3,2,1,0:T(8,128)(2,1)}), bf16[32,4,3,32,128]{4,3,2,1,0:T(8,128)(2,1)}, u32[]{:S(2)}, u32[]{:S(2)}) async-start(bf16[32,4,3,32,128]{4,3,2,1,0:T(8,128)(2,1)} %shard_map.97), calls=%async_computation.3 | async-start | bytes 6291456 | tf_op jit(solution)/shard_map/all_to_all | solution.py:30
  153.9 0.1 copy.46.tgt_ref
  154.0 45.5 %all-to-all-done.3.refs_2_ = bf16[32,4,3,32,128]{4,3,2,1,0:T(8,128)(2,1)} async-done(((bf16[32,4,3,32,128]{4,3,2,1,0:T(8,128)(2,1)}), bf16[32,4,3,32,128]{4,3,2,1,0:T(8,128)(2,1)}, u32[]{:S(2)}, u32[]{:S(2)}) %all-to-all-start.3) | async-done | bytes 3145760 | tf_op jit(solution)/shard_map/all_to_all | solution.py:30
  199.5 8.3 %shard_map.98 = bf16[1024,1024]{1,0:T(8,128)(2,1)S(1)} custom-call(s32[8]{0:T(128)S(1)} %compare_select_fusion.z_ref, s32[8,4]{1,0:T(8,128)S(1)} %copy.46.tgt_ref, s32[8]{0:T(128)S(1)} %bitcast.38, bf16[8,4,128,128]{3,2,1,0:T(8,128)(2,1)S(1)} %bitcast.37, bf16[32,4,3,32,128]{4,3,2,1,0:T(8,128)(2,1)} %all-to-all-done.1.refs_0_, ...), custom_call_target="tpu_custom_call" | custom-call | flops 1000000000 | bytes 12582912 | tf_op jit(solution)/shard_map/pallas_call | solution.py:90
  207.8 1.3 copy-done
  209.1 14.8 %all-gather.2.cloned.1.call-done = bf16[1024,1024]{1,0:T(8,128)(2,1)} async-done(((bf16[32,1024]{1,0:T(8,128)(2,1)}), bf16[1024,1024]{1,0:T(8,128)(2,1)}) %all-gather.2.cloned.1.call-update) | async-done | bytes 2097168 | tf_op jit(solution)/shard_map/all_gather | solution.py:125
  223.9 6.7 %multiply_convert_fusion.1 = (bf16[1024,1024]{1,0:T(8,128)(2,1)}, f32[1024,1024]{1,0:T(8,128)S(1)}) fusion(bf16[1024,1024]{1,0:T(8,128)(2,1)} %copy-done, bf16[1024,1024]{1,0:T(8,128)(2,1)} %all-gather.2.cloned.1.call-done), kind=kOutput, calls=%fused_computation.1 | convolution fusion | flops 2152726528 | bytes 10485760 | tf_op jit(solution)/shard_map/dot_general | solution.py:152
  230.6 2.6 fusion.1
  233.2 1.9 copy-done.7
  235.2 0.2 fusion.2
  235.3 0.3 collective-permute-start.8
  235.7 2.4 collective-permute-done.8
  238.1 1.9 fusion
  240.0 0.3 copy.54
  240.3 0.2 copy.48
  240.5 21.2 %all_to_all.36 = bf16[16,8,32,128]{3,2,1,0:T(8,128)(2,1)S(1)} all-to-all(bf16[16,8,32,128]{3,2,1,0:T(8,128)(2,1)S(1)} %bitcast.41), channel_id=1, replica_groups=mesh['ylo'=2,'x'=4,'z'=8,'yhi'=2,'core'=2] {'ylo','x','yhi'}, dimensions={0} | all-to-all | bytes 2097152 | tf_op jit(solution)/shard_map/all_to_all | solution.py:30
  261.7 0.1 convert_reduce_fusion
  261.8 13.2 %all_to_all.37 = f32[8,32,128]{2,1,0:T(8,128)S(1)} all-to-all(f32[8,32,128]{2,1,0:T(8,128)S(1)} %convert_reduce_fusion), channel_id=1, replica_groups=mesh['ylo'=2,'x'=4,'z'=8,'yhi'=2,'core'=2] {'z'}, dimensions={0} | all-to-all | bytes 262144 | tf_op jit(solution)/shard_map/all_to_all | solution.py:30
  275.1 10.0 %all_to_all.38 = f32[8,32,128]{2,1,0:T(8,128)S(1)} all-to-all(f32[8,32,128]{2,1,0:T(8,128)S(1)} %broadcast_in_dim.10), channel_id=1, replica_groups=mesh['ylo'=2,'x'=4,'z'=8,'yhi'=2,'core'=2] {'ylo','x'}, dimensions={0} | all-to-all | bytes 262144 | tf_op jit(solution)/shard_map/all_to_all | solution.py:30
  285.1 0.7 copy_bitcast_fusion
  (27 shorter events, 0.1 us)
Async XLA Ops:
  7.2 29.3 %collective-permute-start = (bf16[32,16384]{1,0:T(8,128)(2,1)}, bf16[32,16384]{1,0:T(8,128)(2,1)S(1)}, u32[]{:S(2)}, u32[]{:S(2)}) collective-permute-start(bf16[32,16384]{1,0:T(8,128)(2,1)} %bitcast.34), channel_id=1, source_target_pairs={{0,4},{4,8},{8,12},{12,16},{16,20},{20,24},{24,28},{28,0},{1,5},{5... | collective-permute-start | bytes 3145736 | tf_op jit(solution)/shard_map/ppermute | solution.py:26
  9.2 27.3 %collective-permute-start.1 = (bf16[32,16384]{1,0:T(8,128)(2,1)}, bf16[32,16384]{1,0:T(8,128)(2,1)S(1)}, u32[]{:S(2)}, u32[]{:S(2)}) collective-permute-start(bf16[32,16384]{1,0:T(8,128)(2,1)} %bitcast.35), channel_id=1, source_target_pairs={{0,28},{4,0},{8,4},{12,8},{16,12},{20,16},{24,20},{28,24},{1,29},{... | collective-permute-start | bytes 3145736 | tf_op jit(solution)/shard_map/ppermute | solution.py:26
  36.5 1.2 copy-start.2
  42.1 51.4 %all-to-all-start.1 = ((bf16[32,4,3,32,128]{4,3,2,1,0:T(8,128)(2,1)}), bf16[32,4,3,32,128]{4,3,2,1,0:T(8,128)(2,1)}, u32[]{:S(2)}, u32[]{:S(2)}) async-start(bf16[32,4,3,32,128]{4,3,2,1,0:T(8,128)(2,1)} %shard_map.95), calls=%async_computation.1 | async-start | bytes 6291456 | tf_op jit(solution)/shard_map/all_to_all | solution.py:30
  49.8 26.6 %collective-permute-start.2 = (bf16[32,16384]{1,0:T(8,128)(2,1)S(1)}, bf16[32,16384]{1,0:T(8,128)(2,1)S(1)}, u32[]{:S(2)}, u32[]{:S(2)}) collective-permute-start(bf16[32,16384]{1,0:T(8,128)(2,1)S(1)} %collective-permute-done.refs_1_), channel_id=1, source_target_pairs={{0,4},{4,8},{8,12},{12,16},{16,20},{20,24},{24,28},{28,0},{1,5},{5... | collective-permute-start | bytes 3145736 | tf_op jit(solution)/shard_map/ppermute | solution.py:26
  49.9 26.5 %collective-permute-start.3 = (bf16[32,16384]{1,0:T(8,128)(2,1)S(1)}, bf16[32,16384]{1,0:T(8,128)(2,1)S(1)}, u32[]{:S(2)}, u32[]{:S(2)}) collective-permute-start(bf16[32,16384]{1,0:T(8,128)(2,1)S(1)} %collective-permute-done.1.refs_2_), channel_id=1, source_target_pairs={{0,28},{4,0},{8,4},{12,8},{16,12},{20,16},{24,20},{28,24},{1,29},{... | collective-permute-start | bytes 3145736 | tf_op jit(solution)/shard_map/ppermute | solution.py:26
  80.2 1.0 copy-start.3
  81.2 1.1 copy-start.4
  93.5 53.0 %all-to-all-start.2 = ((bf16[32,4,2,32,128]{4,3,2,1,0:T(8,128)(2,1)}), bf16[32,4,2,32,128]{4,3,2,1,0:T(8,128)(2,1)S(1)}, u32[]{:S(2)}, u32[]{:S(2)}) async-start(bf16[32,4,2,32,128]{4,3,2,1,0:T(8,128)(2,1)} %shard_map.96), calls=%async_computation.2 | async-start | bytes 4194304 | tf_op jit(solution)/shard_map/all_to_all | solution.py:30
  97.7 126.2 %all-gather.2.cloned.1.call-start = ((), (), s32[]{:S(2)}) async-start(), calls=%async_computation.7 | async-start | bytes 2162688 | tf_op jit(solution)/shard_map/all_gather | solution.py:125
  97.8 27.3 %collective-permute-start.4 = (bf16[32,16384]{1,0:T(8,128)(2,1)}, bf16[32,16384]{1,0:T(8,128)(2,1)S(1)}, u32[]{:S(2)}, u32[]{:S(2)}) collective-permute-start(bf16[32,16384]{1,0:T(8,128)(2,1)} %copy-done.4), channel_id=1, source_target_pairs={{0,4},{4,8},{8,12},{12,16},{16,20},{20,24},{24,28},{28,0},{1,5},{5... | collective-permute-start | bytes 3145736 | tf_op jit(solution)/shard_map/ppermute | solution.py:26
  97.9 27.4 %collective-permute-start.5 = (bf16[32,16384]{1,0:T(8,128)(2,1)}, bf16[32,16384]{1,0:T(8,128)(2,1)}, u32[]{:S(2)}, u32[]{:S(2)}) collective-permute-start(bf16[32,16384]{1,0:T(8,128)(2,1)} %copy-done.3), channel_id=1, source_target_pairs={{0,28},{4,0},{8,4},{12,8},{16,12},{20,16},{24,20},{28,24},{1,29},{... | collective-permute-start | bytes 3145736 | tf_op jit(solution)/shard_map/ppermute | solution.py:26
  125.1 15.8 %collective-permute-start.6 = (bf16[16,16384]{1,0:T(8,128)(2,1)S(1)}, bf16[16,16384]{1,0:T(8,128)(2,1)S(1)}, u32[]{:S(2)}, u32[]{:S(2)}) collective-permute-start(bf16[16,16384]{1,0:T(8,128)(2,1)S(1)} %slice.8), channel_id=1, source_target_pairs={{0,4},{4,8},{8,12},{12,16},{16,20},{20,24},{24,28},{28,0},{1,5},{5... | collective-permute-start | bytes 1572872 | tf_op jit(solution)/shard_map/ppermute | solution.py:26
  126.3 15.3 %collective-permute-start.7 = (bf16[16,16384]{1,0:T(8,128)(2,1)S(1)}, bf16[16,16384]{1,0:T(8,128)(2,1)S(1)}, u32[]{:S(2)}, u32[]{:S(2)}) collective-permute-start(bf16[16,16384]{1,0:T(8,128)(2,1)S(1)} %slice.9), channel_id=1, source_target_pairs={{0,28},{4,0},{8,4},{12,8},{16,12},{20,16},{24,20},{28,24},{1,29},{... | collective-permute-start | bytes 1572872 | tf_op jit(solution)/shard_map/ppermute | solution.py:26
  146.5 7.4 %copy-start.8 = (s32[1,1,8,4]{2,3,1,0:T(4,128)S(1)}, s32[1,1,8,4]{2,3,1,0:T(4,128)}, u32[]{:S(2)}) copy-start(s32[1,1,8,4]{2,3,1,0:T(4,128)} %param.9) | copy-start | bytes 388
  146.5 7.5 %copy-start.10 = (s32[8]{0:T(128)S(1)}, s32[8]{0:T(128)}, u32[]{:S(2)}) copy-start(s32[8]{0:T(128)} %constant.45) | copy-start | bytes 100
  146.5 53.0 %copy-start.5 = (bf16[1,1,8,4,128,128]{5,4,3,2,1,0:T(8,128)(2,1)S(1)}, bf16[1,1,8,4,128,128]{5,4,3,2,1,0:T(8,128)(2,1)}, u32[]{:S(2)}) copy-start(bf16[1,1,8,4,128,128]{5,4,3,2,1,0:T(8,128)(2,1)} %param.12) | copy-start | bytes 3145732
  146.5 53.0 %copy-start.6 = (s32[1,1,8]{2,1,0:T(1,128)S(1)}, s32[1,1,8]{2,1,0:T(1,128)}, u32[]{:S(2)}) copy-start(s32[1,1,8]{2,1,0:T(1,128)} %param.11) | copy-start | bytes 100
  146.5 53.0 %all-to-all-start.3 = ((bf16[32,4,3,32,128]{4,3,2,1,0:T(8,128)(2,1)}), bf16[32,4,3,32,128]{4,3,2,1,0:T(8,128)(2,1)}, u32[]{:S(2)}, u32[]{:S(2)}) async-start(bf16[32,4,3,32,128]{4,3,2,1,0:T(8,128)(2,1)} %shard_map.97), calls=%async_computation.3 | async-start | bytes 6291456 | tf_op jit(solution)/shard_map/all_to_all | solution.py:30
  207.8 1.3 copy-start
  209.1 21.5 %copy-start.9 = (bf16[1024,1024]{1,0:T(8,128)(2,1)S(1)}, bf16[1024,1024]{1,0:T(8,128)(2,1)}, u32[]{:S(2)}) copy-start(bf16[1024,1024]{1,0:T(8,128)(2,1)} %param.14) | copy-start | bytes 6291460
  223.9 6.7 %copy-start.1 = (bf16[1024,1024]{1,0:T(8,128)(2,1)S(1)}, bf16[1024,1024]{1,0:T(8,128)(2,1)}, u32[]{:S(2)}) copy-start(bf16[1024,1024]{1,0:T(8,128)(2,1)} %copy-done) | copy-start | bytes 6291460
  233.2 1.9 copy-start.7
  235.3 2.7 collective-permute-start.8
Sparse Core Ops, SparseCore 0:
  101.3 122.5 all-gather.1

commit v2 on v1

v2 whole, which is shorter than its diff:
```python
import functools
import math

import jax
import jax.numpy as jnp
from jax import lax
from jax.experimental import pallas as pl
from jax.experimental.pallas import tpu as pltpu
from jax.sharding import Mesh, PartitionSpec as P

REP = ("ylo", "x")
PLANE = ("ylo", "x", "yhi", "core")
CHIPS_XY = ("ylo", "x", "yhi")
ZN = 8
PARTS = ((0, 1, -1), (2, -2), (3, -3, 4))
PICK_COSTS = (20, 20, 20)
ORDER = tuple(d for part in PARTS for d in part)
VMEM = pl.BlockSpec(memory_space=pltpu.VMEM)
SMEM = pl.BlockSpec(memory_space=pltpu.SMEM)


def silu_grad(preact):
    sigmoid_val = jax.nn.sigmoid(preact)
    return sigmoid_val * (1.0 + preact * (1.0 - sigmoid_val))


def shift_z(value, step):
    return lax.ppermute(value, "z", [(i, (i + step) % ZN) for i in range(ZN)])


def exchange(value, axes):
    return lax.all_to_all(value, axes, split_axis=0, concat_axis=0, tiled=True)


def pick_kernel(pieces, block, wanted_ref, *refs):
    slices, out_ref = refs[:-1], refs[-1]
    slots = out_ref.shape[1]

    def one(step, carry):
        dest, slot = step // slots, step % slots
        start = pl.multiple_of(wanted_ref[dest, slot] * block, block)
        for ref, (place, low, high) in zip(slices, pieces):
            out_ref[dest, slot, place, low:high, :] = ref[:, pl.ds(start, block)]
        return carry

    lax.fori_loop(0, out_ref.shape[0] * slots, one, 0, unroll=4)


def pick(wanted, slices, pieces, places, rows, block, cost):
    askers, slots = wanted.shape
    return pl.pallas_call(
        functools.partial(pick_kernel, pieces, block),
        out_shape=jax.ShapeDtypeStruct((askers, slots, places, rows, block), jnp.bfloat16),
        in_specs=[SMEM] + [VMEM] * len(slices),
        out_specs=VMEM,
        compiler_params=pltpu.CompilerParams(vmem_limit_bytes=40 * 2**20),
        cost_estimate=pl.CostEstimate(flops=cost * 10**9, bytes_accessed=len(slices) * 2**21, transcendentals=0),
    )(wanted, *slices)


def aggregate_kernel(core_ref, tgt_ref, count_ref, vals_ref, part, out_ref, acc):
    sections, slots, block, _ = vals_ref.shape
    places, rows = part.shape[2:4]
    lanes = part.shape[0] // sections
    acc[...] = jnp.zeros_like(acc)
    core = core_ref[0]

    def one(step, carry):
        section, slot = step // slots, step % slots

        @pl.when(slot < count_ref[section])
        def _():
            column = pl.multiple_of(tgt_ref[section, slot] * block, block)
            tile = vals_ref[section, slot]
            for lane in range(lanes):
                source = section * lanes + lane + core * (1 - 2 * (lane % 2))
                columns_in = part[source, slot].reshape(places * rows, block)
                contrib = lax.dot_general(
                    columns_in, tile, (((1,), (1,)), ((), ())), preferred_element_type=jnp.float32
                )
                for place in range(places):
                    low = (place * lanes + lane) * rows
                    acc[low : low + rows, pl.ds(column, block)] += contrib[place * rows : (place + 1) * rows]

        return carry

    lax.fori_loop(0, sections * slots, one, 0)
    out_ref[...] = acc[...].astype(out_ref.dtype)


def aggregate(core, targets, counts, values, part, num_rows):
    sections = values.shape[0]
    num_feats = part.shape[0] // sections * part.shape[2] * part.shape[3]
    return pl.pallas_call(
        aggregate_kernel,
        out_shape=jax.ShapeDtypeStruct((num_feats, num_rows), jnp.bfloat16),
        in_specs=[SMEM] * 3 + [VMEM] * 2,
        out_specs=VMEM,
        scratch_shapes=[pltpu.VMEM((num_feats, num_rows), jnp.float32)],
        compiler_params=pltpu.CompilerParams(vmem_limit_bytes=32 * 2**20),
        cost_estimate=pl.CostEstimate(flops=3 * 10**9, bytes_accessed=8 * 2**20, transcendentals=0),
    )(core, targets, counts, values, part)


def sum_plane_kernel(z_ref, came_ref, out_ref):
    for place, distance in enumerate(ORDER):
        total = came_ref[:, place].astype(jnp.float32).sum(0)
        out_ref[lax.rem(z_ref[0] + (ZN - distance), ZN)] = total


def sum_plane(came):
    return pl.pallas_call(
        sum_plane_kernel,
        out_shape=jax.ShapeDtypeStruct(came.shape[1:], jnp.float32),
        in_specs=[SMEM, VMEM],
        out_specs=VMEM,
        compiler_params=pltpu.CompilerParams(vmem_limit_bytes=16 * 2**20),
    )(lax.axis_index("z").astype(jnp.int32)[None], came)


def sum_over_devices(partial):
    zs, _, _, rows, cols = partial.shape
    came = lax.ppermute(partial[:, :, 1].astype(jnp.bfloat16), "core", [(0, 1), (1, 0)])
    chip = (partial[:, :, 0] + came.astype(jnp.float32)).astype(jnp.bfloat16)
    chip = chip.reshape(zs, 2, rows, 8, cols // 8).transpose(3, 1, 0, 2, 4)
    chip = chip.reshape(16, zs, rows, cols // 8)
    plane = sum_plane(exchange(chip, CHIPS_XY))
    column = exchange(plane, "z").sum(0)
    whole = exchange(jnp.broadcast_to(column[None], (8, *column.shape)), REP)
    return whole.transpose(1, 0, 2).reshape(rows, cols)


def whole_weight(own):
    flip = [(0, 3), (1, 2), (2, 1), (3, 0)]
    other = lax.ppermute(own, ("ylo", "yhi"), flip)
    first = lax.axis_index("yhi") == 0
    both = jnp.stack([jnp.where(first, own, other), jnp.where(first, other, own)], axis=1)
    return jnp.stack([both, lax.ppermute(both, "core", [(0, 1), (1, 0)])], axis=2)


def per_device(features, tile_tgt, tile_src, tile_count, tile_vals, weight, cotangent):
    group_size = 32
    block_size = tile_vals.shape[-1]
    rows, panel = features.shape[1:]
    tgt_rows, out_width = cotangent.shape
    targets, sources, counts, values = tile_tgt[0, 0], tile_src[0, 0], tile_count[0, 0], tile_vals[0, 0]

    wanted = exchange(jnp.repeat(sources, 4, axis=0)[:, None, :], PLANE)[:, 0]

    held = {0: jnp.concatenate([features[0], weight], axis=1)}
    for step in range(1, 4):
        held[step] = shift_z(held[step - 1], 1)
        held[-step] = shift_z(held[1 - step], -1)
    up, down = shift_z(held[3][: rows // 2], 1), shift_z(held[-3][rows // 2 :], -1)

    core = lax.axis_index("core").astype(jnp.int32)[None]
    mixed_t, weights = [], []
    for distances, cost in zip(PARTS, PICK_COSTS):
        slices, pieces = [], []
        for place, distance in enumerate(distances):
            if distance == 4:
                slices += [up, down]
                pieces += [(place, 0, rows // 2), (place, rows // 2, rows)]
                weights.append(jnp.concatenate([up[:, panel:], down[:, panel:]], axis=0))
            else:
                slices.append(held[distance])
                pieces.append((place, 0, rows))
                weights.append(held[distance][:, panel:])
        picked = pick(wanted, slices, tuple(pieces), len(distances), rows, block_size, cost)
        arrived = exchange(picked, PLANE)
        mixed_t.append(aggregate(core, targets, counts, values, arrived, tgt_rows))
    mixed_t = jnp.concatenate(mixed_t, axis=0)
    weight_in = whole_weight(jnp.stack(weights)).reshape(-1, out_width)

    preact = lax.dot_general(mixed_t, weight_in, (((0,), (0,)), ((), ())), preferred_element_type=jnp.float32)
    activations = jax.nn.silu(preact).astype(jnp.bfloat16)
    dpre = (cotangent.astype(jnp.float32) * silu_grad(preact)).astype(jnp.bfloat16)
    partial = jnp.dot(mixed_t, dpre, preferred_element_type=jnp.float32)
    total_rows = tgt_rows * 8 * group_size
    weight_grad = sum_over_devices(partial.reshape(ZN, 2, 2, rows, out_width)) / math.sqrt(total_rows)
    return (activations, weight_grad)


def solution(mesh):
    row = ("z", "yhi", "core")
    fine = Mesh(mesh.devices.reshape(2, 4, 8, 2, 2), ("ylo", "x", "z", "yhi", "core"))
    in_specs = (
        P(REP, row, None),
        P(REP, row, None, None),
        P(REP, row, None, None),
        P(REP, row, None),
        P(REP, row, None, None, None, None),
        P(row, None),
        P(REP + row, None),
    )
    out_specs = (P(REP + row, None), P(row, None))
    return jax.shard_map(per_device, mesh=fine, in_specs=in_specs, out_specs=out_specs, check_vma=False)
```

time: 293 us -> 273 us (0.932)
  blocking collectives: 57.9 us -> 35.5 us
  waiting for transfers between devices: 142 us -> 120 us
  local copies, waits for them, and re-layouts: 9.3 us -> 25.9 us
  between operations: 14.2 us -> 0.91 us
  starting transfers between devices: 35.6 us -> 48.2 us
  other arithmetic: 2.77 us -> 7.19 us
  Pallas kernels: 21.4 us -> 25.6 us
    ppermute x1 -> x3, waiting for transfers between devices: 2.41 us -> 40.7 us  [the longest x1 38 us: whole_weight(): other = lax.ppermute(own, ('ylo', 'yhi'), flip)]
    ppermute x8, waiting for transfers between devices: 68.1 us -> 40.6 us  [shift_z(): return lax.ppermute(value, 'z', [(i, (i + step) % ZN) for i in range(ZN)])]
    all_to_all x4 -> x3, blocking collectives: 57.9 us -> 35.5 us  [exchange(): return lax.all_to_all(value, axes, split_axis=0, concat_axis=0, tiled=True)]
    all_to_all x3 -> x4, waiting for transfers between devices: 56.8 us -> 38.9 us  [exchange(): return lax.all_to_all(value, axes, split_axis=0, concat_axis=0, tiled=True)]
    all_gather x1 -> x0, waiting for transfers between devices: 14.8 us -> none  [per_device(): lax.all_gather(weight, ('z', 'yhi', 'core'), axis=0, tiled=True)]
    unnamed x24 -> x47, local copies, waits for them, and re-layouts: 7.56 us -> 19.4 us
    all_to_all x3 -> x4, starting transfers between devices: 19.2 us -> 28.3 us  [exchange(): return lax.all_to_all(value, axes, split_axis=0, concat_axis=0, tiled=True)]
    pallas_call x1 -> x4, Pallas kernels: 8.29 us -> 15.7 us  [the longest x3 15.5 us: aggregate(): pl.pallas_call(aggregate_kernel, out_shape=jax.ShapeDtypeStruct((num_feat...]
  transfers between devices with their start and end apart: 13 -> 15, of which waited for: 9 -> 7; matrix products, arithmetic and copies ran while one was open for 1% -> 7% of each run, Pallas kernels for 6% -> 7%
where the time goes in v2:
time: 273 us; the launch traced here: 270 us
  waiting for transfers between devices  120 us (44%)
  starting transfers between devices  48.2 us (18%)
  blocking collectives  35.5 us (13%)
  local copies, waits for them, and re-layouts  25.9 us (9%)
  Pallas kernels  25.6 us (9%)
  other arithmetic  7.19 us (3%)
  matrix products  6.9 us (3%)
    ppermute x8, waiting for transfers between devices, shift_z(): return lax.ppermute(value, 'z', [(i, (i + step) % ZN) for i in range(ZN)])  40.6 us
    all_to_all x4, waiting for transfers between devices, exchange(): return lax.all_to_all(value, axes, split_axis=0, concat_axis=0, tiled=True)  38.9 us
    ppermute x1, waiting for transfers between devices, whole_weight(): other = lax.ppermute(own, ('ylo', 'yhi'), flip)  38 us
    all_to_all x3, blocking collectives, exchange(): return lax.all_to_all(value, axes, split_axis=0, concat_axis=0, tiled=True)  35.5 us
    all_to_all x4, starting transfers between devices, exchange(): return lax.all_to_all(value, axes, split_axis=0, concat_axis=0, tiled=True)  28.3 us
    unnamed x47, local copies, waits for them, and re-layouts  19.4 us
    ppermute x8, starting transfers between devices, shift_z(): return lax.ppermute(value, 'z', [(i, (i + step) % ZN) for i in range(ZN)])  17 us
    pallas_call x3, Pallas kernels, aggregate(): pl.pallas_call(aggregate_kernel, out_shape=jax.ShapeDtypeStruct((num_feat...  15.5 us
  transfers between devices with their start and end apart: 15, of which 7 were waited for; matrix products, arithmetic and copies ran while one was open for 7% of the time, Pallas kernels for 7%

profile of v2, /device:TPU:2, one launch (start us, length us, event | category | flops | bytes accessed | tf_op | source)
XLA Modules:
  0.0 270.4 jit_solution(15828709349269559951)
XLA Ops:
  0.6 1.3 pad_maximum_fusion.2.refs_0_
  2.0 5.9 %collective-permute-start.1 = (bf16[32,17408]{1,0:T(8,128)(2,1)S(1)}, bf16[32,17408]{1,0:T(8,128)(2,1)}, u32[]{:S(2)}, u32[]{:S(2)}) collective-permute-start(bf16[32,17408]{1,0:T(8,128)(2,1)S(1)} %pad_maximum_fusion.2.refs_0_), channel_id=1, source_target_pairs={{0,28},{4,0},{8,4},{12,8},{16,12},{20,16},{24,20},{28,24},{1,29},{... | collective-permute-start | bytes 3342344 | tf_op jit(solution)/shard_map/ppermute | solution.py:28
  8.0 13.5 %all_to_all.35 = s32[32,1,4]{2,1,0:T(1,128)S(1)} all-to-all(s32[32,1,4]{2,1,0:T(1,128)S(1)} %bitcast.83), channel_id=1, replica_groups=mesh['ylo'=2,'x'=4,'z'=8,'yhi'=2,'core'=2] {'ylo','x','yhi','core'}, dimensions={0} | all-to-all | bytes 1024 | tf_op jit(solution)/shard_map/all_to_all | solution.py:32
  21.7 10.0 %collective-permute-done.1.refs_2_ = bf16[32,17408]{1,0:T(8,128)(2,1)} collective-permute-done((bf16[32,17408]{1,0:T(8,128)(2,1)S(1)}, bf16[32,17408]{1,0:T(8,128)(2,1)}, u32[]{:S(2)}, u32[]{:S(2)}) %collective-permute-start.1) | collective-permute-done | bytes 1114144 | tf_op jit(solution)/shard_map/ppermute | solution.py:28
  31.7 3.8 %collective-permute-start.3 = (bf16[32,17408]{1,0:T(8,128)(2,1)}, bf16[32,17408]{1,0:T(8,128)(2,1)}, u32[]{:S(2)}, u32[]{:S(2)}) collective-permute-start(bf16[32,17408]{1,0:T(8,128)(2,1)} %collective-permute-done.1.refs_2_), channel_id=1, source_target_pairs={{0,28},{4,0},{8,4},{12,8},{16,12},{20,16},{24,20},{28,24},{1,29},{... | collective-permute-start | bytes 3342344 | tf_op jit(solution)/shard_map/ppermute | solution.py:28
  35.5 3.5 %shard_map.86 = bf16[32,4,3,32,128]{4,3,2,1,0:T(8,128)(2,1)S(1)} custom-call(s32[32,4]{1,0:T(8,128)S(1)} %copy.40.wanted_ref, bf16[32,17408]{1,0:T(8,128)(2,1)S(1)} %pad_maximum_fusion.2.refs_0_, bf16[32,17408]{1,0:T(8,128)(2,1)} %collective-permute-done.refs_1_, bf16[32,17408]{1,0:T(8,128)(2,1)} %collective-permute-done.1.refs_2_), custom_call_target="tpu_custom_call" | custom-call | flops 20000000000 | bytes 6291456 | tf_op jit(solution)/shard_map/pallas_call | solution.py:51
  39.1 1.6 copy-done.1
  40.7 7.8 %all-to-all-start.1 = ((bf16[32,4,3,32,128]{4,3,2,1,0:T(8,128)(2,1)}), bf16[32,4,3,32,128]{4,3,2,1,0:T(8,128)(2,1)S(1)}, u32[]{:S(2)}, u32[]{:S(2)}) async-start(bf16[32,4,3,32,128]{4,3,2,1,0:T(8,128)(2,1)} %copy-done.1), calls=%async_computation.1 | async-start | bytes 6291456 | tf_op jit(solution)/shard_map/all_to_all | solution.py:32
  48.5 10.3 %collective-permute-done.3.refs_1_ = bf16[32,17408]{1,0:T(8,128)(2,1)} collective-permute-done((bf16[32,17408]{1,0:T(8,128)(2,1)}, bf16[32,17408]{1,0:T(8,128)(2,1)}, u32[]{:S(2)}, u32[]{:S(2)}) %collective-permute-start.3) | collective-permute-done | bytes 1114144 | tf_op jit(solution)/shard_map/ppermute | solution.py:28
  58.8 3.7 %collective-permute-start.5 = (bf16[32,17408]{1,0:T(8,128)(2,1)}, bf16[32,17408]{1,0:T(8,128)(2,1)S(1)}, u32[]{:S(2)}, u32[]{:S(2)}) collective-permute-start(bf16[32,17408]{1,0:T(8,128)(2,1)} %collective-permute-done.3.refs_1_), channel_id=1, source_target_pairs={{0,28},{4,0},{8,4},{12,8},{16,12},{20,16},{24,20},{28,24},{1,29},{... | collective-permute-start | bytes 3342344 | tf_op jit(solution)/shard_map/ppermute | solution.py:28
  63.1 1.5 fusion.10
  64.6 20.2 %collective-permute-done.5.refs_1_ = bf16[32,17408]{1,0:T(8,128)(2,1)S(1)} collective-permute-done((bf16[32,17408]{1,0:T(8,128)(2,1)}, bf16[32,17408]{1,0:T(8,128)(2,1)S(1)}, u32[]{:S(2)}, u32[]{:S(2)}) %collective-permute-start.5) | collective-permute-done | bytes 1114144 | tf_op jit(solution)/shard_map/ppermute | solution.py:28
  84.8 0.9 slice.50
  85.7 3.6 %collective-permute-start.7 = (bf16[16,17408]{1,0:T(8,128)(2,1)}, bf16[16,17408]{1,0:T(8,128)(2,1)}, u32[]{:S(2)}, u32[]{:S(2)}) collective-permute-start(bf16[16,17408]{1,0:T(8,128)(2,1)} %slice.50), channel_id=1, source_target_pairs={{0,28},{4,0},{8,4},{12,8},{16,12},{20,16},{24,20},{28,24},{1,29},{... | collective-permute-start | bytes 1671176 | tf_op jit(solution)/shard_map/ppermute | solution.py:28
  89.3 0.9 slice.49
  90.6 3.3 %shard_map.88 = bf16[32,4,2,32,128]{4,3,2,1,0:T(8,128)(2,1)S(1)} custom-call(s32[32,4]{1,0:T(8,128)S(1)} %copy.40.wanted_ref, bf16[32,17408]{1,0:T(8,128)(2,1)} %collective-permute-done.2.refs_0_, bf16[32,17408]{1,0:T(8,128)(2,1)} %collective-permute-done.3.refs_1_), custom_call_target="tpu_custom_call" | custom-call | flops 20000000000 | bytes 4194304 | tf_op jit(solution)/shard_map/pallas_call | solution.py:51
  93.9 1.3 copy-done.2
  95.2 7.7 %all-to-all-start.2 = ((bf16[32,4,2,32,128]{4,3,2,1,0:T(8,128)(2,1)}), bf16[32,4,2,32,128]{4,3,2,1,0:T(8,128)(2,1)}, u32[]{:S(2)}, u32[]{:S(2)}) async-start(bf16[32,4,2,32,128]{4,3,2,1,0:T(8,128)(2,1)} %copy-done.2), calls=%async_computation.2 | async-start | bytes 4194304 | tf_op jit(solution)/shard_map/all_to_all | solution.py:32
  102.9 1.5 fusion.9
  104.3 1.2 copy-done.4
  105.6 1.2 copy-done.6
  106.8 3.1 %shard_map.90 = bf16[32,4,3,32,128]{4,3,2,1,0:T(8,128)(2,1)S(1)} custom-call(s32[32,4]{1,0:T(8,128)S(1)} %copy.40.wanted_ref, bf16[32,17408]{1,0:T(8,128)(2,1)S(1)} %copy-done.6, bf16[32,17408]{1,0:T(8,128)(2,1)S(1)} %copy-done.4, bf16[16,17408]{1,0:T(8,128)(2,1)} %collective-permute-done.6.refs_2_, bf16[16,17408]{1,0:T(8,128)(2,1)} %collective-permute-done.7.refs_3_), custom_call_target="tpu_custom_call" | custom-call | flops 20000000000 | bytes 8388608 | tf_op jit(solution)/shard_map/pallas_call | solution.py:51
  110.0 1.7 copy-done
  111.7 20.0 %all-to-all-done.2.part = bf16[32,4,2,32,128]{4,3,2,1,0:T(8,128)(2,1)} async-done(((bf16[32,4,2,32,128]{4,3,2,1,0:T(8,128)(2,1)}), bf16[32,4,2,32,128]{4,3,2,1,0:T(8,128)(2,1)}, u32[]{:S(2)}, u32[]{:S(2)}) %all-to-all-start.2) | async-done | bytes 2097184 | tf_op jit(solution)/shard_map/all_to_all | solution.py:32
  131.6 5.9 %all-to-all-start.3 = ((bf16[32,4,3,32,128]{4,3,2,1,0:T(8,128)(2,1)}), bf16[32,4,3,32,128]{4,3,2,1,0:T(8,128)(2,1)}, u32[]{:S(2)}, u32[]{:S(2)}) async-start(bf16[32,4,3,32,128]{4,3,2,1,0:T(8,128)(2,1)} %copy-done), calls=%async_computation.3 | async-start | bytes 6291456 | tf_op jit(solution)/shard_map/all_to_all | solution.py:32
  137.6 1.5 fusion.8
  139.1 1.5 fusion.7
  140.5 1.5 fusion.6
  142.0 1.5 fusion.5
  145.6 2.8 %collective-permute-start.8 = (bf16[8,32,1024]{2,1,0:T(8,128)(2,1)}, bf16[8,32,1024]{2,1,0:T(8,128)(2,1)}, u32[]{:S(2)}, u32[]{:S(2)}) collective-permute-start(bf16[8,32,1024]{2,1,0:T(8,128)(2,1)} %fusion.11), channel_id=1, source_target_pairs={{0,130},{2,128},{128,2},{130,0},{1,131},{3,129},{129,3},{131,1},{4... | collective-permute-start | bytes 1572872 | tf_op jit(solution)/shard_map/ppermute | solution.py:135
  148.4 38.0 %collective-permute-done.8 = bf16[8,32,1024]{2,1,0:T(8,128)(2,1)} collective-permute-done((bf16[8,32,1024]{2,1,0:T(8,128)(2,1)}, bf16[8,32,1024]{2,1,0:T(8,128)(2,1)}, u32[]{:S(2)}, u32[]{:S(2)}) %collective-permute-start.8) | collective-permute-done | bytes 524320 | tf_op jit(solution)/shard_map/ppermute | solution.py:135
  186.5 1.3 select_bitcast_fusion.1
  187.8 1.5 fusion.15
  189.3 1.2 copy-done.7
  190.5 4.5 %shard_map.87 = bf16[384,1024]{1,0:T(8,128)(2,1)S(1)} custom-call(s32[1]{0:T(128)} %bitcast.core_ref, s32[8,4]{1,0:T(8,128)S(1)} %copy.41.tgt_ref, s32[8]{0:T(128)S(1)} %bitcast.74, bf16[8,4,128,128]{3,2,1,0:T(8,128)(2,1)S(1)} %bitcast.71, bf16[32,4,3,32,128]{4,3,2,1,0:T(8,128)(2,1)S(1)} %all-to-all-done.1.part), custom_call_target="tpu_custom_call" | custom-call | flops 3000000000 | bytes 8388608 | tf_op jit(solution)/shard_map/pallas_call | solution.py:94
  195.0 0.9 copy-done.11
  195.9 5.1 %shard_map.89 = bf16[256,1024]{1,0:T(8,128)(2,1)S(1)} custom-call(s32[1]{0:T(128)} %bitcast.core_ref, s32[8,4]{1,0:T(8,128)S(1)} %copy.41.tgt_ref, s32[8]{0:T(128)S(1)} %bitcast.75, bf16[8,4,128,128]{3,2,1,0:T(8,128)(2,1)S(1)} %bitcast.72, bf16[32,4,2,32,128]{4,3,2,1,0:T(8,128)(2,1)} %all-to-all-done.2.part), custom_call_target="tpu_custom_call" | custom-call | flops 3000000000 | bytes 8388608 | tf_op jit(solution)/shard_map/pallas_call | solution.py:94
  201.1 1.4 pad_maximum_fusion.1
  202.5 1.5 copy.46
  204.0 5.9 %shard_map.91 = bf16[384,1024]{1,0:T(8,128)(2,1)S(1)} custom-call(s32[1]{0:T(128)} %bitcast.core_ref, s32[8,4]{1,0:T(8,128)S(1)} %copy.41.tgt_ref, s32[8]{0:T(128)S(1)} %bitcast.76, bf16[8,4,128,128]{3,2,1,0:T(8,128)(2,1)S(1)} %bitcast.73, bf16[32,4,3,32,128]{4,3,2,1,0:T(8,128)(2,1)} %all-to-all-done.3.part), custom_call_target="tpu_custom_call" | custom-call | flops 3000000000 | bytes 8388608 | tf_op jit(solution)/shard_map/pallas_call | solution.py:94
  210.0 4.3 %multiply_convert_fusion.1 = (bf16[1024,1024]{1,0:T(8,128)(2,1)}, f32[1024,1024]{1,0:T(8,128)S(1)}) fusion(bf16[1024,1024]{1,0:T(8,128)(2,1)S(1)} %bitcast.81, bf16[384,1024]{1,0:T(8,128)(2,1)S(1)} %shard_map.91, bf16[256,1024]{1,0:T(8,128)(2,1)S(1)} %shard_map.89, bf16[384,1024]{1,0:T(8,128)(2,1)S(1)} %copy-done.12), kind=kOutput, calls=%fused_computation.1 | convolution fusion | flops 2159017984 | bytes 10485760 | tf_op jit(solution)/shard_map/dot_general | solution.py:175
  214.3 2.6 fusion.2
  217.1 2.6 collective-permute-done.10
  220.5 1.2 copy.49
  221.7 6.9 %all-to-all-start.4 = ((bf16[16,8,32,128]{3,2,1,0:T(8,128)(2,1)}), bf16[16,8,32,128]{3,2,1,0:T(8,128)(2,1)S(1)}, u32[]{:S(2)}, u32[]{:S(2)}) async-start(bf16[16,8,32,128]{3,2,1,0:T(8,128)(2,1)} %bitcast.26), calls=%async_computation.4 | async-start | bytes 2097152 | tf_op jit(solution)/shard_map/all_to_all | solution.py:32
  228.6 19.0 %all-to-all-done.4.came_ref = bf16[16,8,32,128]{3,2,1,0:T(8,128)(2,1)S(1)} async-done(((bf16[16,8,32,128]{3,2,1,0:T(8,128)(2,1)}), bf16[16,8,32,128]{3,2,1,0:T(8,128)(2,1)S(1)}, u32[]{:S(2)}, u32[]{:S(2)}) %all-to-all-start.4) | async-done | bytes 1048608 | tf_op jit(solution)/shard_map/all_to_all | solution.py:32
  247.7 11.8 %all_to_all.36 = f32[8,32,128]{2,1,0:T(8,128)S(1)} all-to-all(f32[8,32,128]{2,1,0:T(8,128)S(1)} %shard_map.92), channel_id=1, replica_groups=mesh['ylo'=2,'x'=4,'z'=8,'yhi'=2,'core'=2] {'z'}, dimensions={0} | all-to-all | bytes 262144 | tf_op jit(solution)/shard_map/all_to_all | solution.py:32
  259.6 10.1 %all_to_all.37 = f32[8,32,128]{2,1,0:T(8,128)S(1)} all-to-all(f32[8,32,128]{2,1,0:T(8,128)S(1)} %broadcast_in_dim.18), channel_id=1, replica_groups=mesh['ylo'=2,'x'=4,'z'=8,'yhi'=2,'core'=2] {'ylo','x'}, dimensions={0} | all-to-all | bytes 262144 | tf_op jit(solution)/shard_map/all_to_all | solution.py:32
  (61 shorter events, 5.3 us)
Async XLA Ops:
  0.6 7.3 %copy-start.16 = (s32[1,1,8,4]{2,3,1,0:T(4,128)S(1)}, s32[1,1,8,4]{2,3,1,0:T(4,128)}, u32[]{:S(2)}) copy-start(s32[1,1,8,4]{2,3,1,0:T(4,128)} %param.9) | copy-start | bytes 388
  2.0 29.8 %collective-permute-start.1 = (bf16[32,17408]{1,0:T(8,128)(2,1)S(1)}, bf16[32,17408]{1,0:T(8,128)(2,1)}, u32[]{:S(2)}, u32[]{:S(2)}) collective-permute-start(bf16[32,17408]{1,0:T(8,128)(2,1)S(1)} %pad_maximum_fusion.2.refs_0_), channel_id=1, source_target_pairs={{0,28},{4,0},{8,4},{12,8},{16,12},{20,16},{24,20},{28,24},{1,29},{... | collective-permute-start | bytes 3342344 | tf_op jit(solution)/shard_map/ppermute | solution.py:28
  7.9 27.6 %collective-permute-start = (bf16[32,17408]{1,0:T(8,128)(2,1)S(1)}, bf16[32,17408]{1,0:T(8,128)(2,1)}, u32[]{:S(2)}, u32[]{:S(2)}) collective-permute-start(bf16[32,17408]{1,0:T(8,128)(2,1)S(1)} %pad_maximum_fusion.2.refs_0_), channel_id=1, source_target_pairs={{0,4},{4,8},{8,12},{12,16},{16,20},{20,24},{24,28},{28,0},{1,5},{5... | collective-permute-start | bytes 3342344 | tf_op jit(solution)/shard_map/ppermute | solution.py:28
  31.7 27.1 %collective-permute-start.3 = (bf16[32,17408]{1,0:T(8,128)(2,1)}, bf16[32,17408]{1,0:T(8,128)(2,1)}, u32[]{:S(2)}, u32[]{:S(2)}) collective-permute-start(bf16[32,17408]{1,0:T(8,128)(2,1)} %collective-permute-done.1.refs_2_), channel_id=1, source_target_pairs={{0,28},{4,0},{8,4},{12,8},{16,12},{20,16},{24,20},{28,24},{1,29},{... | collective-permute-start | bytes 3342344 | tf_op jit(solution)/shard_map/ppermute | solution.py:28
  35.5 27.0 %collective-permute-start.2 = (bf16[32,17408]{1,0:T(8,128)(2,1)}, bf16[32,17408]{1,0:T(8,128)(2,1)}, u32[]{:S(2)}, u32[]{:S(2)}) collective-permute-start(bf16[32,17408]{1,0:T(8,128)(2,1)} %collective-permute-done.refs_1_), channel_id=1, source_target_pairs={{0,4},{4,8},{8,12},{12,16},{16,20},{20,24},{24,28},{28,0},{1,5},{5... | collective-permute-start | bytes 3342344 | tf_op jit(solution)/shard_map/ppermute | solution.py:28
  39.1 1.6 copy-start.1
  40.7 21.8 %copy-start.15 = (bf16[32,1024]{1,0:T(8,128)(2,1)S(1)}, bf16[32,1024]{1,0:T(8,128)(2,1)}, u32[]{:S(2)}) copy-start(bf16[32,1024]{1,0:T(8,128)(2,1)} %param.12) | copy-start | bytes 196612
  40.7 54.5 %all-to-all-start.1 = ((bf16[32,4,3,32,128]{4,3,2,1,0:T(8,128)(2,1)}), bf16[32,4,3,32,128]{4,3,2,1,0:T(8,128)(2,1)S(1)}, u32[]{:S(2)}, u32[]{:S(2)}) async-start(bf16[32,4,3,32,128]{4,3,2,1,0:T(8,128)(2,1)} %copy-done.1), calls=%async_computation.1 | async-start | bytes 6291456 | tf_op jit(solution)/shard_map/all_to_all | solution.py:32
  58.8 26.0 %collective-permute-start.5 = (bf16[32,17408]{1,0:T(8,128)(2,1)}, bf16[32,17408]{1,0:T(8,128)(2,1)S(1)}, u32[]{:S(2)}, u32[]{:S(2)}) collective-permute-start(bf16[32,17408]{1,0:T(8,128)(2,1)} %collective-permute-done.3.refs_1_), channel_id=1, source_target_pairs={{0,28},{4,0},{8,4},{12,8},{16,12},{20,16},{24,20},{28,24},{1,29},{... | collective-permute-start | bytes 3342344 | tf_op jit(solution)/shard_map/ppermute | solution.py:28
  62.5 26.8 %collective-permute-start.4 = (bf16[32,17408]{1,0:T(8,128)(2,1)}, bf16[32,17408]{1,0:T(8,128)(2,1)S(1)}, u32[]{:S(2)}, u32[]{:S(2)}) collective-permute-start(bf16[32,17408]{1,0:T(8,128)(2,1)} %collective-permute-done.2.refs_0_), channel_id=1, source_target_pairs={{0,4},{4,8},{8,12},{12,16},{16,20},{20,24},{24,28},{28,0},{1,5},{5... | collective-permute-start | bytes 3342344 | tf_op jit(solution)/shard_map/ppermute | solution.py:28
  84.8 5.4 %copy-start.3 = (bf16[32,17408]{1,0:T(8,128)(2,1)}, bf16[32,17408]{1,0:T(8,128)(2,1)S(1)}, u32[]{:S(2)}) copy-start(bf16[32,17408]{1,0:T(8,128)(2,1)S(1)} %collective-permute-done.5.refs_1_) | copy-start | bytes 3342340
  85.7 18.6 %collective-permute-start.7 = (bf16[16,17408]{1,0:T(8,128)(2,1)}, bf16[16,17408]{1,0:T(8,128)(2,1)}, u32[]{:S(2)}, u32[]{:S(2)}) collective-permute-start(bf16[16,17408]{1,0:T(8,128)(2,1)} %slice.50), channel_id=1, source_target_pairs={{0,28},{4,0},{8,4},{12,8},{16,12},{20,16},{24,20},{28,24},{1,29},{... | collective-permute-start | bytes 1671176 | tf_op jit(solution)/shard_map/ppermute | solution.py:28
  89.3 1.3 copy-start.5
  90.6 13.7 %collective-permute-start.6 = (bf16[16,17408]{1,0:T(8,128)(2,1)}, bf16[16,17408]{1,0:T(8,128)(2,1)}, u32[]{:S(2)}, u32[]{:S(2)}) collective-permute-start(bf16[16,17408]{1,0:T(8,128)(2,1)} %slice.49), channel_id=1, source_target_pairs={{0,4},{4,8},{8,12},{12,16},{16,20},{20,24},{24,28},{28,0},{1,5},{5... | collective-permute-start | bytes 1671176 | tf_op jit(solution)/shard_map/ppermute | solution.py:28
  93.9 1.3 copy-start.2
  95.2 36.4 %all-to-all-start.2 = ((bf16[32,4,2,32,128]{4,3,2,1,0:T(8,128)(2,1)}), bf16[32,4,2,32,128]{4,3,2,1,0:T(8,128)(2,1)}, u32[]{:S(2)}, u32[]{:S(2)}) async-start(bf16[32,4,2,32,128]{4,3,2,1,0:T(8,128)(2,1)} %copy-done.2), calls=%async_computation.2 | async-start | bytes 4194304 | tf_op jit(solution)/shard_map/all_to_all | solution.py:32
  104.3 1.2 copy-start.4
  105.6 1.2 copy-start.6
  110.0 1.7 copy-start
  131.6 72.4 %all-to-all-start.3 = ((bf16[32,4,3,32,128]{4,3,2,1,0:T(8,128)(2,1)}), bf16[32,4,3,32,128]{4,3,2,1,0:T(8,128)(2,1)}, u32[]{:S(2)}, u32[]{:S(2)}) async-start(bf16[32,4,3,32,128]{4,3,2,1,0:T(8,128)(2,1)} %copy-done), calls=%async_computation.3 | async-start | bytes 6291456 | tf_op jit(solution)/shard_map/all_to_all | solution.py:32
  145.6 40.8 %collective-permute-start.8 = (bf16[8,32,1024]{2,1,0:T(8,128)(2,1)}, bf16[8,32,1024]{2,1,0:T(8,128)(2,1)}, u32[]{:S(2)}, u32[]{:S(2)}) collective-permute-start(bf16[8,32,1024]{2,1,0:T(8,128)(2,1)} %fusion.11), channel_id=1, source_target_pairs={{0,130},{2,128},{128,2},{130,0},{1,131},{3,129},{129,3},{131,1},{4... | collective-permute-start | bytes 1572872 | tf_op jit(solution)/shard_map/ppermute | solution.py:135
  187.7 1.5 copy-start.17
  187.8 1.6 copy-start.10
  189.2 11.8 %collective-permute-start.9 = (bf16[8,2,32,1024]{3,2,0,1:T(8,128)(2,1)}, bf16[8,2,32,1024]{3,2,0,1:T(8,128)(2,1)}, u32[]{:S(2)}, u32[]{:S(2)}) collective-permute-start(bf16[8,2,32,1024]{3,2,0,1:T(8,128)(2,1)} %get-tuple-element.3), channel_id=1, source_target_pairs={{0,1},{1,0},{2,3},{3,2},{4,5},{5,4},{6,7},{7,6},{8,9},{9,8},{10,11... | collective-permute-start | bytes 3145736 | tf_op jit(solution)/shard_map/ppermute | solution.py:138
  189.3 1.2 copy-start.7
  190.5 5.4 %copy-start.8 = (bf16[1,1,8,4,128,128]{5,4,3,2,1,0:T(8,128)(2,1)S(1)}, bf16[1,1,8,4,128,128]{5,4,3,2,1,0:T(8,128)(2,1)}, u32[]{:S(2)}) copy-start(bf16[1,1,8,4,128,128]{5,4,3,2,1,0:T(8,128)(2,1)} %param.11) | copy-start | bytes 3145732
  195.0 0.9 copy-start.11
  195.9 5.1 %copy-start.13 = (bf16[8,2,1,32,1024]{4,3,0,1,2:T(8,128)(2,1)S(1)}, bf16[8,2,1,32,1024]{4,3,0,1,2:T(8,128)(2,1)}, u32[]{:S(2)}) copy-start(bf16[8,2,1,32,1024]{4,3,0,1,2:T(8,128)(2,1)} %get-tuple-element.2) | copy-start | bytes 3145732
  202.5 1.5 copy-start.9
  204.0 6.0 %copy-start.12 = (bf16[384,1024]{1,0:T(8,128)(2,1)S(1)}, bf16[384,1024]{1,0:T(8,128)(2,1)}, u32[]{:S(2)}) copy-start(bf16[384,1024]{1,0:T(8,128)(2,1)} %copy-done.11) | copy-start | bytes 2359300
  204.0 6.0 %copy-start.14 = (bf16[8,2,2,32,1024]{4,3,2,1,0:T(8,128)(2,1)S(1)}, bf16[8,2,2,32,1024]{4,3,2,1,0:T(8,128)(2,1)}, u32[]{:S(2)}) copy-start(bf16[8,2,2,32,1024]{4,3,2,1,0:T(8,128)(2,1)} %copy.46) | copy-start | bytes 6291460
  210.0 4.3 %copy-start.18 = (bf16[1024,1024]{1,0:T(8,128)(2,1)S(1)}, bf16[1024,1024]{1,0:T(8,128)(2,1)}, u32[]{:S(2)}) copy-start(bf16[1024,1024]{1,0:T(8,128)(2,1)} %param.13) | copy-start | bytes 6291460
  217.0 2.7 %collective-permute-start.10 = (bf16[8,2,32,1024]{3,2,1,0:T(8,128)(2,1)S(1)}, bf16[8,2,32,1024]{3,2,1,0:T(8,128)(2,1)S(1)}, u32[]{:S(2)}, u32[]{:S(2)}) collective-permute-start(bf16[8,2,32,1024]{3,2,1,0:T(8,128)(2,1)S(1)} %fusion.3), channel_id=1, source_target_pairs={{0,1},{1,0},{2,3},{3,2},{4,5},{5,4},{6,7},{7,6},{8,9},{9,8},{10,11... | collective-permute-start | bytes 3145736 | tf_op jit(solution)/shard_map/ppermute | solution.py:123
  221.7 25.9 %all-to-all-start.4 = ((bf16[16,8,32,128]{3,2,1,0:T(8,128)(2,1)}), bf16[16,8,32,128]{3,2,1,0:T(8,128)(2,1)S(1)}, u32[]{:S(2)}, u32[]{:S(2)}) async-start(bf16[16,8,32,128]{3,2,1,0:T(8,128)(2,1)} %bitcast.26), calls=%async_computation.4 | async-start | bytes 2097152 | tf_op jit(solution)/shard_map/all_to_all | solution.py:32

commit v3 on v2

v3 whole, which is shorter than its diff:
```python
import functools
import math

import jax
import jax.numpy as jnp
from jax import lax
from jax.experimental import pallas as pl
from jax.experimental.pallas import tpu as pltpu
from jax.sharding import Mesh, PartitionSpec as P

REP = ("ylo", "x")
PLANE = ("ylo", "x", "yhi", "core")
CHIPS_XY = ("ylo", "x", "yhi")
ZN = 8
FIRST = (0, 1, -1)
SECOND = (2, -2, 3, -3, 4)
ORDER = FIRST + SECOND
LANES = 4
VMEM = pl.BlockSpec(memory_space=pltpu.VMEM)
SMEM = pl.BlockSpec(memory_space=pltpu.SMEM)
ANY = pl.BlockSpec(memory_space=pl.ANY)
SWAP = [(0, 1), (1, 0)]


def params(mib):
    return pltpu.CompilerParams(vmem_limit_bytes=mib * 2**20)


def cost(flops, size):
    return pl.CostEstimate(flops=flops, bytes_accessed=size, transcendentals=0)


def shift_z(value, step):
    return lax.ppermute(value, "z", [(i, (i + step) % ZN) for i in range(ZN)])


def exchange(value, axes):
    return lax.all_to_all(value, axes, split_axis=0, concat_axis=0, tiled=True)


def ring(own):
    half = own.shape[0] // 2
    held = {0: own}
    for step in range(1, ZN // 2):
        held[step] = shift_z(held[step - 1], 1)
        held[-step] = shift_z(held[1 - step], -1)
    far = ZN // 2 - 1
    held[ZN // 2] = shift_z(held[far][:half], 1), shift_z(held[-far][half:], -1)
    return held


def pick_into(wanted_ref, slices, places, target, block):
    slots = target.shape[1]

    def one(step, carry):
        dest, slot = step // slots, step % slots
        start = pl.multiple_of(wanted_ref[dest, slot] * block, block)
        for ref, (place, low, high) in zip(slices, places):
            target[dest, slot, place, low:high, :] = ref[:, pl.ds(start, block)]
        return carry

    lax.fori_loop(0, target.shape[0] * slots, one, 0, unroll=4)


def pick_kernel(block, wanted_ref, *refs):
    slices, out_ref = refs[:-1], refs[-1]
    places = [(place, 0, ref.shape[0]) for place, ref in enumerate(slices)]
    pick_into(wanted_ref, slices, places, out_ref, block)


def pick(wanted, slices, block, flops):
    askers, slots = wanted.shape
    return pl.pallas_call(
        functools.partial(pick_kernel, block),
        out_shape=jax.ShapeDtypeStruct((askers, slots, len(slices), slices[0].shape[0], block), jnp.bfloat16),
        in_specs=[SMEM] + [VMEM] * len(slices),
        out_specs=VMEM,
        compiler_params=params(40),
        cost_estimate=cost(flops, len(slices) * 2**21),
    )(wanted, *slices)


def pick_most_kernel(block, wanted_ref, *refs):
    slices, (out_ref, buffer, sem) = refs[:-3], refs[-3:]
    places = [(place, 0, ref.shape[0]) for place, ref in enumerate(slices)]
    pick_into(wanted_ref, slices, places, buffer, block)
    copy = pltpu.make_async_copy(buffer, out_ref.at[:, :, : len(slices)], sem)
    copy.start()
    copy.wait()


def pick_most(wanted, slices, places, block, flops):
    askers, slots = wanted.shape
    rows = slices[0].shape[0]
    return pl.pallas_call(
        functools.partial(pick_most_kernel, block),
        out_shape=jax.ShapeDtypeStruct((askers, slots, places, rows, block), jnp.bfloat16),
        in_specs=[SMEM] + [VMEM] * len(slices),
        out_specs=ANY,
        scratch_shapes=[pltpu.VMEM((askers, slots, len(slices), rows, block), jnp.bfloat16), pltpu.SemaphoreType.DMA],
        compiler_params=params(40),
        cost_estimate=cost(flops, len(slices) * 2**21),
    )(wanted, *slices)


def pick_last_kernel(block, wanted_ref, up_ref, down_ref, _, out_ref, buffer, sem):
    half, rows = up_ref.shape[0], buffer.shape[3]
    pick_into(wanted_ref, (up_ref, down_ref), ((0, 0, half), (0, half, rows)), buffer, block)
    copy = pltpu.make_async_copy(buffer, out_ref.at[:, :, out_ref.shape[2] - 1 :], sem)
    copy.start()
    copy.wait()


def pick_last(wanted, up, down, most, block, flops):
    askers, slots, _, rows, _ = most.shape
    return pl.pallas_call(
        functools.partial(pick_last_kernel, block),
        out_shape=jax.ShapeDtypeStruct(most.shape, most.dtype),
        in_specs=[SMEM, VMEM, VMEM, ANY],
        out_specs=ANY,
        input_output_aliases={3: 0},
        scratch_shapes=[pltpu.VMEM((askers, slots, 1, rows, block), jnp.bfloat16), pltpu.SemaphoreType.DMA],
        compiler_params=params(24),
        cost_estimate=cost(flops, 2**21),
    )(wanted, up, down, most)


def add_tiles(core, tgt_ref, count_ref, vals_ref, part, acc):
    sections, slots, block, _ = vals_ref.shape
    places, rows = part.shape[2:4]
    acc[...] = jnp.zeros_like(acc)

    def one(step, carry):
        section, slot = step // slots, step % slots

        @pl.when(slot < count_ref[section])
        def _():
            column = pl.multiple_of(tgt_ref[section, slot] * block, block)
            sources = [section * LANES + lane + core * (1 - 2 * (lane % 2)) for lane in range(LANES)]
            columns_in = jnp.concatenate([part[source, slot].reshape(places * rows, block) for source in sources])
            contrib = lax.dot_general(
                columns_in, vals_ref[section, slot], (((1,), (1,)), ((), ())), preferred_element_type=jnp.float32
            )
            for lane in range(LANES):
                for place in range(places):
                    low, at = (place * LANES + lane) * rows, (lane * places + place) * rows
                    acc[low : low + rows, pl.ds(column, block)] += contrib[at : at + rows]

        return carry

    lax.fori_loop(0, sections * slots, one, 0)


def aggregate_kernel(core_ref, tgt_ref, count_ref, vals_ref, part, out_ref, acc):
    add_tiles(core_ref[0], tgt_ref, count_ref, vals_ref, part, acc)
    out_ref[...] = acc[...].astype(out_ref.dtype)


def aggregate(core, targets, counts, values, part, num_rows):
    num_feats = LANES * part.shape[2] * part.shape[3]
    return pl.pallas_call(
        aggregate_kernel,
        out_shape=jax.ShapeDtypeStruct((num_feats, num_rows), jnp.bfloat16),
        in_specs=[SMEM] * 3 + [VMEM] * 2,
        out_specs=VMEM,
        scratch_shapes=[pltpu.VMEM((num_feats, num_rows), jnp.float32)],
        compiler_params=params(32),
        cost_estimate=cost(3 * 10**9, 8 * 2**20),
    )(core, targets, counts, values, part)


def layer_kernel(
    core_ref, tgt_ref, count_ref, vals_ref, part, early_ref, weight_ref, cot_ref, act_ref, kept_ref, gone_ref, acc, mixed, dpre
):
    early = early_ref.shape[0]
    add_tiles(core_ref[0], tgt_ref, count_ref, vals_ref, part, acc)
    mixed[:early] = early_ref[...]
    mixed[early:] = acc[...].astype(mixed.dtype)
    step = 256
    for low in range(0, act_ref.shape[0], step):
        at = slice(low, low + step)
        preact = lax.dot_general(
            mixed[:, at], weight_ref[...], (((0,), (0,)), ((), ())), preferred_element_type=jnp.float32
        )
        sigmoid_val = jax.nn.sigmoid(preact)
        act_ref[at] = (preact * sigmoid_val).astype(act_ref.dtype)
        slope = sigmoid_val * (1.0 + preact * (1.0 - sigmoid_val))
        dpre[at] = (cot_ref[at].astype(jnp.float32) * slope).astype(dpre.dtype)
    pieces, his, zs, rows, width = kept_ref.shape
    for low in range(0, mixed.shape[0], step):
        grad = jnp.dot(mixed[low : low + step], dpre[...], preferred_element_type=jnp.float32)
        for at in range(0, step, rows):
            lane = (low + at) // rows
            place, hi, core = lane // LANES, lane % LANES // 2, lane % 2
            for piece in range(pieces):
                value = grad[at : at + rows, piece * width : (piece + 1) * width]
                if core == 0:
                    kept_ref[piece, hi, place] = value
                else:
                    gone_ref[piece, hi, place] = value.astype(gone_ref.dtype)


def layer(core, targets, counts, values, part, early, weight, cotangent):
    tgt_rows, width = cotangent.shape
    feats = weight.shape[0]
    cut = (8, 2, ZN, part.shape[3], width // 8)
    late = feats - early.shape[0]
    return pl.pallas_call(
        layer_kernel,
        out_shape=(
            jax.ShapeDtypeStruct((tgt_rows, width), jnp.bfloat16),
            jax.ShapeDtypeStruct(cut, jnp.float32),
            jax.ShapeDtypeStruct(cut, jnp.bfloat16),
        ),
        in_specs=[SMEM] * 3 + [VMEM] * 5,
        out_specs=(VMEM, VMEM, VMEM),
        scratch_shapes=[
            pltpu.VMEM((late, tgt_rows), jnp.float32),
            pltpu.VMEM((feats, tgt_rows), jnp.bfloat16),
            pltpu.VMEM((tgt_rows, width), jnp.bfloat16),
        ],
        compiler_params=params(48),
        cost_estimate=cost(6 * 10**9, 20 * 2**20),
    )(core, targets, counts, values, part, early, weight, cotangent)


def sum_plane_kernel(z_ref, came_ref, out_ref):
    for place, distance in enumerate(ORDER):
        total = came_ref[:, place].astype(jnp.float32).sum(0)
        out_ref[lax.rem(z_ref[0] + (ZN - distance), ZN)] = total


def sum_plane(came):
    return pl.pallas_call(
        sum_plane_kernel,
        out_shape=jax.ShapeDtypeStruct(came.shape[1:], jnp.float32),
        in_specs=[SMEM, VMEM],
        out_specs=VMEM,
        compiler_params=params(16),
    )(lax.axis_index("z").astype(jnp.int32)[None], came)


def sum_over_devices(kept, gone):
    came = lax.ppermute(gone, "core", SWAP)
    chip = (kept + came.astype(jnp.float32)).astype(jnp.bfloat16)
    chip = chip.reshape(16, *chip.shape[2:])
    plane = sum_plane(exchange(chip, CHIPS_XY))
    column = exchange(plane, "z").sum(0)
    whole = exchange(jnp.broadcast_to(column[None], (8, *column.shape)), REP)
    return whole.transpose(1, 0, 2).reshape(column.shape[0], -1)


def weight_lanes(own):
    other = lax.ppermute(own, ("ylo", "yhi"), [(0, 3), (1, 2), (2, 1), (3, 0)])
    first = lax.axis_index("yhi") == 0
    both = jnp.stack([jnp.where(first, own, other), jnp.where(first, other, own)])
    lanes = jnp.stack([both, lax.ppermute(both, "core", SWAP)], axis=1)
    return lanes.reshape(-1, own.shape[1])


def whole_weight(lanes):
    held = ring(lanes)
    held[ZN // 2] = jnp.concatenate(held[ZN // 2])
    return jnp.concatenate([held[distance] for distance in ORDER])


def per_device(features, tile_tgt, tile_src, tile_count, tile_vals, weight, cotangent):
    block_size = tile_vals.shape[-1]
    tgt_rows = cotangent.shape[0]
    targets, sources, counts, values = tile_tgt[0, 0], tile_src[0, 0], tile_count[0, 0], tile_vals[0, 0]
    core = lax.axis_index("core").astype(jnp.int32)[None]

    wanted = exchange(jnp.repeat(sources, LANES, axis=0)[:, None, :], PLANE)[:, 0]
    wanted, lanes = lax.optimization_barrier((wanted, weight_lanes(weight)))
    held = ring(features[0])
    first = pick(wanted, [held[distance] for distance in FIRST], block_size, PICK_FLOPS[0])
    early = aggregate(core, targets, counts, values, exchange(first, PLANE), tgt_rows)
    most = pick_most(wanted, [held[d] for d in SECOND[:-1]], len(SECOND), block_size, PICK_FLOPS[1])
    second = pick_last(wanted, *held[SECOND[-1]], most, block_size, PICK_FLOPS[2])
    part = exchange(second, PLANE)
    weight_in = whole_weight(lanes)
    activations, kept, gone = layer(core, targets, counts, values, part, early, weight_in, cotangent)
    weight_grad = sum_over_devices(kept, gone) / math.sqrt(tgt_rows * 256)
    return (activations, weight_grad)


PICK_FLOPS = (20 * 10**9, 20 * 10**9, 10**9)


def solution(mesh):
    row = ("z", "yhi", "core")
    fine = Mesh(mesh.devices.reshape(2, 4, 8, 2, 2), ("ylo", "x", "z", "yhi", "core"))
    in_specs = (
        P(REP, row, None),
        P(REP, row, None, None),
        P(REP, row, None, None),
        P(REP, row, None),
        P(REP, row, None, None, None, None),
        P(row, None),
        P(REP + row, None),
    )
    out_specs = (P(REP + row, None), P(row, None))
    return jax.shard_map(per_device, mesh=fine, in_specs=in_specs, out_specs=out_specs, check_vma=False)
```

time: 273 us -> 249 us (0.912)
  local copies, waits for them, and re-layouts: 25.9 us -> 15 us
  matrix products: 6.9 us -> 0 us
  waiting for transfers between devices: 120 us -> 114 us
  starting transfers between devices: 48.2 us -> 52.6 us
  other arithmetic: 7.19 us -> 2.89 us
    ppermute x3, waiting for transfers between devices: 40.7 us -> 4.96 us  [the longest x1 2.67 us: weight_lanes(): other = lax.ppermute(own, ('ylo', 'yhi'), [(0, 3), (1, 2), (2, 1), (3, 0)])]
    all_to_all x4 -> x3, waiting for transfers between devices: 38.9 us -> 55.2 us  [exchange(): return lax.all_to_all(value, axes, split_axis=0, concat_axis=0, tiled=True)]
    ppermute x8 -> x16, waiting for transfers between devices: 40.6 us -> 53.4 us  [shift_z(): return lax.ppermute(value, 'z', [(i, (i + step) % ZN) for i in range(ZN)])]
    pallas_call x3 -> x1, Pallas kernels: 15.5 us -> 3.32 us  [aggregate(): pl.pallas_call(aggregate_kernel, out_shape=jax.ShapeDtypeStruct((num_feat...]
    ppermute x8 -> x16, starting transfers between devices: 17 us -> 29 us  [shift_z(): return lax.ppermute(value, 'z', [(i, (i + step) % ZN) for i in range(ZN)])]
    pallas_call x3 -> x4, Pallas kernels: 9.92 us -> 21.7 us  [the longest x1 11.7 us: layer(): pl.pallas_call(layer_kernel, out_shape=(jax.ShapeDtypeStruct((tgt_rows, w...]
    all_to_all x4 -> x3, starting transfers between devices: 28.3 us -> 19.9 us  [exchange(): return lax.all_to_all(value, axes, split_axis=0, concat_axis=0, tiled=True)]
    dot_general x2 -> x0, matrix products: 6.9 us -> none  [the longest x1 4.33 us: per_device(): lax.dot_general(mixed_t, weight_in, (((0,), (0,)), ((), ())), preferred_e...]
  transfers between devices with their start and end apart: 15 -> 22, of which waited for: 7 -> 12; matrix products, arithmetic and copies ran while one was open for 7% -> 2% of each run, Pallas kernels for 7% -> 5%
where the time goes in v3:
time: 249 us; the launch traced here: 248 us
  waiting for transfers between devices  114 us (46%)
  starting transfers between devices  52.6 us (21%)
  blocking collectives  37.6 us (15%)
  Pallas kernels  25.2 us (10%)
  local copies, waits for them, and re-layouts  15 us (6%)
  other arithmetic  2.89 us (1%)
    all_to_all x3, waiting for transfers between devices, exchange(): return lax.all_to_all(value, axes, split_axis=0, concat_axis=0, tiled=True)  55.2 us
    ppermute x16, waiting for transfers between devices, shift_z(): return lax.ppermute(value, 'z', [(i, (i + step) % ZN) for i in range(ZN)])  53.4 us
    all_to_all x3, blocking collectives, exchange(): return lax.all_to_all(value, axes, split_axis=0, concat_axis=0, tiled=True)  37.6 us
    ppermute x16, starting transfers between devices, shift_z(): return lax.ppermute(value, 'z', [(i, (i + step) % ZN) for i in range(ZN)])  29 us
    all_to_all x3, starting transfers between devices, exchange(): return lax.all_to_all(value, axes, split_axis=0, concat_axis=0, tiled=True)  19.9 us
    unnamed x29, local copies, waits for them, and re-layouts  14.6 us
    pallas_call x1, Pallas kernels, layer(): pl.pallas_call(layer_kernel, out_shape=(jax.ShapeDtypeStruct((tgt_rows, w...  11.7 us
  transfers between devices with their start and end apart: 22, of which 12 were waited for; matrix products, arithmetic and copies ran while one was open for 2% of the time, Pallas kernels for 5%

profile of v3, /device:TPU:2, one launch (start us, length us, event | category | flops | bytes accessed | tf_op | source)
XLA Modules:
  0.0 247.8 jit_solution(7442009022921962939)
XLA Ops:
  0.6 2.0 collective-permute-start.2
  2.6 4.0 %collective-permute-start.6 = (bf16[32,16384]{1,0:T(8,128)(2,1)}, bf16[32,16384]{1,0:T(8,128)(2,1)}, u32[]{:S(2)}, u32[]{:S(2)}) collective-permute-start(bf16[32,16384]{1,0:T(8,128)(2,1)} %bitcast.25), channel_id=1, source_target_pairs={{0,28},{4,0},{8,4},{12,8},{16,12},{20,16},{24,20},{28,24},{1,29},{... | collective-permute-start | bytes 3145736 | tf_op jit(solution)/shard_map/ppermute | solution.py:34
  6.7 3.0 %collective-permute-start = (bf16[32,1024]{1,0:T(8,128)(2,1)}, bf16[32,1024]{1,0:T(8,128)(2,1)S(1)}, u32[]{:S(2)}, u32[]{:S(2)}) collective-permute-start(bf16[32,1024]{1,0:T(8,128)(2,1)} %param.12), channel_id=1, source_target_pairs={{0,130},{2,128},{128,2},{130,0},{1,131},{3,129},{129,3},{131,1},{4... | collective-permute-start | bytes 196616 | tf_op jit(solution)/shard_map/ppermute | solution.py:254
  9.7 2.7 %collective-permute-done = bf16[32,1024]{1,0:T(8,128)(2,1)S(1)} collective-permute-done((bf16[32,1024]{1,0:T(8,128)(2,1)}, bf16[32,1024]{1,0:T(8,128)(2,1)S(1)}, u32[]{:S(2)}, u32[]{:S(2)}) %collective-permute-start) | collective-permute-done | bytes 65568 | tf_op jit(solution)/shard_map/ppermute | solution.py:254
  12.3 0.9 select_bitcast_fusion.1
  13.3 0.8 copy.40
  14.1 13.4 %all_to_all.30 = s32[32,1,4]{2,1,0:T(1,128)S(1)} all-to-all(s32[32,1,4]{2,1,0:T(1,128)S(1)} %bitcast.35), channel_id=1, replica_groups=mesh['ylo'=2,'x'=4,'z'=8,'yhi'=2,'core'=2] {'ylo','x','yhi','core'}, dimensions={0} | all-to-all | bytes 1024 | tf_op jit(solution)/shard_map/all_to_all | solution.py:38
  27.8 2.3 collective-permute-done.2.refs_1_
  30.0 3.2 %collective-permute-start.7 = (bf16[32,16384]{1,0:T(8,128)(2,1)}, bf16[32,16384]{1,0:T(8,128)(2,1)}, u32[]{:S(2)}, u32[]{:S(2)}) collective-permute-start(bf16[32,16384]{1,0:T(8,128)(2,1)} %collective-permute-done.6.refs_2_), channel_id=1, source_target_pairs={{0,28},{4,0},{8,4},{12,8},{16,12},{20,16},{24,20},{28,24},{1,29},{... | collective-permute-start | bytes 3145736 | tf_op jit(solution)/shard_map/ppermute | solution.py:34
  33.3 1.2 copy-done.2
  34.5 3.5 %shard_map.88 = bf16[32,4,3,32,128]{4,3,2,1,0:T(8,128)(2,1)S(1)} custom-call(s32[32,4]{1,0:T(8,128)S(1)} %copy.34.wanted_ref, bf16[32,16384]{1,0:T(8,128)(2,1)S(1)} %bitcast.26, bf16[32,16384]{1,0:T(8,128)(2,1)} %collective-permute-done.2.refs_1_, bf16[32,16384]{1,0:T(8,128)(2,1)} %collective-permute-done.6.refs_2_), custom_call_target="tpu_custom_call" | custom-call | flops 20000000000 | bytes 6291456 | tf_op jit(solution)/shard_map/pallas_call | solution.py:73
  38.0 1.7 copy-done.1
  39.7 7.6 %all-to-all-start.2 = ((bf16[32,4,3,32,128]{4,3,2,1,0:T(8,128)(2,1)}), bf16[32,4,3,32,128]{4,3,2,1,0:T(8,128)(2,1)S(1)}, u32[]{:S(2)}, u32[]{:S(2)}) async-start(bf16[32,4,3,32,128]{4,3,2,1,0:T(8,128)(2,1)} %copy-done.1), calls=%async_computation.2 | async-start | bytes 6291456 | tf_op jit(solution)/shard_map/all_to_all | solution.py:38
  47.3 8.6 %collective-permute-done.3.refs_0_ = bf16[32,16384]{1,0:T(8,128)(2,1)} collective-permute-done((bf16[32,16384]{1,0:T(8,128)(2,1)}, bf16[32,16384]{1,0:T(8,128)(2,1)}, u32[]{:S(2)}, u32[]{:S(2)}) %collective-permute-start.3) | collective-permute-done | bytes 1048608 | tf_op jit(solution)/shard_map/ppermute | solution.py:34
  55.9 3.2 %collective-permute-start.8 = (bf16[32,16384]{1,0:T(8,128)(2,1)}, bf16[32,16384]{1,0:T(8,128)(2,1)S(1)}, u32[]{:S(2)}, u32[]{:S(2)}) collective-permute-start(bf16[32,16384]{1,0:T(8,128)(2,1)} %collective-permute-done.7.refs_1_), channel_id=1, source_target_pairs={{0,28},{4,0},{8,4},{12,8},{16,12},{20,16},{24,20},{28,24},{1,29},{... | collective-permute-start | bytes 3145736 | tf_op jit(solution)/shard_map/ppermute | solution.py:34
  59.2 21.6 %collective-permute-done.4.refs_2_ = bf16[32,16384]{1,0:T(8,128)(2,1)S(1)} collective-permute-done((bf16[32,16384]{1,0:T(8,128)(2,1)}, bf16[32,16384]{1,0:T(8,128)(2,1)S(1)}, u32[]{:S(2)}, u32[]{:S(2)}) %collective-permute-start.4) | collective-permute-done | bytes 1048608 | tf_op jit(solution)/shard_map/ppermute | solution.py:34
  80.9 3.3 %collective-permute-start.9 = (bf16[16,16384]{1,0:T(8,128)(2,1)S(1)}, bf16[16,16384]{1,0:T(8,128)(2,1)S(1)}, u32[]{:S(2)}, u32[]{:S(2)}) collective-permute-start(bf16[16,16384]{1,0:T(8,128)(2,1)S(1)} %slice.17), channel_id=1, source_target_pairs={{0,28},{4,0},{8,4},{12,8},{16,12},{20,16},{24,20},{28,24},{1,29},{... | collective-permute-start | bytes 1572872 | tf_op jit(solution)/shard_map/ppermute | solution.py:34
  84.2 4.3 %shard_map.86._ = bf16[32,4,5,32,128]{4,3,2,1,0:T(8,128)(2,1)S(1)} custom-call(s32[32,4]{1,0:T(8,128)S(1)} %copy.34.wanted_ref, bf16[32,16384]{1,0:T(8,128)(2,1)} %collective-permute-done.3.refs_0_, bf16[32,16384]{1,0:T(8,128)(2,1)} %collective-permute-done.7.refs_1_, bf16[32,16384]{1,0:T(8,128)(2,1)S(1)} %collective-permute-done.4.refs_2_, ...), custom_call_target="tpu_custom_call" | custom-call | flops 20000000000 | bytes 8388608 | tf_op jit(solution)/shard_map/pallas_call | solution.py:95
  88.5 4.8 %collective-permute-done.5.up_ref = bf16[16,16384]{1,0:T(8,128)(2,1)S(1)} collective-permute-done((bf16[16,16384]{1,0:T(8,128)(2,1)S(1)}, bf16[16,16384]{1,0:T(8,128)(2,1)S(1)}, u32[]{:S(2)}, u32[]{:S(2)}) %collective-permute-start.5) | collective-permute-done | bytes 524320 | tf_op jit(solution)/shard_map/ppermute | solution.py:34
  93.4 2.3 shard_map.87
  95.6 2.3 copy-done
  98.0 7.8 %all-to-all-start.1 = ((bf16[32,4,5,32,128]{4,3,2,1,0:T(8,128)(2,1)}), bf16[32,4,5,32,128]{4,3,2,1,0:T(8,128)(2,1)}, u32[]{:S(2)}, u32[]{:S(2)}) async-start(bf16[32,4,5,32,128]{4,3,2,1,0:T(8,128)(2,1)} %copy-done), calls=%async_computation.1 | async-start | bytes 10485760 | tf_op jit(solution)/shard_map/all_to_all | solution.py:38
  105.9 3.2 %collective-permute-start.11 = (bf16[128,1024]{1,0:T(8,128)(2,1)S(1)}, bf16[128,1024]{1,0:T(8,128)(2,1)}, u32[]{:S(2)}, u32[]{:S(2)}) collective-permute-start(bf16[128,1024]{1,0:T(8,128)(2,1)S(1)} %bitcast.32), channel_id=1, source_target_pairs={{0,28},{4,0},{8,4},{12,8},{16,12},{20,16},{24,20},{28,24},{1,29},{... | collective-permute-start | bytes 786440 | tf_op jit(solution)/shard_map/ppermute | solution.py:34
  109.1 6.6 %collective-permute-done.10 = bf16[128,1024]{1,0:T(8,128)(2,1)} collective-permute-done((bf16[128,1024]{1,0:T(8,128)(2,1)S(1)}, bf16[128,1024]{1,0:T(8,128)(2,1)}, u32[]{:S(2)}, u32[]{:S(2)}) %collective-permute-start.10) | collective-permute-done | bytes 262176 | tf_op jit(solution)/shard_map/ppermute | solution.py:34
  115.6 3.2 %collective-permute-start.13 = (bf16[128,1024]{1,0:T(8,128)(2,1)}, bf16[128,1024]{1,0:T(8,128)(2,1)}, u32[]{:S(2)}, u32[]{:S(2)}) collective-permute-start(bf16[128,1024]{1,0:T(8,128)(2,1)} %collective-permute-done.11), channel_id=1, source_target_pairs={{0,28},{4,0},{8,4},{12,8},{16,12},{20,16},{24,20},{28,24},{1,29},{... | collective-permute-start | bytes 786440 | tf_op jit(solution)/shard_map/ppermute | solution.py:34
  119.0 1.1 constant_dynamic-update-slice_fusion.7
  120.1 4.8 %collective-permute-done.12 = bf16[128,1024]{1,0:T(8,128)(2,1)} collective-permute-done((bf16[128,1024]{1,0:T(8,128)(2,1)}, bf16[128,1024]{1,0:T(8,128)(2,1)}, u32[]{:S(2)}, u32[]{:S(2)}) %collective-permute-start.12) | collective-permute-done | bytes 262176 | tf_op jit(solution)/shard_map/ppermute | solution.py:34
  124.8 3.2 %collective-permute-start.15 = (bf16[128,1024]{1,0:T(8,128)(2,1)}, bf16[128,1024]{1,0:T(8,128)(2,1)S(1)}, u32[]{:S(2)}, u32[]{:S(2)}) collective-permute-start(bf16[128,1024]{1,0:T(8,128)(2,1)} %collective-permute-done.13), channel_id=1, source_target_pairs={{0,28},{4,0},{8,4},{12,8},{16,12},{20,16},{24,20},{28,24},{1,29},{... | collective-permute-start | bytes 786440 | tf_op jit(solution)/shard_map/ppermute | solution.py:34
  128.1 1.0 constant_dynamic-update-slice_fusion.6
  129.0 1.0 constant_dynamic-update-slice_fusion.5
  130.0 1.0 constant_dynamic-update-slice_fusion.4
  131.0 2.0 collective-permute-done.14
  133.1 3.3 %collective-permute-start.17 = (bf16[64,1024]{1,0:T(8,128)(2,1)S(1)}, bf16[64,1024]{1,0:T(8,128)(2,1)S(1)}, u32[]{:S(2)}, u32[]{:S(2)}) collective-permute-start(bf16[64,1024]{1,0:T(8,128)(2,1)S(1)} %slice.19), channel_id=1, source_target_pairs={{0,28},{4,0},{8,4},{12,8},{16,12},{20,16},{24,20},{28,24},{1,29},{... | collective-permute-start | bytes 393224 | tf_op jit(solution)/shard_map/ppermute | solution.py:34
  136.5 2.8 %collective-permute-done.16 = bf16[64,1024]{1,0:T(8,128)(2,1)S(1)} collective-permute-done((bf16[64,1024]{1,0:T(8,128)(2,1)S(1)}, bf16[64,1024]{1,0:T(8,128)(2,1)S(1)}, u32[]{:S(2)}, u32[]{:S(2)}) %collective-permute-start.16) | collective-permute-done | bytes 131104 | tf_op jit(solution)/shard_map/ppermute | solution.py:34
  139.3 1.4 copy-done.8
  140.7 3.3 %shard_map.89.early_ref = bf16[384,1024]{1,0:T(8,128)(2,1)S(1)} custom-call(s32[1]{0:T(128)} %bitcast.core_ref, s32[8,4]{1,0:T(8,128)S(1)} %copy.37.tgt_ref, s32[8]{0:T(128)S(1)} %bitcast.29, bf16[8,4,128,128]{3,2,1,0:T(8,128)(2,1)S(1)} %bitcast.27, bf16[32,4,3,32,128]{4,3,2,1,0:T(8,128)(2,1)S(1)} %all-to-all-done.2.part), custom_call_target="tpu_custom_call" | custom-call | flops 3000000000 | bytes 8388608 | tf_op jit(solution)/shard_map/pallas_call | solution.py:161
  144.0 0.9 copy-done.6
  144.9 37.1 %all-to-all-done.1.part = bf16[32,4,5,32,128]{4,3,2,1,0:T(8,128)(2,1)} async-done(((bf16[32,4,5,32,128]{4,3,2,1,0:T(8,128)(2,1)}), bf16[32,4,5,32,128]{4,3,2,1,0:T(8,128)(2,1)}, u32[]{:S(2)}, u32[]{:S(2)}) %all-to-all-start.1) | async-done | bytes 5242912 | tf_op jit(solution)/shard_map/all_to_all | solution.py:38
  182.1 1.2 copy-done.4
  183.3 1.1 copy-done.7
  184.4 11.7 %shard_map.90 = (bf16[1024,1024]{1,0:T(8,128)(2,1)}, f32[8,2,8,32,128]{4,3,2,1,0:T(8,128)S(1)}, bf16[8,2,8,32,128]{4,3,2,1,0:T(8,128)(2,1)S(1)}) custom-call(s32[1]{0:T(128)} %bitcast.core_ref, s32[8,4]{1,0:T(8,128)S(1)} %copy.37.tgt_ref, s32[8]{0:T(128)S(1)} %bitcast.30, bf16[8,4,128,128]{3,2,1,0:T(8,128)(2,1)S(1)} %bitcast.28, ...), custom_call_target="tpu_custom_call" | custom-call | flops 6000000000 | bytes 20971520 | tf_op jit(solution)/shard_map/pallas_call | solution.py:208
  196.7 2.3 collective-permute-done.18
  198.9 1.3 add_convert_fusion
  200.3 4.5 %all-to-all-start.3 = ((bf16[16,8,32,128]{3,2,1,0:T(8,128)(2,1)}), bf16[16,8,32,128]{3,2,1,0:T(8,128)(2,1)S(1)}, u32[]{:S(2)}, u32[]{:S(2)}) async-start(bf16[16,8,32,128]{3,2,1,0:T(8,128)(2,1)} %bitcast.14), calls=%async_computation.3 | async-start | bytes 2097152 | tf_op jit(solution)/shard_map/all_to_all | solution.py:38
  204.7 18.0 %all-to-all-done.3.came_ref = bf16[16,8,32,128]{3,2,1,0:T(8,128)(2,1)S(1)} async-done(((bf16[16,8,32,128]{3,2,1,0:T(8,128)(2,1)}), bf16[16,8,32,128]{3,2,1,0:T(8,128)(2,1)S(1)}, u32[]{:S(2)}, u32[]{:S(2)}) %all-to-all-start.3) | async-done | bytes 1048608 | tf_op jit(solution)/shard_map/all_to_all | solution.py:38
  222.9 14.3 %all_to_all.31 = f32[8,32,128]{2,1,0:T(8,128)S(1)} all-to-all(f32[8,32,128]{2,1,0:T(8,128)S(1)} %shard_map.91), channel_id=1, replica_groups=mesh['ylo'=2,'x'=4,'z'=8,'yhi'=2,'core'=2] {'z'}, dimensions={0} | all-to-all | bytes 262144 | tf_op jit(solution)/shard_map/all_to_all | solution.py:38
  237.2 9.9 %all_to_all.32 = f32[8,32,128]{2,1,0:T(8,128)S(1)} all-to-all(f32[8,32,128]{2,1,0:T(8,128)S(1)} %broadcast_in_dim.18), channel_id=1, replica_groups=mesh['ylo'=2,'x'=4,'z'=8,'yhi'=2,'core'=2] {'ylo','x'}, dimensions={0} | all-to-all | bytes 262144 | tf_op jit(solution)/shard_map/all_to_all | solution.py:38
  247.1 0.7 copy_bitcast_fusion
  (51 shorter events, 1.6 us)
Async XLA Ops:
  0.6 29.4 %collective-permute-start.2 = (bf16[32,16384]{1,0:T(8,128)(2,1)}, bf16[32,16384]{1,0:T(8,128)(2,1)}, u32[]{:S(2)}, u32[]{:S(2)}) collective-permute-start(bf16[32,16384]{1,0:T(8,128)(2,1)} %bitcast.24), channel_id=1, source_target_pairs={{0,4},{4,8},{8,12},{12,16},{16,20},{20,24},{24,28},{28,0},{1,5},{5... | collective-permute-start | bytes 3145736 | tf_op jit(solution)/shard_map/ppermute | solution.py:34
  2.6 27.4 %collective-permute-start.6 = (bf16[32,16384]{1,0:T(8,128)(2,1)}, bf16[32,16384]{1,0:T(8,128)(2,1)}, u32[]{:S(2)}, u32[]{:S(2)}) collective-permute-start(bf16[32,16384]{1,0:T(8,128)(2,1)} %bitcast.25), channel_id=1, source_target_pairs={{0,28},{4,0},{8,4},{12,8},{16,12},{20,16},{24,20},{28,24},{1,29},{... | collective-permute-start | bytes 3145736 | tf_op jit(solution)/shard_map/ppermute | solution.py:34
  6.7 5.7 %collective-permute-start = (bf16[32,1024]{1,0:T(8,128)(2,1)}, bf16[32,1024]{1,0:T(8,128)(2,1)S(1)}, u32[]{:S(2)}, u32[]{:S(2)}) collective-permute-start(bf16[32,1024]{1,0:T(8,128)(2,1)} %param.12), channel_id=1, source_target_pairs={{0,130},{2,128},{128,2},{130,0},{1,131},{3,129},{129,3},{131,1},{4... | collective-permute-start | bytes 196616 | tf_op jit(solution)/shard_map/ppermute | solution.py:254
  13.2 14.4 %collective-permute-start.1 = (bf16[2,32,1024]{2,1,0:T(8,128)(2,1)S(1)}, bf16[2,32,1024]{2,1,0:T(8,128)(2,1)S(1)}, u32[]{:S(2)}, u32[]{:S(2)}) collective-permute-start(bf16[2,32,1024]{2,1,0:T(8,128)(2,1)S(1)} %get-tuple-element.13), channel_id=1, source_target_pairs={{0,1},{1,0},{2,3},{3,2},{4,5},{5,4},{6,7},{7,6},{8,9},{9,8},{10,11... | collective-permute-start | bytes 393224 | tf_op jit(solution)/shard_map/ppermute | solution.py:257
  30.0 25.9 %collective-permute-start.3 = (bf16[32,16384]{1,0:T(8,128)(2,1)}, bf16[32,16384]{1,0:T(8,128)(2,1)}, u32[]{:S(2)}, u32[]{:S(2)}) collective-permute-start(bf16[32,16384]{1,0:T(8,128)(2,1)} %collective-permute-done.2.refs_1_), channel_id=1, source_target_pairs={{0,4},{4,8},{8,12},{12,16},{16,20},{20,24},{24,28},{28,0},{1,5},{5... | collective-permute-start | bytes 3145736 | tf_op jit(solution)/shard_map/ppermute | solution.py:34
  30.0 25.9 %collective-permute-start.7 = (bf16[32,16384]{1,0:T(8,128)(2,1)}, bf16[32,16384]{1,0:T(8,128)(2,1)}, u32[]{:S(2)}, u32[]{:S(2)}) collective-permute-start(bf16[32,16384]{1,0:T(8,128)(2,1)} %collective-permute-done.6.refs_2_), channel_id=1, source_target_pairs={{0,28},{4,0},{8,4},{12,8},{16,12},{20,16},{24,20},{28,24},{1,29},{... | collective-permute-start | bytes 3145736 | tf_op jit(solution)/shard_map/ppermute | solution.py:34
  33.3 1.2 copy-start.2
  38.0 1.7 copy-start.1
  39.7 58.3 %all-to-all-start.2 = ((bf16[32,4,3,32,128]{4,3,2,1,0:T(8,128)(2,1)}), bf16[32,4,3,32,128]{4,3,2,1,0:T(8,128)(2,1)S(1)}, u32[]{:S(2)}, u32[]{:S(2)}) async-start(bf16[32,4,3,32,128]{4,3,2,1,0:T(8,128)(2,1)} %copy-done.1), calls=%async_computation.2 | async-start | bytes 6291456 | tf_op jit(solution)/shard_map/all_to_all | solution.py:38
  55.9 24.8 %collective-permute-start.4 = (bf16[32,16384]{1,0:T(8,128)(2,1)}, bf16[32,16384]{1,0:T(8,128)(2,1)S(1)}, u32[]{:S(2)}, u32[]{:S(2)}) collective-permute-start(bf16[32,16384]{1,0:T(8,128)(2,1)} %collective-permute-done.3.refs_0_), channel_id=1, source_target_pairs={{0,4},{4,8},{8,12},{12,16},{16,20},{20,24},{24,28},{28,0},{1,5},{5... | collective-permute-start | bytes 3145736 | tf_op jit(solution)/shard_map/ppermute | solution.py:34
  55.9 25.0 %collective-permute-start.8 = (bf16[32,16384]{1,0:T(8,128)(2,1)}, bf16[32,16384]{1,0:T(8,128)(2,1)S(1)}, u32[]{:S(2)}, u32[]{:S(2)}) collective-permute-start(bf16[32,16384]{1,0:T(8,128)(2,1)} %collective-permute-done.7.refs_1_), channel_id=1, source_target_pairs={{0,28},{4,0},{8,4},{12,8},{16,12},{20,16},{24,20},{28,24},{1,29},{... | collective-permute-start | bytes 3145736 | tf_op jit(solution)/shard_map/ppermute | solution.py:34
  80.8 12.6 %collective-permute-start.5 = (bf16[16,16384]{1,0:T(8,128)(2,1)S(1)}, bf16[16,16384]{1,0:T(8,128)(2,1)S(1)}, u32[]{:S(2)}, u32[]{:S(2)}) collective-permute-start(bf16[16,16384]{1,0:T(8,128)(2,1)S(1)} %slice.16), channel_id=1, source_target_pairs={{0,4},{4,8},{8,12},{12,16},{16,20},{20,24},{24,28},{28,0},{1,5},{5... | collective-permute-start | bytes 1572872 | tf_op jit(solution)/shard_map/ppermute | solution.py:34
  80.9 12.4 %collective-permute-start.9 = (bf16[16,16384]{1,0:T(8,128)(2,1)S(1)}, bf16[16,16384]{1,0:T(8,128)(2,1)S(1)}, u32[]{:S(2)}, u32[]{:S(2)}) collective-permute-start(bf16[16,16384]{1,0:T(8,128)(2,1)S(1)} %slice.17), channel_id=1, source_target_pairs={{0,28},{4,0},{8,4},{12,8},{16,12},{20,16},{24,20},{28,24},{1,29},{... | collective-permute-start | bytes 1572872 | tf_op jit(solution)/shard_map/ppermute | solution.py:34
  95.6 2.3 copy-start
  98.0 20.9 %copy-start.9 = (s32[1,1,8,4]{2,3,1,0:T(4,128)S(1)}, s32[1,1,8,4]{2,3,1,0:T(4,128)}, u32[]{:S(2)}) copy-start(s32[1,1,8,4]{2,3,1,0:T(4,128)} %param.8) | copy-start | bytes 388
  98.0 84.1 %all-to-all-start.1 = ((bf16[32,4,5,32,128]{4,3,2,1,0:T(8,128)(2,1)}), bf16[32,4,5,32,128]{4,3,2,1,0:T(8,128)(2,1)}, u32[]{:S(2)}, u32[]{:S(2)}) async-start(bf16[32,4,5,32,128]{4,3,2,1,0:T(8,128)(2,1)} %copy-done), calls=%async_computation.1 | async-start | bytes 10485760 | tf_op jit(solution)/shard_map/all_to_all | solution.py:38
  105.8 9.9 %collective-permute-start.10 = (bf16[128,1024]{1,0:T(8,128)(2,1)S(1)}, bf16[128,1024]{1,0:T(8,128)(2,1)}, u32[]{:S(2)}, u32[]{:S(2)}) collective-permute-start(bf16[128,1024]{1,0:T(8,128)(2,1)S(1)} %bitcast.31), channel_id=1, source_target_pairs={{0,4},{4,8},{8,12},{12,16},{16,20},{20,24},{24,28},{28,0},{1,5},{5... | collective-permute-start | bytes 786440 | tf_op jit(solution)/shard_map/ppermute | solution.py:34
  105.9 9.8 %collective-permute-start.11 = (bf16[128,1024]{1,0:T(8,128)(2,1)S(1)}, bf16[128,1024]{1,0:T(8,128)(2,1)}, u32[]{:S(2)}, u32[]{:S(2)}) collective-permute-start(bf16[128,1024]{1,0:T(8,128)(2,1)S(1)} %bitcast.32), channel_id=1, source_target_pairs={{0,28},{4,0},{8,4},{12,8},{16,12},{20,16},{24,20},{28,24},{1,29},{... | collective-permute-start | bytes 786440 | tf_op jit(solution)/shard_map/ppermute | solution.py:34
  115.6 9.2 %collective-permute-start.12 = (bf16[128,1024]{1,0:T(8,128)(2,1)}, bf16[128,1024]{1,0:T(8,128)(2,1)}, u32[]{:S(2)}, u32[]{:S(2)}) collective-permute-start(bf16[128,1024]{1,0:T(8,128)(2,1)} %collective-permute-done.10), channel_id=1, source_target_pairs={{0,4},{4,8},{8,12},{12,16},{16,20},{20,24},{24,28},{28,0},{1,5},{5... | collective-permute-start | bytes 786440 | tf_op jit(solution)/shard_map/ppermute | solution.py:34
  115.6 9.2 %collective-permute-start.13 = (bf16[128,1024]{1,0:T(8,128)(2,1)}, bf16[128,1024]{1,0:T(8,128)(2,1)}, u32[]{:S(2)}, u32[]{:S(2)}) collective-permute-start(bf16[128,1024]{1,0:T(8,128)(2,1)} %collective-permute-done.11), channel_id=1, source_target_pairs={{0,28},{4,0},{8,4},{12,8},{16,12},{20,16},{24,20},{28,24},{1,29},{... | collective-permute-start | bytes 786440 | tf_op jit(solution)/shard_map/ppermute | solution.py:34
  119.0 21.7 %copy-start.3 = (bf16[1,1,8,4,128,128]{5,4,3,2,1,0:T(8,128)(2,1)S(1)}, bf16[1,1,8,4,128,128]{5,4,3,2,1,0:T(8,128)(2,1)}, u32[]{:S(2)}) copy-start(bf16[1,1,8,4,128,128]{5,4,3,2,1,0:T(8,128)(2,1)} %param.11) | copy-start | bytes 3145732
  119.0 21.7 %copy-start.5 = (s32[1,1,8]{2,1,0:T(1,128)S(1)}, s32[1,1,8]{2,1,0:T(1,128)}, u32[]{:S(2)}) copy-start(s32[1,1,8]{2,1,0:T(1,128)} %param.10) | copy-start | bytes 100
  124.8 8.2 %collective-permute-start.14 = (bf16[128,1024]{1,0:T(8,128)(2,1)}, bf16[128,1024]{1,0:T(8,128)(2,1)S(1)}, u32[]{:S(2)}, u32[]{:S(2)}) collective-permute-start(bf16[128,1024]{1,0:T(8,128)(2,1)} %collective-permute-done.12), channel_id=1, source_target_pairs={{0,4},{4,8},{8,12},{12,16},{16,20},{20,24},{24,28},{28,0},{1,5},{5... | collective-permute-start | bytes 786440 | tf_op jit(solution)/shard_map/ppermute | solution.py:34
  124.8 8.3 %collective-permute-start.15 = (bf16[128,1024]{1,0:T(8,128)(2,1)}, bf16[128,1024]{1,0:T(8,128)(2,1)S(1)}, u32[]{:S(2)}, u32[]{:S(2)}) collective-permute-start(bf16[128,1024]{1,0:T(8,128)(2,1)} %collective-permute-done.13), channel_id=1, source_target_pairs={{0,28},{4,0},{8,4},{12,8},{16,12},{20,16},{24,20},{28,24},{1,29},{... | collective-permute-start | bytes 786440 | tf_op jit(solution)/shard_map/ppermute | solution.py:34
  133.0 6.3 %collective-permute-start.16 = (bf16[64,1024]{1,0:T(8,128)(2,1)S(1)}, bf16[64,1024]{1,0:T(8,128)(2,1)S(1)}, u32[]{:S(2)}, u32[]{:S(2)}) collective-permute-start(bf16[64,1024]{1,0:T(8,128)(2,1)S(1)} %slice.18), channel_id=1, source_target_pairs={{0,4},{4,8},{8,12},{12,16},{16,20},{20,24},{24,28},{28,0},{1,5},{5... | collective-permute-start | bytes 393224 | tf_op jit(solution)/shard_map/ppermute | solution.py:34
  133.1 6.2 %collective-permute-start.17 = (bf16[64,1024]{1,0:T(8,128)(2,1)S(1)}, bf16[64,1024]{1,0:T(8,128)(2,1)S(1)}, u32[]{:S(2)}, u32[]{:S(2)}) collective-permute-start(bf16[64,1024]{1,0:T(8,128)(2,1)S(1)} %slice.19), channel_id=1, source_target_pairs={{0,28},{4,0},{8,4},{12,8},{16,12},{20,16},{24,20},{28,24},{1,29},{... | collective-permute-start | bytes 393224 | tf_op jit(solution)/shard_map/ppermute | solution.py:34
  139.3 1.4 copy-start.8
  144.0 0.9 copy-start.6
  182.1 1.2 copy-start.4
  183.3 1.1 copy-start.7
  196.1 2.8 %collective-permute-start.18 = (bf16[8,2,8,32,128]{4,3,2,1,0:T(8,128)(2,1)S(1)}, bf16[8,2,8,32,128]{4,3,2,1,0:T(8,128)(2,1)S(1)}, u32[]{:S(2)}, u32[]{:S(2)}) collective-permute-start(bf16[8,2,8,32,128]{4,3,2,1,0:T(8,128)(2,1)S(1)} %get-tuple-element.11), channel_id=1, source_target_pairs={{0,1},{1,0},{2,3},{3,2},{4,5},{5,4},{6,7},{7,6},{8,9},{9,8},{10,11... | collective-permute-start | bytes 3145736 | tf_op jit(solution)/shard_map/ppermute | solution.py:244
  200.3 22.5 %all-to-all-start.3 = ((bf16[16,8,32,128]{3,2,1,0:T(8,128)(2,1)}), bf16[16,8,32,128]{3,2,1,0:T(8,128)(2,1)S(1)}, u32[]{:S(2)}, u32[]{:S(2)}) async-start(bf16[16,8,32,128]{3,2,1,0:T(8,128)(2,1)} %bitcast.14), calls=%async_computation.3 | async-start | bytes 2097152 | tf_op jit(solution)/shard_map/all_to_all | solution.py:38

commit v4 on v3

v4 whole, which is shorter than its diff:
```python
import functools
import math

import jax
import jax.numpy as jnp
from jax import lax
from jax.experimental import pallas as pl
from jax.experimental.pallas import tpu as pltpu
from jax.sharding import Mesh, PartitionSpec as P

REP = ("ylo", "x")
PLANE = ("ylo", "x", "yhi", "core")
CHIPS_XY = ("ylo", "x", "yhi")
ZN = 8
FIRST = (0, 1, -1)
SECOND = (2, -2, 3, -3, 4)
ORDER = FIRST + SECOND
LANES = 4
VMEM = pl.BlockSpec(memory_space=pltpu.VMEM)
SMEM = pl.BlockSpec(memory_space=pltpu.SMEM)
HBM = pl.BlockSpec(memory_space=pltpu.HBM)
SWAP = [(0, 1), (1, 0)]


def params(mib):
    return pltpu.CompilerParams(vmem_limit_bytes=mib * 2**20)


def cost(flops, size):
    return pl.CostEstimate(flops=flops, bytes_accessed=size, transcendentals=0)


def shift_z(value, step):
    return lax.ppermute(value, "z", [(i, (i + step) % ZN) for i in range(ZN)])


def exchange(value, axes):
    return lax.all_to_all(value, axes, split_axis=0, concat_axis=0, tiled=True)


def ring(upper, lower):
    held = {0: (upper, lower)}
    for step in range(1, ZN // 2):
        for sign in (1, -1):
            before = held[sign * (step - 1)]
            held[sign * step] = shift_z(before[0], sign), shift_z(before[1], sign)
    far = ZN // 2 - 1
    held[ZN // 2] = shift_z(held[far][0], 1), shift_z(held[-far][1], -1)
    return held


def short_ring(own):
    half = own.shape[0] // 2
    held = {0: own}
    for step in range(1, ZN // 2):
        held[step] = shift_z(held[step - 1], 1)
        held[-step] = shift_z(held[1 - step], -1)
    far = ZN // 2 - 1
    held[ZN // 2] = jnp.concatenate([shift_z(held[far][:half], 1), shift_z(held[-far][half:], -1)])
    return held


def pick_kernel(block, first_place, num_slices, wanted_ref, *refs):
    slices, (out_ref, buffer, sems) = refs[:num_slices], refs[-3:]
    dests, slots, places = buffer.shape[:3]
    half = slices[0].shape[0]
    groups = sems.shape[0]
    each = dests // groups

    def one(step, carry):
        dest, slot = step // slots, step % slots
        start = pl.multiple_of(wanted_ref[dest, slot] * block, block)
        for index, ref in enumerate(slices):
            low = index % 2 * half
            buffer[dest, slot, index // 2, low : low + half, :] = ref[:, pl.ds(start, block)]
        return carry

    copies = []
    for group in range(groups):
        at = slice(group * each, group * each + each)
        lax.fori_loop(group * each * slots, (group + 1) * each * slots, one, 0, unroll=4)
        copies.append(
            pltpu.make_async_copy(
                buffer.at[at], out_ref.at[at, :, first_place : first_place + places], sems.at[group]
            )
        )
        copies[-1].start()
    for copy in copies:
        copy.wait()


def pick(wanted, slices, block, flops, places=None, before=None):
    askers, slots = wanted.shape
    count, rows = len(slices) // 2, 2 * slices[0].shape[0]
    places = before.shape[2] if before is not None else places or count
    first_place = places - count if before is not None else 0
    more = [] if before is None else [before]
    return pl.pallas_call(
        functools.partial(pick_kernel, block, first_place, len(slices)),
        out_shape=jax.ShapeDtypeStruct((askers, slots, places, rows, block), jnp.bfloat16),
        in_specs=[SMEM] + [VMEM] * len(slices) + [HBM] * len(more),
        out_specs=HBM,
        input_output_aliases={1 + len(slices): 0} if more else {},
        scratch_shapes=[pltpu.VMEM((askers, slots, count, rows, block), jnp.bfloat16), pltpu.SemaphoreType.DMA((4,))],
        compiler_params=params(58),
        cost_estimate=cost(flops, count * 2**21),
    )(wanted, *slices, *more)


def add_tiles(core, tgt_ref, count_ref, vals_ref, part, acc, ready):
    sections, slots, block, _ = vals_ref.shape
    places, rows = part.shape[2:4]
    acc[...] = jnp.zeros_like(acc)

    def one(section, slot):
        column = pl.multiple_of(tgt_ref[section, slot] * block, block)
        sources = [section * LANES + lane + core * (1 - 2 * (lane % 2)) for lane in range(LANES)]
        columns_in = jnp.concatenate([part[source, slot].reshape(places * rows, block) for source in sources])
        contrib = lax.dot_general(
            columns_in, vals_ref[section, slot], (((1,), (1,)), ((), ())), preferred_element_type=jnp.float32
        )
        for lane in range(LANES):
            for place in range(places):
                low, at = (place * LANES + lane) * rows, (lane * places + place) * rows
                acc[low : low + rows, pl.ds(column, block)] += contrib[at : at + rows]

    @pl.loop(0, sections)
    def _(section):
        ready(section)

        @pl.loop(0, jnp.minimum(count_ref[section], slots))
        def _(slot):
            one(section, slot)


def aggregate_kernel(core_ref, tgt_ref, count_ref, vals_ref, part, out_ref, acc):
    add_tiles(core_ref[0], tgt_ref, count_ref, vals_ref, part, acc, lambda section: None)
    out_ref[...] = acc[...].astype(out_ref.dtype)


def aggregate(core, targets, counts, values, part, num_rows):
    num_feats = LANES * part.shape[2] * part.shape[3]
    return pl.pallas_call(
        aggregate_kernel,
        out_shape=jax.ShapeDtypeStruct((num_feats, num_rows), jnp.bfloat16),
        in_specs=[SMEM] * 3 + [VMEM] * 2,
        out_specs=VMEM,
        scratch_shapes=[pltpu.VMEM((num_feats, num_rows), jnp.float32)],
        compiler_params=params(16),
        cost_estimate=cost(3 * 10**9, 8 * 2**20),
    )(core, targets, counts, values, part)


def layer_kernel(
    core_ref,
    tgt_ref,
    count_ref,
    vals_hbm,
    part_hbm,
    early_hbm,
    weight_hbm,
    cot_hbm,
    act_hbm,
    kept_ref,
    gone_ref,
    vals,
    part,
    weight,
    cot,
    act,
    acc,
    mixed,
    dpre,
    part_sems,
    sems,
    act_sems,
):
    early = early_hbm.shape[0]

    def section_copy(section):
        at = pl.ds(section * LANES, LANES)
        return pltpu.make_async_copy(part_hbm.at[at], part.at[at], part_sems.at[section])

    vals_copy = pltpu.make_async_copy(vals_hbm, vals, sems.at[0])
    early_copy = pltpu.make_async_copy(early_hbm, mixed.at[:early], sems.at[1])
    weight_copy = pltpu.make_async_copy(weight_hbm, weight, sems.at[2])
    cot_copy = pltpu.make_async_copy(cot_hbm, cot, sems.at[3])
    vals_copy.start()
    for section in range(part_sems.shape[0]):
        section_copy(section).start()
    for copy in (early_copy, weight_copy, cot_copy):
        copy.start()
    vals_copy.wait()
    add_tiles(core_ref[0], tgt_ref, count_ref, vals, part, acc, lambda section: section_copy(section).wait())
    mixed[early:] = acc[...].astype(mixed.dtype)
    for copy in (early_copy, weight_copy, cot_copy):
        copy.wait()

    step = act.shape[0] // act_sems.shape[0]
    act_copies = []
    for index in range(act_sems.shape[0]):
        at = slice(index * step, index * step + step)
        preact = lax.dot_general(
            mixed[:, at], weight[...], (((0,), (0,)), ((), ())), preferred_element_type=jnp.float32
        )
        sigmoid_val = jax.nn.sigmoid(preact)
        act[at] = (preact * sigmoid_val).astype(act.dtype)
        act_copies.append(pltpu.make_async_copy(act.at[at], act_hbm.at[at], act_sems.at[index]))
        act_copies[-1].start()
        slope = sigmoid_val * (1.0 + preact * (1.0 - sigmoid_val))
        dpre[at] = (cot[at].astype(jnp.float32) * slope).astype(dpre.dtype)
    pieces, _, _, rows, width = kept_ref.shape
    for low in range(0, mixed.shape[0], step):
        grad = jnp.dot(mixed[low : low + step], dpre[...], preferred_element_type=jnp.float32)
        for at in range(0, step, rows):
            lane = (low + at) // rows
            place, hi, core = lane // LANES, lane % LANES // 2, lane % 2
            for piece in range(pieces):
                value = grad[at : at + rows, piece * width : (piece + 1) * width]
                if core == 0:
                    kept_ref[piece, hi, place] = value
                else:
                    gone_ref[piece, hi, place] = value.astype(gone_ref.dtype)
    for copy in act_copies:
        copy.wait()


def layer(core, targets, counts, values, part, early, weight, cotangent):
    tgt_rows, width = cotangent.shape
    feats = weight.shape[0]
    cut = (8, 2, ZN, part.shape[3], width // 8)
    late = feats - early.shape[0]
    return pl.pallas_call(
        layer_kernel,
        out_shape=(
            jax.ShapeDtypeStruct((tgt_rows, width), jnp.bfloat16),
            jax.ShapeDtypeStruct(cut, jnp.float32),
            jax.ShapeDtypeStruct(cut, jnp.bfloat16),
        ),
        in_specs=[SMEM] * 3 + [HBM] * 5,
        out_specs=(HBM, VMEM, VMEM),
        scratch_shapes=[
            pltpu.VMEM(values.shape, values.dtype),
            pltpu.VMEM(part.shape, part.dtype),
            pltpu.VMEM(weight.shape, weight.dtype),
            pltpu.VMEM((tgt_rows, width), cotangent.dtype),
            pltpu.VMEM((tgt_rows, width), jnp.bfloat16),
            pltpu.VMEM((late, tgt_rows), jnp.float32),
            pltpu.VMEM((feats, tgt_rows), jnp.bfloat16),
            pltpu.VMEM((tgt_rows, width), jnp.bfloat16),
            pltpu.SemaphoreType.DMA((values.shape[0],)),
            pltpu.SemaphoreType.DMA((4,)),
            pltpu.SemaphoreType.DMA((4,)),
        ],
        compiler_params=params(56),
        cost_estimate=cost(6 * 10**9, 20 * 2**20),
    )(core, targets, counts, values, part, early, weight, cotangent)


def sum_plane_kernel(z_ref, came_ref, out_ref):
    for place, distance in enumerate(ORDER):
        total = came_ref[:, place].astype(jnp.float32).sum(0)
        out_ref[lax.rem(z_ref[0] + (ZN - distance), ZN)] = total


def sum_plane(came):
    return pl.pallas_call(
        sum_plane_kernel,
        out_shape=jax.ShapeDtypeStruct(came.shape[1:], jnp.float32),
        in_specs=[SMEM, VMEM],
        out_specs=VMEM,
        compiler_params=params(16),
    )(lax.axis_index("z").astype(jnp.int32)[None], came)


def sum_over_devices(kept, gone):
    came = lax.ppermute(gone, "core", SWAP)
    chip = (kept + came.astype(jnp.float32)).astype(jnp.bfloat16)
    chip = chip.reshape(16, *chip.shape[2:])
    plane = sum_plane(exchange(chip, CHIPS_XY))
    column = exchange(plane, "z").sum(0)
    whole = exchange(jnp.broadcast_to(column[None], (8, *column.shape)), REP)
    return whole.transpose(1, 0, 2).reshape(column.shape[0], -1)


def weight_lanes(own):
    other = lax.ppermute(own, ("ylo", "yhi"), [(0, 3), (1, 2), (2, 1), (3, 0)])
    first = lax.axis_index("yhi") == 0
    both = jnp.stack([jnp.where(first, own, other), jnp.where(first, other, own)])
    lanes = jnp.stack([both, lax.ppermute(both, "core", SWAP)], axis=1)
    return lanes.reshape(-1, own.shape[1])


def whole_weight(lanes):
    held = short_ring(lanes)
    return jnp.concatenate([held[distance] for distance in ORDER])


def per_device(features, tile_tgt, tile_src, tile_count, tile_vals, weight, cotangent):
    block_size = tile_vals.shape[-1]
    tgt_rows = cotangent.shape[0]
    targets, sources, counts, values = tile_tgt[0, 0], tile_src[0, 0], tile_count[0, 0], tile_vals[0, 0]
    core = lax.axis_index("core").astype(jnp.int32)[None]

    wanted = exchange(jnp.repeat(sources, LANES, axis=0)[:, None, :], PLANE)[:, 0]
    wanted, lanes = lax.optimization_barrier((wanted, weight_lanes(weight)))
    half = features.shape[1] // 2
    held = ring(features[0, :half], features[0, half:])
    first = pick(wanted, [piece for d in FIRST for piece in held[d]], block_size, PICK_FLOPS[0])
    early = aggregate(core, targets, counts, values, exchange(first, PLANE), tgt_rows)
    most = pick(wanted, [piece for d in SECOND[:-1] for piece in held[d]], block_size, PICK_FLOPS[1], len(SECOND))
    second = pick(wanted, held[SECOND[-1]], block_size, PICK_FLOPS[2], before=most)
    part = exchange(second, PLANE)
    weight_in = whole_weight(lanes)
    activations, kept, gone = layer(core, targets, counts, values, part, early, weight_in, cotangent)
    weight_grad = sum_over_devices(kept, gone) / math.sqrt(tgt_rows * 256)
    return (activations, weight_grad)


PICK_FLOPS = (25 * 10**9, 25 * 10**9, 1 * 10**9)


def solution(mesh):
    row = ("z", "yhi", "core")
    fine = Mesh(mesh.devices.reshape(2, 4, 8, 2, 2), ("ylo", "x", "z", "yhi", "core"))
    in_specs = (
        P(REP, row, None),
        P(REP, row, None, None),
        P(REP, row, None, None),
        P(REP, row, None),
        P(REP, row, None, None, None, None),
        P(row, None),
        P(REP + row, None),
    )
    out_specs = (P(REP + row, None), P(row, None))
    return jax.shard_map(per_device, mesh=fine, in_specs=in_specs, out_specs=out_specs, check_vma=False)
```

time: 249 us -> 244 us (0.980)
  local copies, waits for them, and re-layouts: 15 us -> 10.2 us
  Pallas kernels: 25.2 us -> 29.4 us
  blocking collectives: 37.6 us -> 34.1 us
  waiting for transfers between devices: 114 us -> 111 us
    ppermute x16 -> x22, starting transfers between devices: 29 us -> 36.9 us  [shift_z(): return lax.ppermute(value, 'z', [(i, (i + step) % ZN) for i in range(ZN)])]
    unnamed x29 -> x39, local copies, waits for them, and re-layouts: 14.6 us -> 8 us
    all_to_all x3, starting transfers between devices: 19.9 us -> 14 us  [exchange(): return lax.all_to_all(value, axes, split_axis=0, concat_axis=0, tiled=True)]
    pallas_call x3, Pallas kernels: 10 us -> 13.7 us  [pick(): pl.pallas_call(functools.partial(pick_kernel, block, first_place, len(sli...]
    all_to_all x3, blocking collectives: 37.6 us -> 34.1 us  [exchange(): return lax.all_to_all(value, axes, split_axis=0, concat_axis=0, tiled=True)]
    ppermute x1, waiting for transfers between devices: 2.67 us -> 0.01 us  [weight_lanes(): other = lax.ppermute(own, ('ylo', 'yhi'), [(0, 3), (1, 2), (2, 1), (3, 0)])]
    ppermute x16 -> x22, waiting for transfers between devices: 53.4 us -> 52.7 us  [shift_z(): return lax.ppermute(value, 'z', [(i, (i + step) % ZN) for i in range(ZN)])]
  transfers between devices with their start and end apart: 22 -> 28, of which waited for: 12 -> 14; matrix products, arithmetic and copies ran while one was open for 2% -> 3% of each run, Pallas kernels for 5% -> 7%
where the time goes in v4:
time: 244 us; the launch traced here: 243 us
  waiting for transfers between devices  111 us (45%)
  starting transfers between devices  54.3 us (22%)
  blocking collectives  34.1 us (14%)
  Pallas kernels  29.4 us (12%)
  local copies, waits for them, and re-layouts  10.2 us (4%)
  other arithmetic  3.69 us (2%)
    all_to_all x3, waiting for transfers between devices, exchange(): return lax.all_to_all(value, axes, split_axis=0, concat_axis=0, tiled=True)  54.9 us
    ppermute x22, waiting for transfers between devices, shift_z(): return lax.ppermute(value, 'z', [(i, (i + step) % ZN) for i in range(ZN)])  52.7 us
    ppermute x22, starting transfers between devices, shift_z(): return lax.ppermute(value, 'z', [(i, (i + step) % ZN) for i in range(ZN)])  36.9 us
    all_to_all x3, blocking collectives, exchange(): return lax.all_to_all(value, axes, split_axis=0, concat_axis=0, tiled=True)  34.1 us
    all_to_all x3, starting transfers between devices, exchange(): return lax.all_to_all(value, axes, split_axis=0, concat_axis=0, tiled=True)  14 us
    pallas_call x3, Pallas kernels, pick(): pl.pallas_call(functools.partial(pick_kernel, block, first_place, len(sli...  13.7 us
    pallas_call x1, Pallas kernels, layer(): pl.pallas_call(layer_kernel, out_shape=(jax.ShapeDtypeStruct((tgt_rows, w...  12.5 us
    unnamed x39, local copies, waits for them, and re-layouts  8 us
  transfers between devices with their start and end apart: 28, of which 14 were waited for; matrix products, arithmetic and copies ran while one was open for 3% of the time, Pallas kernels for 7%

profile of v4, /device:TPU:2, one launch (start us, length us, event | category | flops | bytes accessed | tf_op | source)
XLA Modules:
  0.0 243.1 jit_solution(2521745385059609462)
XLA Ops:
  0.6 3.1 %collective-permute-start = (bf16[32,1024]{1,0:T(8,128)(2,1)}, bf16[32,1024]{1,0:T(8,128)(2,1)S(1)}, u32[]{:S(2)}, u32[]{:S(2)}) collective-permute-start(bf16[32,1024]{1,0:T(8,128)(2,1)} %param.12), channel_id=1, source_target_pairs={{0,130},{2,128},{128,2},{130,0},{1,131},{3,129},{129,3},{131,1},{4... | collective-permute-start | bytes 196616 | tf_op jit(solution)/shard_map/ppermute | solution.py:287
  3.8 1.3 slice_bitcast_fusion
  5.0 2.0 collective-permute-start.10
  7.0 4.0 %collective-permute-start.6 = (bf16[16,16384]{1,0:T(8,128)(2,1)S(1)}, bf16[16,16384]{1,0:T(8,128)(2,1)}, u32[]{:S(2)}, u32[]{:S(2)}) collective-permute-start(bf16[16,16384]{1,0:T(8,128)(2,1)S(1)} %get-tuple-element.12.refs_1_), channel_id=1, source_target_pairs={{0,28},{4,0},{8,4},{12,8},{16,12},{20,16},{24,20},{28,24},{1,29},{... | collective-permute-start | bytes 1572872 | tf_op jit(solution)/shard_map/ppermute | solution.py:34
  11.1 1.9 collective-permute-start.12
  13.3 11.1 %all_to_all.30 = s32[32,1,4]{2,1,0:T(1,128)S(1)} all-to-all(s32[32,1,4]{2,1,0:T(1,128)S(1)} %bitcast.35), channel_id=1, replica_groups=mesh['ylo'=2,'x'=4,'z'=8,'yhi'=2,'core'=2] {'ylo','x','yhi','core'}, dimensions={0} | all-to-all | bytes 1024 | tf_op jit(solution)/shard_map/all_to_all | solution.py:38
  25.3 3.2 %collective-permute-start.7 = (bf16[16,16384]{1,0:T(8,128)(2,1)}, bf16[16,16384]{1,0:T(8,128)(2,1)}, u32[]{:S(2)}, u32[]{:S(2)}) collective-permute-start(bf16[16,16384]{1,0:T(8,128)(2,1)} %collective-permute-done.6.refs_5_), channel_id=1, source_target_pairs={{0,28},{4,0},{8,4},{12,8},{16,12},{20,16},{24,20},{28,24},{1,29},{... | collective-permute-start | bytes 1572872 | tf_op jit(solution)/shard_map/ppermute | solution.py:34
  28.5 6.2 %collective-permute-done.12.refs_4_ = bf16[16,16384]{1,0:T(8,128)(2,1)} collective-permute-done((bf16[16,16384]{1,0:T(8,128)(2,1)S(1)}, bf16[16,16384]{1,0:T(8,128)(2,1)}, u32[]{:S(2)}, u32[]{:S(2)}) %collective-permute-start.12) | collective-permute-done | bytes 524320 | tf_op jit(solution)/shard_map/ppermute | solution.py:34
  34.7 3.8 %collective-permute-start.13 = (bf16[16,16384]{1,0:T(8,128)(2,1)}, bf16[16,16384]{1,0:T(8,128)(2,1)}, u32[]{:S(2)}, u32[]{:S(2)}) collective-permute-start(bf16[16,16384]{1,0:T(8,128)(2,1)} %collective-permute-done.12.refs_4_), channel_id=1, source_target_pairs={{0,28},{4,0},{8,4},{12,8},{16,12},{20,16},{24,20},{28,24},{1,29},{... | collective-permute-start | bytes 1572872 | tf_op jit(solution)/shard_map/ppermute | solution.py:34
  38.5 4.7 %shard_map.88 = bf16[32,4,3,32,128]{4,3,2,1,0:T(8,128)(2,1)} custom-call(s32[32,4]{1,0:T(8,128)} %copy.34.wanted_ref, bf16[16,16384]{1,0:T(8,128)(2,1)} %copy-done.7, bf16[16,16384]{1,0:T(8,128)(2,1)} %copy-done.6, bf16[16,16384]{1,0:T(8,128)(2,1)} %collective-permute-done.2.refs_2_, bf16[16,16384]{1,0:T(8,128)(2,1)} %collective-permute-done.10.refs_3_, ...), custom_call_target="tpu_custom_call" | custom-call | flops 24999999488 | bytes 6291456 | tf_op jit(solution)/shard_map/pallas_call | solution.py:98
  43.2 5.1 %all-to-all-start.2 = ((bf16[32,4,3,32,128]{4,3,2,1,0:T(8,128)(2,1)}), bf16[32,4,3,32,128]{4,3,2,1,0:T(8,128)(2,1)S(1)}, u32[]{:S(2)}, u32[]{:S(2)}) async-start(bf16[32,4,3,32,128]{4,3,2,1,0:T(8,128)(2,1)} %shard_map.88), calls=%async_computation.2 | async-start | bytes 6291456 | tf_op jit(solution)/shard_map/all_to_all | solution.py:38
  48.3 3.3 %collective-permute-start.8 = (bf16[16,16384]{1,0:T(8,128)(2,1)}, bf16[16,16384]{1,0:T(8,128)(2,1)S(1)}, u32[]{:S(2)}, u32[]{:S(2)}) collective-permute-start(bf16[16,16384]{1,0:T(8,128)(2,1)} %collective-permute-done.7.refs_3_), channel_id=1, source_target_pairs={{0,28},{4,0},{8,4},{12,8},{16,12},{20,16},{24,20},{28,24},{1,29},{... | collective-permute-start | bytes 1572872 | tf_op jit(solution)/shard_map/ppermute | solution.py:34
  51.6 4.8 %collective-permute-done.3.refs_0_ = bf16[16,16384]{1,0:T(8,128)(2,1)} collective-permute-done((bf16[16,16384]{1,0:T(8,128)(2,1)}, bf16[16,16384]{1,0:T(8,128)(2,1)}, u32[]{:S(2)}, u32[]{:S(2)}) %collective-permute-start.3) | collective-permute-done | bytes 524320 | tf_op jit(solution)/shard_map/ppermute | solution.py:34
  56.4 0.8 collective-permute-done.13.refs_2_
  57.2 3.7 %collective-permute-start.15 = (bf16[16,16384]{1,0:T(8,128)(2,1)}, bf16[16,16384]{1,0:T(8,128)(2,1)}, u32[]{:S(2)}, u32[]{:S(2)}) collective-permute-start(bf16[16,16384]{1,0:T(8,128)(2,1)} %collective-permute-done.13.refs_2_), channel_id=1, source_target_pairs={{0,28},{4,0},{8,4},{12,8},{16,12},{20,16},{24,20},{28,24},{1,29},{... | collective-permute-start | bytes 1572872 | tf_op jit(solution)/shard_map/ppermute | solution.py:34
  60.9 7.5 %collective-permute-done.8.refs_7_ = bf16[16,16384]{1,0:T(8,128)(2,1)S(1)} collective-permute-done((bf16[16,16384]{1,0:T(8,128)(2,1)}, bf16[16,16384]{1,0:T(8,128)(2,1)S(1)}, u32[]{:S(2)}, u32[]{:S(2)}) %collective-permute-start.8) | collective-permute-done | bytes 524320 | tf_op jit(solution)/shard_map/ppermute | solution.py:34
  68.5 3.6 %collective-permute-start.9 = (bf16[16,16384]{1,0:T(8,128)(2,1)S(1)}, bf16[16,16384]{1,0:T(8,128)(2,1)S(1)}, u32[]{:S(2)}, u32[]{:S(2)}) collective-permute-start(bf16[16,16384]{1,0:T(8,128)(2,1)S(1)} %collective-permute-done.8.refs_7_), channel_id=1, source_target_pairs={{0,28},{4,0},{8,4},{12,8},{16,12},{20,16},{24,20},{28,24},{1,29},{... | collective-permute-start | bytes 1572872 | tf_op jit(solution)/shard_map/ppermute | solution.py:34
  72.7 11.2 %collective-permute-done.14.refs_5_ = bf16[16,16384]{1,0:T(8,128)(2,1)S(1)} collective-permute-done((bf16[16,16384]{1,0:T(8,128)(2,1)}, bf16[16,16384]{1,0:T(8,128)(2,1)S(1)}, u32[]{:S(2)}, u32[]{:S(2)}) %collective-permute-start.14) | collective-permute-done | bytes 524320 | tf_op jit(solution)/shard_map/ppermute | solution.py:34
  84.0 0.8 copy-done.14
  84.8 5.5 %shard_map.86.refs_2_ = bf16[32,4,5,32,128]{4,3,2,1,0:T(8,128)(2,1)} custom-call(s32[32,4]{1,0:T(8,128)} %copy.34.wanted_ref, bf16[16,16384]{1,0:T(8,128)(2,1)} %collective-permute-done.3.refs_0_, bf16[16,16384]{1,0:T(8,128)(2,1)} %collective-permute-done.11.refs_1_, bf16[16,16384]{1,0:T(8,128)(2,1)} %collective-permute-done.13.refs_2_, ...), custom_call_target="tpu_custom_call" | custom-call | flops 24999999488 | bytes 8388608 | tf_op jit(solution)/shard_map/pallas_call | solution.py:98
  90.3 2.8 %collective-permute-done.5.refs_0_ = bf16[16,16384]{1,0:T(8,128)(2,1)S(1)} collective-permute-done((bf16[16,16384]{1,0:T(8,128)(2,1)S(1)}, bf16[16,16384]{1,0:T(8,128)(2,1)S(1)}, u32[]{:S(2)}, u32[]{:S(2)}) %collective-permute-start.5) | collective-permute-done | bytes 524320 | tf_op jit(solution)/shard_map/ppermute | solution.py:34
  93.1 0.8 copy-done.5
  93.9 3.4 %shard_map.87 = bf16[32,4,5,32,128]{4,3,2,1,0:T(8,128)(2,1)} custom-call(s32[32,4]{1,0:T(8,128)} %copy.34.wanted_ref, bf16[16,16384]{1,0:T(8,128)(2,1)} %copy-done.5, bf16[16,16384]{1,0:T(8,128)(2,1)} %copy-done.4, bf16[32,4,5,32,128]{4,3,2,1,0:T(8,128)(2,1)} %shard_map.86.refs_2_), custom_call_target="tpu_custom_call", output_to_operand_aliasing={{}: (3, {})} | custom-call | flops 1000000000 | bytes 2097152 | tf_op jit(solution)/shard_map/pallas_call | solution.py:98
  97.3 5.1 %all-to-all-start.1 = ((bf16[32,4,5,32,128]{4,3,2,1,0:T(8,128)(2,1)}), bf16[32,4,5,32,128]{4,3,2,1,0:T(8,128)(2,1)}, u32[]{:S(2)}, u32[]{:S(2)}) async-start(bf16[32,4,5,32,128]{4,3,2,1,0:T(8,128)(2,1)} %shard_map.87), calls=%async_computation.1 | async-start | bytes 10485760 | tf_op jit(solution)/shard_map/all_to_all | solution.py:38
  102.4 0.8 collective-permute-start.17
  103.3 1.3 collective-permute-start.16
  104.5 6.4 %collective-permute-done.17 = bf16[128,1024]{1,0:T(8,128)(2,1)} collective-permute-done((bf16[128,1024]{1,0:T(8,128)(2,1)S(1)}, bf16[128,1024]{1,0:T(8,128)(2,1)}, u32[]{:S(2)}, u32[]{:S(2)}) %collective-permute-start.17) | collective-permute-done | bytes 262176 | tf_op jit(solution)/shard_map/ppermute | solution.py:34
  111.0 2.0 collective-permute-start.19
  113.1 1.1 constant_dynamic-update-slice_fusion.7
  114.2 4.6 %collective-permute-done.19 = bf16[128,1024]{1,0:T(8,128)(2,1)} collective-permute-done((bf16[128,1024]{1,0:T(8,128)(2,1)}, bf16[128,1024]{1,0:T(8,128)(2,1)}, u32[]{:S(2)}, u32[]{:S(2)}) %collective-permute-start.19) | collective-permute-done | bytes 262176 | tf_op jit(solution)/shard_map/ppermute | solution.py:34
  118.8 3.2 %collective-permute-start.21 = (bf16[128,1024]{1,0:T(8,128)(2,1)}, bf16[128,1024]{1,0:T(8,128)(2,1)S(1)}, u32[]{:S(2)}, u32[]{:S(2)}) collective-permute-start(bf16[128,1024]{1,0:T(8,128)(2,1)} %collective-permute-done.19), channel_id=1, source_target_pairs={{0,28},{4,0},{8,4},{12,8},{16,12},{20,16},{24,20},{28,24},{1,29},{... | collective-permute-start | bytes 786440 | tf_op jit(solution)/shard_map/ppermute | solution.py:34
  122.0 1.0 constant_dynamic-update-slice_fusion.6
  123.0 1.0 constant_dynamic-update-slice_fusion.5
  123.9 1.0 constant_dynamic-update-slice_fusion.4
  124.9 1.5 collective-permute-done.21
  126.4 3.7 %collective-permute-start.23 = (bf16[64,1024]{1,0:T(8,128)(2,1)S(1)}, bf16[64,1024]{1,0:T(8,128)(2,1)S(1)}, u32[]{:S(2)}, u32[]{:S(2)}) collective-permute-start(bf16[64,1024]{1,0:T(8,128)(2,1)S(1)} %slice.17), channel_id=1, source_target_pairs={{0,28},{4,0},{8,4},{12,8},{16,12},{20,16},{24,20},{28,24},{1,29},{... | collective-permute-start | bytes 393224 | tf_op jit(solution)/shard_map/ppermute | solution.py:34
  130.5 6.1 %collective-permute-done.22 = bf16[64,1024]{1,0:T(8,128)(2,1)S(1)} collective-permute-done((bf16[64,1024]{1,0:T(8,128)(2,1)S(1)}, bf16[64,1024]{1,0:T(8,128)(2,1)S(1)}, u32[]{:S(2)}, u32[]{:S(2)}) %collective-permute-start.22) | collective-permute-done | bytes 131104 | tf_op jit(solution)/shard_map/ppermute | solution.py:34
  136.7 1.4 copy-done.9
  138.1 3.1 %shard_map.89.early_hbm = bf16[384,1024]{1,0:T(8,128)(2,1)S(1)} custom-call(s32[1]{0:T(128)} %bitcast.core_ref, s32[8,4]{1,0:T(8,128)S(1)} %copy.37.tgt_ref, s32[8]{0:T(128)S(1)} %bitcast.30, bf16[8,4,128,128]{3,2,1,0:T(8,128)(2,1)S(1)} %bitcast.28, bf16[32,4,3,32,128]{4,3,2,1,0:T(8,128)(2,1)S(1)} %all-to-all-done.2.part), custom_call_target="tpu_custom_call" | custom-call | flops 3000000000 | bytes 8388608 | tf_op jit(solution)/shard_map/pallas_call | solution.py:143
  141.1 0.9 copy-done.3
  142.0 36.6 %all-to-all-done.1.part_hbm = bf16[32,4,5,32,128]{4,3,2,1,0:T(8,128)(2,1)} async-done(((bf16[32,4,5,32,128]{4,3,2,1,0:T(8,128)(2,1)}), bf16[32,4,5,32,128]{4,3,2,1,0:T(8,128)(2,1)}, u32[]{:S(2)}, u32[]{:S(2)}) %all-to-all-start.1) | async-done | bytes 5242912 | tf_op jit(solution)/shard_map/all_to_all | solution.py:38
  178.6 12.5 %shard_map.90 = (bf16[1024,1024]{1,0:T(8,128)(2,1)}, f32[8,2,8,32,128]{4,3,2,1,0:T(8,128)}, bf16[8,2,8,32,128]{4,3,2,1,0:T(8,128)(2,1)}) custom-call(s32[1]{0:T(128)} %bitcast.core_ref, s32[8,4]{1,0:T(8,128)} %copy-done, s32[8]{0:T(128)} %bitcast.29, bf16[8,4,128,128]{3,2,1,0:T(8,128)(2,1)} %bitcast.27, ...), custom_call_target="tpu_custom_call" | custom-call | flops 6000000000 | bytes 20971520 | tf_op jit(solution)/shard_map/pallas_call | solution.py:233
  191.2 2.9 %collective-permute-done.24 = bf16[8,2,8,32,128]{4,3,2,1,0:T(8,128)(2,1)S(1)} collective-permute-done((bf16[8,2,8,32,128]{4,3,2,1,0:T(8,128)(2,1)}, bf16[8,2,8,32,128]{4,3,2,1,0:T(8,128)(2,1)S(1)}, u32[]{:S(2)}, u32[]{:S(2)}) %collective-permute-start.24) | collective-permute-done | bytes 1048608 | tf_op jit(solution)/shard_map/ppermute | solution.py:277
  194.1 2.9 %add_convert_fusion = bf16[8,2,8,32,128]{4,3,2,1,0:T(8,128)(2,1)} fusion(f32[8,2,8,32,128]{4,3,2,1,0:T(8,128)} %get-tuple-element.10, bf16[8,2,8,32,128]{4,3,2,1,0:T(8,128)(2,1)S(1)} %collective-permute-done.24), kind=kLoop, calls=%fused_computation | loop fusion | flops 1572864 | bytes 4194304 | tf_op jit(solution)/shard_map/convert_element_type | solution.py:278
  197.0 3.9 %all-to-all-start.3 = ((bf16[16,8,32,128]{3,2,1,0:T(8,128)(2,1)}), bf16[16,8,32,128]{3,2,1,0:T(8,128)(2,1)S(1)}, u32[]{:S(2)}, u32[]{:S(2)}) async-start(bf16[16,8,32,128]{3,2,1,0:T(8,128)(2,1)} %bitcast.15), calls=%async_computation.3 | async-start | bytes 2097152 | tf_op jit(solution)/shard_map/all_to_all | solution.py:38
  200.9 18.3 %all-to-all-done.3.came_ref = bf16[16,8,32,128]{3,2,1,0:T(8,128)(2,1)S(1)} async-done(((bf16[16,8,32,128]{3,2,1,0:T(8,128)(2,1)}), bf16[16,8,32,128]{3,2,1,0:T(8,128)(2,1)S(1)}, u32[]{:S(2)}, u32[]{:S(2)}) %all-to-all-start.3) | async-done | bytes 1048608 | tf_op jit(solution)/shard_map/all_to_all | solution.py:38
  219.4 13.2 %all_to_all.31 = f32[8,32,128]{2,1,0:T(8,128)S(1)} all-to-all(f32[8,32,128]{2,1,0:T(8,128)S(1)} %shard_map.91), channel_id=1, replica_groups=mesh['ylo'=2,'x'=4,'z'=8,'yhi'=2,'core'=2] {'z'}, dimensions={0} | all-to-all | bytes 262144 | tf_op jit(solution)/shard_map/all_to_all | solution.py:38
  232.6 9.9 %all_to_all.32 = f32[8,32,128]{2,1,0:T(8,128)S(1)} all-to-all(f32[8,32,128]{2,1,0:T(8,128)S(1)} %broadcast_in_dim.18), channel_id=1, replica_groups=mesh['ylo'=2,'x'=4,'z'=8,'yhi'=2,'core'=2] {'ylo','x'}, dimensions={0} | all-to-all | bytes 262144 | tf_op jit(solution)/shard_map/all_to_all | solution.py:38
  (72 shorter events, 3.4 us)
Async XLA Ops:
  0.6 12.5 %copy-start.8 = (bf16[32,1024]{1,0:T(8,128)(2,1)S(1)}, bf16[32,1024]{1,0:T(8,128)(2,1)}, u32[]{:S(2)}) copy-start(bf16[32,1024]{1,0:T(8,128)(2,1)} %param.12) | copy-start | bytes 196612
  0.6 12.6 %copy-start.10 = (s32[1,1,8,4]{2,3,1,0:T(4,128)S(1)}, s32[1,1,8,4]{2,3,1,0:T(4,128)}, u32[]{:S(2)}) copy-start(s32[1,1,8,4]{2,3,1,0:T(4,128)} %param.9) | copy-start | bytes 388
  0.6 12.4 %collective-permute-start = (bf16[32,1024]{1,0:T(8,128)(2,1)}, bf16[32,1024]{1,0:T(8,128)(2,1)S(1)}, u32[]{:S(2)}, u32[]{:S(2)}) collective-permute-start(bf16[32,1024]{1,0:T(8,128)(2,1)} %param.12), channel_id=1, source_target_pairs={{0,130},{2,128},{128,2},{130,0},{1,131},{3,129},{129,3},{131,1},{4... | collective-permute-start | bytes 196616 | tf_op jit(solution)/shard_map/ppermute | solution.py:287
  5.0 33.5 %copy-start.6 = (bf16[16,16384]{1,0:T(8,128)(2,1)}, bf16[16,16384]{1,0:T(8,128)(2,1)S(1)}, u32[]{:S(2)}) copy-start(bf16[16,16384]{1,0:T(8,128)(2,1)S(1)} %get-tuple-element.12.refs_1_) | copy-start | bytes 1572868
  5.0 33.4 %copy-start.7 = (bf16[16,16384]{1,0:T(8,128)(2,1)}, bf16[16,16384]{1,0:T(8,128)(2,1)S(1)}, u32[]{:S(2)}) copy-start(bf16[16,16384]{1,0:T(8,128)(2,1)S(1)} %get-tuple-element.13.refs_0_) | copy-start | bytes 1572868
  5.0 20.2 %collective-permute-start.10 = (bf16[16,16384]{1,0:T(8,128)(2,1)S(1)}, bf16[16,16384]{1,0:T(8,128)(2,1)}, u32[]{:S(2)}, u32[]{:S(2)}) collective-permute-start(bf16[16,16384]{1,0:T(8,128)(2,1)S(1)} %get-tuple-element.12.refs_1_), channel_id=1, source_target_pairs={{0,4},{4,8},{8,12},{12,16},{16,20},{20,24},{24,28},{28,0},{1,5},{5... | collective-permute-start | bytes 1572872 | tf_op jit(solution)/shard_map/ppermute | solution.py:34
  7.0 18.2 %collective-permute-start.6 = (bf16[16,16384]{1,0:T(8,128)(2,1)S(1)}, bf16[16,16384]{1,0:T(8,128)(2,1)}, u32[]{:S(2)}, u32[]{:S(2)}) collective-permute-start(bf16[16,16384]{1,0:T(8,128)(2,1)S(1)} %get-tuple-element.12.refs_1_), channel_id=1, source_target_pairs={{0,28},{4,0},{8,4},{12,8},{16,12},{20,16},{24,20},{28,24},{1,29},{... | collective-permute-start | bytes 1572872 | tf_op jit(solution)/shard_map/ppermute | solution.py:34
  11.1 23.6 %collective-permute-start.12 = (bf16[16,16384]{1,0:T(8,128)(2,1)S(1)}, bf16[16,16384]{1,0:T(8,128)(2,1)}, u32[]{:S(2)}, u32[]{:S(2)}) collective-permute-start(bf16[16,16384]{1,0:T(8,128)(2,1)S(1)} %get-tuple-element.13.refs_0_), channel_id=1, source_target_pairs={{0,28},{4,0},{8,4},{12,8},{16,12},{20,16},{24,20},{28,24},{1,29},{... | collective-permute-start | bytes 1572872 | tf_op jit(solution)/shard_map/ppermute | solution.py:34
  13.0 25.5 %collective-permute-start.2 = (bf16[16,16384]{1,0:T(8,128)(2,1)S(1)}, bf16[16,16384]{1,0:T(8,128)(2,1)}, u32[]{:S(2)}, u32[]{:S(2)}) collective-permute-start(bf16[16,16384]{1,0:T(8,128)(2,1)S(1)} %get-tuple-element.13.refs_0_), channel_id=1, source_target_pairs={{0,4},{4,8},{8,12},{12,16},{16,20},{20,24},{24,28},{28,0},{1,5},{5... | collective-permute-start | bytes 1572872 | tf_op jit(solution)/shard_map/ppermute | solution.py:34
  13.1 11.3 %collective-permute-start.1 = (bf16[2,32,1024]{2,1,0:T(8,128)(2,1)S(1)}, bf16[2,32,1024]{2,1,0:T(8,128)(2,1)S(1)}, u32[]{:S(2)}, u32[]{:S(2)}) collective-permute-start(bf16[2,32,1024]{2,1,0:T(8,128)(2,1)S(1)} %get-tuple-element.15), channel_id=1, source_target_pairs={{0,1},{1,0},{2,3},{3,2},{4,5},{5,4},{6,7},{7,6},{8,9},{9,8},{10,11... | collective-permute-start | bytes 393224 | tf_op jit(solution)/shard_map/ppermute | solution.py:290
  25.2 31.2 %collective-permute-start.11 = (bf16[16,16384]{1,0:T(8,128)(2,1)}, bf16[16,16384]{1,0:T(8,128)(2,1)}, u32[]{:S(2)}, u32[]{:S(2)}) collective-permute-start(bf16[16,16384]{1,0:T(8,128)(2,1)} %collective-permute-done.10.refs_3_), channel_id=1, source_target_pairs={{0,4},{4,8},{8,12},{12,16},{16,20},{20,24},{24,28},{28,0},{1,5},{5... | collective-permute-start | bytes 1572872 | tf_op jit(solution)/shard_map/ppermute | solution.py:34
  25.3 23.1 %collective-permute-start.7 = (bf16[16,16384]{1,0:T(8,128)(2,1)}, bf16[16,16384]{1,0:T(8,128)(2,1)}, u32[]{:S(2)}, u32[]{:S(2)}) collective-permute-start(bf16[16,16384]{1,0:T(8,128)(2,1)} %collective-permute-done.6.refs_5_), channel_id=1, source_target_pairs={{0,28},{4,0},{8,4},{12,8},{16,12},{20,16},{24,20},{28,24},{1,29},{... | collective-permute-start | bytes 1572872 | tf_op jit(solution)/shard_map/ppermute | solution.py:34
  34.7 22.6 %collective-permute-start.13 = (bf16[16,16384]{1,0:T(8,128)(2,1)}, bf16[16,16384]{1,0:T(8,128)(2,1)}, u32[]{:S(2)}, u32[]{:S(2)}) collective-permute-start(bf16[16,16384]{1,0:T(8,128)(2,1)} %collective-permute-done.12.refs_4_), channel_id=1, source_target_pairs={{0,28},{4,0},{8,4},{12,8},{16,12},{20,16},{24,20},{28,24},{1,29},{... | collective-permute-start | bytes 1572872 | tf_op jit(solution)/shard_map/ppermute | solution.py:34
  38.5 18.0 %collective-permute-start.3 = (bf16[16,16384]{1,0:T(8,128)(2,1)}, bf16[16,16384]{1,0:T(8,128)(2,1)}, u32[]{:S(2)}, u32[]{:S(2)}) collective-permute-start(bf16[16,16384]{1,0:T(8,128)(2,1)} %collective-permute-done.2.refs_2_), channel_id=1, source_target_pairs={{0,4},{4,8},{8,12},{12,16},{16,20},{20,24},{24,28},{28,0},{1,5},{5... | collective-permute-start | bytes 1572872 | tf_op jit(solution)/shard_map/ppermute | solution.py:34
  43.2 54.1 %all-to-all-start.2 = ((bf16[32,4,3,32,128]{4,3,2,1,0:T(8,128)(2,1)}), bf16[32,4,3,32,128]{4,3,2,1,0:T(8,128)(2,1)S(1)}, u32[]{:S(2)}, u32[]{:S(2)}) async-start(bf16[32,4,3,32,128]{4,3,2,1,0:T(8,128)(2,1)} %shard_map.88), calls=%async_computation.2 | async-start | bytes 6291456 | tf_op jit(solution)/shard_map/all_to_all | solution.py:38
  48.3 20.2 %collective-permute-start.8 = (bf16[16,16384]{1,0:T(8,128)(2,1)}, bf16[16,16384]{1,0:T(8,128)(2,1)S(1)}, u32[]{:S(2)}, u32[]{:S(2)}) collective-permute-start(bf16[16,16384]{1,0:T(8,128)(2,1)} %collective-permute-done.7.refs_3_), channel_id=1, source_target_pairs={{0,28},{4,0},{8,4},{12,8},{16,12},{20,16},{24,20},{28,24},{1,29},{... | collective-permute-start | bytes 1572872 | tf_op jit(solution)/shard_map/ppermute | solution.py:34
  56.4 16.3 %collective-permute-start.4 = (bf16[16,16384]{1,0:T(8,128)(2,1)}, bf16[16,16384]{1,0:T(8,128)(2,1)S(1)}, u32[]{:S(2)}, u32[]{:S(2)}) collective-permute-start(bf16[16,16384]{1,0:T(8,128)(2,1)} %collective-permute-done.3.refs_0_), channel_id=1, source_target_pairs={{0,4},{4,8},{8,12},{12,16},{16,20},{20,24},{24,28},{28,0},{1,5},{5... | collective-permute-start | bytes 1572872 | tf_op jit(solution)/shard_map/ppermute | solution.py:34
  56.4 27.5 %collective-permute-start.14 = (bf16[16,16384]{1,0:T(8,128)(2,1)}, bf16[16,16384]{1,0:T(8,128)(2,1)S(1)}, u32[]{:S(2)}, u32[]{:S(2)}) collective-permute-start(bf16[16,16384]{1,0:T(8,128)(2,1)} %collective-permute-done.11.refs_1_), channel_id=1, source_target_pairs={{0,4},{4,8},{8,12},{12,16},{16,20},{20,24},{24,28},{28,0},{1,5},{5... | collective-permute-start | bytes 1572872 | tf_op jit(solution)/shard_map/ppermute | solution.py:34
  57.2 26.7 %collective-permute-start.15 = (bf16[16,16384]{1,0:T(8,128)(2,1)}, bf16[16,16384]{1,0:T(8,128)(2,1)}, u32[]{:S(2)}, u32[]{:S(2)}) collective-permute-start(bf16[16,16384]{1,0:T(8,128)(2,1)} %collective-permute-done.13.refs_2_), channel_id=1, source_target_pairs={{0,28},{4,0},{8,4},{12,8},{16,12},{20,16},{24,20},{28,24},{1,29},{... | collective-permute-start | bytes 1572872 | tf_op jit(solution)/shard_map/ppermute | solution.py:34
  68.5 15.5 %copy-start.12 = (bf16[16,16384]{1,0:T(8,128)(2,1)}, bf16[16,16384]{1,0:T(8,128)(2,1)S(1)}, u32[]{:S(2)}) copy-start(bf16[16,16384]{1,0:T(8,128)(2,1)S(1)} %collective-permute-done.8.refs_7_) | copy-start | bytes 1572868
  68.5 21.8 %collective-permute-start.9 = (bf16[16,16384]{1,0:T(8,128)(2,1)S(1)}, bf16[16,16384]{1,0:T(8,128)(2,1)S(1)}, u32[]{:S(2)}, u32[]{:S(2)}) collective-permute-start(bf16[16,16384]{1,0:T(8,128)(2,1)S(1)} %collective-permute-done.8.refs_7_), channel_id=1, source_target_pairs={{0,28},{4,0},{8,4},{12,8},{16,12},{20,16},{24,20},{28,24},{1,29},{... | collective-permute-start | bytes 1572872 | tf_op jit(solution)/shard_map/ppermute | solution.py:34
  72.7 11.2 %copy-start.13 = (bf16[16,16384]{1,0:T(8,128)(2,1)}, bf16[16,16384]{1,0:T(8,128)(2,1)S(1)}, u32[]{:S(2)}) copy-start(bf16[16,16384]{1,0:T(8,128)(2,1)S(1)} %collective-permute-done.4.refs_4_) | copy-start | bytes 1572868
  72.7 20.4 %collective-permute-start.5 = (bf16[16,16384]{1,0:T(8,128)(2,1)S(1)}, bf16[16,16384]{1,0:T(8,128)(2,1)S(1)}, u32[]{:S(2)}, u32[]{:S(2)}) collective-permute-start(bf16[16,16384]{1,0:T(8,128)(2,1)S(1)} %collective-permute-done.4.refs_4_), channel_id=1, source_target_pairs={{0,4},{4,8},{8,12},{12,16},{16,20},{20,24},{24,28},{28,0},{1,5},{5... | collective-permute-start | bytes 1572872 | tf_op jit(solution)/shard_map/ppermute | solution.py:34
  84.0 0.8 copy-start.14
  90.3 2.8 %copy-start.4 = (bf16[16,16384]{1,0:T(8,128)(2,1)}, bf16[16,16384]{1,0:T(8,128)(2,1)S(1)}, u32[]{:S(2)}) copy-start(bf16[16,16384]{1,0:T(8,128)(2,1)S(1)} %collective-permute-done.9.refs_1_) | copy-start | bytes 1572868
  93.1 0.8 copy-start.5
  97.3 15.7 %copy-start.11 = (s32[1,1,8,4]{2,3,1,0:T(4,128)S(1)}, s32[1,1,8,4]{2,3,1,0:T(4,128)}, u32[]{:S(2)}) copy-start(s32[1,1,8,4]{2,3,1,0:T(4,128)} %param.8) | copy-start | bytes 388
  97.3 81.3 %all-to-all-start.1 = ((bf16[32,4,5,32,128]{4,3,2,1,0:T(8,128)(2,1)}), bf16[32,4,5,32,128]{4,3,2,1,0:T(8,128)(2,1)}, u32[]{:S(2)}, u32[]{:S(2)}) async-start(bf16[32,4,5,32,128]{4,3,2,1,0:T(8,128)(2,1)} %shard_map.87), calls=%async_computation.1 | async-start | bytes 10485760 | tf_op jit(solution)/shard_map/all_to_all | solution.py:38
  102.4 8.5 %collective-permute-start.17 = (bf16[128,1024]{1,0:T(8,128)(2,1)S(1)}, bf16[128,1024]{1,0:T(8,128)(2,1)}, u32[]{:S(2)}, u32[]{:S(2)}) collective-permute-start(bf16[128,1024]{1,0:T(8,128)(2,1)S(1)} %bitcast.31), channel_id=1, source_target_pairs={{0,28},{4,0},{8,4},{12,8},{16,12},{20,16},{24,20},{28,24},{1,29},{... | collective-permute-start | bytes 786440 | tf_op jit(solution)/shard_map/ppermute | solution.py:34
  103.3 9.7 %collective-permute-start.16 = (bf16[128,1024]{1,0:T(8,128)(2,1)S(1)}, bf16[128,1024]{1,0:T(8,128)(2,1)}, u32[]{:S(2)}, u32[]{:S(2)}) collective-permute-start(bf16[128,1024]{1,0:T(8,128)(2,1)S(1)} %bitcast.32), channel_id=1, source_target_pairs={{0,4},{4,8},{8,12},{12,16},{16,20},{20,24},{24,28},{28,0},{1,5},{5... | collective-permute-start | bytes 786440 | tf_op jit(solution)/shard_map/ppermute | solution.py:34
  111.0 7.8 %collective-permute-start.19 = (bf16[128,1024]{1,0:T(8,128)(2,1)}, bf16[128,1024]{1,0:T(8,128)(2,1)}, u32[]{:S(2)}, u32[]{:S(2)}) collective-permute-start(bf16[128,1024]{1,0:T(8,128)(2,1)} %collective-permute-done.17), channel_id=1, source_target_pairs={{0,28},{4,0},{8,4},{12,8},{16,12},{20,16},{24,20},{28,24},{1,29},{... | collective-permute-start | bytes 786440 | tf_op jit(solution)/shard_map/ppermute | solution.py:34
  112.9 9.1 %collective-permute-start.18 = (bf16[128,1024]{1,0:T(8,128)(2,1)}, bf16[128,1024]{1,0:T(8,128)(2,1)}, u32[]{:S(2)}, u32[]{:S(2)}) collective-permute-start(bf16[128,1024]{1,0:T(8,128)(2,1)} %collective-permute-done.16), channel_id=1, source_target_pairs={{0,4},{4,8},{8,12},{12,16},{16,20},{20,24},{24,28},{28,0},{1,5},{5... | collective-permute-start | bytes 786440 | tf_op jit(solution)/shard_map/ppermute | solution.py:34
  113.1 25.0 %copy-start = (s32[8,4]{1,0:T(8,128)}, s32[8,4]{1,0:T(8,128)S(1)}, u32[]{:S(2)}) copy-start(s32[8,4]{1,0:T(8,128)S(1)} %copy.37.tgt_ref) | copy-start | bytes 388
  113.1 24.9 %copy-start.1 = (bf16[1,1,8,4,128,128]{5,4,3,2,1,0:T(8,128)(2,1)S(1)}, bf16[1,1,8,4,128,128]{5,4,3,2,1,0:T(8,128)(2,1)}, u32[]{:S(2)}) copy-start(bf16[1,1,8,4,128,128]{5,4,3,2,1,0:T(8,128)(2,1)} %param.11) | copy-start | bytes 3145732
  113.1 24.9 %copy-start.2 = (s32[1,1,8]{2,1,0:T(1,128)S(1)}, s32[1,1,8]{2,1,0:T(1,128)}, u32[]{:S(2)}) copy-start(s32[1,1,8]{2,1,0:T(1,128)} %param.10) | copy-start | bytes 100
  118.8 7.6 %collective-permute-start.21 = (bf16[128,1024]{1,0:T(8,128)(2,1)}, bf16[128,1024]{1,0:T(8,128)(2,1)S(1)}, u32[]{:S(2)}, u32[]{:S(2)}) collective-permute-start(bf16[128,1024]{1,0:T(8,128)(2,1)} %collective-permute-done.19), channel_id=1, source_target_pairs={{0,28},{4,0},{8,4},{12,8},{16,12},{20,16},{24,20},{28,24},{1,29},{... | collective-permute-start | bytes 786440 | tf_op jit(solution)/shard_map/ppermute | solution.py:34
  122.0 8.1 %collective-permute-start.20 = (bf16[128,1024]{1,0:T(8,128)(2,1)}, bf16[128,1024]{1,0:T(8,128)(2,1)S(1)}, u32[]{:S(2)}, u32[]{:S(2)}) collective-permute-start(bf16[128,1024]{1,0:T(8,128)(2,1)} %collective-permute-done.18), channel_id=1, source_target_pairs={{0,4},{4,8},{8,12},{12,16},{16,20},{20,24},{24,28},{28,0},{1,5},{5... | collective-permute-start | bytes 786440 | tf_op jit(solution)/shard_map/ppermute | solution.py:34
  126.4 10.2 %collective-permute-start.23 = (bf16[64,1024]{1,0:T(8,128)(2,1)S(1)}, bf16[64,1024]{1,0:T(8,128)(2,1)S(1)}, u32[]{:S(2)}, u32[]{:S(2)}) collective-permute-start(bf16[64,1024]{1,0:T(8,128)(2,1)S(1)} %slice.17), channel_id=1, source_target_pairs={{0,28},{4,0},{8,4},{12,8},{16,12},{20,16},{24,20},{28,24},{1,29},{... | collective-permute-start | bytes 393224 | tf_op jit(solution)/shard_map/ppermute | solution.py:34
  130.1 6.5 %collective-permute-start.22 = (bf16[64,1024]{1,0:T(8,128)(2,1)S(1)}, bf16[64,1024]{1,0:T(8,128)(2,1)S(1)}, u32[]{:S(2)}, u32[]{:S(2)}) collective-permute-start(bf16[64,1024]{1,0:T(8,128)(2,1)S(1)} %slice.16), channel_id=1, source_target_pairs={{0,4},{4,8},{8,12},{12,16},{16,20},{20,24},{24,28},{28,0},{1,5},{5... | collective-permute-start | bytes 393224 | tf_op jit(solution)/shard_map/ppermute | solution.py:34
  136.6 1.4 copy-start.9
  141.1 0.9 copy-start.3
  191.1 3.0 %collective-permute-start.24 = (bf16[8,2,8,32,128]{4,3,2,1,0:T(8,128)(2,1)}, bf16[8,2,8,32,128]{4,3,2,1,0:T(8,128)(2,1)S(1)}, u32[]{:S(2)}, u32[]{:S(2)}) collective-permute-start(bf16[8,2,8,32,128]{4,3,2,1,0:T(8,128)(2,1)} %get-tuple-element.11), channel_id=1, source_target_pairs={{0,1},{1,0},{2,3},{3,2},{4,5},{5,4},{6,7},{7,6},{8,9},{9,8},{10,11... | collective-permute-start | bytes 3145736 | tf_op jit(solution)/shard_map/ppermute | solution.py:277
  197.0 22.2 %all-to-all-start.3 = ((bf16[16,8,32,128]{3,2,1,0:T(8,128)(2,1)}), bf16[16,8,32,128]{3,2,1,0:T(8,128)(2,1)S(1)}, u32[]{:S(2)}, u32[]{:S(2)}) async-start(bf16[16,8,32,128]{3,2,1,0:T(8,128)(2,1)} %bitcast.15), calls=%async_computation.3 | async-start | bytes 2097152 | tf_op jit(solution)/shard_map/all_to_all | solution.py:38

commit v5 on v4

v5 whole, which is shorter than its diff:
```python
import functools
import math

import jax
import jax.numpy as jnp
from jax import lax
from jax.experimental import pallas as pl
from jax.experimental.pallas import tpu as pltpu
from jax.sharding import Mesh, PartitionSpec as P

REP = ("ylo", "x")
PLANE = ("ylo", "x", "yhi", "core")
CHIPS_XY = ("ylo", "x", "yhi")
ZN = 8
PARTS = ((0, 1, -1), (2, -2, 3, -3), (4,))
ORDER = tuple(d for part in PARTS for d in part)
LANES = 4
LAYER_MIB = 56
VMEM = pl.BlockSpec(memory_space=pltpu.VMEM)
SMEM = pl.BlockSpec(memory_space=pltpu.SMEM)
HBM = pl.BlockSpec(memory_space=pltpu.HBM)
SWAP = [(0, 1), (1, 0)]


def params(mib):
    return pltpu.CompilerParams(vmem_limit_bytes=mib * 2**20)


def cost(flops, size):
    return pl.CostEstimate(flops=flops, bytes_accessed=size, transcendentals=0)


def shift_z(value, step):
    return lax.ppermute(value, "z", [(i, (i + step) % ZN) for i in range(ZN)])


def exchange(value, axes):
    return lax.all_to_all(value, axes, split_axis=0, concat_axis=0, tiled=True)


def ring(own):
    half = own.shape[0] // 2
    held = {0: own}
    for step in range(1, ZN // 2):
        held[step] = shift_z(held[step - 1], 1)
        held[-step] = shift_z(held[1 - step], -1)
    far = ZN // 2 - 1
    ends = [shift_z(held[far][:half], 1), shift_z(held[-far][half:], -1)]
    return {distance: [value] for distance, value in held.items()} | {ZN // 2: ends}


def pick_kernel(block, layout, wanted_ref, *refs):
    slices, (out_ref, buffer, sems) = refs[: len(layout)], refs[-3:]
    dests, slots = buffer.shape[:2]
    groups = sems.shape[0]
    each = dests // groups

    def one(step, carry):
        dest, slot = step // slots, step % slots
        start = pl.multiple_of(wanted_ref[dest, slot] * block, block)
        for ref, (place, low) in zip(slices, layout):
            buffer[dest, slot, place, low : low + ref.shape[0], :] = ref[:, pl.ds(start, block)]
        return carry

    copies = []
    for group in range(groups):
        at = slice(group * each, group * each + each)
        lax.fori_loop(group * each * slots, (group + 1) * each * slots, one, 0, unroll=4)
        copies.append(pltpu.make_async_copy(buffer.at[at], out_ref.at[at], sems.at[group]))
        copies[-1].start()
    for copy in copies:
        copy.wait()


def pick(wanted, slices, block, flops):
    askers, slots = wanted.shape
    count, rows = len(slices), sum(piece.shape[0] for piece in slices[0])
    layout = [(place, rows // len(pieces) * index) for place, pieces in enumerate(slices) for index in range(len(pieces))]
    refs = [piece for pieces in slices for piece in pieces]
    shape = (askers, slots, count, rows, block)
    return pl.pallas_call(
        functools.partial(pick_kernel, block, layout),
        out_shape=jax.ShapeDtypeStruct(shape, jnp.bfloat16),
        in_specs=[SMEM] + [VMEM] * len(refs),
        out_specs=HBM,
        scratch_shapes=[pltpu.VMEM(shape, jnp.bfloat16), pltpu.SemaphoreType.DMA((4,))],
        compiler_params=params(58),
        cost_estimate=cost(flops, count * 2**21),
    )(wanted, *refs)


def add_tiles(core, tgt_ref, count_ref, vals_ref, part, acc, ready):
    sections, slots, block, _ = vals_ref.shape
    places, rows = part.shape[2:4]
    acc[...] = jnp.zeros_like(acc)

    def one(section, slot):
        column = pl.multiple_of(tgt_ref[section, slot] * block, block)
        sources = [section * LANES + lane + core * (1 - 2 * (lane % 2)) for lane in range(LANES)]
        columns_in = jnp.concatenate([part[source, slot].reshape(places * rows, block) for source in sources])
        contrib = lax.dot_general(
            columns_in, vals_ref[section, slot], (((1,), (1,)), ((), ())), preferred_element_type=jnp.float32
        )
        for lane in range(LANES):
            for place in range(places):
                low, at = (place * LANES + lane) * rows, (lane * places + place) * rows
                acc[low : low + rows, pl.ds(column, block)] += contrib[at : at + rows]

    @pl.loop(0, sections)
    def _(section):
        ready(section)

        @pl.loop(0, jnp.minimum(count_ref[section], slots))
        def _(slot):
            one(section, slot)


def aggregate_kernel(core_ref, tgt_ref, count_ref, vals_ref, part, turned_ref, plain_ref, acc):
    add_tiles(core_ref[0], tgt_ref, count_ref, vals_ref, part, acc, lambda section: None)
    step = vals_ref.shape[-1]
    for low in range(0, acc.shape[1], step):
        at = slice(low, low + step)
        value = acc[:, at]
        turned_ref[:, at] = value.astype(turned_ref.dtype)
        plain_ref[at] = value.T.astype(plain_ref.dtype)


def aggregate(core, targets, counts, values, part, num_rows):
    num_feats = LANES * part.shape[2] * part.shape[3]
    return pl.pallas_call(
        aggregate_kernel,
        out_shape=(
            jax.ShapeDtypeStruct((num_feats, num_rows), jnp.bfloat16),
            jax.ShapeDtypeStruct((num_rows, num_feats), jnp.bfloat16),
        ),
        in_specs=[SMEM] * 3 + [VMEM] * 2,
        out_specs=(VMEM, VMEM),
        scratch_shapes=[pltpu.VMEM((num_feats, num_rows), jnp.float32)],
        compiler_params=params(20),
        cost_estimate=cost(3 * 10**9, 8 * 2**20),
    )(core, targets, counts, values, part)


def layer_kernel(num_early, core_ref, tgt_ref, count_ref, *refs):
    early, refs = refs[: 2 * num_early], refs[2 * num_early :]
    vals_hbm, part_hbm, weight_hbm, cot_hbm, act_hbm, kept_hbm, gone_hbm = refs[:7]
    vals, part, weight, cot, act, kept, gone, acc, turned, plain, dpre, part_sem, sems, early_sems, out_sems = refs[7:]
    part_copy = pltpu.make_async_copy(part_hbm, part, part_sem)
    vals_copy = pltpu.make_async_copy(vals_hbm, vals, sems.at[0])
    weight_copy = pltpu.make_async_copy(weight_hbm, weight, sems.at[1])
    cot_copy = pltpu.make_async_copy(cot_hbm, cot, sems.at[2])
    turned_copies, plain_copies = [], []
    low = 0
    for index in range(num_early):
        at = slice(low, low + early[2 * index].shape[0])
        low = at.stop
        turned_copies.append(pltpu.make_async_copy(early[2 * index], turned.at[at], early_sems.at[2 * index]))
        plain_copies.append(pltpu.make_async_copy(early[2 * index + 1], plain.at[:, at], early_sems.at[2 * index + 1]))
    for copy in (vals_copy, part_copy, *plain_copies, weight_copy, cot_copy, *turned_copies):
        copy.start()
    vals_copy.wait()
    part_copy.wait()
    add_tiles(core_ref[0], tgt_ref, count_ref, vals, part, acc, lambda section: None)
    width = vals.shape[-1]
    for first in range(0, acc.shape[1], width):
        at = slice(first, first + width)
        value = acc[:, at]
        turned[low:, at] = value.astype(turned.dtype)
        plain[at, low:] = value.T.astype(plain.dtype)
    for copy in (*plain_copies, weight_copy, cot_copy):
        copy.wait()

    blocks = out_sems.shape[1]
    step = act.shape[0] // blocks
    out_copies = []

    def send(source, target, sem):
        out_copies.append(pltpu.make_async_copy(source, target, sem))
        out_copies[-1].start()

    for index in range(blocks):
        at = slice(index * step, index * step + step)
        preact = jnp.dot(plain[at], weight[...], preferred_element_type=jnp.float32)
        sigmoid_val = jax.nn.sigmoid(preact)
        act[at] = (preact * sigmoid_val).astype(act.dtype)
        send(act.at[at], act_hbm.at[at], out_sems.at[0, index])
        slope = sigmoid_val * (1.0 + preact * (1.0 - sigmoid_val))
        dpre[at] = (cot[at].astype(jnp.float32) * slope).astype(dpre.dtype)
    for copy in turned_copies:
        copy.wait()
    pieces, _, _, rows, width = kept.shape
    step = turned.shape[0] // blocks
    for index in range(blocks):
        low = index * step
        grad = jnp.dot(turned[low : low + step], dpre[...], preferred_element_type=jnp.float32)
        for at in range(0, step, rows):
            lane = (low + at) // rows
            place, hi, core = lane // LANES, lane % LANES // 2, lane % 2
            for piece in range(pieces):
                value = grad[at : at + rows, piece * width : (piece + 1) * width]
                if core == 0:
                    kept[piece, hi, place] = value
                else:
                    gone[piece, hi, place] = value.astype(gone.dtype)
        done = slice(low // (LANES * rows), (low + step) // (LANES * rows))
        send(gone.at[:, :, done], gone_hbm.at[:, :, done], out_sems.at[1, index])
        send(kept.at[:, :, done], kept_hbm.at[:, :, done], out_sems.at[2, index])
    for copy in out_copies:
        copy.wait()


def layer(core, targets, counts, values, part, early, weight, cotangent):
    tgt_rows, width = cotangent.shape
    feats = weight.shape[0]
    cut = (8, 2, ZN, part.shape[3], width // 8)
    early = [value for pair in early for value in pair]
    late = feats - sum(value.shape[0] for value in early[::2])
    return pl.pallas_call(
        functools.partial(layer_kernel, len(early) // 2),
        out_shape=(
            jax.ShapeDtypeStruct((tgt_rows, width), jnp.bfloat16),
            jax.ShapeDtypeStruct(cut, jnp.float32),
            jax.ShapeDtypeStruct(cut, jnp.bfloat16),
        ),
        in_specs=[SMEM] * 3 + [HBM] * (len(early) + 4),
        out_specs=(HBM, HBM, HBM),
        scratch_shapes=[
            pltpu.VMEM(values.shape, values.dtype),
            pltpu.VMEM(part.shape, part.dtype),
            pltpu.VMEM(weight.shape, weight.dtype),
            pltpu.VMEM((tgt_rows, width), cotangent.dtype),
            pltpu.VMEM((tgt_rows, width), jnp.bfloat16),
            pltpu.VMEM(cut, jnp.float32),
            pltpu.VMEM(cut, jnp.bfloat16),
            pltpu.VMEM((late, tgt_rows), jnp.float32),
            pltpu.VMEM((feats, tgt_rows), jnp.bfloat16),
            pltpu.VMEM((tgt_rows, feats), jnp.bfloat16),
            pltpu.VMEM((tgt_rows, width), jnp.bfloat16),
            pltpu.SemaphoreType.DMA,
            pltpu.SemaphoreType.DMA((3,)),
            pltpu.SemaphoreType.DMA((len(early),)),
            pltpu.SemaphoreType.DMA((3, 4)),
        ],
        compiler_params=params(LAYER_MIB),
        cost_estimate=cost(6 * 10**9, 20 * 2**20),
    )(core, targets, counts, *early, values, part, weight, cotangent)


def sum_plane_kernel(z_ref, came_ref, out_ref):
    for place, distance in enumerate(ORDER):
        total = came_ref[:, place].astype(jnp.float32).sum(0)
        out_ref[lax.rem(z_ref[0] + (ZN - distance), ZN)] = total


def sum_plane(came):
    return pl.pallas_call(
        sum_plane_kernel,
        out_shape=jax.ShapeDtypeStruct(came.shape[1:], jnp.float32),
        in_specs=[SMEM, VMEM],
        out_specs=VMEM,
        compiler_params=params(16),
    )(lax.axis_index("z").astype(jnp.int32)[None], came)


def sum_over_devices(kept, gone):
    came = lax.ppermute(gone, "core", SWAP)
    chip = (kept + came.astype(jnp.float32)).astype(jnp.bfloat16)
    chip = chip.reshape(16, *chip.shape[2:])
    plane = sum_plane(exchange(chip, CHIPS_XY))
    column = exchange(plane, "z").sum(0)
    whole = exchange(jnp.broadcast_to(column[None], (8, *column.shape)), REP)
    return whole.transpose(1, 0, 2).reshape(column.shape[0], -1)


def weight_lanes(own):
    other = lax.ppermute(own, ("ylo", "yhi"), [(0, 3), (1, 2), (2, 1), (3, 0)])
    first = lax.axis_index("yhi") == 0
    return jnp.concatenate([jnp.where(first, own, other), jnp.where(first, other, own)])


def whole_weight(lanes):
    held = ring(lanes)
    mine = jnp.concatenate([piece for distance in ORDER for piece in held[distance]])
    other = lax.ppermute(mine, "core", SWAP)
    shape = (ZN * 2, lanes.shape[0] // 2, lanes.shape[1])
    return jnp.stack([mine.reshape(shape), other.reshape(shape)], axis=1).reshape(-1, lanes.shape[1])


def per_device(features, tile_tgt, tile_src, tile_count, tile_vals, weight, cotangent):
    block_size = tile_vals.shape[-1]
    tgt_rows = cotangent.shape[0]
    targets, sources, counts, values = tile_tgt[0, 0], tile_src[0, 0], tile_count[0, 0], tile_vals[0, 0]
    core = lax.axis_index("core").astype(jnp.int32)[None]

    wanted = exchange(jnp.repeat(sources, LANES, axis=0)[:, None, :], PLANE)[:, 0]
    wanted, lanes = lax.optimization_barrier((wanted, weight_lanes(weight)))
    held = ring(features[0])
    early = []
    for distances, flops in zip(PARTS, PICK_FLOPS):
        part = exchange(pick(wanted, [held[d] for d in distances], block_size, flops), PLANE)
        if distances != PARTS[-1]:
            early.append(aggregate(core, targets, counts, values, part, tgt_rows))
    weight_in = whole_weight(lanes)
    activations, kept, gone = layer(core, targets, counts, values, part, early, weight_in, cotangent)
    weight_grad = sum_over_devices(kept, gone) / math.sqrt(tgt_rows * 256)
    return (activations, weight_grad)


PICK_FLOPS = (20 * 10**9, 20 * 10**9, 1 * 10**9)


def solution(mesh):
    row = ("z", "yhi", "core")
    fine = Mesh(mesh.devices.reshape(2, 4, 8, 2, 2), ("ylo", "x", "z", "yhi", "core"))
    in_specs = (
        P(REP, row, None),
        P(REP, row, None, None),
        P(REP, row, None, None),
        P(REP, row, None),
        P(REP, row, None, None, None, None),
        P(row, None),
        P(REP + row, None),
    )
    out_specs = (P(REP + row, None), P(row, None))
    return jax.shard_map(per_device, mesh=fine, in_specs=in_specs, out_specs=out_specs, check_vma=False)
```

time: 244 us -> 247 us (1.012)
  waiting for transfers between devices: 111 us -> 98 us
  blocking collectives: 34.1 us -> 24.3 us
  Pallas kernels: 29.4 us -> 38.4 us
  starting transfers between devices: 54.3 us -> 61.1 us
  local copies, waits for them, and re-layouts: 10.2 us -> 15.7 us
  other arithmetic: 3.69 us -> 7.68 us
    all_to_all x3 -> x5, waiting for transfers between devices: 54.9 us -> 37.9 us  [exchange(): return lax.all_to_all(value, axes, split_axis=0, concat_axis=0, tiled=True)]
    all_to_all x3 -> x5, starting transfers between devices: 14 us -> 29 us  [exchange(): return lax.all_to_all(value, axes, split_axis=0, concat_axis=0, tiled=True)]
    all_to_all x3 -> x2, blocking collectives: 34.1 us -> 24.3 us  [exchange(): return lax.all_to_all(value, axes, split_axis=0, concat_axis=0, tiled=True)]
    pallas_call x5 -> x6, Pallas kernels: 29.2 us -> 38.2 us  [the longest x3 13.4 us: pick(): pl.pallas_call(functools.partial(pick_kernel, block, layout), out_shape=j...]
    ppermute x22 -> x16, starting transfers between devices: 36.9 us -> 28.9 us  [shift_z(): return lax.ppermute(value, 'z', [(i, (i + step) % ZN) for i in range(ZN)])]
    unnamed x39 -> x37, local copies, waits for them, and re-layouts: 8 us -> 13.5 us
    ppermute x22 -> x16, waiting for transfers between devices: 52.7 us -> 57.2 us  [shift_z(): return lax.ppermute(value, 'z', [(i, (i + step) % ZN) for i in range(ZN)])]
    another operation x3 -> x1, other arithmetic: 0.06 us -> 3.21 us  [whole_weight(): jnp.stack([mine.reshape(shape), other.reshape(shape)], axis=1)]
  transfers between devices with their start and end apart: 28 -> 24, of which waited for: 14 -> 13; matrix products, arithmetic and copies ran while one was open for 3% -> 5% of each run, Pallas kernels for 7% -> 10%
where the time goes in v5:
time: 247 us; the launch traced here: 246 us
  waiting for transfers between devices  98 us (40%)
  starting transfers between devices  61.1 us (25%)
  Pallas kernels  38.4 us (16%)
  blocking collectives  24.3 us (10%)
  local copies, waits for them, and re-layouts  15.7 us (6%)
  other arithmetic  7.68 us (3%)
    ppermute x16, waiting for transfers between devices, shift_z(): return lax.ppermute(value, 'z', [(i, (i + step) % ZN) for i in range(ZN)])  57.2 us
    all_to_all x5, waiting for transfers between devices, exchange(): return lax.all_to_all(value, axes, split_axis=0, concat_axis=0, tiled=True)  37.9 us
    all_to_all x5, starting transfers between devices, exchange(): return lax.all_to_all(value, axes, split_axis=0, concat_axis=0, tiled=True)  29 us
    ppermute x16, starting transfers between devices, shift_z(): return lax.ppermute(value, 'z', [(i, (i + step) % ZN) for i in range(ZN)])  28.9 us
    all_to_all x2, blocking collectives, exchange(): return lax.all_to_all(value, axes, split_axis=0, concat_axis=0, tiled=True)  24.3 us
    unnamed x37, local copies, waits for them, and re-layouts  13.5 us
    pallas_call x3, Pallas kernels, pick(): pl.pallas_call(functools.partial(pick_kernel, block, layout), out_shape=j...  13.4 us
    pallas_call x1, Pallas kernels, layer(): pl.pallas_call(functools.partial(layer_kernel, len(early) // 2), out_shap...  13.4 us
  transfers between devices with their start and end apart: 24, of which 13 were waited for; matrix products, arithmetic and copies ran while one was open for 5% of the time, Pallas kernels for 10%

profile of v5, /device:TPU:2, one launch (start us, length us, event | category | flops | bytes accessed | tf_op | source)
XLA Modules:
  0.0 246.0 jit_solution(15954961126545775479)
XLA Ops:
  0.6 2.0 collective-permute-start.1
  2.6 4.0 %collective-permute-start.2 = (bf16[32,16384]{1,0:T(8,128)(2,1)}, bf16[32,16384]{1,0:T(8,128)(2,1)}, u32[]{:S(2)}, u32[]{:S(2)}) collective-permute-start(bf16[32,16384]{1,0:T(8,128)(2,1)} %bitcast.34), channel_id=1, source_target_pairs={{0,28},{4,0},{8,4},{12,8},{16,12},{20,16},{24,20},{28,24},{1,29},{... | collective-permute-start | bytes 3145736 | tf_op jit(solution)/shard_map/ppermute | solution.py:34
  6.7 3.0 %collective-permute-start = (bf16[32,1024]{1,0:T(8,128)(2,1)}, bf16[32,1024]{1,0:T(8,128)(2,1)S(1)}, u32[]{:S(2)}, u32[]{:S(2)}) collective-permute-start(bf16[32,1024]{1,0:T(8,128)(2,1)} %param.12), channel_id=1, source_target_pairs={{0,130},{2,128},{128,2},{130,0},{1,131},{3,129},{129,3},{131,1},{4... | collective-permute-start | bytes 196616 | tf_op jit(solution)/shard_map/ppermute | solution.py:276
  9.7 0.8 copy.47
  11.0 5.1 %all-to-all-start = ((s32[32,1,4]{2,1,0:T(1,128)}), s32[32,1,4]{2,1,0:T(1,128)S(1)}, u32[]{:S(2)}, u32[]{:S(2)}) async-start(s32[32,1,4]{2,1,0:T(1,128)} %bitcast.5), calls=%async_computation | async-start | bytes 32768 | tf_op jit(solution)/shard_map/all_to_all | solution.py:38
  16.1 6.0 %all-to-all-done = s32[32,1,4]{2,1,0:T(1,128)S(1)} async-done(((s32[32,1,4]{2,1,0:T(1,128)}), s32[32,1,4]{2,1,0:T(1,128)S(1)}, u32[]{:S(2)}, u32[]{:S(2)}) %all-to-all-start) | async-done | bytes 544 | tf_op jit(solution)/shard_map/all_to_all | solution.py:38
  22.2 0.9 broadcast_select_fusion.1
  23.8 6.2 %collective-permute-done.1.refs_1_ = bf16[32,16384]{1,0:T(8,128)(2,1)} collective-permute-done((bf16[32,16384]{1,0:T(8,128)(2,1)}, bf16[32,16384]{1,0:T(8,128)(2,1)}, u32[]{:S(2)}, u32[]{:S(2)}) %collective-permute-start.1) | collective-permute-done | bytes 1048608 | tf_op jit(solution)/shard_map/ppermute | solution.py:34
  30.0 3.2 %collective-permute-start.4 = (bf16[32,16384]{1,0:T(8,128)(2,1)}, bf16[32,16384]{1,0:T(8,128)(2,1)}, u32[]{:S(2)}, u32[]{:S(2)}) collective-permute-start(bf16[32,16384]{1,0:T(8,128)(2,1)} %collective-permute-done.2.refs_2_), channel_id=1, source_target_pairs={{0,28},{4,0},{8,4},{12,8},{16,12},{20,16},{24,20},{28,24},{1,29},{... | collective-permute-start | bytes 3145736 | tf_op jit(solution)/shard_map/ppermute | solution.py:34
  33.3 4.8 %shard_map.86 = bf16[32,4,3,32,128]{4,3,2,1,0:T(8,128)(2,1)} custom-call(s32[32,4]{1,0:T(8,128)} %copy.37.wanted_ref, bf16[32,16384]{1,0:T(8,128)(2,1)} %bitcast.35, bf16[32,16384]{1,0:T(8,128)(2,1)} %collective-permute-done.1.refs_1_, bf16[32,16384]{1,0:T(8,128)(2,1)} %collective-permute-done.2.refs_2_), custom_call_target="tpu_custom_call" | custom-call | flops 20000000000 | bytes 6291456 | tf_op jit(solution)/shard_map/pallas_call | solution.py:81
  38.1 7.6 %all-to-all-start.1 = ((bf16[32,4,3,32,128]{4,3,2,1,0:T(8,128)(2,1)}), bf16[32,4,3,32,128]{4,3,2,1,0:T(8,128)(2,1)S(1)}, u32[]{:S(2)}, u32[]{:S(2)}) async-start(bf16[32,4,3,32,128]{4,3,2,1,0:T(8,128)(2,1)} %shard_map.86), calls=%async_computation.1 | async-start | bytes 6291456 | tf_op jit(solution)/shard_map/all_to_all | solution.py:38
  45.7 10.2 %collective-permute-done.3.refs_0_ = bf16[32,16384]{1,0:T(8,128)(2,1)} collective-permute-done((bf16[32,16384]{1,0:T(8,128)(2,1)}, bf16[32,16384]{1,0:T(8,128)(2,1)}, u32[]{:S(2)}, u32[]{:S(2)}) %collective-permute-start.3) | collective-permute-done | bytes 1048608 | tf_op jit(solution)/shard_map/ppermute | solution.py:34
  55.9 3.2 %collective-permute-start.6 = (bf16[32,16384]{1,0:T(8,128)(2,1)}, bf16[32,16384]{1,0:T(8,128)(2,1)S(1)}, u32[]{:S(2)}, u32[]{:S(2)}) collective-permute-start(bf16[32,16384]{1,0:T(8,128)(2,1)} %collective-permute-done.4.refs_1_), channel_id=1, source_target_pairs={{0,28},{4,0},{8,4},{12,8},{16,12},{20,16},{24,20},{28,24},{1,29},{... | collective-permute-start | bytes 3145736 | tf_op jit(solution)/shard_map/ppermute | solution.py:34
  59.2 21.6 %collective-permute-done.5.refs_2_ = bf16[32,16384]{1,0:T(8,128)(2,1)S(1)} collective-permute-done((bf16[32,16384]{1,0:T(8,128)(2,1)}, bf16[32,16384]{1,0:T(8,128)(2,1)S(1)}, u32[]{:S(2)}, u32[]{:S(2)}) %collective-permute-start.5) | collective-permute-done | bytes 1048608 | tf_op jit(solution)/shard_map/ppermute | solution.py:34
  80.8 1.0 copy-done.7
  81.7 1.0 copy-done.9
  82.7 5.4 %shard_map.88 = bf16[32,4,4,32,128]{4,3,2,1,0:T(8,128)(2,1)} custom-call(s32[32,4]{1,0:T(8,128)} %copy.37.wanted_ref, bf16[32,16384]{1,0:T(8,128)(2,1)} %collective-permute-done.3.refs_0_, bf16[32,16384]{1,0:T(8,128)(2,1)} %collective-permute-done.4.refs_1_, bf16[32,16384]{1,0:T(8,128)(2,1)} %copy-done.7, bf16[32,16384]{1,0:T(8,128)(2,1)} %copy-done.9), custom_call_target="tpu_custom_call" | custom-call | flops 20000000000 | bytes 8388608 | tf_op jit(solution)/shard_map/pallas_call | solution.py:81
  88.1 1.3 all-to-all-done.1.part
  89.4 6.4 %all-to-all-start.2 = ((bf16[32,4,4,32,128]{4,3,2,1,0:T(8,128)(2,1)}), bf16[32,4,4,32,128]{4,3,2,1,0:T(8,128)(2,1)}, u32[]{:S(2)}, u32[]{:S(2)}) async-start(bf16[32,4,4,32,128]{4,3,2,1,0:T(8,128)(2,1)} %shard_map.88), calls=%async_computation.2 | async-start | bytes 8388608 | tf_op jit(solution)/shard_map/all_to_all | solution.py:38
  95.9 3.2 %collective-permute-start.10 = (bf16[64,1024]{1,0:T(8,128)(2,1)S(1)}, bf16[64,1024]{1,0:T(8,128)(2,1)S(1)}, u32[]{:S(2)}, u32[]{:S(2)}) collective-permute-start(bf16[64,1024]{1,0:T(8,128)(2,1)S(1)} %pad_maximum_fusion.1), channel_id=1, source_target_pairs={{0,28},{4,0},{8,4},{12,8},{16,12},{20,16},{24,20},{28,24},{1,29},{... | collective-permute-start | bytes 393224 | tf_op jit(solution)/shard_map/ppermute | solution.py:34
  99.8 2.9 %collective-permute-done.9 = bf16[64,1024]{1,0:T(8,128)(2,1)S(1)} collective-permute-done((bf16[64,1024]{1,0:T(8,128)(2,1)S(1)}, bf16[64,1024]{1,0:T(8,128)(2,1)S(1)}, u32[]{:S(2)}, u32[]{:S(2)}) %collective-permute-start.9) | collective-permute-done | bytes 131104 | tf_op jit(solution)/shard_map/ppermute | solution.py:34
  102.7 3.2 %collective-permute-start.12 = (bf16[64,1024]{1,0:T(8,128)(2,1)S(1)}, bf16[64,1024]{1,0:T(8,128)(2,1)S(1)}, u32[]{:S(2)}, u32[]{:S(2)}) collective-permute-start(bf16[64,1024]{1,0:T(8,128)(2,1)S(1)} %collective-permute-done.10), channel_id=1, source_target_pairs={{0,28},{4,0},{8,4},{12,8},{16,12},{20,16},{24,20},{28,24},{1,29},{... | collective-permute-start | bytes 393224 | tf_op jit(solution)/shard_map/ppermute | solution.py:34
  107.2 1.6 collective-permute-done.11
  108.8 3.2 %collective-permute-start.14 = (bf16[64,1024]{1,0:T(8,128)(2,1)S(1)}, bf16[64,1024]{1,0:T(8,128)(2,1)S(1)}, u32[]{:S(2)}, u32[]{:S(2)}) collective-permute-start(bf16[64,1024]{1,0:T(8,128)(2,1)S(1)} %collective-permute-done.12), channel_id=1, source_target_pairs={{0,28},{4,0},{8,4},{12,8},{16,12},{20,16},{24,20},{28,24},{1,29},{... | collective-permute-start | bytes 393224 | tf_op jit(solution)/shard_map/ppermute | solution.py:34
  113.4 1.6 collective-permute-done.13
  115.0 3.3 %collective-permute-start.16 = (bf16[32,1024]{1,0:T(8,128)(2,1)S(1)}, bf16[32,1024]{1,0:T(8,128)(2,1)S(1)}, u32[]{:S(2)}, u32[]{:S(2)}) collective-permute-start(bf16[32,1024]{1,0:T(8,128)(2,1)S(1)} %slice.19), channel_id=1, source_target_pairs={{0,28},{4,0},{8,4},{12,8},{16,12},{20,16},{24,20},{28,24},{1,29},{... | collective-permute-start | bytes 196616 | tf_op jit(solution)/shard_map/ppermute | solution.py:34
  119.7 0.8 collective-permute-done.15
  121.9 3.3 %collective-permute-start.8 = (bf16[16,16384]{1,0:T(8,128)(2,1)S(1)}, bf16[16,16384]{1,0:T(8,128)(2,1)S(1)}, u32[]{:S(2)}, u32[]{:S(2)}) collective-permute-start(bf16[16,16384]{1,0:T(8,128)(2,1)S(1)} %slice.17), channel_id=1, source_target_pairs={{0,28},{4,0},{8,4},{12,8},{16,12},{20,16},{24,20},{28,24},{1,29},{... | collective-permute-start | bytes 1572872 | tf_op jit(solution)/shard_map/ppermute | solution.py:34
  125.2 12.2 %collective-permute-done.7.refs_0_ = bf16[16,16384]{1,0:T(8,128)(2,1)S(1)} collective-permute-done((bf16[16,16384]{1,0:T(8,128)(2,1)S(1)}, bf16[16,16384]{1,0:T(8,128)(2,1)S(1)}, u32[]{:S(2)}, u32[]{:S(2)}) %collective-permute-start.7) | collective-permute-done | bytes 524320 | tf_op jit(solution)/shard_map/ppermute | solution.py:34
  137.4 0.8 copy-done.12
  138.2 0.8 copy-done.13
  139.0 3.3 %shard_map.90 = bf16[32,4,1,32,128]{4,3,2,1,0:T(8,128)(2,1)} custom-call(s32[32,4]{1,0:T(8,128)} %copy.37.wanted_ref, bf16[16,16384]{1,0:T(8,128)(2,1)} %copy-done.12, bf16[16,16384]{1,0:T(8,128)(2,1)} %copy-done.13), custom_call_target="tpu_custom_call" | custom-call | flops 1000000000 | bytes 2097152 | tf_op jit(solution)/shard_map/pallas_call | solution.py:81
  142.3 12.6 %all-to-all-done.2.part = bf16[32,4,4,32,128]{4,3,2,1,0:T(8,128)(2,1)} async-done(((bf16[32,4,4,32,128]{4,3,2,1,0:T(8,128)(2,1)}), bf16[32,4,4,32,128]{4,3,2,1,0:T(8,128)(2,1)}, u32[]{:S(2)}, u32[]{:S(2)}) %all-to-all-start.2) | async-done | bytes 4194336 | tf_op jit(solution)/shard_map/all_to_all | solution.py:38
  154.9 4.5 %all-to-all-start.3 = ((bf16[32,4,1,32,128]{4,3,2,1,0:T(8,128)(2,1)}), bf16[32,4,1,32,128]{4,3,2,1,0:T(8,128)(2,1)}, u32[]{:S(2)}, u32[]{:S(2)}) async-start(bf16[32,4,1,32,128]{4,3,2,1,0:T(8,128)(2,1)} %shard_map.90), calls=%async_computation.3 | async-start | bytes 2097152 | tf_op jit(solution)/shard_map/all_to_all | solution.py:38
  159.5 3.2 %pad_maximum_fusion = bf16[16,2,32,1024]{3,2,1,0:T(8,128)(2,1)} fusion(bf16[16,1,32,1024]{3,2,1,0:T(8,128)(2,1)} %bitcast.11, bf16[16,1,32,1024]{3,2,1,0:T(8,128)(2,1)} %bitcast.9), kind=kLoop, calls=%fused_computation | loop fusion | flops 1048576 | bytes 4194304 | tf_op jit(solution)/shard_map/stack | solution.py:286
  162.7 4.6 %shard_map.87 = (bf16[384,1024]{1,0:T(8,128)(2,1)S(1)}, bf16[1024,384]{1,0:T(8,128)(2,1)S(1)}) custom-call(s32[1]{0:T(128)} %bitcast.core_ref, s32[8,4]{1,0:T(8,128)S(1)} %copy.44.tgt_ref, s32[8]{0:T(128)S(1)} %bitcast.27, bf16[8,4,128,128]{3,2,1,0:T(8,128)(2,1)S(1)} %bitcast.24, bf16[32,4,3,32,128]{4,3,2,1,0:T(8,128)(2,1)S(1)} %all-to-all-done.1.part), custom_call_target="tpu_custom_call" | custom-call | flops 3000000000 | bytes 8388608 | tf_op jit(solution)/shard_map/pallas_call | solution.py:130
  167.4 1.0 copy-done.5
  168.4 1.0 copy-done.6
  169.3 6.8 %shard_map.89 = (bf16[512,1024]{1,0:T(8,128)(2,1)S(1)}, bf16[1024,512]{1,0:T(8,128)(2,1)S(1)}) custom-call(s32[1]{0:T(128)} %bitcast.core_ref, s32[8,4]{1,0:T(8,128)S(1)} %copy.44.tgt_ref, s32[8]{0:T(128)S(1)} %bitcast.28, bf16[8,4,128,128]{3,2,1,0:T(8,128)(2,1)S(1)} %bitcast.25, bf16[32,4,4,32,128]{4,3,2,1,0:T(8,128)(2,1)} %all-to-all-done.2.part), custom_call_target="tpu_custom_call" | custom-call | flops 3000000000 | bytes 8388608 | tf_op jit(solution)/shard_map/pallas_call | solution.py:130
  176.1 1.0 copy-done.3
  177.1 1.0 copy-done.4
  178.1 13.4 %shard_map.91 = (bf16[1024,1024]{1,0:T(8,128)(2,1)}, f32[8,2,8,32,128]{4,3,2,1,0:T(8,128)}, bf16[8,2,8,32,128]{4,3,2,1,0:T(8,128)(2,1)}) custom-call(s32[1]{0:T(128)} %bitcast.core_ref, s32[8,4]{1,0:T(8,128)} %copy-done, s32[8]{0:T(128)} %bitcast.26, bf16[384,1024]{1,0:T(8,128)(2,1)} %copy-done.5, bf16[1024,384]{1,0:T(8,128)(2,1)} %copy-done.6, ...), custom_call_target="tpu_custom_call" | custom-call | flops 6000000000 | bytes 20971520 | tf_op jit(solution)/shard_map/pallas_call | solution.py:218
  191.6 2.9 %collective-permute-done.18 = bf16[8,2,8,32,128]{4,3,2,1,0:T(8,128)(2,1)S(1)} collective-permute-done((bf16[8,2,8,32,128]{4,3,2,1,0:T(8,128)(2,1)}, bf16[8,2,8,32,128]{4,3,2,1,0:T(8,128)(2,1)S(1)}, u32[]{:S(2)}, u32[]{:S(2)}) %collective-permute-start.18) | collective-permute-done | bytes 1048608 | tf_op jit(solution)/shard_map/ppermute | solution.py:266
  194.4 2.9 %add_convert_fusion = bf16[8,2,8,32,128]{4,3,2,1,0:T(8,128)(2,1)} fusion(f32[8,2,8,32,128]{4,3,2,1,0:T(8,128)} %get-tuple-element.18, bf16[8,2,8,32,128]{4,3,2,1,0:T(8,128)(2,1)S(1)} %collective-permute-done.18), kind=kLoop, calls=%fused_computation.1 | loop fusion | flops 1572864 | bytes 4194304 | tf_op jit(solution)/shard_map/convert_element_type | solution.py:267
  197.3 5.5 %all-to-all-start.4 = ((bf16[16,8,32,128]{3,2,1,0:T(8,128)(2,1)}), bf16[16,8,32,128]{3,2,1,0:T(8,128)(2,1)S(1)}, u32[]{:S(2)}, u32[]{:S(2)}) async-start(bf16[16,8,32,128]{3,2,1,0:T(8,128)(2,1)} %bitcast.14), calls=%async_computation.4 | async-start | bytes 2097152 | tf_op jit(solution)/shard_map/all_to_all | solution.py:38
  202.8 18.0 %all-to-all-done.4.came_ref = bf16[16,8,32,128]{3,2,1,0:T(8,128)(2,1)S(1)} async-done(((bf16[16,8,32,128]{3,2,1,0:T(8,128)(2,1)}), bf16[16,8,32,128]{3,2,1,0:T(8,128)(2,1)S(1)}, u32[]{:S(2)}, u32[]{:S(2)}) %all-to-all-start.4) | async-done | bytes 1048608 | tf_op jit(solution)/shard_map/all_to_all | solution.py:38
  221.0 14.2 %all_to_all.35 = f32[8,32,128]{2,1,0:T(8,128)S(1)} all-to-all(f32[8,32,128]{2,1,0:T(8,128)S(1)} %shard_map.92), channel_id=1, replica_groups=mesh['ylo'=2,'x'=4,'z'=8,'yhi'=2,'core'=2] {'z'}, dimensions={0} | all-to-all | bytes 262144 | tf_op jit(solution)/shard_map/all_to_all | solution.py:38
  235.2 10.1 %all_to_all.36 = f32[8,32,128]{2,1,0:T(8,128)S(1)} all-to-all(f32[8,32,128]{2,1,0:T(8,128)S(1)} %broadcast_in_dim.18), channel_id=1, replica_groups=mesh['ylo'=2,'x'=4,'z'=8,'yhi'=2,'core'=2] {'ylo','x'}, dimensions={0} | all-to-all | bytes 262144 | tf_op jit(solution)/shard_map/all_to_all | solution.py:38
  (62 shorter events, 8.6 us)
Async XLA Ops:
  0.6 29.4 %collective-permute-start.1 = (bf16[32,16384]{1,0:T(8,128)(2,1)}, bf16[32,16384]{1,0:T(8,128)(2,1)}, u32[]{:S(2)}, u32[]{:S(2)}) collective-permute-start(bf16[32,16384]{1,0:T(8,128)(2,1)} %bitcast.33), channel_id=1, source_target_pairs={{0,4},{4,8},{8,12},{12,16},{16,20},{20,24},{24,28},{28,0},{1,5},{5... | collective-permute-start | bytes 3145736 | tf_op jit(solution)/shard_map/ppermute | solution.py:34
  2.6 27.4 %collective-permute-start.2 = (bf16[32,16384]{1,0:T(8,128)(2,1)}, bf16[32,16384]{1,0:T(8,128)(2,1)}, u32[]{:S(2)}, u32[]{:S(2)}) collective-permute-start(bf16[32,16384]{1,0:T(8,128)(2,1)} %bitcast.34), channel_id=1, source_target_pairs={{0,28},{4,0},{8,4},{12,8},{16,12},{20,16},{24,20},{28,24},{1,29},{... | collective-permute-start | bytes 3145736 | tf_op jit(solution)/shard_map/ppermute | solution.py:34
  6.7 15.6 %collective-permute-start = (bf16[32,1024]{1,0:T(8,128)(2,1)}, bf16[32,1024]{1,0:T(8,128)(2,1)S(1)}, u32[]{:S(2)}, u32[]{:S(2)}) collective-permute-start(bf16[32,1024]{1,0:T(8,128)(2,1)} %param.12), channel_id=1, source_target_pairs={{0,130},{2,128},{128,2},{130,0},{1,131},{3,129},{129,3},{131,1},{4... | collective-permute-start | bytes 196616 | tf_op jit(solution)/shard_map/ppermute | solution.py:276
  11.0 11.1 %all-to-all-start = ((s32[32,1,4]{2,1,0:T(1,128)}), s32[32,1,4]{2,1,0:T(1,128)S(1)}, u32[]{:S(2)}, u32[]{:S(2)}) async-start(s32[32,1,4]{2,1,0:T(1,128)} %bitcast.5), calls=%async_computation | async-start | bytes 32768 | tf_op jit(solution)/shard_map/all_to_all | solution.py:38
  30.0 25.9 %collective-permute-start.3 = (bf16[32,16384]{1,0:T(8,128)(2,1)}, bf16[32,16384]{1,0:T(8,128)(2,1)}, u32[]{:S(2)}, u32[]{:S(2)}) collective-permute-start(bf16[32,16384]{1,0:T(8,128)(2,1)} %collective-permute-done.1.refs_1_), channel_id=1, source_target_pairs={{0,4},{4,8},{8,12},{12,16},{16,20},{20,24},{24,28},{28,0},{1,5},{5... | collective-permute-start | bytes 3145736 | tf_op jit(solution)/shard_map/ppermute | solution.py:34
  30.0 25.9 %collective-permute-start.4 = (bf16[32,16384]{1,0:T(8,128)(2,1)}, bf16[32,16384]{1,0:T(8,128)(2,1)}, u32[]{:S(2)}, u32[]{:S(2)}) collective-permute-start(bf16[32,16384]{1,0:T(8,128)(2,1)} %collective-permute-done.2.refs_2_), channel_id=1, source_target_pairs={{0,28},{4,0},{8,4},{12,8},{16,12},{20,16},{24,20},{28,24},{1,29},{... | collective-permute-start | bytes 3145736 | tf_op jit(solution)/shard_map/ppermute | solution.py:34
  38.1 51.3 %all-to-all-start.1 = ((bf16[32,4,3,32,128]{4,3,2,1,0:T(8,128)(2,1)}), bf16[32,4,3,32,128]{4,3,2,1,0:T(8,128)(2,1)S(1)}, u32[]{:S(2)}, u32[]{:S(2)}) async-start(bf16[32,4,3,32,128]{4,3,2,1,0:T(8,128)(2,1)} %shard_map.86), calls=%async_computation.1 | async-start | bytes 6291456 | tf_op jit(solution)/shard_map/all_to_all | solution.py:38
  55.9 24.8 %collective-permute-start.5 = (bf16[32,16384]{1,0:T(8,128)(2,1)}, bf16[32,16384]{1,0:T(8,128)(2,1)S(1)}, u32[]{:S(2)}, u32[]{:S(2)}) collective-permute-start(bf16[32,16384]{1,0:T(8,128)(2,1)} %collective-permute-done.3.refs_0_), channel_id=1, source_target_pairs={{0,4},{4,8},{8,12},{12,16},{16,20},{20,24},{24,28},{28,0},{1,5},{5... | collective-permute-start | bytes 3145736 | tf_op jit(solution)/shard_map/ppermute | solution.py:34
  55.9 24.8 %collective-permute-start.6 = (bf16[32,16384]{1,0:T(8,128)(2,1)}, bf16[32,16384]{1,0:T(8,128)(2,1)S(1)}, u32[]{:S(2)}, u32[]{:S(2)}) collective-permute-start(bf16[32,16384]{1,0:T(8,128)(2,1)} %collective-permute-done.4.refs_1_), channel_id=1, source_target_pairs={{0,28},{4,0},{8,4},{12,8},{16,12},{20,16},{24,20},{28,24},{1,29},{... | collective-permute-start | bytes 3145736 | tf_op jit(solution)/shard_map/ppermute | solution.py:34
  80.8 1.0 copy-start.7
  81.7 1.0 copy-start.9
  89.4 65.5 %all-to-all-start.2 = ((bf16[32,4,4,32,128]{4,3,2,1,0:T(8,128)(2,1)}), bf16[32,4,4,32,128]{4,3,2,1,0:T(8,128)(2,1)}, u32[]{:S(2)}, u32[]{:S(2)}) async-start(bf16[32,4,4,32,128]{4,3,2,1,0:T(8,128)(2,1)} %shard_map.88), calls=%async_computation.2 | async-start | bytes 8388608 | tf_op jit(solution)/shard_map/all_to_all | solution.py:38
  95.8 26.0 %copy-start.8 = (bf16[32,16384]{1,0:T(8,128)(2,1)S(1)}, bf16[32,16384]{1,0:T(8,128)(2,1)}, u32[]{:S(2)}) copy-start(bf16[32,16384]{1,0:T(8,128)(2,1)} %copy-done.7) | copy-start | bytes 3145732
  95.8 26.1 %copy-start.10 = (bf16[32,16384]{1,0:T(8,128)(2,1)S(1)}, bf16[32,16384]{1,0:T(8,128)(2,1)}, u32[]{:S(2)}) copy-start(bf16[32,16384]{1,0:T(8,128)(2,1)} %copy-done.9) | copy-start | bytes 3145732
  95.8 6.8 %collective-permute-start.9 = (bf16[64,1024]{1,0:T(8,128)(2,1)S(1)}, bf16[64,1024]{1,0:T(8,128)(2,1)S(1)}, u32[]{:S(2)}, u32[]{:S(2)}) collective-permute-start(bf16[64,1024]{1,0:T(8,128)(2,1)S(1)} %pad_maximum_fusion.1), channel_id=1, source_target_pairs={{0,4},{4,8},{8,12},{12,16},{16,20},{20,24},{24,28},{28,0},{1,5},{5... | collective-permute-start | bytes 393224 | tf_op jit(solution)/shard_map/ppermute | solution.py:34
  95.9 6.8 %collective-permute-start.10 = (bf16[64,1024]{1,0:T(8,128)(2,1)S(1)}, bf16[64,1024]{1,0:T(8,128)(2,1)S(1)}, u32[]{:S(2)}, u32[]{:S(2)}) collective-permute-start(bf16[64,1024]{1,0:T(8,128)(2,1)S(1)} %pad_maximum_fusion.1), channel_id=1, source_target_pairs={{0,28},{4,0},{8,4},{12,8},{16,12},{20,16},{24,20},{28,24},{1,29},{... | collective-permute-start | bytes 393224 | tf_op jit(solution)/shard_map/ppermute | solution.py:34
  102.6 6.2 %collective-permute-start.11 = (bf16[64,1024]{1,0:T(8,128)(2,1)S(1)}, bf16[64,1024]{1,0:T(8,128)(2,1)S(1)}, u32[]{:S(2)}, u32[]{:S(2)}) collective-permute-start(bf16[64,1024]{1,0:T(8,128)(2,1)S(1)} %collective-permute-done.9), channel_id=1, source_target_pairs={{0,4},{4,8},{8,12},{12,16},{16,20},{20,24},{24,28},{28,0},{1,5},{5... | collective-permute-start | bytes 393224 | tf_op jit(solution)/shard_map/ppermute | solution.py:34
  102.7 6.2 %collective-permute-start.12 = (bf16[64,1024]{1,0:T(8,128)(2,1)S(1)}, bf16[64,1024]{1,0:T(8,128)(2,1)S(1)}, u32[]{:S(2)}, u32[]{:S(2)}) collective-permute-start(bf16[64,1024]{1,0:T(8,128)(2,1)S(1)} %collective-permute-done.10), channel_id=1, source_target_pairs={{0,28},{4,0},{8,4},{12,8},{16,12},{20,16},{24,20},{28,24},{1,29},{... | collective-permute-start | bytes 393224 | tf_op jit(solution)/shard_map/ppermute | solution.py:34
  108.8 6.2 %collective-permute-start.13 = (bf16[64,1024]{1,0:T(8,128)(2,1)S(1)}, bf16[64,1024]{1,0:T(8,128)(2,1)S(1)}, u32[]{:S(2)}, u32[]{:S(2)}) collective-permute-start(bf16[64,1024]{1,0:T(8,128)(2,1)S(1)} %collective-permute-done.11), channel_id=1, source_target_pairs={{0,4},{4,8},{8,12},{12,16},{16,20},{20,24},{24,28},{28,0},{1,5},{5... | collective-permute-start | bytes 393224 | tf_op jit(solution)/shard_map/ppermute | solution.py:34
  108.8 6.2 %collective-permute-start.14 = (bf16[64,1024]{1,0:T(8,128)(2,1)S(1)}, bf16[64,1024]{1,0:T(8,128)(2,1)S(1)}, u32[]{:S(2)}, u32[]{:S(2)}) collective-permute-start(bf16[64,1024]{1,0:T(8,128)(2,1)S(1)} %collective-permute-done.12), channel_id=1, source_target_pairs={{0,28},{4,0},{8,4},{12,8},{16,12},{20,16},{24,20},{28,24},{1,29},{... | collective-permute-start | bytes 393224 | tf_op jit(solution)/shard_map/ppermute | solution.py:34
  115.0 5.5 %collective-permute-start.15 = (bf16[32,1024]{1,0:T(8,128)(2,1)S(1)}, bf16[32,1024]{1,0:T(8,128)(2,1)S(1)}, u32[]{:S(2)}, u32[]{:S(2)}) collective-permute-start(bf16[32,1024]{1,0:T(8,128)(2,1)S(1)} %slice.18), channel_id=1, source_target_pairs={{0,4},{4,8},{8,12},{12,16},{16,20},{20,24},{24,28},{28,0},{1,5},{5... | collective-permute-start | bytes 196616 | tf_op jit(solution)/shard_map/ppermute | solution.py:34
  115.0 6.1 %collective-permute-start.16 = (bf16[32,1024]{1,0:T(8,128)(2,1)S(1)}, bf16[32,1024]{1,0:T(8,128)(2,1)S(1)}, u32[]{:S(2)}, u32[]{:S(2)}) collective-permute-start(bf16[32,1024]{1,0:T(8,128)(2,1)S(1)} %slice.19), channel_id=1, source_target_pairs={{0,28},{4,0},{8,4},{12,8},{16,12},{20,16},{24,20},{28,24},{1,29},{... | collective-permute-start | bytes 196616 | tf_op jit(solution)/shard_map/ppermute | solution.py:34
  121.7 37.7 %collective-permute-start.17 = (bf16[512,1024]{1,0:T(8,128)(2,1)}, bf16[512,1024]{1,0:T(8,128)(2,1)}, u32[]{:S(2)}, u32[]{:S(2)}) collective-permute-start(bf16[512,1024]{1,0:T(8,128)(2,1)} %constant_dynamic-update-slice_fusion), channel_id=1, source_target_pairs={{0,1},{1,0},{2,3},{3,2},{4,5},{5,4},{6,7},{7,6},{8,9},{9,8},{10,11... | collective-permute-start | bytes 3145736 | tf_op jit(solution)/shard_map/ppermute | solution.py:284
  121.8 15.6 %collective-permute-start.7 = (bf16[16,16384]{1,0:T(8,128)(2,1)S(1)}, bf16[16,16384]{1,0:T(8,128)(2,1)S(1)}, u32[]{:S(2)}, u32[]{:S(2)}) collective-permute-start(bf16[16,16384]{1,0:T(8,128)(2,1)S(1)} %slice.16), channel_id=1, source_target_pairs={{0,4},{4,8},{8,12},{12,16},{16,20},{20,24},{24,28},{28,0},{1,5},{5... | collective-permute-start | bytes 1572872 | tf_op jit(solution)/shard_map/ppermute | solution.py:34
  121.9 37.5 %copy-start.11 = (s32[1,1,8,4]{2,3,1,0:T(4,128)S(1)}, s32[1,1,8,4]{2,3,1,0:T(4,128)}, u32[]{:S(2)}) copy-start(s32[1,1,8,4]{2,3,1,0:T(4,128)} %param.8) | copy-start | bytes 388
  121.9 15.5 %collective-permute-start.8 = (bf16[16,16384]{1,0:T(8,128)(2,1)S(1)}, bf16[16,16384]{1,0:T(8,128)(2,1)S(1)}, u32[]{:S(2)}, u32[]{:S(2)}) collective-permute-start(bf16[16,16384]{1,0:T(8,128)(2,1)S(1)} %slice.17), channel_id=1, source_target_pairs={{0,28},{4,0},{8,4},{12,8},{16,12},{20,16},{24,20},{28,24},{1,29},{... | collective-permute-start | bytes 1572872 | tf_op jit(solution)/shard_map/ppermute | solution.py:34
  137.4 0.8 copy-start.12
  138.2 0.8 copy-start.13
  154.9 23.2 %all-to-all-start.3 = ((bf16[32,4,1,32,128]{4,3,2,1,0:T(8,128)(2,1)}), bf16[32,4,1,32,128]{4,3,2,1,0:T(8,128)(2,1)}, u32[]{:S(2)}, u32[]{:S(2)}) async-start(bf16[32,4,1,32,128]{4,3,2,1,0:T(8,128)(2,1)} %shard_map.90), calls=%async_computation.3 | async-start | bytes 2097152 | tf_op jit(solution)/shard_map/all_to_all | solution.py:38
  159.5 7.9 %copy-start = (s32[8,4]{1,0:T(8,128)}, s32[8,4]{1,0:T(8,128)S(1)}, u32[]{:S(2)}) copy-start(s32[8,4]{1,0:T(8,128)S(1)} %copy.44.tgt_ref) | copy-start | bytes 388
  159.5 3.2 %copy-start.1 = (bf16[1,1,8,4,128,128]{5,4,3,2,1,0:T(8,128)(2,1)S(1)}, bf16[1,1,8,4,128,128]{5,4,3,2,1,0:T(8,128)(2,1)}, u32[]{:S(2)}) copy-start(bf16[1,1,8,4,128,128]{5,4,3,2,1,0:T(8,128)(2,1)} %param.11) | copy-start | bytes 3145732
  159.5 3.2 %copy-start.2 = (s32[1,1,8]{2,1,0:T(1,128)S(1)}, s32[1,1,8]{2,1,0:T(1,128)}, u32[]{:S(2)}) copy-start(s32[1,1,8]{2,1,0:T(1,128)} %param.10) | copy-start | bytes 100
  167.4 1.0 copy-start.5
  168.4 1.0 copy-start.6
  176.1 1.0 copy-start.3
  177.1 1.0 copy-start.4
  191.5 3.0 %collective-permute-start.18 = (bf16[8,2,8,32,128]{4,3,2,1,0:T(8,128)(2,1)}, bf16[8,2,8,32,128]{4,3,2,1,0:T(8,128)(2,1)S(1)}, u32[]{:S(2)}, u32[]{:S(2)}) collective-permute-start(bf16[8,2,8,32,128]{4,3,2,1,0:T(8,128)(2,1)} %get-tuple-element.19), channel_id=1, source_target_pairs={{0,1},{1,0},{2,3},{3,2},{4,5},{5,4},{6,7},{7,6},{8,9},{9,8},{10,11... | collective-permute-start | bytes 3145736 | tf_op jit(solution)/shard_map/ppermute | solution.py:266
  197.3 23.5 %all-to-all-start.4 = ((bf16[16,8,32,128]{3,2,1,0:T(8,128)(2,1)}), bf16[16,8,32,128]{3,2,1,0:T(8,128)(2,1)S(1)}, u32[]{:S(2)}, u32[]{:S(2)}) async-start(bf16[16,8,32,128]{3,2,1,0:T(8,128)(2,1)} %bitcast.14), calls=%async_computation.4 | async-start | bytes 2097152 | tf_op jit(solution)/shard_map/all_to_all | solution.py:38

commit v6 on v5

--- a/solution.py
+++ b/solution.py
@@ -144,19 +144,27 @@
 def layer_kernel(num_early, core_ref, tgt_ref, count_ref, *refs):
     early, refs = refs[: 2 * num_early], refs[2 * num_early :]
     vals_hbm, part_hbm, weight_hbm, cot_hbm, act_hbm, kept_hbm, gone_hbm = refs[:7]
-    vals, part, weight, cot, act, kept, gone, acc, turned, plain, dpre, part_sem, sems, early_sems, out_sems = refs[7:]
-    part_copy = pltpu.make_async_copy(part_hbm, part, part_sem)
+    vals, part, weight, cot, act, kept, gone, acc, turned, plain, dpre, sems, block_sems, out_sems = refs[7:]
+    blocks = out_sems.shape[1]
+    step = act.shape[0] // blocks
     vals_copy = pltpu.make_async_copy(vals_hbm, vals, sems.at[0])
-    weight_copy = pltpu.make_async_copy(weight_hbm, weight, sems.at[1])
-    cot_copy = pltpu.make_async_copy(cot_hbm, cot, sems.at[2])
-    turned_copies, plain_copies = [], []
-    low = 0
-    for index in range(num_early):
-        at = slice(low, low + early[2 * index].shape[0])
-        low = at.stop
-        turned_copies.append(pltpu.make_async_copy(early[2 * index], turned.at[at], early_sems.at[2 * index]))
-        plain_copies.append(pltpu.make_async_copy(early[2 * index + 1], plain.at[:, at], early_sems.at[2 * index + 1]))
-    for copy in (vals_copy, part_copy, *plain_copies, weight_copy, cot_copy, *turned_copies):
+    part_copy = pltpu.make_async_copy(part_hbm, part, sems.at[1])
+    weight_copy = pltpu.make_async_copy(weight_hbm, weight, sems.at[2])
+    block_copies = [[] for _ in range(blocks)]
+    turned_copies = []
+    for index, copies in enumerate(block_copies):
+        at = slice(index * step, index * step + step)
+        copies.append(pltpu.make_async_copy(cot_hbm.at[at], cot.at[at], block_sems.at[index, 0]))
+        low = 0
+        for number in range(num_early):
+            columns = slice(low, low + early[2 * number].shape[0])
+            low = columns.stop
+            copies.append(
+                pltpu.make_async_copy(early[2 * number + 1].at[at], plain.at[at, columns], block_sems.at[index, 1 + number])
+            )
+            if index == 0:
+                turned_copies.append(pltpu.make_async_copy(early[2 * number], turned.at[columns], sems.at[3 + number]))
+    for copy in (vals_copy, part_copy, weight_copy, *sum(block_copies, []), *turned_copies):
         copy.start()
     vals_copy.wait()
     part_copy.wait()
@@ -167,11 +175,7 @@
         value = acc[:, at]
         turned[low:, at] = value.astype(turned.dtype)
         plain[at, low:] = value.T.astype(plain.dtype)
-    for copy in (*plain_copies, weight_copy, cot_copy):
-        copy.wait()
-
-    blocks = out_sems.shape[1]
-    step = act.shape[0] // blocks
+    weight_copy.wait()
     out_copies = []
 
     def send(source, target, sem):
@@ -180,6 +184,8 @@
 
     for index in range(blocks):
         at = slice(index * step, index * step + step)
+        for copy in block_copies[index]:
+            copy.wait()
         preact = jnp.dot(plain[at], weight[...], preferred_element_type=jnp.float32)
         sigmoid_val = jax.nn.sigmoid(preact)
         act[at] = (preact * sigmoid_val).astype(act.dtype)
@@ -198,10 +204,8 @@
             place, hi, core = lane // LANES, lane % LANES // 2, lane % 2
             for piece in range(pieces):
                 value = grad[at : at + rows, piece * width : (piece + 1) * width]
-                if core == 0:
-                    kept[piece, hi, place] = value
-                else:
-                    gone[piece, hi, place] = value.astype(gone.dtype)
+                target = gone if core else kept
+                target[piece, hi, place] = value.astype(target.dtype)
         done = slice(low // (LANES * rows), (low + step) // (LANES * rows))
         send(gone.at[:, :, done], gone_hbm.at[:, :, done], out_sems.at[1, index])
         send(kept.at[:, :, done], kept_hbm.at[:, :, done], out_sems.at[2, index])
@@ -219,7 +223,7 @@
         functools.partial(layer_kernel, len(early) // 2),
         out_shape=(
             jax.ShapeDtypeStruct((tgt_rows, width), jnp.bfloat16),
-            jax.ShapeDtypeStruct(cut, jnp.float32),
+            jax.ShapeDtypeStruct(cut, jnp.bfloat16),
             jax.ShapeDtypeStruct(cut, jnp.bfloat16),
         ),
         in_specs=[SMEM] * 3 + [HBM] * (len(early) + 4),
@@ -230,15 +234,14 @@
             pltpu.VMEM(weight.shape, weight.dtype),
             pltpu.VMEM((tgt_rows, width), cotangent.dtype),
             pltpu.VMEM((tgt_rows, width), jnp.bfloat16),
-            pltpu.VMEM(cut, jnp.float32),
+            pltpu.VMEM(cut, jnp.bfloat16),
             pltpu.VMEM(cut, jnp.bfloat16),
             pltpu.VMEM((late, tgt_rows), jnp.float32),
             pltpu.VMEM((feats, tgt_rows), jnp.bfloat16),
             pltpu.VMEM((tgt_rows, feats), jnp.bfloat16),
             pltpu.VMEM((tgt_rows, width), jnp.bfloat16),
-            pltpu.SemaphoreType.DMA,
-            pltpu.SemaphoreType.DMA((3,)),
-            pltpu.SemaphoreType.DMA((len(early),)),
+            pltpu.SemaphoreType.DMA((3 + len(early) // 2,)),
+            pltpu.SemaphoreType.DMA((4, 1 + len(early) // 2)),
             pltpu.SemaphoreType.DMA((3, 4)),
         ],
         compiler_params=params(LAYER_MIB),
@@ -264,7 +267,7 @@
 
 def sum_over_devices(kept, gone):
     came = lax.ppermute(gone, "core", SWAP)
-    chip = (kept + came.astype(jnp.float32)).astype(jnp.bfloat16)
+    chip = (kept.astype(jnp.float32) + came.astype(jnp.float32)).astype(jnp.bfloat16)
     chip = chip.reshape(16, *chip.shape[2:])
     plane = sum_plane(exchange(chip, CHIPS_XY))
     column = exchange(plane, "z").sum(0)
@@ -295,12 +298,14 @@
     wanted = exchange(jnp.repeat(sources, LANES, axis=0)[:, None, :], PLANE)[:, 0]
     wanted, lanes = lax.optimization_barrier((wanted, weight_lanes(weight)))
     held = ring(features[0])
+    weight_in = whole_weight(lanes)
     early = []
     for distances, flops in zip(PARTS, PICK_FLOPS):
+        if distances == PARTS[-1]:
+            wanted, weight_in, early[0] = lax.optimization_barrier((wanted, weight_in, early[0]))
         part = exchange(pick(wanted, [held[d] for d in distances], block_size, flops), PLANE)
         if distances != PARTS[-1]:
             early.append(aggregate(core, targets, counts, values, part, tgt_rows))
-    weight_in = whole_weight(lanes)
     activations, kept, gone = layer(core, targets, counts, values, part, early, weight_in, cotangent)
     weight_grad = sum_over_devices(kept, gone) / math.sqrt(tgt_rows * 256)
     return (activations, weight_grad)

time: 247 us -> 242 us (0.980)
  Pallas kernels: 38.4 us -> 35.4 us
    ppermute x16, waiting for transfers between devices: 57.2 us -> 47.4 us  [shift_z(): return lax.ppermute(value, 'z', [(i, (i + step) % ZN) for i in range(ZN)])]
    all_to_all x5, waiting for transfers between devices: 37.9 us -> 46.7 us  [exchange(): return lax.all_to_all(value, axes, split_axis=0, concat_axis=0, tiled=True)]
    unnamed x37 -> x35, local copies, waits for them, and re-layouts: 13.5 us -> 11.7 us
  transfers between devices with their start and end apart: 24 -> 24, of which waited for: 13 -> 15; matrix products, arithmetic and copies ran while one was open for 5% -> 6% of each run, Pallas kernels for 10% -> 9%
where the time goes in v6:
time: 242 us; the launch traced here: 240 us
  waiting for transfers between devices  96.6 us (40%)
  starting transfers between devices  60.6 us (25%)
  Pallas kernels  35.4 us (15%)
  blocking collectives  23.5 us (10%)
  local copies, waits for them, and re-layouts  16.2 us (7%)
  other arithmetic  7.24 us (3%)
    ppermute x16, waiting for transfers between devices, shift_z(): return lax.ppermute(value, 'z', [(i, (i + step) % ZN) for i in range(ZN)])  47.4 us
    all_to_all x5, waiting for transfers between devices, exchange(): return lax.all_to_all(value, axes, split_axis=0, concat_axis=0, tiled=True)  46.7 us
    ppermute x16, starting transfers between devices, shift_z(): return lax.ppermute(value, 'z', [(i, (i + step) % ZN) for i in range(ZN)])  28.8 us
    all_to_all x5, starting transfers between devices, exchange(): return lax.all_to_all(value, axes, split_axis=0, concat_axis=0, tiled=True)  28 us
    all_to_all x2, blocking collectives, exchange(): return lax.all_to_all(value, axes, split_axis=0, concat_axis=0, tiled=True)  23.5 us
    pallas_call x3, Pallas kernels, pick(): pl.pallas_call(functools.partial(pick_kernel, block, layout), out_shape=j...  13.4 us
    pallas_call x1, Pallas kernels, layer(): pl.pallas_call(functools.partial(layer_kernel, len(early) // 2), out_shap...  12.5 us
    unnamed x35, local copies, waits for them, and re-layouts  11.7 us
  transfers between devices with their start and end apart: 24, of which 15 were waited for; matrix products, arithmetic and copies ran while one was open for 6% of the time, Pallas kernels for 9%

profile of v6, /device:TPU:2, one launch (start us, length us, event | category | flops | bytes accessed | tf_op | source)
XLA Modules:
  0.0 240.4 jit_solution(13436488523476243374)
XLA Ops:
  0.6 2.0 collective-permute-start.10
  2.6 4.0 %collective-permute-start.11 = (bf16[32,16384]{1,0:T(8,128)(2,1)}, bf16[32,16384]{1,0:T(8,128)(2,1)}, u32[]{:S(2)}, u32[]{:S(2)}) collective-permute-start(bf16[32,16384]{1,0:T(8,128)(2,1)} %bitcast.35), channel_id=1, source_target_pairs={{0,28},{4,0},{8,4},{12,8},{16,12},{20,16},{24,20},{28,24},{1,29},{... | collective-permute-start | bytes 3145736 | tf_op jit(solution)/shard_map/ppermute | solution.py:34
  6.7 3.0 %collective-permute-start = (bf16[32,1024]{1,0:T(8,128)(2,1)}, bf16[32,1024]{1,0:T(8,128)(2,1)S(1)}, u32[]{:S(2)}, u32[]{:S(2)}) collective-permute-start(bf16[32,1024]{1,0:T(8,128)(2,1)} %param.12), channel_id=1, source_target_pairs={{0,130},{2,128},{128,2},{130,0},{1,131},{3,129},{129,3},{131,1},{4... | collective-permute-start | bytes 196616 | tf_op jit(solution)/shard_map/ppermute | solution.py:279
  11.0 5.1 %all-to-all-start = ((s32[32,1,4]{2,1,0:T(1,128)}), s32[32,1,4]{2,1,0:T(1,128)S(1)}, u32[]{:S(2)}, u32[]{:S(2)}) async-start(s32[32,1,4]{2,1,0:T(1,128)} %bitcast.4), calls=%async_computation | async-start | bytes 32768 | tf_op jit(solution)/shard_map/all_to_all | solution.py:38
  16.1 6.0 %all-to-all-done = s32[32,1,4]{2,1,0:T(1,128)S(1)} async-done(((s32[32,1,4]{2,1,0:T(1,128)}), s32[32,1,4]{2,1,0:T(1,128)S(1)}, u32[]{:S(2)}, u32[]{:S(2)}) %all-to-all-start) | async-done | bytes 544 | tf_op jit(solution)/shard_map/all_to_all | solution.py:38
  22.2 0.9 broadcast_select_fusion.1
  23.8 6.2 %collective-permute-done.10.refs_1_ = bf16[32,16384]{1,0:T(8,128)(2,1)} collective-permute-done((bf16[32,16384]{1,0:T(8,128)(2,1)}, bf16[32,16384]{1,0:T(8,128)(2,1)}, u32[]{:S(2)}, u32[]{:S(2)}) %collective-permute-start.10) | collective-permute-done | bytes 1048608 | tf_op jit(solution)/shard_map/ppermute | solution.py:34
  30.0 3.2 %collective-permute-start.13 = (bf16[32,16384]{1,0:T(8,128)(2,1)}, bf16[32,16384]{1,0:T(8,128)(2,1)}, u32[]{:S(2)}, u32[]{:S(2)}) collective-permute-start(bf16[32,16384]{1,0:T(8,128)(2,1)} %collective-permute-done.11.refs_2_), channel_id=1, source_target_pairs={{0,28},{4,0},{8,4},{12,8},{16,12},{20,16},{24,20},{28,24},{1,29},{... | collective-permute-start | bytes 3145736 | tf_op jit(solution)/shard_map/ppermute | solution.py:34
  33.3 4.7 %shard_map.86 = bf16[32,4,3,32,128]{4,3,2,1,0:T(8,128)(2,1)} custom-call(s32[32,4]{1,0:T(8,128)} %copy.39.wanted_ref, bf16[32,16384]{1,0:T(8,128)(2,1)} %bitcast.36, bf16[32,16384]{1,0:T(8,128)(2,1)} %collective-permute-done.10.refs_1_, bf16[32,16384]{1,0:T(8,128)(2,1)} %collective-permute-done.11.refs_2_), custom_call_target="tpu_custom_call" | custom-call | flops 20000000000 | bytes 6291456 | tf_op jit(solution)/shard_map/pallas_call | solution.py:81
  38.0 7.6 %all-to-all-start.1 = ((bf16[32,4,3,32,128]{4,3,2,1,0:T(8,128)(2,1)}), bf16[32,4,3,32,128]{4,3,2,1,0:T(8,128)(2,1)S(1)}, u32[]{:S(2)}, u32[]{:S(2)}) async-start(bf16[32,4,3,32,128]{4,3,2,1,0:T(8,128)(2,1)} %shard_map.86), calls=%async_computation.1 | async-start | bytes 6291456 | tf_op jit(solution)/shard_map/all_to_all | solution.py:38
  45.7 10.2 %collective-permute-done.12.refs_0_ = bf16[32,16384]{1,0:T(8,128)(2,1)} collective-permute-done((bf16[32,16384]{1,0:T(8,128)(2,1)}, bf16[32,16384]{1,0:T(8,128)(2,1)}, u32[]{:S(2)}, u32[]{:S(2)}) %collective-permute-start.12) | collective-permute-done | bytes 1048608 | tf_op jit(solution)/shard_map/ppermute | solution.py:34
  55.9 3.2 %collective-permute-start.15 = (bf16[32,16384]{1,0:T(8,128)(2,1)}, bf16[32,16384]{1,0:T(8,128)(2,1)S(1)}, u32[]{:S(2)}, u32[]{:S(2)}) collective-permute-start(bf16[32,16384]{1,0:T(8,128)(2,1)} %collective-permute-done.13.refs_1_), channel_id=1, source_target_pairs={{0,28},{4,0},{8,4},{12,8},{16,12},{20,16},{24,20},{28,24},{1,29},{... | collective-permute-start | bytes 3145736 | tf_op jit(solution)/shard_map/ppermute | solution.py:34
  59.2 21.6 %collective-permute-done.14.refs_2_ = bf16[32,16384]{1,0:T(8,128)(2,1)S(1)} collective-permute-done((bf16[32,16384]{1,0:T(8,128)(2,1)}, bf16[32,16384]{1,0:T(8,128)(2,1)S(1)}, u32[]{:S(2)}, u32[]{:S(2)}) %collective-permute-start.14) | collective-permute-done | bytes 1048608 | tf_op jit(solution)/shard_map/ppermute | solution.py:34
  80.8 1.0 copy-done.8
  81.7 1.0 copy-done.10
  82.7 5.3 %shard_map.88 = bf16[32,4,4,32,128]{4,3,2,1,0:T(8,128)(2,1)} custom-call(s32[32,4]{1,0:T(8,128)} %copy.39.wanted_ref, bf16[32,16384]{1,0:T(8,128)(2,1)} %collective-permute-done.12.refs_0_, bf16[32,16384]{1,0:T(8,128)(2,1)} %collective-permute-done.13.refs_1_, bf16[32,16384]{1,0:T(8,128)(2,1)} %copy-done.8, bf16[32,16384]{1,0:T(8,128)(2,1)} %copy-done.10), custom_call_target="tpu_custom_call" | custom-call | flops 20000000000 | bytes 8388608 | tf_op jit(solution)/shard_map/pallas_call | solution.py:81
  88.0 1.3 all-to-all-done.1.part
  89.3 6.4 %all-to-all-start.2 = ((bf16[32,4,4,32,128]{4,3,2,1,0:T(8,128)(2,1)}), bf16[32,4,4,32,128]{4,3,2,1,0:T(8,128)(2,1)}, u32[]{:S(2)}, u32[]{:S(2)}) async-start(bf16[32,4,4,32,128]{4,3,2,1,0:T(8,128)(2,1)} %shard_map.88), calls=%async_computation.2 | async-start | bytes 8388608 | tf_op jit(solution)/shard_map/all_to_all | solution.py:38
  95.8 3.2 %collective-permute-start.2 = (bf16[64,1024]{1,0:T(8,128)(2,1)S(1)}, bf16[64,1024]{1,0:T(8,128)(2,1)S(1)}, u32[]{:S(2)}, u32[]{:S(2)}) collective-permute-start(bf16[64,1024]{1,0:T(8,128)(2,1)S(1)} %pad_maximum_fusion.1), channel_id=1, source_target_pairs={{0,28},{4,0},{8,4},{12,8},{16,12},{20,16},{24,20},{28,24},{1,29},{... | collective-permute-start | bytes 393224 | tf_op jit(solution)/shard_map/ppermute | solution.py:34
  99.7 2.9 %collective-permute-done.1 = bf16[64,1024]{1,0:T(8,128)(2,1)S(1)} collective-permute-done((bf16[64,1024]{1,0:T(8,128)(2,1)S(1)}, bf16[64,1024]{1,0:T(8,128)(2,1)S(1)}, u32[]{:S(2)}, u32[]{:S(2)}) %collective-permute-start.1) | collective-permute-done | bytes 131104 | tf_op jit(solution)/shard_map/ppermute | solution.py:34
  102.6 3.2 %collective-permute-start.4 = (bf16[64,1024]{1,0:T(8,128)(2,1)S(1)}, bf16[64,1024]{1,0:T(8,128)(2,1)S(1)}, u32[]{:S(2)}, u32[]{:S(2)}) collective-permute-start(bf16[64,1024]{1,0:T(8,128)(2,1)S(1)} %collective-permute-done.2), channel_id=1, source_target_pairs={{0,28},{4,0},{8,4},{12,8},{16,12},{20,16},{24,20},{28,24},{1,29},{... | collective-permute-start | bytes 393224 | tf_op jit(solution)/shard_map/ppermute | solution.py:34
  107.1 1.6 collective-permute-done.3
  108.8 3.2 %collective-permute-start.6 = (bf16[64,1024]{1,0:T(8,128)(2,1)S(1)}, bf16[64,1024]{1,0:T(8,128)(2,1)S(1)}, u32[]{:S(2)}, u32[]{:S(2)}) collective-permute-start(bf16[64,1024]{1,0:T(8,128)(2,1)S(1)} %collective-permute-done.4), channel_id=1, source_target_pairs={{0,28},{4,0},{8,4},{12,8},{16,12},{20,16},{24,20},{28,24},{1,29},{... | collective-permute-start | bytes 393224 | tf_op jit(solution)/shard_map/ppermute | solution.py:34
  113.3 1.6 collective-permute-done.5
  115.0 3.3 %collective-permute-start.8 = (bf16[32,1024]{1,0:T(8,128)(2,1)S(1)}, bf16[32,1024]{1,0:T(8,128)(2,1)S(1)}, u32[]{:S(2)}, u32[]{:S(2)}) collective-permute-start(bf16[32,1024]{1,0:T(8,128)(2,1)S(1)} %slice.17), channel_id=1, source_target_pairs={{0,28},{4,0},{8,4},{12,8},{16,12},{20,16},{24,20},{28,24},{1,29},{... | collective-permute-start | bytes 196616 | tf_op jit(solution)/shard_map/ppermute | solution.py:34
  119.6 0.8 collective-permute-done.7
  121.7 0.8 slice.18
  122.5 0.8 slice.19
  123.3 3.2 %collective-permute-start.17 = (bf16[16,16384]{1,0:T(8,128)(2,1)}, bf16[16,16384]{1,0:T(8,128)(2,1)}, u32[]{:S(2)}, u32[]{:S(2)}) collective-permute-start(bf16[16,16384]{1,0:T(8,128)(2,1)} %slice.19), channel_id=1, source_target_pairs={{0,28},{4,0},{8,4},{12,8},{16,12},{20,16},{24,20},{28,24},{1,29},{... | collective-permute-start | bytes 1572872 | tf_op jit(solution)/shard_map/ppermute | solution.py:34
  126.7 3.2 %pad_maximum_fusion = bf16[16,2,32,1024]{3,2,1,0:T(8,128)(2,1)} fusion(bf16[16,1,32,1024]{3,2,1,0:T(8,128)(2,1)} %bitcast.9, bf16[16,1,32,1024]{3,2,1,0:T(8,128)(2,1)} %bitcast.7), kind=kLoop, calls=%fused_computation | loop fusion | flops 1048576 | bytes 4194304 | tf_op jit(solution)/shard_map/stack | solution.py:289
  129.8 3.7 %shard_map.87 = (bf16[384,1024]{1,0:T(8,128)(2,1)S(1)}, bf16[1024,384]{1,0:T(8,128)(2,1)S(1)}) custom-call(s32[1]{0:T(128)} %bitcast.core_ref, s32[8,4]{1,0:T(8,128)S(1)} %copy.44.tgt_ref, s32[8]{0:T(128)S(1)} %bitcast.27, bf16[8,4,128,128]{3,2,1,0:T(8,128)(2,1)S(1)} %bitcast.24, bf16[32,4,3,32,128]{4,3,2,1,0:T(8,128)(2,1)S(1)} %all-to-all-done.1.part), custom_call_target="tpu_custom_call" | custom-call | flops 3000000000 | bytes 8388608 | tf_op jit(solution)/shard_map/pallas_call | solution.py:130
  133.6 0.9 copy-done.6
  134.5 0.9 copy-done.7
  136.0 2.3 collective-permute-done.16.refs_0_
  138.5 3.3 %shard_map.90 = bf16[32,4,1,32,128]{4,3,2,1,0:T(8,128)(2,1)} custom-call(s32[32,4]{1,0:T(8,128)} %copy.43.wanted_ref, bf16[16,16384]{1,0:T(8,128)(2,1)} %collective-permute-done.16.refs_0_, bf16[16,16384]{1,0:T(8,128)(2,1)} %collective-permute-done.17.refs_1_), custom_call_target="tpu_custom_call" | custom-call | flops 1000000000 | bytes 2097152 | tf_op jit(solution)/shard_map/pallas_call | solution.py:81
  141.8 13.1 %all-to-all-done.2.part = bf16[32,4,4,32,128]{4,3,2,1,0:T(8,128)(2,1)} async-done(((bf16[32,4,4,32,128]{4,3,2,1,0:T(8,128)(2,1)}), bf16[32,4,4,32,128]{4,3,2,1,0:T(8,128)(2,1)}, u32[]{:S(2)}, u32[]{:S(2)}) %all-to-all-start.2) | async-done | bytes 4194336 | tf_op jit(solution)/shard_map/all_to_all | solution.py:38
  154.8 4.5 %all-to-all-start.3 = ((bf16[32,4,1,32,128]{4,3,2,1,0:T(8,128)(2,1)}), bf16[32,4,1,32,128]{4,3,2,1,0:T(8,128)(2,1)}, u32[]{:S(2)}, u32[]{:S(2)}) async-start(bf16[32,4,1,32,128]{4,3,2,1,0:T(8,128)(2,1)} %shard_map.90), calls=%async_computation.3 | async-start | bytes 2097152 | tf_op jit(solution)/shard_map/all_to_all | solution.py:38
  159.3 5.7 %shard_map.89 = (bf16[512,1024]{1,0:T(8,128)(2,1)S(1)}, bf16[1024,512]{1,0:T(8,128)(2,1)S(1)}) custom-call(s32[1]{0:T(128)} %bitcast.core_ref, s32[8,4]{1,0:T(8,128)S(1)} %copy.44.tgt_ref, s32[8]{0:T(128)S(1)} %bitcast.28, bf16[8,4,128,128]{3,2,1,0:T(8,128)(2,1)S(1)} %bitcast.25, bf16[32,4,4,32,128]{4,3,2,1,0:T(8,128)(2,1)} %all-to-all-done.2.part), custom_call_target="tpu_custom_call" | custom-call | flops 3000000000 | bytes 8388608 | tf_op jit(solution)/shard_map/pallas_call | solution.py:130
  165.1 1.0 copy-done.4
  166.1 1.0 copy-done.5
  167.1 7.9 %all-to-all-done.3.refs_5_ = bf16[32,4,1,32,128]{4,3,2,1,0:T(8,128)(2,1)} async-done(((bf16[32,4,1,32,128]{4,3,2,1,0:T(8,128)(2,1)}), bf16[32,4,1,32,128]{4,3,2,1,0:T(8,128)(2,1)}, u32[]{:S(2)}, u32[]{:S(2)}) %all-to-all-start.3) | async-done | bytes 1048608 | tf_op jit(solution)/shard_map/all_to_all | solution.py:38
  175.0 12.5 %shard_map.91 = (bf16[1024,1024]{1,0:T(8,128)(2,1)}, bf16[8,2,8,32,128]{4,3,2,1,0:T(8,128)(2,1)}, bf16[8,2,8,32,128]{4,3,2,1,0:T(8,128)(2,1)}) custom-call(s32[1]{0:T(128)} %bitcast.core_ref, s32[8,4]{1,0:T(8,128)} %copy-done, s32[8]{0:T(128)} %bitcast.26, bf16[384,1024]{1,0:T(8,128)(2,1)} %copy-done.6, bf16[1024,384]{1,0:T(8,128)(2,1)} %copy-done.7, ...), custom_call_target="tpu_custom_call" | custom-call | flops 6000000000 | bytes 20971520 | tf_op jit(solution)/shard_map/pallas_call | solution.py:222
  188.2 2.5 %collective-permute-done.18 = bf16[8,2,8,32,128]{4,3,2,1,0:T(8,128)(2,1)S(1)} collective-permute-done((bf16[8,2,8,32,128]{4,3,2,1,0:T(8,128)(2,1)}, bf16[8,2,8,32,128]{4,3,2,1,0:T(8,128)(2,1)S(1)}, u32[]{:S(2)}, u32[]{:S(2)}) %collective-permute-start.18) | collective-permute-done | bytes 1048608 | tf_op jit(solution)/shard_map/ppermute | solution.py:269
  190.7 2.5 %add_convert_fusion = bf16[8,2,8,32,128]{4,3,2,1,0:T(8,128)(2,1)} fusion(bf16[8,2,8,32,128]{4,3,2,1,0:T(8,128)(2,1)S(1)} %collective-permute-done.18, bf16[8,2,8,32,128]{4,3,2,1,0:T(8,128)(2,1)} %get-tuple-element.26), kind=kLoop, calls=%fused_computation.1 | loop fusion | flops 2097152 | bytes 3145728 | tf_op jit(solution)/shard_map/convert_element_type | solution.py:270
  193.2 4.6 %all-to-all-start.4 = ((bf16[16,8,32,128]{3,2,1,0:T(8,128)(2,1)}), bf16[16,8,32,128]{3,2,1,0:T(8,128)(2,1)S(1)}, u32[]{:S(2)}, u32[]{:S(2)}) async-start(bf16[16,8,32,128]{3,2,1,0:T(8,128)(2,1)} %bitcast.14), calls=%async_computation.4 | async-start | bytes 2097152 | tf_op jit(solution)/shard_map/all_to_all | solution.py:38
  197.8 18.3 %all-to-all-done.4.came_ref = bf16[16,8,32,128]{3,2,1,0:T(8,128)(2,1)S(1)} async-done(((bf16[16,8,32,128]{3,2,1,0:T(8,128)(2,1)}), bf16[16,8,32,128]{3,2,1,0:T(8,128)(2,1)S(1)}, u32[]{:S(2)}, u32[]{:S(2)}) %all-to-all-start.4) | async-done | bytes 1048608 | tf_op jit(solution)/shard_map/all_to_all | solution.py:38
  216.2 13.4 %all_to_all.35 = f32[8,32,128]{2,1,0:T(8,128)S(1)} all-to-all(f32[8,32,128]{2,1,0:T(8,128)S(1)} %shard_map.92), channel_id=1, replica_groups=mesh['ylo'=2,'x'=4,'z'=8,'yhi'=2,'core'=2] {'z'}, dimensions={0} | all-to-all | bytes 262144 | tf_op jit(solution)/shard_map/all_to_all | solution.py:38
  229.7 10.1 %all_to_all.36 = f32[8,32,128]{2,1,0:T(8,128)S(1)} all-to-all(f32[8,32,128]{2,1,0:T(8,128)S(1)} %broadcast_in_dim.18), channel_id=1, replica_groups=mesh['ylo'=2,'x'=4,'z'=8,'yhi'=2,'core'=2] {'ylo','x'}, dimensions={0} | all-to-all | bytes 262144 | tf_op jit(solution)/shard_map/all_to_all | solution.py:38
  (61 shorter events, 10.6 us)
Async XLA Ops:
  0.6 29.4 %collective-permute-start.10 = (bf16[32,16384]{1,0:T(8,128)(2,1)}, bf16[32,16384]{1,0:T(8,128)(2,1)}, u32[]{:S(2)}, u32[]{:S(2)}) collective-permute-start(bf16[32,16384]{1,0:T(8,128)(2,1)} %bitcast.34), channel_id=1, source_target_pairs={{0,4},{4,8},{8,12},{12,16},{16,20},{20,24},{24,28},{28,0},{1,5},{5... | collective-permute-start | bytes 3145736 | tf_op jit(solution)/shard_map/ppermute | solution.py:34
  2.6 27.4 %collective-permute-start.11 = (bf16[32,16384]{1,0:T(8,128)(2,1)}, bf16[32,16384]{1,0:T(8,128)(2,1)}, u32[]{:S(2)}, u32[]{:S(2)}) collective-permute-start(bf16[32,16384]{1,0:T(8,128)(2,1)} %bitcast.35), channel_id=1, source_target_pairs={{0,28},{4,0},{8,4},{12,8},{16,12},{20,16},{24,20},{28,24},{1,29},{... | collective-permute-start | bytes 3145736 | tf_op jit(solution)/shard_map/ppermute | solution.py:34
  6.7 15.6 %collective-permute-start = (bf16[32,1024]{1,0:T(8,128)(2,1)}, bf16[32,1024]{1,0:T(8,128)(2,1)S(1)}, u32[]{:S(2)}, u32[]{:S(2)}) collective-permute-start(bf16[32,1024]{1,0:T(8,128)(2,1)} %param.12), channel_id=1, source_target_pairs={{0,130},{2,128},{128,2},{130,0},{1,131},{3,129},{129,3},{131,1},{4... | collective-permute-start | bytes 196616 | tf_op jit(solution)/shard_map/ppermute | solution.py:279
  11.0 11.1 %all-to-all-start = ((s32[32,1,4]{2,1,0:T(1,128)}), s32[32,1,4]{2,1,0:T(1,128)S(1)}, u32[]{:S(2)}, u32[]{:S(2)}) async-start(s32[32,1,4]{2,1,0:T(1,128)} %bitcast.4), calls=%async_computation | async-start | bytes 32768 | tf_op jit(solution)/shard_map/all_to_all | solution.py:38
  30.0 25.9 %collective-permute-start.12 = (bf16[32,16384]{1,0:T(8,128)(2,1)}, bf16[32,16384]{1,0:T(8,128)(2,1)}, u32[]{:S(2)}, u32[]{:S(2)}) collective-permute-start(bf16[32,16384]{1,0:T(8,128)(2,1)} %collective-permute-done.10.refs_1_), channel_id=1, source_target_pairs={{0,4},{4,8},{8,12},{12,16},{16,20},{20,24},{24,28},{28,0},{1,5},{5... | collective-permute-start | bytes 3145736 | tf_op jit(solution)/shard_map/ppermute | solution.py:34
  30.0 25.9 %collective-permute-start.13 = (bf16[32,16384]{1,0:T(8,128)(2,1)}, bf16[32,16384]{1,0:T(8,128)(2,1)}, u32[]{:S(2)}, u32[]{:S(2)}) collective-permute-start(bf16[32,16384]{1,0:T(8,128)(2,1)} %collective-permute-done.11.refs_2_), channel_id=1, source_target_pairs={{0,28},{4,0},{8,4},{12,8},{16,12},{20,16},{24,20},{28,24},{1,29},{... | collective-permute-start | bytes 3145736 | tf_op jit(solution)/shard_map/ppermute | solution.py:34
  38.0 51.3 %all-to-all-start.1 = ((bf16[32,4,3,32,128]{4,3,2,1,0:T(8,128)(2,1)}), bf16[32,4,3,32,128]{4,3,2,1,0:T(8,128)(2,1)S(1)}, u32[]{:S(2)}, u32[]{:S(2)}) async-start(bf16[32,4,3,32,128]{4,3,2,1,0:T(8,128)(2,1)} %shard_map.86), calls=%async_computation.1 | async-start | bytes 6291456 | tf_op jit(solution)/shard_map/all_to_all | solution.py:38
  55.9 24.8 %collective-permute-start.14 = (bf16[32,16384]{1,0:T(8,128)(2,1)}, bf16[32,16384]{1,0:T(8,128)(2,1)S(1)}, u32[]{:S(2)}, u32[]{:S(2)}) collective-permute-start(bf16[32,16384]{1,0:T(8,128)(2,1)} %collective-permute-done.12.refs_0_), channel_id=1, source_target_pairs={{0,4},{4,8},{8,12},{12,16},{16,20},{20,24},{24,28},{28,0},{1,5},{5... | collective-permute-start | bytes 3145736 | tf_op jit(solution)/shard_map/ppermute | solution.py:34
  55.9 24.8 %collective-permute-start.15 = (bf16[32,16384]{1,0:T(8,128)(2,1)}, bf16[32,16384]{1,0:T(8,128)(2,1)S(1)}, u32[]{:S(2)}, u32[]{:S(2)}) collective-permute-start(bf16[32,16384]{1,0:T(8,128)(2,1)} %collective-permute-done.13.refs_1_), channel_id=1, source_target_pairs={{0,28},{4,0},{8,4},{12,8},{16,12},{20,16},{24,20},{28,24},{1,29},{... | collective-permute-start | bytes 3145736 | tf_op jit(solution)/shard_map/ppermute | solution.py:34
  80.8 1.0 copy-start.8
  81.7 1.0 copy-start.10
  89.3 65.5 %all-to-all-start.2 = ((bf16[32,4,4,32,128]{4,3,2,1,0:T(8,128)(2,1)}), bf16[32,4,4,32,128]{4,3,2,1,0:T(8,128)(2,1)}, u32[]{:S(2)}, u32[]{:S(2)}) async-start(bf16[32,4,4,32,128]{4,3,2,1,0:T(8,128)(2,1)} %shard_map.88), calls=%async_computation.2 | async-start | bytes 8388608 | tf_op jit(solution)/shard_map/all_to_all | solution.py:38
  95.7 26.0 %copy-start.9 = (bf16[32,16384]{1,0:T(8,128)(2,1)S(1)}, bf16[32,16384]{1,0:T(8,128)(2,1)}, u32[]{:S(2)}) copy-start(bf16[32,16384]{1,0:T(8,128)(2,1)} %copy-done.8) | copy-start | bytes 3145732
  95.7 26.8 %copy-start.11 = (bf16[32,16384]{1,0:T(8,128)(2,1)S(1)}, bf16[32,16384]{1,0:T(8,128)(2,1)}, u32[]{:S(2)}) copy-start(bf16[32,16384]{1,0:T(8,128)(2,1)} %copy-done.10) | copy-start | bytes 3145732
  95.7 6.8 %collective-permute-start.1 = (bf16[64,1024]{1,0:T(8,128)(2,1)S(1)}, bf16[64,1024]{1,0:T(8,128)(2,1)S(1)}, u32[]{:S(2)}, u32[]{:S(2)}) collective-permute-start(bf16[64,1024]{1,0:T(8,128)(2,1)S(1)} %pad_maximum_fusion.1), channel_id=1, source_target_pairs={{0,4},{4,8},{8,12},{12,16},{16,20},{20,24},{24,28},{28,0},{1,5},{5... | collective-permute-start | bytes 393224 | tf_op jit(solution)/shard_map/ppermute | solution.py:34
  95.8 6.8 %collective-permute-start.2 = (bf16[64,1024]{1,0:T(8,128)(2,1)S(1)}, bf16[64,1024]{1,0:T(8,128)(2,1)S(1)}, u32[]{:S(2)}, u32[]{:S(2)}) collective-permute-start(bf16[64,1024]{1,0:T(8,128)(2,1)S(1)} %pad_maximum_fusion.1), channel_id=1, source_target_pairs={{0,28},{4,0},{8,4},{12,8},{16,12},{20,16},{24,20},{28,24},{1,29},{... | collective-permute-start | bytes 393224 | tf_op jit(solution)/shard_map/ppermute | solution.py:34
  99.7 26.9 %copy-start.12 = (s32[1,1,8,4]{2,3,1,0:T(4,128)S(1)}, s32[1,1,8,4]{2,3,1,0:T(4,128)}, u32[]{:S(2)}) copy-start(s32[1,1,8,4]{2,3,1,0:T(4,128)} %param.8) | copy-start | bytes 388
  102.6 6.2 %collective-permute-start.3 = (bf16[64,1024]{1,0:T(8,128)(2,1)S(1)}, bf16[64,1024]{1,0:T(8,128)(2,1)S(1)}, u32[]{:S(2)}, u32[]{:S(2)}) collective-permute-start(bf16[64,1024]{1,0:T(8,128)(2,1)S(1)} %collective-permute-done.1), channel_id=1, source_target_pairs={{0,4},{4,8},{8,12},{12,16},{16,20},{20,24},{24,28},{28,0},{1,5},{5... | collective-permute-start | bytes 393224 | tf_op jit(solution)/shard_map/ppermute | solution.py:34
  102.6 6.2 %collective-permute-start.4 = (bf16[64,1024]{1,0:T(8,128)(2,1)S(1)}, bf16[64,1024]{1,0:T(8,128)(2,1)S(1)}, u32[]{:S(2)}, u32[]{:S(2)}) collective-permute-start(bf16[64,1024]{1,0:T(8,128)(2,1)S(1)} %collective-permute-done.2), channel_id=1, source_target_pairs={{0,28},{4,0},{8,4},{12,8},{16,12},{20,16},{24,20},{28,24},{1,29},{... | collective-permute-start | bytes 393224 | tf_op jit(solution)/shard_map/ppermute | solution.py:34
  108.8 6.2 %collective-permute-start.5 = (bf16[64,1024]{1,0:T(8,128)(2,1)S(1)}, bf16[64,1024]{1,0:T(8,128)(2,1)S(1)}, u32[]{:S(2)}, u32[]{:S(2)}) collective-permute-start(bf16[64,1024]{1,0:T(8,128)(2,1)S(1)} %collective-permute-done.3), channel_id=1, source_target_pairs={{0,4},{4,8},{8,12},{12,16},{16,20},{20,24},{24,28},{28,0},{1,5},{5... | collective-permute-start | bytes 393224 | tf_op jit(solution)/shard_map/ppermute | solution.py:34
  108.8 6.2 %collective-permute-start.6 = (bf16[64,1024]{1,0:T(8,128)(2,1)S(1)}, bf16[64,1024]{1,0:T(8,128)(2,1)S(1)}, u32[]{:S(2)}, u32[]{:S(2)}) collective-permute-start(bf16[64,1024]{1,0:T(8,128)(2,1)S(1)} %collective-permute-done.4), channel_id=1, source_target_pairs={{0,28},{4,0},{8,4},{12,8},{16,12},{20,16},{24,20},{28,24},{1,29},{... | collective-permute-start | bytes 393224 | tf_op jit(solution)/shard_map/ppermute | solution.py:34
  114.9 5.5 %collective-permute-start.7 = (bf16[32,1024]{1,0:T(8,128)(2,1)S(1)}, bf16[32,1024]{1,0:T(8,128)(2,1)S(1)}, u32[]{:S(2)}, u32[]{:S(2)}) collective-permute-start(bf16[32,1024]{1,0:T(8,128)(2,1)S(1)} %slice.16), channel_id=1, source_target_pairs={{0,4},{4,8},{8,12},{12,16},{16,20},{20,24},{24,28},{28,0},{1,5},{5... | collective-permute-start | bytes 196616 | tf_op jit(solution)/shard_map/ppermute | solution.py:34
  115.0 6.1 %collective-permute-start.8 = (bf16[32,1024]{1,0:T(8,128)(2,1)S(1)}, bf16[32,1024]{1,0:T(8,128)(2,1)S(1)}, u32[]{:S(2)}, u32[]{:S(2)}) collective-permute-start(bf16[32,1024]{1,0:T(8,128)(2,1)S(1)} %slice.17), channel_id=1, source_target_pairs={{0,28},{4,0},{8,4},{12,8},{16,12},{20,16},{24,20},{28,24},{1,29},{... | collective-permute-start | bytes 196616 | tf_op jit(solution)/shard_map/ppermute | solution.py:34
  121.7 5.0 %collective-permute-start.9 = (bf16[512,1024]{1,0:T(8,128)(2,1)}, bf16[512,1024]{1,0:T(8,128)(2,1)}, u32[]{:S(2)}, u32[]{:S(2)}) collective-permute-start(bf16[512,1024]{1,0:T(8,128)(2,1)} %constant_dynamic-update-slice_fusion), channel_id=1, source_target_pairs={{0,1},{1,0},{2,3},{3,2},{4,5},{5,4},{6,7},{7,6},{8,9},{9,8},{10,11... | collective-permute-start | bytes 3145736 | tf_op jit(solution)/shard_map/ppermute | solution.py:287
  122.5 15.9 %collective-permute-start.16 = (bf16[16,16384]{1,0:T(8,128)(2,1)}, bf16[16,16384]{1,0:T(8,128)(2,1)}, u32[]{:S(2)}, u32[]{:S(2)}) collective-permute-start(bf16[16,16384]{1,0:T(8,128)(2,1)} %slice.18), channel_id=1, source_target_pairs={{0,4},{4,8},{8,12},{12,16},{16,20},{20,24},{24,28},{28,0},{1,5},{5... | collective-permute-start | bytes 1572872 | tf_op jit(solution)/shard_map/ppermute | solution.py:34
  123.3 15.1 %collective-permute-start.17 = (bf16[16,16384]{1,0:T(8,128)(2,1)}, bf16[16,16384]{1,0:T(8,128)(2,1)}, u32[]{:S(2)}, u32[]{:S(2)}) collective-permute-start(bf16[16,16384]{1,0:T(8,128)(2,1)} %slice.19), channel_id=1, source_target_pairs={{0,28},{4,0},{8,4},{12,8},{16,12},{20,16},{24,20},{28,24},{1,29},{... | collective-permute-start | bytes 1572872 | tf_op jit(solution)/shard_map/ppermute | solution.py:34
  126.7 32.7 %copy-start = (s32[8,4]{1,0:T(8,128)}, s32[8,4]{1,0:T(8,128)S(1)}, u32[]{:S(2)}) copy-start(s32[8,4]{1,0:T(8,128)S(1)} %copy.44.tgt_ref) | copy-start | bytes 388
  126.7 3.2 %copy-start.1 = (bf16[1,1,8,4,128,128]{5,4,3,2,1,0:T(8,128)(2,1)S(1)}, bf16[1,1,8,4,128,128]{5,4,3,2,1,0:T(8,128)(2,1)}, u32[]{:S(2)}) copy-start(bf16[1,1,8,4,128,128]{5,4,3,2,1,0:T(8,128)(2,1)} %param.11) | copy-start | bytes 3145732
  126.7 3.2 %copy-start.3 = (s32[1,1,8]{2,1,0:T(1,128)S(1)}, s32[1,1,8]{2,1,0:T(1,128)}, u32[]{:S(2)}) copy-start(s32[1,1,8]{2,1,0:T(1,128)} %param.10) | copy-start | bytes 100
  133.6 0.9 copy-start.6
  134.5 0.9 copy-start.7
  136.0 23.3 %copy-start.2 = (bf16[1,1,8,4,128,128]{5,4,3,2,1,0:T(8,128)(2,1)S(1)}, bf16[1,1,8,4,128,128]{5,4,3,2,1,0:T(8,128)(2,1)}, u32[]{:S(2)}) copy-start(bf16[1,1,8,4,128,128]{5,4,3,2,1,0:T(8,128)(2,1)} %param.11) | copy-start | bytes 3145732
  154.8 20.1 %all-to-all-start.3 = ((bf16[32,4,1,32,128]{4,3,2,1,0:T(8,128)(2,1)}), bf16[32,4,1,32,128]{4,3,2,1,0:T(8,128)(2,1)}, u32[]{:S(2)}, u32[]{:S(2)}) async-start(bf16[32,4,1,32,128]{4,3,2,1,0:T(8,128)(2,1)} %shard_map.90), calls=%async_computation.3 | async-start | bytes 2097152 | tf_op jit(solution)/shard_map/all_to_all | solution.py:38
  165.1 1.0 copy-start.4
  166.1 1.0 copy-start.5
  187.5 3.3 %collective-permute-start.18 = (bf16[8,2,8,32,128]{4,3,2,1,0:T(8,128)(2,1)}, bf16[8,2,8,32,128]{4,3,2,1,0:T(8,128)(2,1)S(1)}, u32[]{:S(2)}, u32[]{:S(2)}) collective-permute-start(bf16[8,2,8,32,128]{4,3,2,1,0:T(8,128)(2,1)} %get-tuple-element.27), channel_id=1, source_target_pairs={{0,1},{1,0},{2,3},{3,2},{4,5},{5,4},{6,7},{7,6},{8,9},{9,8},{10,11... | collective-permute-start | bytes 3145736 | tf_op jit(solution)/shard_map/ppermute | solution.py:269
  193.2 22.9 %all-to-all-start.4 = ((bf16[16,8,32,128]{3,2,1,0:T(8,128)(2,1)}), bf16[16,8,32,128]{3,2,1,0:T(8,128)(2,1)S(1)}, u32[]{:S(2)}, u32[]{:S(2)}) async-start(bf16[16,8,32,128]{3,2,1,0:T(8,128)(2,1)} %bitcast.14), calls=%async_computation.4 | async-start | bytes 2097152 | tf_op jit(solution)/shard_map/all_to_all | solution.py:38

commit v7 on v6

--- a/solution.py
+++ b/solution.py
@@ -15,7 +15,8 @@
 PARTS = ((0, 1, -1), (2, -2, 3, -3), (4,))
 ORDER = tuple(d for part in PARTS for d in part)
 LANES = 4
-LAYER_MIB = 56
+EARLY_MIB = (20, 60)
+LAYER_MIB = 50
 VMEM = pl.BlockSpec(memory_space=pltpu.VMEM)
 SMEM = pl.BlockSpec(memory_space=pltpu.SMEM)
 HBM = pl.BlockSpec(memory_space=pltpu.HBM)
@@ -84,48 +85,53 @@
         in_specs=[SMEM] + [VMEM] * len(refs),
         out_specs=HBM,
         scratch_shapes=[pltpu.VMEM(shape, jnp.bfloat16), pltpu.SemaphoreType.DMA((4,))],
-        compiler_params=params(58),
+        compiler_params=params(60),
         cost_estimate=cost(flops, count * 2**21),
     )(wanted, *refs)
 
 
-def add_tiles(core, tgt_ref, count_ref, vals_ref, part, acc, ready):
+def add_tiles(core, tgt_ref, count_ref, vals_ref, part, acc, live):
     sections, slots, block, _ = vals_ref.shape
     places, rows = part.shape[2:4]
+    spare = acc.shape[1] - block
     acc[...] = jnp.zeros_like(acc)
 
-    def one(section, slot):
-        column = pl.multiple_of(tgt_ref[section, slot] * block, block)
-        sources = [section * LANES + lane + core * (1 - 2 * (lane % 2)) for lane in range(LANES)]
-        columns_in = jnp.concatenate([part[source, slot].reshape(places * rows, block) for source in sources])
-        contrib = lax.dot_general(
-            columns_in, vals_ref[section, slot], (((1,), (1,)), ((), ())), preferred_element_type=jnp.float32
-        )
-        for lane in range(LANES):
-            for place in range(places):
-                low, at = (place * LANES + lane) * rows, (lane * places + place) * rows
-                acc[low : low + rows, pl.ds(column, block)] += contrib[at : at + rows]
-
-    @pl.loop(0, sections)
-    def _(section):
-        ready(section)
-
-        @pl.loop(0, jnp.minimum(count_ref[section], slots))
-        def _(slot):
-            one(section, slot)
-
-
-def aggregate_kernel(core_ref, tgt_ref, count_ref, vals_ref, part, turned_ref, plain_ref, acc):
-    add_tiles(core_ref[0], tgt_ref, count_ref, vals_ref, part, acc, lambda section: None)
+    def enter(tile, found):
+        live[found] = tile
+        return found + (tile % slots < count_ref[tile // slots]).astype(jnp.int32)
+
+    found = lax.fori_loop(0, sections * slots, enter, 0)
+    each = 4
+
+    @pl.loop(0, (found + each - 1) // each)
+    def _(step):
+        for index in range(each):
+            at = step * each + index
+            tile = jnp.where(at < found, live[jnp.minimum(at, sections * slots - 1)], 0)
+            section, slot = tile // slots, tile % slots
+            column = pl.multiple_of(jnp.where(at < found, tgt_ref[section, slot] * block, spare), block)
+            sources = [section * LANES + lane + core * (1 - 2 * (lane % 2)) for lane in range(LANES)]
+            columns_in = jnp.concatenate([part[source, slot].reshape(places * rows, block) for source in sources])
+            contrib = lax.dot_general(
+                columns_in, vals_ref[section, slot], (((1,), (1,)), ((), ())), preferred_element_type=jnp.float32
+            )
+            for lane in range(LANES):
+                for place in range(places):
+                    low, first = (place * LANES + lane) * rows, (lane * places + place) * rows
+                    acc[low : low + rows, pl.ds(column, block)] += contrib[first : first + rows]
+
+
+def aggregate_kernel(core_ref, tgt_ref, count_ref, vals_ref, part, turned_ref, plain_ref, acc, live):
+    add_tiles(core_ref[0], tgt_ref, count_ref, vals_ref, part, acc, live)
     step = vals_ref.shape[-1]
-    for low in range(0, acc.shape[1], step):
+    for low in range(0, turned_ref.shape[1], step):
         at = slice(low, low + step)
         value = acc[:, at]
         turned_ref[:, at] = value.astype(turned_ref.dtype)
         plain_ref[at] = value.T.astype(plain_ref.dtype)
 
 
-def aggregate(core, targets, counts, values, part, num_rows):
+def aggregate(core, targets, counts, values, part, num_rows, mib):
     num_feats = LANES * part.shape[2] * part.shape[3]
     return pl.pallas_call(
         aggregate_kernel,
@@ -135,8 +141,11 @@
         ),
         in_specs=[SMEM] * 3 + [VMEM] * 2,
         out_specs=(VMEM, VMEM),
-        scratch_shapes=[pltpu.VMEM((num_feats, num_rows), jnp.float32)],
-        compiler_params=params(20),
+        scratch_shapes=[
+            pltpu.VMEM((num_feats, num_rows + values.shape[-1]), jnp.float32),
+            pltpu.SMEM((values.shape[0] * values.shape[1],), jnp.int32),
+        ],
+        compiler_params=params(mib),
         cost_estimate=cost(3 * 10**9, 8 * 2**20),
     )(core, targets, counts, values, part)
 
@@ -144,7 +153,7 @@
 def layer_kernel(num_early, core_ref, tgt_ref, count_ref, *refs):
     early, refs = refs[: 2 * num_early], refs[2 * num_early :]
     vals_hbm, part_hbm, weight_hbm, cot_hbm, act_hbm, kept_hbm, gone_hbm = refs[:7]
-    vals, part, weight, cot, act, kept, gone, acc, turned, plain, dpre, sems, block_sems, out_sems = refs[7:]
+    vals, part, weight, cot, act, kept, gone, acc, live, turned, plain, dpre, sems, block_sems, out_sems = refs[7:]
     blocks = out_sems.shape[1]
     step = act.shape[0] // blocks
     vals_copy = pltpu.make_async_copy(vals_hbm, vals, sems.at[0])
@@ -168,9 +177,9 @@
         copy.start()
     vals_copy.wait()
     part_copy.wait()
-    add_tiles(core_ref[0], tgt_ref, count_ref, vals, part, acc, lambda section: None)
+    add_tiles(core_ref[0], tgt_ref, count_ref, vals, part, acc, live)
     width = vals.shape[-1]
-    for first in range(0, acc.shape[1], width):
+    for first in range(0, turned.shape[1], width):
         at = slice(first, first + width)
         value = acc[:, at]
         turned[low:, at] = value.astype(turned.dtype)
@@ -236,7 +245,8 @@
             pltpu.VMEM((tgt_rows, width), jnp.bfloat16),
             pltpu.VMEM(cut, jnp.bfloat16),
             pltpu.VMEM(cut, jnp.bfloat16),
-            pltpu.VMEM((late, tgt_rows), jnp.float32),
+            pltpu.VMEM((late, tgt_rows + values.shape[-1]), jnp.float32),
+            pltpu.SMEM((values.shape[0] * values.shape[1],), jnp.int32),
             pltpu.VMEM((feats, tgt_rows), jnp.bfloat16),
             pltpu.VMEM((tgt_rows, feats), jnp.bfloat16),
             pltpu.VMEM((tgt_rows, width), jnp.bfloat16),
@@ -305,7 +315,7 @@
             wanted, weight_in, early[0] = lax.optimization_barrier((wanted, weight_in, early[0]))
         part = exchange(pick(wanted, [held[d] for d in distances], block_size, flops), PLANE)
         if distances != PARTS[-1]:
-            early.append(aggregate(core, targets, counts, values, part, tgt_rows))
+            early.append(aggregate(core, targets, counts, values, part, tgt_rows, EARLY_MIB[len(early)]))
     activations, kept, gone = layer(core, targets, counts, values, part, early, weight_in, cotangent)
     weight_grad = sum_over_devices(kept, gone) / math.sqrt(tgt_rows * 256)
     return (activations, weight_grad)

time: 242 us -> 238 us (0.983)
  starting transfers between devices: 60.6 us -> 57.1 us
  waiting for transfers between devices: 96.6 us -> 99.1 us
    unnamed x35 -> x31, local copies, waits for them, and re-layouts: 11.7 us -> 8.85 us
    all_to_all x5, starting transfers between devices: 28 us -> 25.2 us  [exchange(): return lax.all_to_all(value, axes, split_axis=0, concat_axis=0, tiled=True)]
  transfers between devices with their start and end apart: 24 -> 24, of which waited for: 15 -> 15; matrix products, arithmetic and copies ran while one was open for 6% -> 7% of each run, Pallas kernels for 9% -> 10%
where the time goes in v7:
time: 238 us; the launch traced here: 237 us
  waiting for transfers between devices  99.1 us (42%)
  starting transfers between devices  57.1 us (24%)
  Pallas kernels  33.9 us (14%)
  blocking collectives  24.9 us (10%)
  local copies, waits for them, and re-layouts  15.4 us (6%)
  other arithmetic  6.03 us (3%)
    all_to_all x5, waiting for transfers between devices, exchange(): return lax.all_to_all(value, axes, split_axis=0, concat_axis=0, tiled=True)  48.3 us
    ppermute x16, waiting for transfers between devices, shift_z(): return lax.ppermute(value, 'z', [(i, (i + step) % ZN) for i in range(ZN)])  48.1 us
    ppermute x16, starting transfers between devices, shift_z(): return lax.ppermute(value, 'z', [(i, (i + step) % ZN) for i in range(ZN)])  28.8 us
    all_to_all x5, starting transfers between devices, exchange(): return lax.all_to_all(value, axes, split_axis=0, concat_axis=0, tiled=True)  25.2 us
    all_to_all x2, blocking collectives, exchange(): return lax.all_to_all(value, axes, split_axis=0, concat_axis=0, tiled=True)  24.9 us
    pallas_call x3, Pallas kernels, pick(): pl.pallas_call(functools.partial(pick_kernel, block, layout), out_shape=j...  13.4 us
    pallas_call x1, Pallas kernels, layer(): pl.pallas_call(functools.partial(layer_kernel, len(early) // 2), out_shap...  10.9 us
    pallas_call x2, Pallas kernels, aggregate(): pl.pallas_call(aggregate_kernel, out_shape=(jax.ShapeDtypeStruct((num_fea...  9.54 us
  transfers between devices with their start and end apart: 24, of which 15 were waited for; matrix products, arithmetic and copies ran while one was open for 7% of the time, Pallas kernels for 10%

profile of v7, /device:TPU:2, one launch (start us, length us, event | category | flops | bytes accessed | tf_op | source)
XLA Modules:
  0.0 237.4 jit_solution(890396119545366823)
XLA Ops:
  0.6 2.0 collective-permute-start.10
  2.6 4.0 %collective-permute-start.11 = (bf16[32,16384]{1,0:T(8,128)(2,1)}, bf16[32,16384]{1,0:T(8,128)(2,1)}, u32[]{:S(2)}, u32[]{:S(2)}) collective-permute-start(bf16[32,16384]{1,0:T(8,128)(2,1)} %bitcast.35), channel_id=1, source_target_pairs={{0,28},{4,0},{8,4},{12,8},{16,12},{20,16},{24,20},{28,24},{1,29},{... | collective-permute-start | bytes 3145736 | tf_op jit(solution)/shard_map/ppermute | solution.py:35
  6.7 3.0 %collective-permute-start = (bf16[32,1024]{1,0:T(8,128)(2,1)}, bf16[32,1024]{1,0:T(8,128)(2,1)S(1)}, u32[]{:S(2)}, u32[]{:S(2)}) collective-permute-start(bf16[32,1024]{1,0:T(8,128)(2,1)} %param.12), channel_id=1, source_target_pairs={{0,130},{2,128},{128,2},{130,0},{1,131},{3,129},{129,3},{131,1},{4... | collective-permute-start | bytes 196616 | tf_op jit(solution)/shard_map/ppermute | solution.py:289
  9.7 0.8 copy.47
  11.0 5.1 %all-to-all-start = ((s32[32,1,4]{2,1,0:T(1,128)}), s32[32,1,4]{2,1,0:T(1,128)S(1)}, u32[]{:S(2)}, u32[]{:S(2)}) async-start(s32[32,1,4]{2,1,0:T(1,128)} %bitcast.4), calls=%async_computation | async-start | bytes 32768 | tf_op jit(solution)/shard_map/all_to_all | solution.py:39
  16.1 6.0 %all-to-all-done = s32[32,1,4]{2,1,0:T(1,128)S(1)} async-done(((s32[32,1,4]{2,1,0:T(1,128)}), s32[32,1,4]{2,1,0:T(1,128)S(1)}, u32[]{:S(2)}, u32[]{:S(2)}) %all-to-all-start) | async-done | bytes 544 | tf_op jit(solution)/shard_map/all_to_all | solution.py:39
  22.2 0.9 broadcast_select_fusion.1
  23.1 0.7 copy.39.wanted_ref
  23.8 6.2 %collective-permute-done.10.refs_1_ = bf16[32,16384]{1,0:T(8,128)(2,1)} collective-permute-done((bf16[32,16384]{1,0:T(8,128)(2,1)}, bf16[32,16384]{1,0:T(8,128)(2,1)}, u32[]{:S(2)}, u32[]{:S(2)}) %collective-permute-start.10) | collective-permute-done | bytes 1048608 | tf_op jit(solution)/shard_map/ppermute | solution.py:35
  30.0 3.2 %collective-permute-start.13 = (bf16[32,16384]{1,0:T(8,128)(2,1)}, bf16[32,16384]{1,0:T(8,128)(2,1)}, u32[]{:S(2)}, u32[]{:S(2)}) collective-permute-start(bf16[32,16384]{1,0:T(8,128)(2,1)} %collective-permute-done.11.refs_2_), channel_id=1, source_target_pairs={{0,28},{4,0},{8,4},{12,8},{16,12},{20,16},{24,20},{28,24},{1,29},{... | collective-permute-start | bytes 3145736 | tf_op jit(solution)/shard_map/ppermute | solution.py:35
  33.3 4.8 %shard_map.86 = bf16[32,4,3,32,128]{4,3,2,1,0:T(8,128)(2,1)} custom-call(s32[32,4]{1,0:T(8,128)} %copy.39.wanted_ref, bf16[32,16384]{1,0:T(8,128)(2,1)} %bitcast.36, bf16[32,16384]{1,0:T(8,128)(2,1)} %collective-permute-done.10.refs_1_, bf16[32,16384]{1,0:T(8,128)(2,1)} %collective-permute-done.11.refs_2_), custom_call_target="tpu_custom_call" | custom-call | flops 20000000000 | bytes 6291456 | tf_op jit(solution)/shard_map/pallas_call | solution.py:82
  38.0 7.6 %all-to-all-start.1 = ((bf16[32,4,3,32,128]{4,3,2,1,0:T(8,128)(2,1)}), bf16[32,4,3,32,128]{4,3,2,1,0:T(8,128)(2,1)S(1)}, u32[]{:S(2)}, u32[]{:S(2)}) async-start(bf16[32,4,3,32,128]{4,3,2,1,0:T(8,128)(2,1)} %shard_map.86), calls=%async_computation.1 | async-start | bytes 6291456 | tf_op jit(solution)/shard_map/all_to_all | solution.py:39
  45.7 10.2 %collective-permute-done.12.refs_0_ = bf16[32,16384]{1,0:T(8,128)(2,1)} collective-permute-done((bf16[32,16384]{1,0:T(8,128)(2,1)}, bf16[32,16384]{1,0:T(8,128)(2,1)}, u32[]{:S(2)}, u32[]{:S(2)}) %collective-permute-start.12) | collective-permute-done | bytes 1048608 | tf_op jit(solution)/shard_map/ppermute | solution.py:35
  55.9 3.2 %collective-permute-start.15 = (bf16[32,16384]{1,0:T(8,128)(2,1)}, bf16[32,16384]{1,0:T(8,128)(2,1)}, u32[]{:S(2)}, u32[]{:S(2)}) collective-permute-start(bf16[32,16384]{1,0:T(8,128)(2,1)} %collective-permute-done.13.refs_1_), channel_id=1, source_target_pairs={{0,28},{4,0},{8,4},{12,8},{16,12},{20,16},{24,20},{28,24},{1,29},{... | collective-permute-start | bytes 3145736 | tf_op jit(solution)/shard_map/ppermute | solution.py:35
  59.2 21.7 %collective-permute-done.14.refs_2_ = bf16[32,16384]{1,0:T(8,128)(2,1)} collective-permute-done((bf16[32,16384]{1,0:T(8,128)(2,1)}, bf16[32,16384]{1,0:T(8,128)(2,1)}, u32[]{:S(2)}, u32[]{:S(2)}) %collective-permute-start.14) | collective-permute-done | bytes 1048608 | tf_op jit(solution)/shard_map/ppermute | solution.py:35
  80.9 5.3 %shard_map.88 = bf16[32,4,4,32,128]{4,3,2,1,0:T(8,128)(2,1)} custom-call(s32[32,4]{1,0:T(8,128)} %copy.39.wanted_ref, bf16[32,16384]{1,0:T(8,128)(2,1)} %collective-permute-done.12.refs_0_, bf16[32,16384]{1,0:T(8,128)(2,1)} %collective-permute-done.13.refs_1_, bf16[32,16384]{1,0:T(8,128)(2,1)} %collective-permute-done.14.refs_2_, ...), custom_call_target="tpu_custom_call" | custom-call | flops 20000000000 | bytes 8388608 | tf_op jit(solution)/shard_map/pallas_call | solution.py:82
  86.2 3.2 %all-to-all-done.1.part = bf16[32,4,3,32,128]{4,3,2,1,0:T(8,128)(2,1)S(1)} async-done(((bf16[32,4,3,32,128]{4,3,2,1,0:T(8,128)(2,1)}), bf16[32,4,3,32,128]{4,3,2,1,0:T(8,128)(2,1)S(1)}, u32[]{:S(2)}, u32[]{:S(2)}) %all-to-all-start.1) | async-done | bytes 3145760 | tf_op jit(solution)/shard_map/all_to_all | solution.py:39
  89.4 4.6 %all-to-all-start.2 = ((bf16[32,4,4,32,128]{4,3,2,1,0:T(8,128)(2,1)}), bf16[32,4,4,32,128]{4,3,2,1,0:T(8,128)(2,1)}, u32[]{:S(2)}, u32[]{:S(2)}) async-start(bf16[32,4,4,32,128]{4,3,2,1,0:T(8,128)(2,1)} %shard_map.88), calls=%async_computation.2 | async-start | bytes 8388608 | tf_op jit(solution)/shard_map/all_to_all | solution.py:39
  94.1 3.2 %collective-permute-start.2 = (bf16[64,1024]{1,0:T(8,128)(2,1)S(1)}, bf16[64,1024]{1,0:T(8,128)(2,1)S(1)}, u32[]{:S(2)}, u32[]{:S(2)}) collective-permute-start(bf16[64,1024]{1,0:T(8,128)(2,1)S(1)} %pad_maximum_fusion.1), channel_id=1, source_target_pairs={{0,28},{4,0},{8,4},{12,8},{16,12},{20,16},{24,20},{28,24},{1,29},{... | collective-permute-start | bytes 393224 | tf_op jit(solution)/shard_map/ppermute | solution.py:35
  98.0 2.7 %collective-permute-done.1 = bf16[64,1024]{1,0:T(8,128)(2,1)S(1)} collective-permute-done((bf16[64,1024]{1,0:T(8,128)(2,1)S(1)}, bf16[64,1024]{1,0:T(8,128)(2,1)S(1)}, u32[]{:S(2)}, u32[]{:S(2)}) %collective-permute-start.1) | collective-permute-done | bytes 131104 | tf_op jit(solution)/shard_map/ppermute | solution.py:35
  100.7 3.2 %collective-permute-start.4 = (bf16[64,1024]{1,0:T(8,128)(2,1)S(1)}, bf16[64,1024]{1,0:T(8,128)(2,1)S(1)}, u32[]{:S(2)}, u32[]{:S(2)}) collective-permute-start(bf16[64,1024]{1,0:T(8,128)(2,1)S(1)} %collective-permute-done.2), channel_id=1, source_target_pairs={{0,28},{4,0},{8,4},{12,8},{16,12},{20,16},{24,20},{28,24},{1,29},{... | collective-permute-start | bytes 393224 | tf_op jit(solution)/shard_map/ppermute | solution.py:35
  105.3 1.6 collective-permute-done.3
  106.9 3.2 %collective-permute-start.6 = (bf16[64,1024]{1,0:T(8,128)(2,1)S(1)}, bf16[64,1024]{1,0:T(8,128)(2,1)S(1)}, u32[]{:S(2)}, u32[]{:S(2)}) collective-permute-start(bf16[64,1024]{1,0:T(8,128)(2,1)S(1)} %collective-permute-done.4), channel_id=1, source_target_pairs={{0,28},{4,0},{8,4},{12,8},{16,12},{20,16},{24,20},{28,24},{1,29},{... | collective-permute-start | bytes 393224 | tf_op jit(solution)/shard_map/ppermute | solution.py:35
  111.5 1.6 collective-permute-done.5
  113.1 3.3 %collective-permute-start.8 = (bf16[32,1024]{1,0:T(8,128)(2,1)S(1)}, bf16[32,1024]{1,0:T(8,128)(2,1)S(1)}, u32[]{:S(2)}, u32[]{:S(2)}) collective-permute-start(bf16[32,1024]{1,0:T(8,128)(2,1)S(1)} %slice.17), channel_id=1, source_target_pairs={{0,28},{4,0},{8,4},{12,8},{16,12},{20,16},{24,20},{28,24},{1,29},{... | collective-permute-start | bytes 196616 | tf_op jit(solution)/shard_map/ppermute | solution.py:35
  117.8 0.8 collective-permute-done.7
  119.9 1.9 slice.18
  121.7 1.9 slice.19
  123.6 3.2 %collective-permute-start.17 = (bf16[16,16384]{1,0:T(8,128)(2,1)}, bf16[16,16384]{1,0:T(8,128)(2,1)}, u32[]{:S(2)}, u32[]{:S(2)}) collective-permute-start(bf16[16,16384]{1,0:T(8,128)(2,1)} %slice.19), channel_id=1, source_target_pairs={{0,28},{4,0},{8,4},{12,8},{16,12},{20,16},{24,20},{28,24},{1,29},{... | collective-permute-start | bytes 1572872 | tf_op jit(solution)/shard_map/ppermute | solution.py:35
  127.0 3.2 %pad_maximum_fusion = bf16[16,2,32,1024]{3,2,1,0:T(8,128)(2,1)} fusion(bf16[16,1,32,1024]{3,2,1,0:T(8,128)(2,1)} %bitcast.9, bf16[16,1,32,1024]{3,2,1,0:T(8,128)(2,1)} %bitcast.7), kind=kLoop, calls=%fused_computation | loop fusion | flops 1048576 | bytes 4194304 | tf_op jit(solution)/shard_map/stack | solution.py:299
  130.2 3.0 %shard_map.87 = (bf16[384,1024]{1,0:T(8,128)(2,1)S(1)}, bf16[1024,384]{1,0:T(8,128)(2,1)S(1)}) custom-call(s32[1]{0:T(128)} %bitcast.core_ref, s32[8,4]{1,0:T(8,128)S(1)} %copy.44.tgt_ref, s32[8]{0:T(128)S(1)} %bitcast.27, bf16[8,4,128,128]{3,2,1,0:T(8,128)(2,1)S(1)} %bitcast.25, bf16[32,4,3,32,128]{4,3,2,1,0:T(8,128)(2,1)S(1)} %all-to-all-done.1.part), custom_call_target="tpu_custom_call" | custom-call | flops 3000000000 | bytes 8388608 | tf_op jit(solution)/shard_map/pallas_call | solution.py:136
  133.1 0.9 copy-done.5
  134.0 0.9 copy-done.7
  135.6 2.0 collective-permute-done.16.refs_0_
  137.6 1.1 collective-permute-done.17.refs_1_
  138.7 3.3 %shard_map.90 = bf16[32,4,1,32,128]{4,3,2,1,0:T(8,128)(2,1)} custom-call(s32[32,4]{1,0:T(8,128)} %copy.43.wanted_ref, bf16[16,16384]{1,0:T(8,128)(2,1)} %collective-permute-done.16.refs_0_, bf16[16,16384]{1,0:T(8,128)(2,1)} %collective-permute-done.17.refs_1_), custom_call_target="tpu_custom_call" | custom-call | flops 1000000000 | bytes 2097152 | tf_op jit(solution)/shard_map/pallas_call | solution.py:82
  142.1 11.0 %all-to-all-done.2.part = bf16[32,4,4,32,128]{4,3,2,1,0:T(8,128)(2,1)} async-done(((bf16[32,4,4,32,128]{4,3,2,1,0:T(8,128)(2,1)}), bf16[32,4,4,32,128]{4,3,2,1,0:T(8,128)(2,1)}, u32[]{:S(2)}, u32[]{:S(2)}) %all-to-all-start.2) | async-done | bytes 4194336 | tf_op jit(solution)/shard_map/all_to_all | solution.py:39
  153.0 3.7 %all-to-all-start.3 = ((bf16[32,4,1,32,128]{4,3,2,1,0:T(8,128)(2,1)}), bf16[32,4,1,32,128]{4,3,2,1,0:T(8,128)(2,1)S(1)}, u32[]{:S(2)}, u32[]{:S(2)}) async-start(bf16[32,4,1,32,128]{4,3,2,1,0:T(8,128)(2,1)} %shard_map.90), calls=%async_computation.3 | async-start | bytes 2097152 | tf_op jit(solution)/shard_map/all_to_all | solution.py:39
  156.8 6.6 %shard_map.89 = (bf16[512,1024]{1,0:T(8,128)(2,1)}, bf16[1024,512]{1,0:T(8,128)(2,1)}) custom-call(s32[1]{0:T(128)} %bitcast.core_ref, s32[8,4]{1,0:T(8,128)} %copy-done, s32[8]{0:T(128)} %bitcast.26, bf16[8,4,128,128]{3,2,1,0:T(8,128)(2,1)} %bitcast.23, bf16[32,4,4,32,128]{4,3,2,1,0:T(8,128)(2,1)} %all-to-all-done.2.part), custom_call_target="tpu_custom_call" | custom-call | flops 3000000000 | bytes 8388608 | tf_op jit(solution)/shard_map/pallas_call | solution.py:136
  163.4 9.7 %all-to-all-done.3.refs_5_ = bf16[32,4,1,32,128]{4,3,2,1,0:T(8,128)(2,1)S(1)} async-done(((bf16[32,4,1,32,128]{4,3,2,1,0:T(8,128)(2,1)}), bf16[32,4,1,32,128]{4,3,2,1,0:T(8,128)(2,1)S(1)}, u32[]{:S(2)}, u32[]{:S(2)}) %all-to-all-start.3) | async-done | bytes 1048608 | tf_op jit(solution)/shard_map/all_to_all | solution.py:39
  173.0 1.0 copy-done.9
  174.0 10.9 %shard_map.91 = (bf16[1024,1024]{1,0:T(8,128)(2,1)}, bf16[8,2,8,32,128]{4,3,2,1,0:T(8,128)(2,1)S(1)}, bf16[8,2,8,32,128]{4,3,2,1,0:T(8,128)(2,1)S(1)}) custom-call(s32[1]{0:T(128)} %bitcast.core_ref, s32[8,4]{1,0:T(8,128)S(1)} %copy-done.1, s32[8]{0:T(128)S(1)} %bitcast.28, bf16[384,1024]{1,0:T(8,128)(2,1)S(1)} %copy-done.6, ...), custom_call_target="tpu_custom_call" | custom-call | flops 6000000000 | bytes 20971520 | tf_op jit(solution)/shard_map/pallas_call | solution.py:231
  185.0 2.6 %collective-permute-done.18 = bf16[8,2,8,32,128]{4,3,2,1,0:T(8,128)(2,1)S(1)} collective-permute-done((bf16[8,2,8,32,128]{4,3,2,1,0:T(8,128)(2,1)S(1)}, bf16[8,2,8,32,128]{4,3,2,1,0:T(8,128)(2,1)S(1)}, u32[]{:S(2)}, u32[]{:S(2)}) %collective-permute-start.18) | collective-permute-done | bytes 1048608 | tf_op jit(solution)/shard_map/ppermute | solution.py:279
  187.7 1.3 add_convert_fusion
  189.0 4.2 %all-to-all-start.4 = ((bf16[16,8,32,128]{3,2,1,0:T(8,128)(2,1)}), bf16[16,8,32,128]{3,2,1,0:T(8,128)(2,1)S(1)}, u32[]{:S(2)}, u32[]{:S(2)}) async-start(bf16[16,8,32,128]{3,2,1,0:T(8,128)(2,1)} %bitcast.14), calls=%async_computation.4 | async-start | bytes 2097152 | tf_op jit(solution)/shard_map/all_to_all | solution.py:39
  193.1 18.5 %all-to-all-done.4.came_ref = bf16[16,8,32,128]{3,2,1,0:T(8,128)(2,1)S(1)} async-done(((bf16[16,8,32,128]{3,2,1,0:T(8,128)(2,1)}), bf16[16,8,32,128]{3,2,1,0:T(8,128)(2,1)S(1)}, u32[]{:S(2)}, u32[]{:S(2)}) %all-to-all-start.4) | async-done | bytes 1048608 | tf_op jit(solution)/shard_map/all_to_all | solution.py:39
  211.7 14.6 %all_to_all.35 = f32[8,32,128]{2,1,0:T(8,128)S(1)} all-to-all(f32[8,32,128]{2,1,0:T(8,128)S(1)} %shard_map.92), channel_id=1, replica_groups=mesh['ylo'=2,'x'=4,'z'=8,'yhi'=2,'core'=2] {'z'}, dimensions={0} | all-to-all | bytes 262144 | tf_op jit(solution)/shard_map/all_to_all | solution.py:39
  226.4 10.3 %all_to_all.36 = f32[8,32,128]{2,1,0:T(8,128)S(1)} all-to-all(f32[8,32,128]{2,1,0:T(8,128)S(1)} %broadcast_in_dim.18), channel_id=1, replica_groups=mesh['ylo'=2,'x'=4,'z'=8,'yhi'=2,'core'=2] {'ylo','x'}, dimensions={0} | all-to-all | bytes 262144 | tf_op jit(solution)/shard_map/all_to_all | solution.py:39
  (57 shorter events, 8.5 us)
Async XLA Ops:
  0.6 29.4 %collective-permute-start.10 = (bf16[32,16384]{1,0:T(8,128)(2,1)}, bf16[32,16384]{1,0:T(8,128)(2,1)}, u32[]{:S(2)}, u32[]{:S(2)}) collective-permute-start(bf16[32,16384]{1,0:T(8,128)(2,1)} %bitcast.34), channel_id=1, source_target_pairs={{0,4},{4,8},{8,12},{12,16},{16,20},{20,24},{24,28},{28,0},{1,5},{5... | collective-permute-start | bytes 3145736 | tf_op jit(solution)/shard_map/ppermute | solution.py:35
  2.6 27.4 %collective-permute-start.11 = (bf16[32,16384]{1,0:T(8,128)(2,1)}, bf16[32,16384]{1,0:T(8,128)(2,1)}, u32[]{:S(2)}, u32[]{:S(2)}) collective-permute-start(bf16[32,16384]{1,0:T(8,128)(2,1)} %bitcast.35), channel_id=1, source_target_pairs={{0,28},{4,0},{8,4},{12,8},{16,12},{20,16},{24,20},{28,24},{1,29},{... | collective-permute-start | bytes 3145736 | tf_op jit(solution)/shard_map/ppermute | solution.py:35
  6.7 15.6 %collective-permute-start = (bf16[32,1024]{1,0:T(8,128)(2,1)}, bf16[32,1024]{1,0:T(8,128)(2,1)S(1)}, u32[]{:S(2)}, u32[]{:S(2)}) collective-permute-start(bf16[32,1024]{1,0:T(8,128)(2,1)} %param.12), channel_id=1, source_target_pairs={{0,130},{2,128},{128,2},{130,0},{1,131},{3,129},{129,3},{131,1},{4... | collective-permute-start | bytes 196616 | tf_op jit(solution)/shard_map/ppermute | solution.py:289
  11.0 11.1 %all-to-all-start = ((s32[32,1,4]{2,1,0:T(1,128)}), s32[32,1,4]{2,1,0:T(1,128)S(1)}, u32[]{:S(2)}, u32[]{:S(2)}) async-start(s32[32,1,4]{2,1,0:T(1,128)} %bitcast.4), calls=%async_computation | async-start | bytes 32768 | tf_op jit(solution)/shard_map/all_to_all | solution.py:39
  30.0 25.9 %collective-permute-start.12 = (bf16[32,16384]{1,0:T(8,128)(2,1)}, bf16[32,16384]{1,0:T(8,128)(2,1)}, u32[]{:S(2)}, u32[]{:S(2)}) collective-permute-start(bf16[32,16384]{1,0:T(8,128)(2,1)} %collective-permute-done.10.refs_1_), channel_id=1, source_target_pairs={{0,4},{4,8},{8,12},{12,16},{16,20},{20,24},{24,28},{28,0},{1,5},{5... | collective-permute-start | bytes 3145736 | tf_op jit(solution)/shard_map/ppermute | solution.py:35
  30.0 25.9 %collective-permute-start.13 = (bf16[32,16384]{1,0:T(8,128)(2,1)}, bf16[32,16384]{1,0:T(8,128)(2,1)}, u32[]{:S(2)}, u32[]{:S(2)}) collective-permute-start(bf16[32,16384]{1,0:T(8,128)(2,1)} %collective-permute-done.11.refs_2_), channel_id=1, source_target_pairs={{0,28},{4,0},{8,4},{12,8},{16,12},{20,16},{24,20},{28,24},{1,29},{... | collective-permute-start | bytes 3145736 | tf_op jit(solution)/shard_map/ppermute | solution.py:35
  38.0 51.3 %all-to-all-start.1 = ((bf16[32,4,3,32,128]{4,3,2,1,0:T(8,128)(2,1)}), bf16[32,4,3,32,128]{4,3,2,1,0:T(8,128)(2,1)S(1)}, u32[]{:S(2)}, u32[]{:S(2)}) async-start(bf16[32,4,3,32,128]{4,3,2,1,0:T(8,128)(2,1)} %shard_map.86), calls=%async_computation.1 | async-start | bytes 6291456 | tf_op jit(solution)/shard_map/all_to_all | solution.py:39
  55.9 24.9 %collective-permute-start.14 = (bf16[32,16384]{1,0:T(8,128)(2,1)}, bf16[32,16384]{1,0:T(8,128)(2,1)}, u32[]{:S(2)}, u32[]{:S(2)}) collective-permute-start(bf16[32,16384]{1,0:T(8,128)(2,1)} %collective-permute-done.12.refs_0_), channel_id=1, source_target_pairs={{0,4},{4,8},{8,12},{12,16},{16,20},{20,24},{24,28},{28,0},{1,5},{5... | collective-permute-start | bytes 3145736 | tf_op jit(solution)/shard_map/ppermute | solution.py:35
  55.9 24.9 %collective-permute-start.15 = (bf16[32,16384]{1,0:T(8,128)(2,1)}, bf16[32,16384]{1,0:T(8,128)(2,1)}, u32[]{:S(2)}, u32[]{:S(2)}) collective-permute-start(bf16[32,16384]{1,0:T(8,128)(2,1)} %collective-permute-done.13.refs_1_), channel_id=1, source_target_pairs={{0,28},{4,0},{8,4},{12,8},{16,12},{20,16},{24,20},{28,24},{1,29},{... | collective-permute-start | bytes 3145736 | tf_op jit(solution)/shard_map/ppermute | solution.py:35
  89.4 63.7 %all-to-all-start.2 = ((bf16[32,4,4,32,128]{4,3,2,1,0:T(8,128)(2,1)}), bf16[32,4,4,32,128]{4,3,2,1,0:T(8,128)(2,1)}, u32[]{:S(2)}, u32[]{:S(2)}) async-start(bf16[32,4,4,32,128]{4,3,2,1,0:T(8,128)(2,1)} %shard_map.88), calls=%async_computation.2 | async-start | bytes 8388608 | tf_op jit(solution)/shard_map/all_to_all | solution.py:39
  94.0 6.7 %collective-permute-start.1 = (bf16[64,1024]{1,0:T(8,128)(2,1)S(1)}, bf16[64,1024]{1,0:T(8,128)(2,1)S(1)}, u32[]{:S(2)}, u32[]{:S(2)}) collective-permute-start(bf16[64,1024]{1,0:T(8,128)(2,1)S(1)} %pad_maximum_fusion.1), channel_id=1, source_target_pairs={{0,4},{4,8},{8,12},{12,16},{16,20},{20,24},{24,28},{28,0},{1,5},{5... | collective-permute-start | bytes 393224 | tf_op jit(solution)/shard_map/ppermute | solution.py:35
  94.1 6.6 %collective-permute-start.2 = (bf16[64,1024]{1,0:T(8,128)(2,1)S(1)}, bf16[64,1024]{1,0:T(8,128)(2,1)S(1)}, u32[]{:S(2)}, u32[]{:S(2)}) collective-permute-start(bf16[64,1024]{1,0:T(8,128)(2,1)S(1)} %pad_maximum_fusion.1), channel_id=1, source_target_pairs={{0,28},{4,0},{8,4},{12,8},{16,12},{20,16},{24,20},{28,24},{1,29},{... | collective-permute-start | bytes 393224 | tf_op jit(solution)/shard_map/ppermute | solution.py:35
  98.0 28.9 %copy-start.10 = (s32[1,1,8,4]{2,3,1,0:T(4,128)S(1)}, s32[1,1,8,4]{2,3,1,0:T(4,128)}, u32[]{:S(2)}) copy-start(s32[1,1,8,4]{2,3,1,0:T(4,128)} %param.8) | copy-start | bytes 388
  100.7 6.2 %collective-permute-start.3 = (bf16[64,1024]{1,0:T(8,128)(2,1)S(1)}, bf16[64,1024]{1,0:T(8,128)(2,1)S(1)}, u32[]{:S(2)}, u32[]{:S(2)}) collective-permute-start(bf16[64,1024]{1,0:T(8,128)(2,1)S(1)} %collective-permute-done.1), channel_id=1, source_target_pairs={{0,4},{4,8},{8,12},{12,16},{16,20},{20,24},{24,28},{28,0},{1,5},{5... | collective-permute-start | bytes 393224 | tf_op jit(solution)/shard_map/ppermute | solution.py:35
  100.7 6.2 %collective-permute-start.4 = (bf16[64,1024]{1,0:T(8,128)(2,1)S(1)}, bf16[64,1024]{1,0:T(8,128)(2,1)S(1)}, u32[]{:S(2)}, u32[]{:S(2)}) collective-permute-start(bf16[64,1024]{1,0:T(8,128)(2,1)S(1)} %collective-permute-done.2), channel_id=1, source_target_pairs={{0,28},{4,0},{8,4},{12,8},{16,12},{20,16},{24,20},{28,24},{1,29},{... | collective-permute-start | bytes 393224 | tf_op jit(solution)/shard_map/ppermute | solution.py:35
  106.9 6.2 %collective-permute-start.5 = (bf16[64,1024]{1,0:T(8,128)(2,1)S(1)}, bf16[64,1024]{1,0:T(8,128)(2,1)S(1)}, u32[]{:S(2)}, u32[]{:S(2)}) collective-permute-start(bf16[64,1024]{1,0:T(8,128)(2,1)S(1)} %collective-permute-done.3), channel_id=1, source_target_pairs={{0,4},{4,8},{8,12},{12,16},{16,20},{20,24},{24,28},{28,0},{1,5},{5... | collective-permute-start | bytes 393224 | tf_op jit(solution)/shard_map/ppermute | solution.py:35
  106.9 6.2 %collective-permute-start.6 = (bf16[64,1024]{1,0:T(8,128)(2,1)S(1)}, bf16[64,1024]{1,0:T(8,128)(2,1)S(1)}, u32[]{:S(2)}, u32[]{:S(2)}) collective-permute-start(bf16[64,1024]{1,0:T(8,128)(2,1)S(1)} %collective-permute-done.4), channel_id=1, source_target_pairs={{0,28},{4,0},{8,4},{12,8},{16,12},{20,16},{24,20},{28,24},{1,29},{... | collective-permute-start | bytes 393224 | tf_op jit(solution)/shard_map/ppermute | solution.py:35
  113.1 5.5 %collective-permute-start.7 = (bf16[32,1024]{1,0:T(8,128)(2,1)S(1)}, bf16[32,1024]{1,0:T(8,128)(2,1)S(1)}, u32[]{:S(2)}, u32[]{:S(2)}) collective-permute-start(bf16[32,1024]{1,0:T(8,128)(2,1)S(1)} %slice.16), channel_id=1, source_target_pairs={{0,4},{4,8},{8,12},{12,16},{16,20},{20,24},{24,28},{28,0},{1,5},{5... | collective-permute-start | bytes 196616 | tf_op jit(solution)/shard_map/ppermute | solution.py:35
  113.1 6.1 %collective-permute-start.8 = (bf16[32,1024]{1,0:T(8,128)(2,1)S(1)}, bf16[32,1024]{1,0:T(8,128)(2,1)S(1)}, u32[]{:S(2)}, u32[]{:S(2)}) collective-permute-start(bf16[32,1024]{1,0:T(8,128)(2,1)S(1)} %slice.17), channel_id=1, source_target_pairs={{0,28},{4,0},{8,4},{12,8},{16,12},{20,16},{24,20},{28,24},{1,29},{... | collective-permute-start | bytes 196616 | tf_op jit(solution)/shard_map/ppermute | solution.py:35
  119.8 7.1 %collective-permute-start.9 = (bf16[512,1024]{1,0:T(8,128)(2,1)}, bf16[512,1024]{1,0:T(8,128)(2,1)}, u32[]{:S(2)}, u32[]{:S(2)}) collective-permute-start(bf16[512,1024]{1,0:T(8,128)(2,1)} %constant_dynamic-update-slice_fusion), channel_id=1, source_target_pairs={{0,1},{1,0},{2,3},{3,2},{4,5},{5,4},{6,7},{7,6},{8,9},{9,8},{10,11... | collective-permute-start | bytes 3145736 | tf_op jit(solution)/shard_map/ppermute | solution.py:297
  121.7 15.9 %collective-permute-start.16 = (bf16[16,16384]{1,0:T(8,128)(2,1)}, bf16[16,16384]{1,0:T(8,128)(2,1)}, u32[]{:S(2)}, u32[]{:S(2)}) collective-permute-start(bf16[16,16384]{1,0:T(8,128)(2,1)} %slice.18), channel_id=1, source_target_pairs={{0,4},{4,8},{8,12},{12,16},{16,20},{20,24},{24,28},{28,0},{1,5},{5... | collective-permute-start | bytes 1572872 | tf_op jit(solution)/shard_map/ppermute | solution.py:35
  123.6 15.1 %collective-permute-start.17 = (bf16[16,16384]{1,0:T(8,128)(2,1)}, bf16[16,16384]{1,0:T(8,128)(2,1)}, u32[]{:S(2)}, u32[]{:S(2)}) collective-permute-start(bf16[16,16384]{1,0:T(8,128)(2,1)} %slice.19), channel_id=1, source_target_pairs={{0,28},{4,0},{8,4},{12,8},{16,12},{20,16},{24,20},{28,24},{1,29},{... | collective-permute-start | bytes 1572872 | tf_op jit(solution)/shard_map/ppermute | solution.py:35
  126.9 3.2 %copy-start = (s32[8,4]{1,0:T(8,128)}, s32[8,4]{1,0:T(8,128)S(1)}, u32[]{:S(2)}) copy-start(s32[8,4]{1,0:T(8,128)S(1)} %copy.44.tgt_ref) | copy-start | bytes 388
  126.9 3.2 %copy-start.2 = (bf16[1,1,8,4,128,128]{5,4,3,2,1,0:T(8,128)(2,1)S(1)}, bf16[1,1,8,4,128,128]{5,4,3,2,1,0:T(8,128)(2,1)}, u32[]{:S(2)}) copy-start(bf16[1,1,8,4,128,128]{5,4,3,2,1,0:T(8,128)(2,1)} %param.11) | copy-start | bytes 3145732
  126.9 3.2 %copy-start.3 = (s32[1,1,8]{2,1,0:T(1,128)S(1)}, s32[1,1,8]{2,1,0:T(1,128)}, u32[]{:S(2)}) copy-start(s32[1,1,8]{2,1,0:T(1,128)} %param.10) | copy-start | bytes 100
  133.1 0.9 copy-start.5
  134.0 0.9 copy-start.7
  153.0 20.0 %all-to-all-start.3 = ((bf16[32,4,1,32,128]{4,3,2,1,0:T(8,128)(2,1)}), bf16[32,4,1,32,128]{4,3,2,1,0:T(8,128)(2,1)S(1)}, u32[]{:S(2)}, u32[]{:S(2)}) async-start(bf16[32,4,1,32,128]{4,3,2,1,0:T(8,128)(2,1)} %shard_map.90), calls=%async_computation.3 | async-start | bytes 2097152 | tf_op jit(solution)/shard_map/all_to_all | solution.py:39
  156.8 17.3 %copy-start.1 = (s32[8,4]{1,0:T(8,128)S(1)}, s32[8,4]{1,0:T(8,128)}, u32[]{:S(2)}) copy-start(s32[8,4]{1,0:T(8,128)} %copy-done) | copy-start | bytes 388
  156.8 17.3 %copy-start.4 = (s32[1,1,8]{2,1,0:T(1,128)S(1)}, s32[1,1,8]{2,1,0:T(1,128)}, u32[]{:S(2)}) copy-start(s32[1,1,8]{2,1,0:T(1,128)} %param.10) | copy-start | bytes 100
  156.8 17.3 %copy-start.6 = (bf16[384,1024]{1,0:T(8,128)(2,1)S(1)}, bf16[384,1024]{1,0:T(8,128)(2,1)}, u32[]{:S(2)}) copy-start(bf16[384,1024]{1,0:T(8,128)(2,1)} %copy-done.5) | copy-start | bytes 2359300
  156.8 17.3 %copy-start.8 = (bf16[1024,384]{1,0:T(8,128)(2,1)S(1)}, bf16[1024,384]{1,0:T(8,128)(2,1)}, u32[]{:S(2)}) copy-start(bf16[1024,384]{1,0:T(8,128)(2,1)} %copy-done.7) | copy-start | bytes 2359300
  173.0 1.0 copy-start.9
  184.9 2.7 %collective-permute-start.18 = (bf16[8,2,8,32,128]{4,3,2,1,0:T(8,128)(2,1)S(1)}, bf16[8,2,8,32,128]{4,3,2,1,0:T(8,128)(2,1)S(1)}, u32[]{:S(2)}, u32[]{:S(2)}) collective-permute-start(bf16[8,2,8,32,128]{4,3,2,1,0:T(8,128)(2,1)S(1)} %get-tuple-element.27), channel_id=1, source_target_pairs={{0,1},{1,0},{2,3},{3,2},{4,5},{5,4},{6,7},{7,6},{8,9},{9,8},{10,11... | collective-permute-start | bytes 3145736 | tf_op jit(solution)/shard_map/ppermute | solution.py:279
  189.0 22.6 %all-to-all-start.4 = ((bf16[16,8,32,128]{3,2,1,0:T(8,128)(2,1)}), bf16[16,8,32,128]{3,2,1,0:T(8,128)(2,1)S(1)}, u32[]{:S(2)}, u32[]{:S(2)}) async-start(bf16[16,8,32,128]{3,2,1,0:T(8,128)(2,1)} %bitcast.14), calls=%async_computation.4 | async-start | bytes 2097152 | tf_op jit(solution)/shard_map/all_to_all | solution.py:39

commit v8 on v7

--- a/solution.py
+++ b/solution.py
@@ -15,7 +15,7 @@
 PARTS = ((0, 1, -1), (2, -2, 3, -3), (4,))
 ORDER = tuple(d for part in PARTS for d in part)
 LANES = 4
-EARLY_MIB = (20, 60)
+EARLY_MIB = (20, 20)
 LAYER_MIB = 50
 VMEM = pl.BlockSpec(memory_space=pltpu.VMEM)
 SMEM = pl.BlockSpec(memory_space=pltpu.SMEM)
@@ -151,9 +151,9 @@
 
 
 def layer_kernel(num_early, core_ref, tgt_ref, count_ref, *refs):
-    early, refs = refs[: 2 * num_early], refs[2 * num_early :]
-    vals_hbm, part_hbm, weight_hbm, cot_hbm, act_hbm, kept_hbm, gone_hbm = refs[:7]
-    vals, part, weight, cot, act, kept, gone, acc, live, turned, plain, dpre, sems, block_sems, out_sems = refs[7:]
+    early, refs = refs[:num_early], refs[num_early:]
+    vals_hbm, part_hbm, begun_hbm, weight_hbm, cot_hbm, act_hbm, kept_hbm, gone_hbm = refs[:8]
+    vals, part, begun, weight, cot, act, kept, gone, acc, live, turned, plain, dpre, sems, block_sems, out_sems = refs[8:]
     blocks = out_sems.shape[1]
     step = act.shape[0] // blocks
     vals_copy = pltpu.make_async_copy(vals_hbm, vals, sems.at[0])
@@ -164,15 +164,13 @@
     for index, copies in enumerate(block_copies):
         at = slice(index * step, index * step + step)
         copies.append(pltpu.make_async_copy(cot_hbm.at[at], cot.at[at], block_sems.at[index, 0]))
+        copies.append(pltpu.make_async_copy(begun_hbm.at[at], begun.at[at], block_sems.at[index, 1]))
         low = 0
         for number in range(num_early):
-            columns = slice(low, low + early[2 * number].shape[0])
-            low = columns.stop
-            copies.append(
-                pltpu.make_async_copy(early[2 * number + 1].at[at], plain.at[at, columns], block_sems.at[index, 1 + number])
-            )
+            rows = slice(low, low + early[number].shape[0])
+            low = rows.stop
             if index == 0:
-                turned_copies.append(pltpu.make_async_copy(early[2 * number], turned.at[columns], sems.at[3 + number]))
+                turned_copies.append(pltpu.make_async_copy(early[number], turned.at[rows], sems.at[3 + number]))
     for copy in (vals_copy, part_copy, weight_copy, *sum(block_copies, []), *turned_copies):
         copy.start()
     vals_copy.wait()
@@ -183,7 +181,7 @@
         at = slice(first, first + width)
         value = acc[:, at]
         turned[low:, at] = value.astype(turned.dtype)
-        plain[at, low:] = value.T.astype(plain.dtype)
+        plain[at] = value.T.astype(plain.dtype)
     weight_copy.wait()
     out_copies = []
 
@@ -195,7 +193,7 @@
         at = slice(index * step, index * step + step)
         for copy in block_copies[index]:
             copy.wait()
-        preact = jnp.dot(plain[at], weight[...], preferred_element_type=jnp.float32)
+        preact = begun[at] + jnp.dot(plain[at], weight[...], preferred_element_type=jnp.float32)
         sigmoid_val = jax.nn.sigmoid(preact)
         act[at] = (preact * sigmoid_val).astype(act.dtype)
         send(act.at[at], act_hbm.at[at], out_sems.at[0, index])
@@ -222,24 +220,24 @@
         copy.wait()
 
 
-def layer(core, targets, counts, values, part, early, weight, cotangent):
+def layer(core, targets, counts, values, part, early, begun, weight, cotangent):
     tgt_rows, width = cotangent.shape
-    feats = weight.shape[0]
+    late = weight.shape[0]
+    feats = late + sum(value.shape[0] for value in early)
     cut = (8, 2, ZN, part.shape[3], width // 8)
-    early = [value for pair in early for value in pair]
-    late = feats - sum(value.shape[0] for value in early[::2])
     return pl.pallas_call(
-        functools.partial(layer_kernel, len(early) // 2),
+        functools.partial(layer_kernel, len(early)),
         out_shape=(
             jax.ShapeDtypeStruct((tgt_rows, width), jnp.bfloat16),
             jax.ShapeDtypeStruct(cut, jnp.bfloat16),
             jax.ShapeDtypeStruct(cut, jnp.bfloat16),
         ),
-        in_specs=[SMEM] * 3 + [HBM] * (len(early) + 4),
+        in_specs=[SMEM] * 3 + [HBM] * (len(early) + 5),
         out_specs=(HBM, HBM, HBM),
         scratch_shapes=[
             pltpu.VMEM(values.shape, values.dtype),
             pltpu.VMEM(part.shape, part.dtype),
+            pltpu.VMEM(begun.shape, begun.dtype),
             pltpu.VMEM(weight.shape, weight.dtype),
             pltpu.VMEM((tgt_rows, width), cotangent.dtype),
             pltpu.VMEM((tgt_rows, width), jnp.bfloat16),
@@ -248,15 +246,15 @@
             pltpu.VMEM((late, tgt_rows + values.shape[-1]), jnp.float32),
             pltpu.SMEM((values.shape[0] * values.shape[1],), jnp.int32),
             pltpu.VMEM((feats, tgt_rows), jnp.bfloat16),
-            pltpu.VMEM((tgt_rows, feats), jnp.bfloat16),
+            pltpu.VMEM((tgt_rows, late), jnp.bfloat16),
             pltpu.VMEM((tgt_rows, width), jnp.bfloat16),
-            pltpu.SemaphoreType.DMA((3 + len(early) // 2,)),
-            pltpu.SemaphoreType.DMA((4, 1 + len(early) // 2)),
+            pltpu.SemaphoreType.DMA((3 + len(early),)),
+            pltpu.SemaphoreType.DMA((4, 2)),
             pltpu.SemaphoreType.DMA((3, 4)),
         ],
         compiler_params=params(LAYER_MIB),
         cost_estimate=cost(6 * 10**9, 20 * 2**20),
-    )(core, targets, counts, *early, values, part, weight, cotangent)
+    )(core, targets, counts, *early, values, part, begun, weight, cotangent)
 
 
 def sum_plane_kernel(z_ref, came_ref, out_ref):
@@ -316,7 +314,10 @@
         part = exchange(pick(wanted, [held[d] for d in distances], block_size, flops), PLANE)
         if distances != PARTS[-1]:
             early.append(aggregate(core, targets, counts, values, part, tgt_rows, EARLY_MIB[len(early)]))
-    activations, kept, gone = layer(core, targets, counts, values, part, early, weight_in, cotangent)
+    turned, plain = [pair[0] for pair in early], jnp.concatenate([pair[1] for pair in early], axis=1)
+    split = plain.shape[1]
+    begun = jnp.dot(plain, weight_in[:split], preferred_element_type=jnp.float32)
+    activations, kept, gone = layer(core, targets, counts, values, part, turned, begun, weight_in[split:], cotangent)
     weight_grad = sum_over_devices(kept, gone) / math.sqrt(tgt_rows * 256)
     return (activations, weight_grad)
 

time: 238 us -> 236 us (level)
  matrix products: 0 us -> 4.32 us
  Pallas kernels: 33.9 us -> 30.8 us
  waiting for transfers between devices: 99.1 us -> 96 us
  blocking collectives: 24.9 us -> 22.4 us
    all_to_all x5, waiting for transfers between devices: 48.3 us -> 39 us  [exchange(): return lax.all_to_all(value, axes, split_axis=0, concat_axis=0, tiled=True)]
    ppermute x16, waiting for transfers between devices: 48.1 us -> 54.4 us  [shift_z(): return lax.ppermute(value, 'z', [(i, (i + step) % ZN) for i in range(ZN)])]
    dot_general x0 -> x1, matrix products: none -> 4.32 us  [per_device(): jnp.dot(plain, weight_in[:split], preferred_element_type=jnp.float32)]
    all_to_all x5, starting transfers between devices: 25.2 us -> 28.3 us  [exchange(): return lax.all_to_all(value, axes, split_axis=0, concat_axis=0, tiled=True)]
    ppermute x16, starting transfers between devices: 28.8 us -> 26.2 us  [shift_z(): return lax.ppermute(value, 'z', [(i, (i + step) % ZN) for i in range(ZN)])]
    all_to_all x2, blocking collectives: 24.9 us -> 22.4 us  [exchange(): return lax.all_to_all(value, axes, split_axis=0, concat_axis=0, tiled=True)]
    unnamed x31 -> x29, local copies, waits for them, and re-layouts: 8.85 us -> 9.98 us
  transfers between devices with their start and end apart: 24 -> 24, of which waited for: 15 -> 16; matrix products, arithmetic and copies ran while one was open for 7% -> 9% of each run, Pallas kernels for 10% -> 9%
where the time goes in v8:
time: 236 us
  waiting for transfers between devices  96 us (41%)
  starting transfers between devices  57.7 us (24%)
  Pallas kernels  30.8 us (13%)
  blocking collectives  22.4 us (9%)
  local copies, waits for them, and re-layouts  17.5 us (7%)
  other arithmetic  5.97 us (3%)
  matrix products  4.32 us (2%)
    ppermute x16, waiting for transfers between devices, shift_z(): return lax.ppermute(value, 'z', [(i, (i + step) % ZN) for i in range(ZN)])  54.4 us
    all_to_all x5, waiting for transfers between devices, exchange(): return lax.all_to_all(value, axes, split_axis=0, concat_axis=0, tiled=True)  39 us
    all_to_all x5, starting transfers between devices, exchange(): return lax.all_to_all(value, axes, split_axis=0, concat_axis=0, tiled=True)  28.3 us
    ppermute x16, starting transfers between devices, shift_z(): return lax.ppermute(value, 'z', [(i, (i + step) % ZN) for i in range(ZN)])  26.2 us
    all_to_all x2, blocking collectives, exchange(): return lax.all_to_all(value, axes, split_axis=0, concat_axis=0, tiled=True)  22.4 us
    pallas_call x3, Pallas kernels, pick(): pl.pallas_call(functools.partial(pick_kernel, block, layout), out_shape=j...  13.4 us
    unnamed x29, local copies, waits for them, and re-layouts  9.98 us
    pallas_call x1, Pallas kernels, layer(): pl.pallas_call(functools.partial(layer_kernel, len(early)), out_shape=(ja...  9.25 us
  transfers between devices with their start and end apart: 24, of which 16 were waited for; matrix products, arithmetic and copies ran while one was open for 9% of the time, Pallas kernels for 9%

profile of v8, /device:TPU:2, one launch (start us, length us, event | category | flops | bytes accessed | tf_op | source)
XLA Modules:
  0.0 235.6 jit_solution(16134257108867277572)
XLA Ops:
  0.6 5.9 %collective-permute-start.11 = (bf16[32,16384]{1,0:T(8,128)(2,1)}, bf16[32,16384]{1,0:T(8,128)(2,1)}, u32[]{:S(2)}, u32[]{:S(2)}) collective-permute-start(bf16[32,16384]{1,0:T(8,128)(2,1)} %bitcast.35), channel_id=1, source_target_pairs={{0,28},{4,0},{8,4},{12,8},{16,12},{20,16},{24,20},{28,24},{1,29},{... | collective-permute-start | bytes 3145736 | tf_op jit(solution)/shard_map/ppermute | solution.py:35
  6.6 3.0 %collective-permute-start = (bf16[32,1024]{1,0:T(8,128)(2,1)}, bf16[32,1024]{1,0:T(8,128)(2,1)S(1)}, u32[]{:S(2)}, u32[]{:S(2)}) collective-permute-start(bf16[32,1024]{1,0:T(8,128)(2,1)} %param.12), channel_id=1, source_target_pairs={{0,130},{2,128},{128,2},{130,0},{1,131},{3,129},{129,3},{131,1},{4... | collective-permute-start | bytes 196616 | tf_op jit(solution)/shard_map/ppermute | solution.py:287
  10.9 5.1 %all-to-all-start = ((s32[32,1,4]{2,1,0:T(1,128)}), s32[32,1,4]{2,1,0:T(1,128)S(1)}, u32[]{:S(2)}, u32[]{:S(2)}) async-start(s32[32,1,4]{2,1,0:T(1,128)} %bitcast.4), calls=%async_computation | async-start | bytes 32768 | tf_op jit(solution)/shard_map/all_to_all | solution.py:39
  16.0 6.0 %all-to-all-done = s32[32,1,4]{2,1,0:T(1,128)S(1)} async-done(((s32[32,1,4]{2,1,0:T(1,128)}), s32[32,1,4]{2,1,0:T(1,128)S(1)}, u32[]{:S(2)}, u32[]{:S(2)}) %all-to-all-start) | async-done | bytes 544 | tf_op jit(solution)/shard_map/all_to_all | solution.py:39
  23.7 5.6 %collective-permute-done.11.refs_2_ = bf16[32,16384]{1,0:T(8,128)(2,1)} collective-permute-done((bf16[32,16384]{1,0:T(8,128)(2,1)}, bf16[32,16384]{1,0:T(8,128)(2,1)}, u32[]{:S(2)}, u32[]{:S(2)}) %collective-permute-start.11) | collective-permute-done | bytes 1048608 | tf_op jit(solution)/shard_map/ppermute | solution.py:35
  29.3 3.7 %collective-permute-start.13 = (bf16[32,16384]{1,0:T(8,128)(2,1)}, bf16[32,16384]{1,0:T(8,128)(2,1)}, u32[]{:S(2)}, u32[]{:S(2)}) collective-permute-start(bf16[32,16384]{1,0:T(8,128)(2,1)} %collective-permute-done.11.refs_2_), channel_id=1, source_target_pairs={{0,28},{4,0},{8,4},{12,8},{16,12},{20,16},{24,20},{28,24},{1,29},{... | collective-permute-start | bytes 3145736 | tf_op jit(solution)/shard_map/ppermute | solution.py:35
  33.0 4.7 %shard_map.86 = bf16[32,4,3,32,128]{4,3,2,1,0:T(8,128)(2,1)} custom-call(s32[32,4]{1,0:T(8,128)} %copy.39.wanted_ref, bf16[32,16384]{1,0:T(8,128)(2,1)} %bitcast.37, bf16[32,16384]{1,0:T(8,128)(2,1)} %collective-permute-done.10.refs_1_, bf16[32,16384]{1,0:T(8,128)(2,1)} %collective-permute-done.11.refs_2_), custom_call_target="tpu_custom_call" | custom-call | flops 20000000000 | bytes 6291456 | tf_op jit(solution)/shard_map/pallas_call | solution.py:82
  37.8 7.6 %all-to-all-start.1 = ((bf16[32,4,3,32,128]{4,3,2,1,0:T(8,128)(2,1)}), bf16[32,4,3,32,128]{4,3,2,1,0:T(8,128)(2,1)S(1)}, u32[]{:S(2)}, u32[]{:S(2)}) async-start(bf16[32,4,3,32,128]{4,3,2,1,0:T(8,128)(2,1)} %shard_map.86), calls=%async_computation.1 | async-start | bytes 6291456 | tf_op jit(solution)/shard_map/all_to_all | solution.py:39
  45.4 9.5 %collective-permute-done.13.refs_1_ = bf16[32,16384]{1,0:T(8,128)(2,1)} collective-permute-done((bf16[32,16384]{1,0:T(8,128)(2,1)}, bf16[32,16384]{1,0:T(8,128)(2,1)}, u32[]{:S(2)}, u32[]{:S(2)}) %collective-permute-start.13) | collective-permute-done | bytes 1048608 | tf_op jit(solution)/shard_map/ppermute | solution.py:35
  54.9 3.7 %collective-permute-start.15 = (bf16[32,16384]{1,0:T(8,128)(2,1)}, bf16[32,16384]{1,0:T(8,128)(2,1)}, u32[]{:S(2)}, u32[]{:S(2)}) collective-permute-start(bf16[32,16384]{1,0:T(8,128)(2,1)} %collective-permute-done.13.refs_1_), channel_id=1, source_target_pairs={{0,28},{4,0},{8,4},{12,8},{16,12},{20,16},{24,20},{28,24},{1,29},{... | collective-permute-start | bytes 3145736 | tf_op jit(solution)/shard_map/ppermute | solution.py:35
  58.5 20.9 %collective-permute-done.15.refs_3_ = bf16[32,16384]{1,0:T(8,128)(2,1)} collective-permute-done((bf16[32,16384]{1,0:T(8,128)(2,1)}, bf16[32,16384]{1,0:T(8,128)(2,1)}, u32[]{:S(2)}, u32[]{:S(2)}) %collective-permute-start.15) | collective-permute-done | bytes 1048608 | tf_op jit(solution)/shard_map/ppermute | solution.py:35
  79.5 3.4 %collective-permute-done.14.refs_2_ = bf16[32,16384]{1,0:T(8,128)(2,1)} collective-permute-done((bf16[32,16384]{1,0:T(8,128)(2,1)}, bf16[32,16384]{1,0:T(8,128)(2,1)}, u32[]{:S(2)}, u32[]{:S(2)}) %collective-permute-start.14) | collective-permute-done | bytes 1048608 | tf_op jit(solution)/shard_map/ppermute | solution.py:35
  82.9 5.3 %shard_map.88 = bf16[32,4,4,32,128]{4,3,2,1,0:T(8,128)(2,1)} custom-call(s32[32,4]{1,0:T(8,128)} %copy.39.wanted_ref, bf16[32,16384]{1,0:T(8,128)(2,1)} %collective-permute-done.12.refs_0_, bf16[32,16384]{1,0:T(8,128)(2,1)} %collective-permute-done.13.refs_1_, bf16[32,16384]{1,0:T(8,128)(2,1)} %collective-permute-done.14.refs_2_, ...), custom_call_target="tpu_custom_call" | custom-call | flops 20000000000 | bytes 8388608 | tf_op jit(solution)/shard_map/pallas_call | solution.py:82
  89.1 6.9 %all-to-all-start.2 = ((bf16[32,4,4,32,128]{4,3,2,1,0:T(8,128)(2,1)}), bf16[32,4,4,32,128]{4,3,2,1,0:T(8,128)(2,1)}, u32[]{:S(2)}, u32[]{:S(2)}) async-start(bf16[32,4,4,32,128]{4,3,2,1,0:T(8,128)(2,1)} %shard_map.88), calls=%async_computation.2 | async-start | bytes 8388608 | tf_op jit(solution)/shard_map/all_to_all | solution.py:39
  95.9 1.1 collective-permute-start.2
  97.0 1.0 collective-permute-start.1
  98.7 2.9 %collective-permute-done.2 = bf16[64,1024]{1,0:T(8,128)(2,1)S(1)} collective-permute-done((bf16[64,1024]{1,0:T(8,128)(2,1)S(1)}, bf16[64,1024]{1,0:T(8,128)(2,1)S(1)}, u32[]{:S(2)}, u32[]{:S(2)}) %collective-permute-start.2) | collective-permute-done | bytes 131104 | tf_op jit(solution)/shard_map/ppermute | solution.py:35
  101.6 1.8 collective-permute-start.4
  104.9 1.6 collective-permute-done.4
  106.5 3.0 %collective-permute-start.6 = (bf16[64,1024]{1,0:T(8,128)(2,1)S(1)}, bf16[64,1024]{1,0:T(8,128)(2,1)S(1)}, u32[]{:S(2)}, u32[]{:S(2)}) collective-permute-start(bf16[64,1024]{1,0:T(8,128)(2,1)S(1)} %collective-permute-done.4), channel_id=1, source_target_pairs={{0,28},{4,0},{8,4},{12,8},{16,12},{20,16},{24,20},{28,24},{1,29},{... | collective-permute-start | bytes 393224 | tf_op jit(solution)/shard_map/ppermute | solution.py:35
  110.9 1.2 collective-permute-done.6
  112.1 3.7 %collective-permute-start.8 = (bf16[32,1024]{1,0:T(8,128)(2,1)S(1)}, bf16[32,1024]{1,0:T(8,128)(2,1)S(1)}, u32[]{:S(2)}, u32[]{:S(2)}) collective-permute-start(bf16[32,1024]{1,0:T(8,128)(2,1)S(1)} %slice.25), channel_id=1, source_target_pairs={{0,28},{4,0},{8,4},{12,8},{16,12},{20,16},{24,20},{28,24},{1,29},{... | collective-permute-start | bytes 196616 | tf_op jit(solution)/shard_map/ppermute | solution.py:35
  117.2 4.1 %collective-permute-done.7 = bf16[32,1024]{1,0:T(8,128)(2,1)S(1)} collective-permute-done((bf16[32,1024]{1,0:T(8,128)(2,1)S(1)}, bf16[32,1024]{1,0:T(8,128)(2,1)S(1)}, u32[]{:S(2)}, u32[]{:S(2)}) %collective-permute-start.7) | collective-permute-done | bytes 65568 | tf_op jit(solution)/shard_map/ppermute | solution.py:35
  122.6 1.9 slice.27
  124.5 1.9 slice.26
  126.4 2.0 collective-permute-start.16
  128.5 3.1 %pad_maximum_fusion = bf16[16,2,32,1024]{3,2,1,0:T(8,128)(2,1)} fusion(bf16[16,1,32,1024]{3,2,1,0:T(8,128)(2,1)} %bitcast.9, bf16[16,1,32,1024]{3,2,1,0:T(8,128)(2,1)} %bitcast.7), kind=kLoop, calls=%fused_computation | loop fusion | flops 1048576 | bytes 4194304 | tf_op jit(solution)/shard_map/stack | solution.py:297
  131.6 3.0 %shard_map.87 = (bf16[384,1024]{1,0:T(8,128)(2,1)S(1)}, bf16[1024,384]{1,0:T(8,128)(2,1)S(1)}) custom-call(s32[1]{0:T(128)} %bitcast.core_ref, s32[8,4]{1,0:T(8,128)S(1)} %copy.44.tgt_ref, s32[8]{0:T(128)S(1)} %bitcast.26, bf16[8,4,128,128]{3,2,1,0:T(8,128)(2,1)S(1)} %bitcast.24, bf16[32,4,3,32,128]{4,3,2,1,0:T(8,128)(2,1)S(1)} %all-to-all-done.1.part), custom_call_target="tpu_custom_call" | custom-call | flops 3000000000 | bytes 8388608 | tf_op jit(solution)/shard_map/pallas_call | solution.py:136
  134.6 0.9 copy-done.4
  135.5 0.9 copy-done.6
  137.1 2.1 collective-permute-done.17.refs_1_
  139.1 3.1 %collective-permute-done.16.refs_0_ = bf16[16,16384]{1,0:T(8,128)(2,1)} collective-permute-done((bf16[16,16384]{1,0:T(8,128)(2,1)}, bf16[16,16384]{1,0:T(8,128)(2,1)}, u32[]{:S(2)}, u32[]{:S(2)}) %collective-permute-start.16) | collective-permute-done | bytes 524320 | tf_op jit(solution)/shard_map/ppermute | solution.py:35
  142.2 3.3 %shard_map.90 = bf16[32,4,1,32,128]{4,3,2,1,0:T(8,128)(2,1)} custom-call(s32[32,4]{1,0:T(8,128)} %copy.43.wanted_ref, bf16[16,16384]{1,0:T(8,128)(2,1)} %collective-permute-done.16.refs_0_, bf16[16,16384]{1,0:T(8,128)(2,1)} %collective-permute-done.17.refs_1_), custom_call_target="tpu_custom_call" | custom-call | flops 1000000000 | bytes 2097152 | tf_op jit(solution)/shard_map/pallas_call | solution.py:82
  145.6 9.5 %all-to-all-done.2.part = bf16[32,4,4,32,128]{4,3,2,1,0:T(8,128)(2,1)} async-done(((bf16[32,4,4,32,128]{4,3,2,1,0:T(8,128)(2,1)}), bf16[32,4,4,32,128]{4,3,2,1,0:T(8,128)(2,1)}, u32[]{:S(2)}, u32[]{:S(2)}) %all-to-all-start.2) | async-done | bytes 4194336 | tf_op jit(solution)/shard_map/all_to_all | solution.py:39
  155.1 4.5 %all-to-all-start.3 = ((bf16[32,4,1,32,128]{4,3,2,1,0:T(8,128)(2,1)}), bf16[32,4,1,32,128]{4,3,2,1,0:T(8,128)(2,1)}, u32[]{:S(2)}, u32[]{:S(2)}) async-start(bf16[32,4,1,32,128]{4,3,2,1,0:T(8,128)(2,1)} %shard_map.90), calls=%async_computation.3 | async-start | bytes 2097152 | tf_op jit(solution)/shard_map/all_to_all | solution.py:39
  159.5 1.0 slice.23.refs_5_
  160.5 5.1 %shard_map.89 = (bf16[512,1024]{1,0:T(8,128)(2,1)S(1)}, bf16[1024,512]{1,0:T(8,128)(2,1)S(1)}) custom-call(s32[1]{0:T(128)} %bitcast.core_ref, s32[8,4]{1,0:T(8,128)S(1)} %copy.44.tgt_ref, s32[8]{0:T(128)S(1)} %bitcast.27, bf16[8,4,128,128]{3,2,1,0:T(8,128)(2,1)S(1)} %bitcast.25, bf16[32,4,4,32,128]{4,3,2,1,0:T(8,128)(2,1)} %all-to-all-done.2.part), custom_call_target="tpu_custom_call" | custom-call | flops 3000000000 | bytes 8388608 | tf_op jit(solution)/shard_map/pallas_call | solution.py:136
  165.7 1.0 copy-done.3
  166.7 4.3 %fusion.refs_4_ = f32[1024,1024]{1,0:T(8,128)} fusion(bf16[1024,512]{1,0:T(8,128)(2,1)S(1)} %get-tuple-element.23, bf16[1024,384]{1,0:T(8,128)(2,1)S(1)} %copy-done.5, bf16[1024,1024]{1,0:T(8,128)(2,1)S(1)} %bitcast.30), kind=kOutput, calls=%fused_computation.2 | convolution fusion | flops 1882718208 | bytes 7864320 | tf_op jit(solution)/shard_map/dot_general | solution.py:319
  171.0 4.2 %all-to-all-done.3.refs_3_ = bf16[32,4,1,32,128]{4,3,2,1,0:T(8,128)(2,1)} async-done(((bf16[32,4,1,32,128]{4,3,2,1,0:T(8,128)(2,1)}), bf16[32,4,1,32,128]{4,3,2,1,0:T(8,128)(2,1)}, u32[]{:S(2)}, u32[]{:S(2)}) %all-to-all-start.3) | async-done | bytes 1048608 | tf_op jit(solution)/shard_map/all_to_all | solution.py:39
  175.2 1.1 copy-done.7
  176.3 9.2 %shard_map.91 = (bf16[1024,1024]{1,0:T(8,128)(2,1)}, bf16[8,2,8,32,128]{4,3,2,1,0:T(8,128)(2,1)S(1)}, bf16[8,2,8,32,128]{4,3,2,1,0:T(8,128)(2,1)S(1)}) custom-call(s32[1]{0:T(128)} %bitcast.core_ref, s32[8,4]{1,0:T(8,128)S(1)} %copy.44.tgt_ref, s32[8]{0:T(128)S(1)} %bitcast.28, bf16[384,1024]{1,0:T(8,128)(2,1)S(1)} %copy-done.7, ...), custom_call_target="tpu_custom_call" | custom-call | flops 6000000000 | bytes 20971520 | tf_op jit(solution)/shard_map/pallas_call | solution.py:228
  185.7 2.6 %collective-permute-done.18 = bf16[8,2,8,32,128]{4,3,2,1,0:T(8,128)(2,1)S(1)} collective-permute-done((bf16[8,2,8,32,128]{4,3,2,1,0:T(8,128)(2,1)S(1)}, bf16[8,2,8,32,128]{4,3,2,1,0:T(8,128)(2,1)S(1)}, u32[]{:S(2)}, u32[]{:S(2)}) %collective-permute-start.18) | collective-permute-done | bytes 1048608 | tf_op jit(solution)/shard_map/ppermute | solution.py:277
  188.3 1.3 add_convert_fusion
  189.6 4.3 %all-to-all-start.4 = ((bf16[16,8,32,128]{3,2,1,0:T(8,128)(2,1)}), bf16[16,8,32,128]{3,2,1,0:T(8,128)(2,1)S(1)}, u32[]{:S(2)}, u32[]{:S(2)}) async-start(bf16[16,8,32,128]{3,2,1,0:T(8,128)(2,1)} %bitcast.14), calls=%async_computation.4 | async-start | bytes 2097152 | tf_op jit(solution)/shard_map/all_to_all | solution.py:39
  193.9 18.4 %all-to-all-done.4.came_ref = bf16[16,8,32,128]{3,2,1,0:T(8,128)(2,1)S(1)} async-done(((bf16[16,8,32,128]{3,2,1,0:T(8,128)(2,1)}), bf16[16,8,32,128]{3,2,1,0:T(8,128)(2,1)S(1)}, u32[]{:S(2)}, u32[]{:S(2)}) %all-to-all-start.4) | async-done | bytes 1048608 | tf_op jit(solution)/shard_map/all_to_all | solution.py:39
  212.4 12.2 %all_to_all.35 = f32[8,32,128]{2,1,0:T(8,128)S(1)} all-to-all(f32[8,32,128]{2,1,0:T(8,128)S(1)} %shard_map.92), channel_id=1, replica_groups=mesh['ylo'=2,'x'=4,'z'=8,'yhi'=2,'core'=2] {'z'}, dimensions={0} | all-to-all | bytes 262144 | tf_op jit(solution)/shard_map/all_to_all | solution.py:39
  224.7 10.2 %all_to_all.36 = f32[8,32,128]{2,1,0:T(8,128)S(1)} all-to-all(f32[8,32,128]{2,1,0:T(8,128)S(1)} %broadcast_in_dim.18), channel_id=1, replica_groups=mesh['ylo'=2,'x'=4,'z'=8,'yhi'=2,'core'=2] {'ylo','x'}, dimensions={0} | all-to-all | bytes 262144 | tf_op jit(solution)/shard_map/all_to_all | solution.py:39
  (57 shorter events, 11.8 us)
Async XLA Ops:
  0.6 28.7 %collective-permute-start.11 = (bf16[32,16384]{1,0:T(8,128)(2,1)}, bf16[32,16384]{1,0:T(8,128)(2,1)}, u32[]{:S(2)}, u32[]{:S(2)}) collective-permute-start(bf16[32,16384]{1,0:T(8,128)(2,1)} %bitcast.35), channel_id=1, source_target_pairs={{0,28},{4,0},{8,4},{12,8},{16,12},{20,16},{24,20},{28,24},{1,29},{... | collective-permute-start | bytes 3145736 | tf_op jit(solution)/shard_map/ppermute | solution.py:35
  6.6 26.4 %collective-permute-start.10 = (bf16[32,16384]{1,0:T(8,128)(2,1)}, bf16[32,16384]{1,0:T(8,128)(2,1)}, u32[]{:S(2)}, u32[]{:S(2)}) collective-permute-start(bf16[32,16384]{1,0:T(8,128)(2,1)} %bitcast.36), channel_id=1, source_target_pairs={{0,4},{4,8},{8,12},{12,16},{16,20},{20,24},{24,28},{28,0},{1,5},{5... | collective-permute-start | bytes 3145736 | tf_op jit(solution)/shard_map/ppermute | solution.py:35
  6.6 15.6 %collective-permute-start = (bf16[32,1024]{1,0:T(8,128)(2,1)}, bf16[32,1024]{1,0:T(8,128)(2,1)S(1)}, u32[]{:S(2)}, u32[]{:S(2)}) collective-permute-start(bf16[32,1024]{1,0:T(8,128)(2,1)} %param.12), channel_id=1, source_target_pairs={{0,130},{2,128},{128,2},{130,0},{1,131},{3,129},{129,3},{131,1},{4... | collective-permute-start | bytes 196616 | tf_op jit(solution)/shard_map/ppermute | solution.py:287
  10.9 11.1 %all-to-all-start = ((s32[32,1,4]{2,1,0:T(1,128)}), s32[32,1,4]{2,1,0:T(1,128)S(1)}, u32[]{:S(2)}, u32[]{:S(2)}) async-start(s32[32,1,4]{2,1,0:T(1,128)} %bitcast.4), calls=%async_computation | async-start | bytes 32768 | tf_op jit(solution)/shard_map/all_to_all | solution.py:39
  29.3 25.6 %collective-permute-start.13 = (bf16[32,16384]{1,0:T(8,128)(2,1)}, bf16[32,16384]{1,0:T(8,128)(2,1)}, u32[]{:S(2)}, u32[]{:S(2)}) collective-permute-start(bf16[32,16384]{1,0:T(8,128)(2,1)} %collective-permute-done.11.refs_2_), channel_id=1, source_target_pairs={{0,28},{4,0},{8,4},{12,8},{16,12},{20,16},{24,20},{28,24},{1,29},{... | collective-permute-start | bytes 3145736 | tf_op jit(solution)/shard_map/ppermute | solution.py:35
  33.0 25.6 %collective-permute-start.12 = (bf16[32,16384]{1,0:T(8,128)(2,1)}, bf16[32,16384]{1,0:T(8,128)(2,1)}, u32[]{:S(2)}, u32[]{:S(2)}) collective-permute-start(bf16[32,16384]{1,0:T(8,128)(2,1)} %collective-permute-done.10.refs_1_), channel_id=1, source_target_pairs={{0,4},{4,8},{8,12},{12,16},{16,20},{20,24},{24,28},{28,0},{1,5},{5... | collective-permute-start | bytes 3145736 | tf_op jit(solution)/shard_map/ppermute | solution.py:35
  37.8 51.3 %all-to-all-start.1 = ((bf16[32,4,3,32,128]{4,3,2,1,0:T(8,128)(2,1)}), bf16[32,4,3,32,128]{4,3,2,1,0:T(8,128)(2,1)S(1)}, u32[]{:S(2)}, u32[]{:S(2)}) async-start(bf16[32,4,3,32,128]{4,3,2,1,0:T(8,128)(2,1)} %shard_map.86), calls=%async_computation.1 | async-start | bytes 6291456 | tf_op jit(solution)/shard_map/all_to_all | solution.py:39
  54.9 24.6 %collective-permute-start.15 = (bf16[32,16384]{1,0:T(8,128)(2,1)}, bf16[32,16384]{1,0:T(8,128)(2,1)}, u32[]{:S(2)}, u32[]{:S(2)}) collective-permute-start(bf16[32,16384]{1,0:T(8,128)(2,1)} %collective-permute-done.13.refs_1_), channel_id=1, source_target_pairs={{0,28},{4,0},{8,4},{12,8},{16,12},{20,16},{24,20},{28,24},{1,29},{... | collective-permute-start | bytes 3145736 | tf_op jit(solution)/shard_map/ppermute | solution.py:35
  58.5 24.4 %collective-permute-start.14 = (bf16[32,16384]{1,0:T(8,128)(2,1)}, bf16[32,16384]{1,0:T(8,128)(2,1)}, u32[]{:S(2)}, u32[]{:S(2)}) collective-permute-start(bf16[32,16384]{1,0:T(8,128)(2,1)} %collective-permute-done.12.refs_0_), channel_id=1, source_target_pairs={{0,4},{4,8},{8,12},{12,16},{16,20},{20,24},{24,28},{28,0},{1,5},{5... | collective-permute-start | bytes 3145736 | tf_op jit(solution)/shard_map/ppermute | solution.py:35
  89.1 66.0 %all-to-all-start.2 = ((bf16[32,4,4,32,128]{4,3,2,1,0:T(8,128)(2,1)}), bf16[32,4,4,32,128]{4,3,2,1,0:T(8,128)(2,1)}, u32[]{:S(2)}, u32[]{:S(2)}) async-start(bf16[32,4,4,32,128]{4,3,2,1,0:T(8,128)(2,1)} %shard_map.88), calls=%async_computation.2 | async-start | bytes 8388608 | tf_op jit(solution)/shard_map/all_to_all | solution.py:39
  95.9 5.6 %collective-permute-start.2 = (bf16[64,1024]{1,0:T(8,128)(2,1)S(1)}, bf16[64,1024]{1,0:T(8,128)(2,1)S(1)}, u32[]{:S(2)}, u32[]{:S(2)}) collective-permute-start(bf16[64,1024]{1,0:T(8,128)(2,1)S(1)} %pad_maximum_fusion.1), channel_id=1, source_target_pairs={{0,28},{4,0},{8,4},{12,8},{16,12},{20,16},{24,20},{28,24},{1,29},{... | collective-permute-start | bytes 393224 | tf_op jit(solution)/shard_map/ppermute | solution.py:35
  97.0 6.3 %collective-permute-start.1 = (bf16[64,1024]{1,0:T(8,128)(2,1)S(1)}, bf16[64,1024]{1,0:T(8,128)(2,1)S(1)}, u32[]{:S(2)}, u32[]{:S(2)}) collective-permute-start(bf16[64,1024]{1,0:T(8,128)(2,1)S(1)} %pad_maximum_fusion.1), channel_id=1, source_target_pairs={{0,4},{4,8},{8,12},{12,16},{16,20},{20,24},{24,28},{28,0},{1,5},{5... | collective-permute-start | bytes 393224 | tf_op jit(solution)/shard_map/ppermute | solution.py:35
  98.7 29.7 %copy-start.9 = (s32[1,1,8,4]{2,3,1,0:T(4,128)S(1)}, s32[1,1,8,4]{2,3,1,0:T(4,128)}, u32[]{:S(2)}) copy-start(s32[1,1,8,4]{2,3,1,0:T(4,128)} %param.8) | copy-start | bytes 388
  101.6 5.0 %collective-permute-start.4 = (bf16[64,1024]{1,0:T(8,128)(2,1)S(1)}, bf16[64,1024]{1,0:T(8,128)(2,1)S(1)}, u32[]{:S(2)}, u32[]{:S(2)}) collective-permute-start(bf16[64,1024]{1,0:T(8,128)(2,1)S(1)} %collective-permute-done.2), channel_id=1, source_target_pairs={{0,28},{4,0},{8,4},{12,8},{16,12},{20,16},{24,20},{28,24},{1,29},{... | collective-permute-start | bytes 393224 | tf_op jit(solution)/shard_map/ppermute | solution.py:35
  103.4 6.2 %collective-permute-start.3 = (bf16[64,1024]{1,0:T(8,128)(2,1)S(1)}, bf16[64,1024]{1,0:T(8,128)(2,1)S(1)}, u32[]{:S(2)}, u32[]{:S(2)}) collective-permute-start(bf16[64,1024]{1,0:T(8,128)(2,1)S(1)} %collective-permute-done.1), channel_id=1, source_target_pairs={{0,4},{4,8},{8,12},{12,16},{16,20},{20,24},{24,28},{28,0},{1,5},{5... | collective-permute-start | bytes 393224 | tf_op jit(solution)/shard_map/ppermute | solution.py:35
  106.5 5.5 %collective-permute-start.6 = (bf16[64,1024]{1,0:T(8,128)(2,1)S(1)}, bf16[64,1024]{1,0:T(8,128)(2,1)S(1)}, u32[]{:S(2)}, u32[]{:S(2)}) collective-permute-start(bf16[64,1024]{1,0:T(8,128)(2,1)S(1)} %collective-permute-done.4), channel_id=1, source_target_pairs={{0,28},{4,0},{8,4},{12,8},{16,12},{20,16},{24,20},{28,24},{1,29},{... | collective-permute-start | bytes 393224 | tf_op jit(solution)/shard_map/ppermute | solution.py:35
  109.6 6.2 %collective-permute-start.5 = (bf16[64,1024]{1,0:T(8,128)(2,1)S(1)}, bf16[64,1024]{1,0:T(8,128)(2,1)S(1)}, u32[]{:S(2)}, u32[]{:S(2)}) collective-permute-start(bf16[64,1024]{1,0:T(8,128)(2,1)S(1)} %collective-permute-done.3), channel_id=1, source_target_pairs={{0,4},{4,8},{8,12},{12,16},{16,20},{20,24},{24,28},{28,0},{1,5},{5... | collective-permute-start | bytes 393224 | tf_op jit(solution)/shard_map/ppermute | solution.py:35
  112.1 9.9 %collective-permute-start.8 = (bf16[32,1024]{1,0:T(8,128)(2,1)S(1)}, bf16[32,1024]{1,0:T(8,128)(2,1)S(1)}, u32[]{:S(2)}, u32[]{:S(2)}) collective-permute-start(bf16[32,1024]{1,0:T(8,128)(2,1)S(1)} %slice.25), channel_id=1, source_target_pairs={{0,28},{4,0},{8,4},{12,8},{16,12},{20,16},{24,20},{28,24},{1,29},{... | collective-permute-start | bytes 196616 | tf_op jit(solution)/shard_map/ppermute | solution.py:35
  115.7 5.6 %collective-permute-start.7 = (bf16[32,1024]{1,0:T(8,128)(2,1)S(1)}, bf16[32,1024]{1,0:T(8,128)(2,1)S(1)}, u32[]{:S(2)}, u32[]{:S(2)}) collective-permute-start(bf16[32,1024]{1,0:T(8,128)(2,1)S(1)} %slice.24), channel_id=1, source_target_pairs={{0,4},{4,8},{8,12},{12,16},{16,20},{20,24},{24,28},{28,0},{1,5},{5... | collective-permute-start | bytes 196616 | tf_op jit(solution)/shard_map/ppermute | solution.py:35
  122.6 5.9 %collective-permute-start.9 = (bf16[512,1024]{1,0:T(8,128)(2,1)}, bf16[512,1024]{1,0:T(8,128)(2,1)}, u32[]{:S(2)}, u32[]{:S(2)}) collective-permute-start(bf16[512,1024]{1,0:T(8,128)(2,1)} %constant_dynamic-update-slice_fusion), channel_id=1, source_target_pairs={{0,1},{1,0},{2,3},{3,2},{4,5},{5,4},{6,7},{7,6},{8,9},{9,8},{10,11... | collective-permute-start | bytes 3145736 | tf_op jit(solution)/shard_map/ppermute | solution.py:295
  124.5 14.7 %collective-permute-start.17 = (bf16[16,16384]{1,0:T(8,128)(2,1)}, bf16[16,16384]{1,0:T(8,128)(2,1)}, u32[]{:S(2)}, u32[]{:S(2)}) collective-permute-start(bf16[16,16384]{1,0:T(8,128)(2,1)} %slice.27), channel_id=1, source_target_pairs={{0,28},{4,0},{8,4},{12,8},{16,12},{20,16},{24,20},{28,24},{1,29},{... | collective-permute-start | bytes 1572872 | tf_op jit(solution)/shard_map/ppermute | solution.py:35
  126.4 15.9 %collective-permute-start.16 = (bf16[16,16384]{1,0:T(8,128)(2,1)}, bf16[16,16384]{1,0:T(8,128)(2,1)}, u32[]{:S(2)}, u32[]{:S(2)}) collective-permute-start(bf16[16,16384]{1,0:T(8,128)(2,1)} %slice.26), channel_id=1, source_target_pairs={{0,4},{4,8},{8,12},{12,16},{16,20},{20,24},{24,28},{28,0},{1,5},{5... | collective-permute-start | bytes 1572872 | tf_op jit(solution)/shard_map/ppermute | solution.py:35
  128.5 3.2 %copy-start = (bf16[1,1,8,4,128,128]{5,4,3,2,1,0:T(8,128)(2,1)S(1)}, bf16[1,1,8,4,128,128]{5,4,3,2,1,0:T(8,128)(2,1)}, u32[]{:S(2)}) copy-start(bf16[1,1,8,4,128,128]{5,4,3,2,1,0:T(8,128)(2,1)} %param.11) | copy-start | bytes 3145732
  128.5 3.2 %copy-start.2 = (s32[1,1,8]{2,1,0:T(1,128)S(1)}, s32[1,1,8]{2,1,0:T(1,128)}, u32[]{:S(2)}) copy-start(s32[1,1,8]{2,1,0:T(1,128)} %param.10) | copy-start | bytes 100
  134.6 0.9 copy-start.4
  135.5 0.9 copy-start.6
  145.5 15.0 %copy-start.1 = (bf16[1,1,8,4,128,128]{5,4,3,2,1,0:T(8,128)(2,1)S(1)}, bf16[1,1,8,4,128,128]{5,4,3,2,1,0:T(8,128)(2,1)}, u32[]{:S(2)}) copy-start(bf16[1,1,8,4,128,128]{5,4,3,2,1,0:T(8,128)(2,1)} %param.11) | copy-start | bytes 3145732
  155.1 20.1 %all-to-all-start.3 = ((bf16[32,4,1,32,128]{4,3,2,1,0:T(8,128)(2,1)}), bf16[32,4,1,32,128]{4,3,2,1,0:T(8,128)(2,1)}, u32[]{:S(2)}, u32[]{:S(2)}) async-start(bf16[32,4,1,32,128]{4,3,2,1,0:T(8,128)(2,1)} %shard_map.90), calls=%async_computation.3 | async-start | bytes 2097152 | tf_op jit(solution)/shard_map/all_to_all | solution.py:39
  160.5 6.1 %copy-start.5 = (bf16[1024,384]{1,0:T(8,128)(2,1)S(1)}, bf16[1024,384]{1,0:T(8,128)(2,1)}, u32[]{:S(2)}) copy-start(bf16[1024,384]{1,0:T(8,128)(2,1)} %copy-done.4) | copy-start | bytes 2359300
  160.5 6.1 %copy-start.8 = (bf16[16,2,32,1024]{3,2,1,0:T(8,128)(2,1)S(1)}, bf16[16,2,32,1024]{3,2,1,0:T(8,128)(2,1)}, u32[]{:S(2)}) copy-start(bf16[16,2,32,1024]{3,2,1,0:T(8,128)(2,1)} %pad_maximum_fusion) | copy-start | bytes 6291460
  165.7 1.0 copy-start.3
  175.2 1.1 copy-start.7
  185.6 2.7 %collective-permute-start.18 = (bf16[8,2,8,32,128]{4,3,2,1,0:T(8,128)(2,1)S(1)}, bf16[8,2,8,32,128]{4,3,2,1,0:T(8,128)(2,1)S(1)}, u32[]{:S(2)}, u32[]{:S(2)}) collective-permute-start(bf16[8,2,8,32,128]{4,3,2,1,0:T(8,128)(2,1)S(1)} %get-tuple-element.27), channel_id=1, source_target_pairs={{0,1},{1,0},{2,3},{3,2},{4,5},{5,4},{6,7},{7,6},{8,9},{9,8},{10,11... | collective-permute-start | bytes 3145736 | tf_op jit(solution)/shard_map/ppermute | solution.py:277
  189.6 22.7 %all-to-all-start.4 = ((bf16[16,8,32,128]{3,2,1,0:T(8,128)(2,1)}), bf16[16,8,32,128]{3,2,1,0:T(8,128)(2,1)S(1)}, u32[]{:S(2)}, u32[]{:S(2)}) async-start(bf16[16,8,32,128]{3,2,1,0:T(8,128)(2,1)} %bitcast.14), calls=%async_computation.4 | async-start | bytes 2097152 | tf_op jit(solution)/shard_map/all_to_all | solution.py:39

commit v9 on v8

--- a/solution.py
+++ b/solution.py
@@ -101,7 +101,7 @@
         return found + (tile % slots < count_ref[tile // slots]).astype(jnp.int32)
 
     found = lax.fori_loop(0, sections * slots, enter, 0)
-    each = 4
+    each = 8
 
     @pl.loop(0, (found + each - 1) // each)
     def _(step):
@@ -194,7 +194,7 @@
         for copy in block_copies[index]:
             copy.wait()
         preact = begun[at] + jnp.dot(plain[at], weight[...], preferred_element_type=jnp.float32)
-        sigmoid_val = jax.nn.sigmoid(preact)
+        sigmoid_val = 0.5 * jnp.tanh(0.5 * preact) + 0.5
         act[at] = (preact * sigmoid_val).astype(act.dtype)
         send(act.at[at], act_hbm.at[at], out_sems.at[0, index])
         slope = sigmoid_val * (1.0 + preact * (1.0 - sigmoid_val))

time: 236 us -> 237 us (level)
  no operation moved by 1% of the time
where the time goes in v9:
time: 237 us; the launch traced here: 236 us
  waiting for transfers between devices  97.8 us (41%)
  starting transfers between devices  57.9 us (24%)
  Pallas kernels  29.5 us (12%)
  blocking collectives  22.5 us (9%)
  local copies, waits for them, and re-layouts  17.5 us (7%)
  other arithmetic  5.97 us (3%)
  matrix products  4.32 us (2%)
    ppermute x16, waiting for transfers between devices, shift_z(): return lax.ppermute(value, 'z', [(i, (i + step) % ZN) for i in range(ZN)])  55 us
    all_to_all x5, waiting for transfers between devices, exchange(): return lax.all_to_all(value, axes, split_axis=0, concat_axis=0, tiled=True)  40.2 us
    all_to_all x5, starting transfers between devices, exchange(): return lax.all_to_all(value, axes, split_axis=0, concat_axis=0, tiled=True)  28.5 us
    ppermute x16, starting transfers between devices, shift_z(): return lax.ppermute(value, 'z', [(i, (i + step) % ZN) for i in range(ZN)])  26.2 us
    all_to_all x2, blocking collectives, exchange(): return lax.all_to_all(value, axes, split_axis=0, concat_axis=0, tiled=True)  22.5 us
    pallas_call x3, Pallas kernels, pick(): pl.pallas_call(functools.partial(pick_kernel, block, layout), out_shape=j...  13.4 us
    unnamed x29, local copies, waits for them, and re-layouts  9.98 us
    pallas_call x1, Pallas kernels, layer(): pl.pallas_call(functools.partial(layer_kernel, len(early)), out_shape=(ja...  9.2 us
  transfers between devices with their start and end apart: 24, of which 16 were waited for; matrix products, arithmetic and copies ran while one was open for 9% of the time, Pallas kernels for 9%

profile of v9, /device:TPU:2, one launch (start us, length us, event | category | flops | bytes accessed | tf_op | source)
XLA Modules:
  0.0 236.4 jit_solution(17388132602962552045)
XLA Ops:
  0.6 5.9 %collective-permute-start.11 = (bf16[32,16384]{1,0:T(8,128)(2,1)}, bf16[32,16384]{1,0:T(8,128)(2,1)}, u32[]{:S(2)}, u32[]{:S(2)}) collective-permute-start(bf16[32,16384]{1,0:T(8,128)(2,1)} %bitcast.35), channel_id=1, source_target_pairs={{0,28},{4,0},{8,4},{12,8},{16,12},{20,16},{24,20},{28,24},{1,29},{... | collective-permute-start | bytes 3145736 | tf_op jit(solution)/shard_map/ppermute | solution.py:35
  6.6 3.0 %collective-permute-start = (bf16[32,1024]{1,0:T(8,128)(2,1)}, bf16[32,1024]{1,0:T(8,128)(2,1)S(1)}, u32[]{:S(2)}, u32[]{:S(2)}) collective-permute-start(bf16[32,1024]{1,0:T(8,128)(2,1)} %param.12), channel_id=1, source_target_pairs={{0,130},{2,128},{128,2},{130,0},{1,131},{3,129},{129,3},{131,1},{4... | collective-permute-start | bytes 196616 | tf_op jit(solution)/shard_map/ppermute | solution.py:287
  10.9 5.1 %all-to-all-start = ((s32[32,1,4]{2,1,0:T(1,128)}), s32[32,1,4]{2,1,0:T(1,128)S(1)}, u32[]{:S(2)}, u32[]{:S(2)}) async-start(s32[32,1,4]{2,1,0:T(1,128)} %bitcast.4), calls=%async_computation | async-start | bytes 32768 | tf_op jit(solution)/shard_map/all_to_all | solution.py:39
  16.0 6.0 %all-to-all-done = s32[32,1,4]{2,1,0:T(1,128)S(1)} async-done(((s32[32,1,4]{2,1,0:T(1,128)}), s32[32,1,4]{2,1,0:T(1,128)S(1)}, u32[]{:S(2)}, u32[]{:S(2)}) %all-to-all-start) | async-done | bytes 544 | tf_op jit(solution)/shard_map/all_to_all | solution.py:39
  23.7 5.6 %collective-permute-done.11.refs_2_ = bf16[32,16384]{1,0:T(8,128)(2,1)} collective-permute-done((bf16[32,16384]{1,0:T(8,128)(2,1)}, bf16[32,16384]{1,0:T(8,128)(2,1)}, u32[]{:S(2)}, u32[]{:S(2)}) %collective-permute-start.11) | collective-permute-done | bytes 1048608 | tf_op jit(solution)/shard_map/ppermute | solution.py:35
  29.3 3.7 %collective-permute-start.13 = (bf16[32,16384]{1,0:T(8,128)(2,1)}, bf16[32,16384]{1,0:T(8,128)(2,1)}, u32[]{:S(2)}, u32[]{:S(2)}) collective-permute-start(bf16[32,16384]{1,0:T(8,128)(2,1)} %collective-permute-done.11.refs_2_), channel_id=1, source_target_pairs={{0,28},{4,0},{8,4},{12,8},{16,12},{20,16},{24,20},{28,24},{1,29},{... | collective-permute-start | bytes 3145736 | tf_op jit(solution)/shard_map/ppermute | solution.py:35
  33.0 4.7 %shard_map.86 = bf16[32,4,3,32,128]{4,3,2,1,0:T(8,128)(2,1)} custom-call(s32[32,4]{1,0:T(8,128)} %copy.39.wanted_ref, bf16[32,16384]{1,0:T(8,128)(2,1)} %bitcast.37, bf16[32,16384]{1,0:T(8,128)(2,1)} %collective-permute-done.10.refs_1_, bf16[32,16384]{1,0:T(8,128)(2,1)} %collective-permute-done.11.refs_2_), custom_call_target="tpu_custom_call" | custom-call | flops 20000000000 | bytes 6291456 | tf_op jit(solution)/shard_map/pallas_call | solution.py:82
  37.8 7.6 %all-to-all-start.1 = ((bf16[32,4,3,32,128]{4,3,2,1,0:T(8,128)(2,1)}), bf16[32,4,3,32,128]{4,3,2,1,0:T(8,128)(2,1)S(1)}, u32[]{:S(2)}, u32[]{:S(2)}) async-start(bf16[32,4,3,32,128]{4,3,2,1,0:T(8,128)(2,1)} %shard_map.86), calls=%async_computation.1 | async-start | bytes 6291456 | tf_op jit(solution)/shard_map/all_to_all | solution.py:39
  45.4 9.5 %collective-permute-done.13.refs_1_ = bf16[32,16384]{1,0:T(8,128)(2,1)} collective-permute-done((bf16[32,16384]{1,0:T(8,128)(2,1)}, bf16[32,16384]{1,0:T(8,128)(2,1)}, u32[]{:S(2)}, u32[]{:S(2)}) %collective-permute-start.13) | collective-permute-done | bytes 1048608 | tf_op jit(solution)/shard_map/ppermute | solution.py:35
  54.9 3.7 %collective-permute-start.15 = (bf16[32,16384]{1,0:T(8,128)(2,1)}, bf16[32,16384]{1,0:T(8,128)(2,1)}, u32[]{:S(2)}, u32[]{:S(2)}) collective-permute-start(bf16[32,16384]{1,0:T(8,128)(2,1)} %collective-permute-done.13.refs_1_), channel_id=1, source_target_pairs={{0,28},{4,0},{8,4},{12,8},{16,12},{20,16},{24,20},{28,24},{1,29},{... | collective-permute-start | bytes 3145736 | tf_op jit(solution)/shard_map/ppermute | solution.py:35
  58.5 20.9 %collective-permute-done.15.refs_3_ = bf16[32,16384]{1,0:T(8,128)(2,1)} collective-permute-done((bf16[32,16384]{1,0:T(8,128)(2,1)}, bf16[32,16384]{1,0:T(8,128)(2,1)}, u32[]{:S(2)}, u32[]{:S(2)}) %collective-permute-start.15) | collective-permute-done | bytes 1048608 | tf_op jit(solution)/shard_map/ppermute | solution.py:35
  79.5 3.4 %collective-permute-done.14.refs_2_ = bf16[32,16384]{1,0:T(8,128)(2,1)} collective-permute-done((bf16[32,16384]{1,0:T(8,128)(2,1)}, bf16[32,16384]{1,0:T(8,128)(2,1)}, u32[]{:S(2)}, u32[]{:S(2)}) %collective-permute-start.14) | collective-permute-done | bytes 1048608 | tf_op jit(solution)/shard_map/ppermute | solution.py:35
  82.9 5.3 %shard_map.88 = bf16[32,4,4,32,128]{4,3,2,1,0:T(8,128)(2,1)} custom-call(s32[32,4]{1,0:T(8,128)} %copy.39.wanted_ref, bf16[32,16384]{1,0:T(8,128)(2,1)} %collective-permute-done.12.refs_0_, bf16[32,16384]{1,0:T(8,128)(2,1)} %collective-permute-done.13.refs_1_, bf16[32,16384]{1,0:T(8,128)(2,1)} %collective-permute-done.14.refs_2_, ...), custom_call_target="tpu_custom_call" | custom-call | flops 20000000000 | bytes 8388608 | tf_op jit(solution)/shard_map/pallas_call | solution.py:82
  89.1 6.9 %all-to-all-start.2 = ((bf16[32,4,4,32,128]{4,3,2,1,0:T(8,128)(2,1)}), bf16[32,4,4,32,128]{4,3,2,1,0:T(8,128)(2,1)}, u32[]{:S(2)}, u32[]{:S(2)}) async-start(bf16[32,4,4,32,128]{4,3,2,1,0:T(8,128)(2,1)} %shard_map.88), calls=%async_computation.2 | async-start | bytes 8388608 | tf_op jit(solution)/shard_map/all_to_all | solution.py:39
  95.9 1.1 collective-permute-start.2
  97.0 1.0 collective-permute-start.1
  98.7 2.9 %collective-permute-done.2 = bf16[64,1024]{1,0:T(8,128)(2,1)S(1)} collective-permute-done((bf16[64,1024]{1,0:T(8,128)(2,1)S(1)}, bf16[64,1024]{1,0:T(8,128)(2,1)S(1)}, u32[]{:S(2)}, u32[]{:S(2)}) %collective-permute-start.2) | collective-permute-done | bytes 131104 | tf_op jit(solution)/shard_map/ppermute | solution.py:35
  101.6 1.8 collective-permute-start.4
  104.9 1.6 collective-permute-done.4
  106.5 3.0 %collective-permute-start.6 = (bf16[64,1024]{1,0:T(8,128)(2,1)S(1)}, bf16[64,1024]{1,0:T(8,128)(2,1)S(1)}, u32[]{:S(2)}, u32[]{:S(2)}) collective-permute-start(bf16[64,1024]{1,0:T(8,128)(2,1)S(1)} %collective-permute-done.4), channel_id=1, source_target_pairs={{0,28},{4,0},{8,4},{12,8},{16,12},{20,16},{24,20},{28,24},{1,29},{... | collective-permute-start | bytes 393224 | tf_op jit(solution)/shard_map/ppermute | solution.py:35
  110.9 1.2 collective-permute-done.6
  112.1 3.7 %collective-permute-start.8 = (bf16[32,1024]{1,0:T(8,128)(2,1)S(1)}, bf16[32,1024]{1,0:T(8,128)(2,1)S(1)}, u32[]{:S(2)}, u32[]{:S(2)}) collective-permute-start(bf16[32,1024]{1,0:T(8,128)(2,1)S(1)} %slice.25), channel_id=1, source_target_pairs={{0,28},{4,0},{8,4},{12,8},{16,12},{20,16},{24,20},{28,24},{1,29},{... | collective-permute-start | bytes 196616 | tf_op jit(solution)/shard_map/ppermute | solution.py:35
  117.2 4.1 %collective-permute-done.7 = bf16[32,1024]{1,0:T(8,128)(2,1)S(1)} collective-permute-done((bf16[32,1024]{1,0:T(8,128)(2,1)S(1)}, bf16[32,1024]{1,0:T(8,128)(2,1)S(1)}, u32[]{:S(2)}, u32[]{:S(2)}) %collective-permute-start.7) | collective-permute-done | bytes 65568 | tf_op jit(solution)/shard_map/ppermute | solution.py:35
  122.6 1.9 slice.27
  124.5 1.9 slice.26
  126.4 2.0 collective-permute-start.16
  128.5 3.1 %pad_maximum_fusion = bf16[16,2,32,1024]{3,2,1,0:T(8,128)(2,1)} fusion(bf16[16,1,32,1024]{3,2,1,0:T(8,128)(2,1)} %bitcast.9, bf16[16,1,32,1024]{3,2,1,0:T(8,128)(2,1)} %bitcast.7), kind=kLoop, calls=%fused_computation | loop fusion | flops 1048576 | bytes 4194304 | tf_op jit(solution)/shard_map/stack | solution.py:297
  131.6 2.3 shard_map.87
  134.0 0.9 copy-done.4
  134.8 0.9 copy-done.6
  136.4 2.7 %collective-permute-done.17.refs_1_ = bf16[16,16384]{1,0:T(8,128)(2,1)} collective-permute-done((bf16[16,16384]{1,0:T(8,128)(2,1)}, bf16[16,16384]{1,0:T(8,128)(2,1)}, u32[]{:S(2)}, u32[]{:S(2)}) %collective-permute-start.17) | collective-permute-done | bytes 524320 | tf_op jit(solution)/shard_map/ppermute | solution.py:35
  139.1 3.1 %collective-permute-done.16.refs_0_ = bf16[16,16384]{1,0:T(8,128)(2,1)} collective-permute-done((bf16[16,16384]{1,0:T(8,128)(2,1)}, bf16[16,16384]{1,0:T(8,128)(2,1)}, u32[]{:S(2)}, u32[]{:S(2)}) %collective-permute-start.16) | collective-permute-done | bytes 524320 | tf_op jit(solution)/shard_map/ppermute | solution.py:35
  142.2 3.3 %shard_map.90 = bf16[32,4,1,32,128]{4,3,2,1,0:T(8,128)(2,1)} custom-call(s32[32,4]{1,0:T(8,128)} %copy.43.wanted_ref, bf16[16,16384]{1,0:T(8,128)(2,1)} %collective-permute-done.16.refs_0_, bf16[16,16384]{1,0:T(8,128)(2,1)} %collective-permute-done.17.refs_1_), custom_call_target="tpu_custom_call" | custom-call | flops 1000000000 | bytes 2097152 | tf_op jit(solution)/shard_map/pallas_call | solution.py:82
  145.6 9.5 %all-to-all-done.2.part = bf16[32,4,4,32,128]{4,3,2,1,0:T(8,128)(2,1)} async-done(((bf16[32,4,4,32,128]{4,3,2,1,0:T(8,128)(2,1)}), bf16[32,4,4,32,128]{4,3,2,1,0:T(8,128)(2,1)}, u32[]{:S(2)}, u32[]{:S(2)}) %all-to-all-start.2) | async-done | bytes 4194336 | tf_op jit(solution)/shard_map/all_to_all | solution.py:39
  155.1 4.5 %all-to-all-start.3 = ((bf16[32,4,1,32,128]{4,3,2,1,0:T(8,128)(2,1)}), bf16[32,4,1,32,128]{4,3,2,1,0:T(8,128)(2,1)}, u32[]{:S(2)}, u32[]{:S(2)}) async-start(bf16[32,4,1,32,128]{4,3,2,1,0:T(8,128)(2,1)} %shard_map.90), calls=%async_computation.3 | async-start | bytes 2097152 | tf_op jit(solution)/shard_map/all_to_all | solution.py:39
  159.5 1.0 slice.23.refs_5_
  160.5 4.4 %shard_map.89 = (bf16[512,1024]{1,0:T(8,128)(2,1)S(1)}, bf16[1024,512]{1,0:T(8,128)(2,1)S(1)}) custom-call(s32[1]{0:T(128)} %bitcast.core_ref, s32[8,4]{1,0:T(8,128)S(1)} %copy.44.tgt_ref, s32[8]{0:T(128)S(1)} %bitcast.27, bf16[8,4,128,128]{3,2,1,0:T(8,128)(2,1)S(1)} %bitcast.25, bf16[32,4,4,32,128]{4,3,2,1,0:T(8,128)(2,1)} %all-to-all-done.2.part), custom_call_target="tpu_custom_call" | custom-call | flops 3000000000 | bytes 8388608 | tf_op jit(solution)/shard_map/pallas_call | solution.py:136
  165.0 1.0 copy-done.3
  166.0 4.3 %fusion.refs_4_ = f32[1024,1024]{1,0:T(8,128)} fusion(bf16[1024,512]{1,0:T(8,128)(2,1)S(1)} %get-tuple-element.23, bf16[1024,384]{1,0:T(8,128)(2,1)S(1)} %copy-done.5, bf16[1024,1024]{1,0:T(8,128)(2,1)S(1)} %bitcast.30), kind=kOutput, calls=%fused_computation.2 | convolution fusion | flops 1882718208 | bytes 7864320 | tf_op jit(solution)/shard_map/dot_general | solution.py:319
  170.3 4.8 %all-to-all-done.3.refs_3_ = bf16[32,4,1,32,128]{4,3,2,1,0:T(8,128)(2,1)} async-done(((bf16[32,4,1,32,128]{4,3,2,1,0:T(8,128)(2,1)}), bf16[32,4,1,32,128]{4,3,2,1,0:T(8,128)(2,1)}, u32[]{:S(2)}, u32[]{:S(2)}) %all-to-all-start.3) | async-done | bytes 1048608 | tf_op jit(solution)/shard_map/all_to_all | solution.py:39
  175.2 1.1 copy-done.7
  176.3 9.2 %shard_map.91 = (bf16[1024,1024]{1,0:T(8,128)(2,1)}, bf16[8,2,8,32,128]{4,3,2,1,0:T(8,128)(2,1)S(1)}, bf16[8,2,8,32,128]{4,3,2,1,0:T(8,128)(2,1)S(1)}) custom-call(s32[1]{0:T(128)} %bitcast.core_ref, s32[8,4]{1,0:T(8,128)S(1)} %copy.44.tgt_ref, s32[8]{0:T(128)S(1)} %bitcast.28, bf16[384,1024]{1,0:T(8,128)(2,1)S(1)} %copy-done.7, ...), custom_call_target="tpu_custom_call" | custom-call | flops 6000000000 | bytes 20971520 | tf_op jit(solution)/shard_map/pallas_call | solution.py:228
  185.6 2.6 %collective-permute-done.18 = bf16[8,2,8,32,128]{4,3,2,1,0:T(8,128)(2,1)S(1)} collective-permute-done((bf16[8,2,8,32,128]{4,3,2,1,0:T(8,128)(2,1)S(1)}, bf16[8,2,8,32,128]{4,3,2,1,0:T(8,128)(2,1)S(1)}, u32[]{:S(2)}, u32[]{:S(2)}) %collective-permute-start.18) | collective-permute-done | bytes 1048608 | tf_op jit(solution)/shard_map/ppermute | solution.py:277
  188.3 1.3 add_convert_fusion
  189.6 4.5 %all-to-all-start.4 = ((bf16[16,8,32,128]{3,2,1,0:T(8,128)(2,1)}), bf16[16,8,32,128]{3,2,1,0:T(8,128)(2,1)S(1)}, u32[]{:S(2)}, u32[]{:S(2)}) async-start(bf16[16,8,32,128]{3,2,1,0:T(8,128)(2,1)} %bitcast.14), calls=%async_computation.4 | async-start | bytes 2097152 | tf_op jit(solution)/shard_map/all_to_all | solution.py:39
  194.1 19.0 %all-to-all-done.4.came_ref = bf16[16,8,32,128]{3,2,1,0:T(8,128)(2,1)S(1)} async-done(((bf16[16,8,32,128]{3,2,1,0:T(8,128)(2,1)}), bf16[16,8,32,128]{3,2,1,0:T(8,128)(2,1)S(1)}, u32[]{:S(2)}, u32[]{:S(2)}) %all-to-all-start.4) | async-done | bytes 1048608 | tf_op jit(solution)/shard_map/all_to_all | solution.py:39
  213.2 12.2 %all_to_all.35 = f32[8,32,128]{2,1,0:T(8,128)S(1)} all-to-all(f32[8,32,128]{2,1,0:T(8,128)S(1)} %shard_map.92), channel_id=1, replica_groups=mesh['ylo'=2,'x'=4,'z'=8,'yhi'=2,'core'=2] {'z'}, dimensions={0} | all-to-all | bytes 262144 | tf_op jit(solution)/shard_map/all_to_all | solution.py:39
  225.4 10.3 %all_to_all.36 = f32[8,32,128]{2,1,0:T(8,128)S(1)} all-to-all(f32[8,32,128]{2,1,0:T(8,128)S(1)} %broadcast_in_dim.18), channel_id=1, replica_groups=mesh['ylo'=2,'x'=4,'z'=8,'yhi'=2,'core'=2] {'ylo','x'}, dimensions={0} | all-to-all | bytes 262144 | tf_op jit(solution)/shard_map/all_to_all | solution.py:39
  (57 shorter events, 11.8 us)
Async XLA Ops:
  0.6 28.7 %collective-permute-start.11 = (bf16[32,16384]{1,0:T(8,128)(2,1)}, bf16[32,16384]{1,0:T(8,128)(2,1)}, u32[]{:S(2)}, u32[]{:S(2)}) collective-permute-start(bf16[32,16384]{1,0:T(8,128)(2,1)} %bitcast.35), channel_id=1, source_target_pairs={{0,28},{4,0},{8,4},{12,8},{16,12},{20,16},{24,20},{28,24},{1,29},{... | collective-permute-start | bytes 3145736 | tf_op jit(solution)/shard_map/ppermute | solution.py:35
  6.6 26.4 %collective-permute-start.10 = (bf16[32,16384]{1,0:T(8,128)(2,1)}, bf16[32,16384]{1,0:T(8,128)(2,1)}, u32[]{:S(2)}, u32[]{:S(2)}) collective-permute-start(bf16[32,16384]{1,0:T(8,128)(2,1)} %bitcast.36), channel_id=1, source_target_pairs={{0,4},{4,8},{8,12},{12,16},{16,20},{20,24},{24,28},{28,0},{1,5},{5... | collective-permute-start | bytes 3145736 | tf_op jit(solution)/shard_map/ppermute | solution.py:35
  6.6 15.6 %collective-permute-start = (bf16[32,1024]{1,0:T(8,128)(2,1)}, bf16[32,1024]{1,0:T(8,128)(2,1)S(1)}, u32[]{:S(2)}, u32[]{:S(2)}) collective-permute-start(bf16[32,1024]{1,0:T(8,128)(2,1)} %param.12), channel_id=1, source_target_pairs={{0,130},{2,128},{128,2},{130,0},{1,131},{3,129},{129,3},{131,1},{4... | collective-permute-start | bytes 196616 | tf_op jit(solution)/shard_map/ppermute | solution.py:287
  10.9 11.1 %all-to-all-start = ((s32[32,1,4]{2,1,0:T(1,128)}), s32[32,1,4]{2,1,0:T(1,128)S(1)}, u32[]{:S(2)}, u32[]{:S(2)}) async-start(s32[32,1,4]{2,1,0:T(1,128)} %bitcast.4), calls=%async_computation | async-start | bytes 32768 | tf_op jit(solution)/shard_map/all_to_all | solution.py:39
  29.3 25.6 %collective-permute-start.13 = (bf16[32,16384]{1,0:T(8,128)(2,1)}, bf16[32,16384]{1,0:T(8,128)(2,1)}, u32[]{:S(2)}, u32[]{:S(2)}) collective-permute-start(bf16[32,16384]{1,0:T(8,128)(2,1)} %collective-permute-done.11.refs_2_), channel_id=1, source_target_pairs={{0,28},{4,0},{8,4},{12,8},{16,12},{20,16},{24,20},{28,24},{1,29},{... | collective-permute-start | bytes 3145736 | tf_op jit(solution)/shard_map/ppermute | solution.py:35
  33.0 25.6 %collective-permute-start.12 = (bf16[32,16384]{1,0:T(8,128)(2,1)}, bf16[32,16384]{1,0:T(8,128)(2,1)}, u32[]{:S(2)}, u32[]{:S(2)}) collective-permute-start(bf16[32,16384]{1,0:T(8,128)(2,1)} %collective-permute-done.10.refs_1_), channel_id=1, source_target_pairs={{0,4},{4,8},{8,12},{12,16},{16,20},{20,24},{24,28},{28,0},{1,5},{5... | collective-permute-start | bytes 3145736 | tf_op jit(solution)/shard_map/ppermute | solution.py:35
  37.8 51.3 %all-to-all-start.1 = ((bf16[32,4,3,32,128]{4,3,2,1,0:T(8,128)(2,1)}), bf16[32,4,3,32,128]{4,3,2,1,0:T(8,128)(2,1)S(1)}, u32[]{:S(2)}, u32[]{:S(2)}) async-start(bf16[32,4,3,32,128]{4,3,2,1,0:T(8,128)(2,1)} %shard_map.86), calls=%async_computation.1 | async-start | bytes 6291456 | tf_op jit(solution)/shard_map/all_to_all | solution.py:39
  54.9 24.6 %collective-permute-start.15 = (bf16[32,16384]{1,0:T(8,128)(2,1)}, bf16[32,16384]{1,0:T(8,128)(2,1)}, u32[]{:S(2)}, u32[]{:S(2)}) collective-permute-start(bf16[32,16384]{1,0:T(8,128)(2,1)} %collective-permute-done.13.refs_1_), channel_id=1, source_target_pairs={{0,28},{4,0},{8,4},{12,8},{16,12},{20,16},{24,20},{28,24},{1,29},{... | collective-permute-start | bytes 3145736 | tf_op jit(solution)/shard_map/ppermute | solution.py:35
  58.5 24.4 %collective-permute-start.14 = (bf16[32,16384]{1,0:T(8,128)(2,1)}, bf16[32,16384]{1,0:T(8,128)(2,1)}, u32[]{:S(2)}, u32[]{:S(2)}) collective-permute-start(bf16[32,16384]{1,0:T(8,128)(2,1)} %collective-permute-done.12.refs_0_), channel_id=1, source_target_pairs={{0,4},{4,8},{8,12},{12,16},{16,20},{20,24},{24,28},{28,0},{1,5},{5... | collective-permute-start | bytes 3145736 | tf_op jit(solution)/shard_map/ppermute | solution.py:35
  89.1 66.0 %all-to-all-start.2 = ((bf16[32,4,4,32,128]{4,3,2,1,0:T(8,128)(2,1)}), bf16[32,4,4,32,128]{4,3,2,1,0:T(8,128)(2,1)}, u32[]{:S(2)}, u32[]{:S(2)}) async-start(bf16[32,4,4,32,128]{4,3,2,1,0:T(8,128)(2,1)} %shard_map.88), calls=%async_computation.2 | async-start | bytes 8388608 | tf_op jit(solution)/shard_map/all_to_all | solution.py:39
  95.9 5.6 %collective-permute-start.2 = (bf16[64,1024]{1,0:T(8,128)(2,1)S(1)}, bf16[64,1024]{1,0:T(8,128)(2,1)S(1)}, u32[]{:S(2)}, u32[]{:S(2)}) collective-permute-start(bf16[64,1024]{1,0:T(8,128)(2,1)S(1)} %pad_maximum_fusion.1), channel_id=1, source_target_pairs={{0,28},{4,0},{8,4},{12,8},{16,12},{20,16},{24,20},{28,24},{1,29},{... | collective-permute-start | bytes 393224 | tf_op jit(solution)/shard_map/ppermute | solution.py:35
  97.0 6.3 %collective-permute-start.1 = (bf16[64,1024]{1,0:T(8,128)(2,1)S(1)}, bf16[64,1024]{1,0:T(8,128)(2,1)S(1)}, u32[]{:S(2)}, u32[]{:S(2)}) collective-permute-start(bf16[64,1024]{1,0:T(8,128)(2,1)S(1)} %pad_maximum_fusion.1), channel_id=1, source_target_pairs={{0,4},{4,8},{8,12},{12,16},{16,20},{20,24},{24,28},{28,0},{1,5},{5... | collective-permute-start | bytes 393224 | tf_op jit(solution)/shard_map/ppermute | solution.py:35
  98.7 29.7 %copy-start.9 = (s32[1,1,8,4]{2,3,1,0:T(4,128)S(1)}, s32[1,1,8,4]{2,3,1,0:T(4,128)}, u32[]{:S(2)}) copy-start(s32[1,1,8,4]{2,3,1,0:T(4,128)} %param.8) | copy-start | bytes 388
  101.6 5.0 %collective-permute-start.4 = (bf16[64,1024]{1,0:T(8,128)(2,1)S(1)}, bf16[64,1024]{1,0:T(8,128)(2,1)S(1)}, u32[]{:S(2)}, u32[]{:S(2)}) collective-permute-start(bf16[64,1024]{1,0:T(8,128)(2,1)S(1)} %collective-permute-done.2), channel_id=1, source_target_pairs={{0,28},{4,0},{8,4},{12,8},{16,12},{20,16},{24,20},{28,24},{1,29},{... | collective-permute-start | bytes 393224 | tf_op jit(solution)/shard_map/ppermute | solution.py:35
  103.4 6.2 %collective-permute-start.3 = (bf16[64,1024]{1,0:T(8,128)(2,1)S(1)}, bf16[64,1024]{1,0:T(8,128)(2,1)S(1)}, u32[]{:S(2)}, u32[]{:S(2)}) collective-permute-start(bf16[64,1024]{1,0:T(8,128)(2,1)S(1)} %collective-permute-done.1), channel_id=1, source_target_pairs={{0,4},{4,8},{8,12},{12,16},{16,20},{20,24},{24,28},{28,0},{1,5},{5... | collective-permute-start | bytes 393224 | tf_op jit(solution)/shard_map/ppermute | solution.py:35
  106.5 5.5 %collective-permute-start.6 = (bf16[64,1024]{1,0:T(8,128)(2,1)S(1)}, bf16[64,1024]{1,0:T(8,128)(2,1)S(1)}, u32[]{:S(2)}, u32[]{:S(2)}) collective-permute-start(bf16[64,1024]{1,0:T(8,128)(2,1)S(1)} %collective-permute-done.4), channel_id=1, source_target_pairs={{0,28},{4,0},{8,4},{12,8},{16,12},{20,16},{24,20},{28,24},{1,29},{... | collective-permute-start | bytes 393224 | tf_op jit(solution)/shard_map/ppermute | solution.py:35
  109.6 6.2 %collective-permute-start.5 = (bf16[64,1024]{1,0:T(8,128)(2,1)S(1)}, bf16[64,1024]{1,0:T(8,128)(2,1)S(1)}, u32[]{:S(2)}, u32[]{:S(2)}) collective-permute-start(bf16[64,1024]{1,0:T(8,128)(2,1)S(1)} %collective-permute-done.3), channel_id=1, source_target_pairs={{0,4},{4,8},{8,12},{12,16},{16,20},{20,24},{24,28},{28,0},{1,5},{5... | collective-permute-start | bytes 393224 | tf_op jit(solution)/shard_map/ppermute | solution.py:35
  112.1 9.9 %collective-permute-start.8 = (bf16[32,1024]{1,0:T(8,128)(2,1)S(1)}, bf16[32,1024]{1,0:T(8,128)(2,1)S(1)}, u32[]{:S(2)}, u32[]{:S(2)}) collective-permute-start(bf16[32,1024]{1,0:T(8,128)(2,1)S(1)} %slice.25), channel_id=1, source_target_pairs={{0,28},{4,0},{8,4},{12,8},{16,12},{20,16},{24,20},{28,24},{1,29},{... | collective-permute-start | bytes 196616 | tf_op jit(solution)/shard_map/ppermute | solution.py:35
  115.7 5.6 %collective-permute-start.7 = (bf16[32,1024]{1,0:T(8,128)(2,1)S(1)}, bf16[32,1024]{1,0:T(8,128)(2,1)S(1)}, u32[]{:S(2)}, u32[]{:S(2)}) collective-permute-start(bf16[32,1024]{1,0:T(8,128)(2,1)S(1)} %slice.24), channel_id=1, source_target_pairs={{0,4},{4,8},{8,12},{12,16},{16,20},{20,24},{24,28},{28,0},{1,5},{5... | collective-permute-start | bytes 196616 | tf_op jit(solution)/shard_map/ppermute | solution.py:35
  122.6 5.9 %collective-permute-start.9 = (bf16[512,1024]{1,0:T(8,128)(2,1)}, bf16[512,1024]{1,0:T(8,128)(2,1)}, u32[]{:S(2)}, u32[]{:S(2)}) collective-permute-start(bf16[512,1024]{1,0:T(8,128)(2,1)} %constant_dynamic-update-slice_fusion), channel_id=1, source_target_pairs={{0,1},{1,0},{2,3},{3,2},{4,5},{5,4},{6,7},{7,6},{8,9},{9,8},{10,11... | collective-permute-start | bytes 3145736 | tf_op jit(solution)/shard_map/ppermute | solution.py:295
  124.5 14.7 %collective-permute-start.17 = (bf16[16,16384]{1,0:T(8,128)(2,1)}, bf16[16,16384]{1,0:T(8,128)(2,1)}, u32[]{:S(2)}, u32[]{:S(2)}) collective-permute-start(bf16[16,16384]{1,0:T(8,128)(2,1)} %slice.27), channel_id=1, source_target_pairs={{0,28},{4,0},{8,4},{12,8},{16,12},{20,16},{24,20},{28,24},{1,29},{... | collective-permute-start | bytes 1572872 | tf_op jit(solution)/shard_map/ppermute | solution.py:35
  126.4 15.9 %collective-permute-start.16 = (bf16[16,16384]{1,0:T(8,128)(2,1)}, bf16[16,16384]{1,0:T(8,128)(2,1)}, u32[]{:S(2)}, u32[]{:S(2)}) collective-permute-start(bf16[16,16384]{1,0:T(8,128)(2,1)} %slice.26), channel_id=1, source_target_pairs={{0,4},{4,8},{8,12},{12,16},{16,20},{20,24},{24,28},{28,0},{1,5},{5... | collective-permute-start | bytes 1572872 | tf_op jit(solution)/shard_map/ppermute | solution.py:35
  128.5 3.2 %copy-start = (bf16[1,1,8,4,128,128]{5,4,3,2,1,0:T(8,128)(2,1)S(1)}, bf16[1,1,8,4,128,128]{5,4,3,2,1,0:T(8,128)(2,1)}, u32[]{:S(2)}) copy-start(bf16[1,1,8,4,128,128]{5,4,3,2,1,0:T(8,128)(2,1)} %param.11) | copy-start | bytes 3145732
  128.5 3.2 %copy-start.2 = (s32[1,1,8]{2,1,0:T(1,128)S(1)}, s32[1,1,8]{2,1,0:T(1,128)}, u32[]{:S(2)}) copy-start(s32[1,1,8]{2,1,0:T(1,128)} %param.10) | copy-start | bytes 100
  133.9 0.9 copy-start.4
  134.8 0.9 copy-start.6
  145.5 15.0 %copy-start.1 = (bf16[1,1,8,4,128,128]{5,4,3,2,1,0:T(8,128)(2,1)S(1)}, bf16[1,1,8,4,128,128]{5,4,3,2,1,0:T(8,128)(2,1)}, u32[]{:S(2)}) copy-start(bf16[1,1,8,4,128,128]{5,4,3,2,1,0:T(8,128)(2,1)} %param.11) | copy-start | bytes 3145732
  155.1 20.1 %all-to-all-start.3 = ((bf16[32,4,1,32,128]{4,3,2,1,0:T(8,128)(2,1)}), bf16[32,4,1,32,128]{4,3,2,1,0:T(8,128)(2,1)}, u32[]{:S(2)}, u32[]{:S(2)}) async-start(bf16[32,4,1,32,128]{4,3,2,1,0:T(8,128)(2,1)} %shard_map.90), calls=%async_computation.3 | async-start | bytes 2097152 | tf_op jit(solution)/shard_map/all_to_all | solution.py:39
  160.5 5.5 %copy-start.5 = (bf16[1024,384]{1,0:T(8,128)(2,1)S(1)}, bf16[1024,384]{1,0:T(8,128)(2,1)}, u32[]{:S(2)}) copy-start(bf16[1024,384]{1,0:T(8,128)(2,1)} %copy-done.4) | copy-start | bytes 2359300
  160.5 5.5 %copy-start.8 = (bf16[16,2,32,1024]{3,2,1,0:T(8,128)(2,1)S(1)}, bf16[16,2,32,1024]{3,2,1,0:T(8,128)(2,1)}, u32[]{:S(2)}) copy-start(bf16[16,2,32,1024]{3,2,1,0:T(8,128)(2,1)} %pad_maximum_fusion) | copy-start | bytes 6291460
  165.0 1.0 copy-start.3
  175.2 1.1 copy-start.7
  185.5 2.7 %collective-permute-start.18 = (bf16[8,2,8,32,128]{4,3,2,1,0:T(8,128)(2,1)S(1)}, bf16[8,2,8,32,128]{4,3,2,1,0:T(8,128)(2,1)S(1)}, u32[]{:S(2)}, u32[]{:S(2)}) collective-permute-start(bf16[8,2,8,32,128]{4,3,2,1,0:T(8,128)(2,1)S(1)} %get-tuple-element.27), channel_id=1, source_target_pairs={{0,1},{1,0},{2,3},{3,2},{4,5},{5,4},{6,7},{7,6},{8,9},{9,8},{10,11... | collective-permute-start | bytes 3145736 | tf_op jit(solution)/shard_map/ppermute | solution.py:277
  189.6 23.5 %all-to-all-start.4 = ((bf16[16,8,32,128]{3,2,1,0:T(8,128)(2,1)}), bf16[16,8,32,128]{3,2,1,0:T(8,128)(2,1)S(1)}, u32[]{:S(2)}, u32[]{:S(2)}) async-start(bf16[16,8,32,128]{3,2,1,0:T(8,128)(2,1)} %bitcast.14), calls=%async_computation.4 | async-start | bytes 2097152 | tf_op jit(solution)/shard_map/all_to_all | solution.py:39
